TPU v7x, 512 devices: a whole 4x4x16 slice. The times are simulated.
512 devices in a mesh: gx: 64 (over x, z_lo, core), gy: 8 (over z_hi, y).
Axes of the slice: x: 4, y: 4, z: 16 (z_hi: 2, z_lo: 8; z = z_hi * 8 + z_lo), core: 2. Of those that a mesh axis runs over, the one named last changes fastest.
Arguments:
- model_state: float32 [4, 64, 256, 1024], P(None, None, 'gx', 'gy'), may hold values from -6 to 6
- density: float32 [64], replicated, may hold values from 0.3 to 1.2
- layer_in: bfloat16 [256, 256], replicated, may hold values from -0.375 to 0.375
- layer_bias: float32 [256], replicated, may hold values from -4 to 4
- layer_out: bfloat16 [256, 128], replicated, may hold values from -0.375 to 0.375
- mode_forward: float32 [64, 64], replicated, may hold values from -0.75 to 0.75
- mode_back: float32 [64, 64], replicated, may hold values from -0.75 to 0.75
- mode_rate: float32 [64], replicated, may hold values from 0.002 to 0.025
Outputs:
- new_state: float32 [4, 64, 256, 1024], P(None, None, 'gx', 'gy')
All inputs are finite; a program needn't handle non-finite values.
Results may differ from a plain program's by a relative error of at most 0.0003.
Values sent between devices are 32-bit elements; how exact they have to be, the bound alone decides.
No kernel may reach another device: no remote copies, remote signals or barrier semaphores. Data moves between devices by JAX's collectives and lax.ppermute only.
A program may use at most 64 MiB of HBM per device.

v0:
```python
import math

import jax
import jax.numpy as jnp
import ml_dtypes
import numpy as np
from jax import lax
from jax.experimental import pallas as pl
from jax.experimental.pallas import tpu as pltpu
from jax.sharding import PartitionSpec as P

F32 = jnp.float32
BF16 = jnp.bfloat16
LEVELS = 64
ROWS = 4
LANES = 128
LOW = 16
HIGH = 32


def split_table(table):
    high = table.astype(np.float32).astype(ml_dtypes.bfloat16)
    low = (table - high.astype(np.float64)).astype(np.float32).astype(ml_dtypes.bfloat16)
    return high, low


def east_tables(total, blocks):
    rows = total // blocks
    x = (np.arange(rows)[:, None] + rows * np.arange(blocks)[None, :]).reshape(-1)
    k = np.arange(total)
    angle = 2.0 * math.pi * ((k[:, None] * x[None, :]) % total) / total
    basis = np.where((k <= total // 2)[:, None], np.cos(angle), np.sin(angle))
    scale = np.where((k == 0) | (k == total // 2), 1.0, math.sqrt(2.0)) / math.sqrt(total)
    basis = basis * scale[:, None]
    square = np.sin(2.0 * math.pi * k / total) ** 2
    square[total // 2] = 0.0
    return basis, square.astype(np.float32)


def lane_of(shape):
    return lax.broadcasted_iota(jnp.int32, shape, len(shape) - 1)


def row_of(shape):
    return lax.broadcasted_iota(jnp.int32, shape, 0)


def turn(values, shift, axis):
    size = values.shape[axis]
    return pltpu.roll(values, shift % size, axis) if shift % size else values


def parts(values):
    high = values.astype(BF16)
    return high, (values - high.astype(F32)).astype(BF16)


def dot3(left, right):
    dot = lambda a, b: jnp.dot(a, b, preferred_element_type=F32)
    return dot(left[0], right[0]) + (dot(left[0], right[1]) + dot(left[1], right[0]))


def level_difference(values):
    row = row_of(values.shape)
    last = values.shape[0] - 1
    upper = jnp.where(row < last, turn(values, -1, 0), 0.0)
    lower = jnp.where(row > 0, turn(values, 1, 0), 0.0)
    return upper - lower


def north_difference(values, low=0.0, high=0.0):
    lane = lane_of(values.shape)
    after = jnp.where(lane < LANES - 1, turn(values, -1, 1), high)
    before = jnp.where(lane > 0, turn(values, 1, 1), low)
    return after - before


def plane(ref, field, x):
    return ref[pl.ds(field * LEVELS * ROWS + x, LEVELS, stride=ROWS), :]


def edges_kernel(place, state, x_even, x_odd, y_even, y_odd):
    even_x = place[0] % 2 == 0
    even_y = place[1] % 2 == 0
    for slot, (field, depth) in enumerate(((0, 0), (1, 0), (2, 0), (3, 0), (0, 1))):
        low = plane(state, field, depth)
        high = plane(state, field, ROWS - 1 - depth)
        span = pl.ds(slot * LEVELS, LEVELS)
        x_even[span, :] = jnp.where(even_x, high, low)
        x_odd[span, :] = jnp.where(even_x, low, high)
    lane = lane_of((LEVELS, LANES))
    gathered = jnp.zeros((LEVELS, LANES), F32)
    for field in range(4):
        for x in range(ROWS):
            values = plane(state, field, x)
            slot = field * ROWS + x
            gathered = jnp.where(lane == slot, turn(values, slot, 1), gathered)
            gathered = jnp.where(lane == 16 + slot, turn(values, 17 + slot, 1), gathered)
    flat = jnp.transpose(jnp.concatenate([gathered, jnp.zeros_like(gathered)], axis=0))
    low, high = flat[0:16], flat[16:32]
    y_even[...] = jnp.where(even_y, high, low)
    y_odd[...] = jnp.where(even_y, low, high)


def inner_kernel(state, layer_in, bias, layer_out, star):
    fields = [[plane(state, f, x) for x in range(ROWS)] for f in range(4)]
    columns = jnp.concatenate(
        [jnp.concatenate([fields[f][x] for f in range(4)], axis=0).astype(BF16) for x in range(ROWS)],
        axis=1,
    )
    before = jnp.dot(layer_in[...], columns, preferred_element_type=F32) + bias[...]
    hidden = (before * (1.0 / (1.0 + jnp.exp(-before)))).astype(BF16)
    forcing = jnp.dot(layer_out[...], hidden, preferred_element_type=F32)
    for x in range(ROWS):
        u, v, w, th = (fields[f][x] for f in range(4))
        span = slice(x * LANES, (x + 1) * LANES)
        heating, lift = forcing[:LEVELS, span], forcing[LEVELS:, span]
        for f in range(4):
            here = fields[f][x]
            change = v * north_difference(here) + w * level_difference(here)
            if x == 0:
                change = change + u * fields[f][1]
            elif x == ROWS - 1:
                change = change - u * fields[f][x - 1]
            else:
                change = change + u * (fields[f][x + 1] - fields[f][x - 1])
            value = here - 0.1 * change
            if f == 2:
                value = value + 0.2 * (0.5 * th + lift)
            if f == 3:
                value = value + 0.2 * heating
            star[pl.ds((f * ROWS + x) * LEVELS, LEVELS), :] = value


def outer_kernel(
    place, state, inner, x_even, x_odd, y_even, y_odd, level_up, level_down, forward, star, message
):
    even_x = place[0] % 2 == 0
    even_y = place[1] % 2 == 0
    shape = (LEVELS, LANES)
    lane = lane_of(shape)

    def beyond(slot):
        first = x_even[pl.ds(slot * LEVELS, LEVELS), :]
        second = x_odd[pl.ds(slot * LEVELS, LEVELS), :]
        return jnp.where(even_x, second, first), jnp.where(even_x, first, second)

    low_y = jnp.where(even_y, y_odd[...], y_even[...])
    high_y = jnp.where(even_y, y_even[...], y_odd[...])
    columns = jnp.transpose(jnp.concatenate([low_y, high_y, jnp.zeros((96, LANES), F32)], axis=0))
    columns = columns[:LEVELS]
    outer_x = [beyond(slot) for slot in range(5)]

    whole = [[None] * ROWS for _ in range(4)]
    side_u = [None] * ROWS
    for x in range(ROWS):
        u, v = plane(state, 0, x), plane(state, 1, x)
        for f in range(4):
            slot = f * ROWS + x
            side = jnp.where(lane == 0, turn(columns, -slot, 1), 0.0)
            side = jnp.where(lane == LANES - 1, -turn(columns, LANES - 1 - 16 - slot, 1), side)
            side = 0.1 * v * side
            if f == 0:
                side_u[x] = side
            value = inner[pl.ds(slot * LEVELS, LEVELS), :] + side
            if x == 0:
                value = value + 0.1 * u * outer_x[f][0]
            if x == ROWS - 1:
                value = value - 0.1 * u * outer_x[f][1]
            whole[f][x] = value
            star[pl.ds(slot * LEVELS, LEVELS), :] = value

    def east_star(which, neighbour):
        u, v, w = (outer_x[f][which] for f in range(3))
        second = outer_x[4][which]
        along = (neighbour - second) if which == 0 else (second - neighbour)
        return u - 0.1 * (u * along + v * north_difference(u) + w * level_difference(u))

    padded = [east_star(0, plane(state, 0, 0))] + whole[0] + [east_star(1, plane(state, 0, ROWS - 1))]
    divergence = []
    extra = jnp.where(lane == 0, -0.5 * side_u[ROWS - 1], 0.0)
    extra = jnp.where(lane == LANES - 1, -0.5 * side_u[ROWS - 1], extra)
    extra = jnp.where(lane == 1, 0.5 * turn(side_u[0], 1, 1), extra)
    extra = jnp.where(lane == LANES - 2, 0.5 * turn(side_u[0], -1, 1), extra)
    up, down = level_up[...], level_down[...]
    for x in range(ROWS):
        v, w = whole[1][x], whole[2][x]
        upright = up * turn(w, -1, 0) - down * turn(w, 1, 0)
        divergence.append(0.5 * (padded[x + 2] - padded[x]) + 0.5 * north_difference(v) + upright)
        extra = jnp.where(lane == LOW + x, 0.5 * turn(v, LOW + x, 1), extra)
        extra = jnp.where(lane == HIGH + x, -0.5 * turn(v, HIGH + x + 1, 1), extra)
    modal = dot3(parts(forward[...]), parts(jnp.concatenate(divergence + [extra], axis=1)))
    for r in range(ROWS + 1):
        message[pl.ds(r, LEVELS, stride=ROWS + 1), :] = modal[:, r * LANES : (r + 1) * LANES]


def decay(rate, square):
    lam = rate + square
    root = jnp.sqrt(lam * (1.0 + lam))
    inverse = 1.0 + 2.0 * lam + 2.0 * root
    return root, inverse, 1.0 / inverse


def squarings(rho, count):
    powers = [rho]
    for _ in range(count):
        powers.append(powers[-1] * powers[-1])
    return powers


def lane_powers(powers, exponent):
    product = None
    for bit in range(6):
        factor = jnp.where((exponent & (1 << bit)) != 0, powers[bit], 1.0)
        product = factor if product is None else product * factor
    return product


def solve_kernel(place, rates, received, basis_high, basis_low, square, local, moments):
    blocks = received.shape[0] // (ROWS + 1)
    size = blocks * ROWS
    lane = lane_of((blocks, LANES))
    rows = [received[pl.ds(r, blocks, stride=ROWS + 1), :] for r in range(ROWS + 1)]
    extra = rows[ROWS]
    ends = (lane == 0) | (lane == LANES - 1)
    rows[0] = rows[0] + jnp.where(ends, turn(extra, 1, 0), 0.0)
    inward = jnp.where(lane == 0, turn(extra, -1, 1), turn(extra, 1, 1))
    rows[ROWS - 1] = rows[ROWS - 1] + jnp.where(ends, turn(inward, -1, 0), 0.0)
    outside = []
    for r in range(ROWS):
        value = jnp.where((lane == 0), turn(extra, -(HIGH + r), 1), 0.0)
        value = jnp.where((lane == 1), turn(extra, 1 - (LOW + r), 1), value)
        value = jnp.where((lane == 2), turn(extra, 2 - (HIGH + r), 1), value)
        outside.append(jnp.where((lane == 3), turn(extra, 3 - (LOW + r), 1), value))
    right = jnp.concatenate(
        [jnp.concatenate(rows[:ROWS], axis=0), jnp.concatenate(outside, axis=0)], axis=1
    )
    spectral = dot3((basis_high[...], basis_low[...]), parts(right))
    source, ext = spectral[:, :LANES], spectral[:, LANES:]

    rate = rates[place[0]]
    _, _, rho = decay(rate, square[...])
    powers = squarings(rho, 6)
    lane = lane_of((size, LANES))
    ahead, behind = source, source
    for bit in range(6):
        shift = 2 << bit
        ahead = ahead + powers[bit] * jnp.where(lane >= shift, turn(ahead, shift, 1), 0.0)
        behind = behind + powers[bit] * jnp.where(lane < LANES - shift, turn(behind, -shift, 1), 0.0)
    half = lane >> 1
    rising = lane_powers(powers, half)
    falling = lane_powers(powers, 63 - half)
    odd = (lane & 1) != 0
    first = jnp.broadcast_to(ext[:, 0:1], (size, LANES))
    second = jnp.broadcast_to(ext[:, 1:2], (size, LANES))
    border = rho * jnp.where(odd, rising * second, falling * first)
    local[...] = ahead + behind - source + border
    weight = jnp.where((lane == 1) | (lane == 2), powers[6] * rho, 1.0)
    column = jnp.where(lane < 2, turn(rho * ahead, 2, 1), turn(rho * behind, 2, 1)) + ext * weight
    column = jnp.where(lane < 4, column, 0.0)
    across = jnp.transpose(column)[:8]
    for j in range(8):
        moments[pl.ds(j * 8, 8), :] = across


def back_kernel(place, rates, local, moments, basis_high, basis_low, square, square_row, message):
    size = local.shape[0]
    blocks = size // ROWS
    rate = rates[place[0]]
    mine = place[1]
    root, inverse, rho = decay(rate, square_row[...])
    r64 = squarings(rho, 6)[6]
    r128 = r64 * r64
    r256 = r128 * r128
    row = row_of((8, size))
    carry = jnp.zeros((8, size), F32)
    for j in range(8):
        from_low = (mine - j - 1) & 7
        from_high = (j - mine - 1) & 7
        exponent = jnp.where(row < 2, from_low, from_high)
        weight = jnp.where((exponent & 1) != 0, r64, 1.0)
        weight = weight * jnp.where((exponent & 2) != 0, r128, 1.0)
        weight = weight * jnp.where((exponent & 4) != 0, r256, 1.0)
        carry = carry + weight * moments[pl.ds(j * 8, 8), :]
    carry = carry / (1.0 - r256 * r256)
    own = moments[pl.ds(pl.multiple_of(mine * 8, 8), 8), :]
    scale = -1.0 / root[0:1]
    after = scale * (own[0:1] + carry[0:1] * r64[0:1] + carry[2:3] * inverse[0:1])
    before = scale * (own[3:4] + carry[3:4] * r64[0:1] + carry[1:2] * inverse[0:1])
    stacked = jnp.concatenate([carry[0:4], after, before, jnp.zeros((LANES - 6, size), F32)], axis=0)
    columns = jnp.transpose(stacked)

    root, _, rho = decay(rate, square[...])
    powers = squarings(rho, 5)
    lane = lane_of((size, LANES))
    half = lane >> 1
    odd = (lane & 1) != 0
    spread = lambda i: jnp.broadcast_to(columns[:, i : i + 1], (size, LANES))
    total = local[...] + lane_powers(powers, half) * jnp.where(odd, spread(1), spread(0))
    total = total + lane_powers(powers, 63 - half) * jnp.where(odd, spread(3), spread(2))
    total = -total / root
    ext = jnp.where((lane == 4) | (lane == 5), columns, 0.0)
    pressure = dot3(
        (basis_high[...], basis_low[...]), parts(jnp.concatenate([total, ext], axis=1))
    )
    lane = lane_of((blocks, LANES))
    inside = [pressure[r * blocks : (r + 1) * blocks, :LANES] for r in range(ROWS)]
    left = turn(inside[ROWS - 1], 1, 0)
    right = turn(inside[0], -1, 0)
    extra = jnp.where((lane == 0) | (lane == LANES - 1), left, 0.0)
    extra = jnp.where(lane == 1, turn(right, 1, 1), extra)
    extra = jnp.where(lane == LANES - 2, turn(right, -1, 1), extra)
    for r in range(ROWS):
        outside = pressure[r * blocks : (r + 1) * blocks, LANES:]
        extra = jnp.where(lane == HIGH + r, turn(outside, HIGH + r - 4, 1), extra)
        extra = jnp.where(lane == LOW + r, turn(outside, LOW + r - 5, 1), extra)
        message[pl.ds(r, blocks, stride=ROWS + 1), :] = inside[r]
    message[pl.ds(ROWS, blocks, stride=ROWS + 1), :] = extra


def final_kernel(received, sent, star, back, rate, out):
    lane = lane_of((LEVELS, LANES))
    p = [received[pl.ds(r, LEVELS, stride=ROWS + 1), :] for r in range(ROWS)]
    extra = received[pl.ds(ROWS, LEVELS, stride=ROWS + 1), :]
    low = [turn(extra, -(LOW + r), 1) for r in range(ROWS)]
    high = [turn(extra, LANES - 1 - (HIGH + r), 1) for r in range(ROWS)]
    four_rate = 4.0 * rate[...]

    def next_row(r, opposite):
        here = p[r]
        divergence = sent[pl.ds(r, LEVELS, stride=ROWS + 1), :]
        plus = jnp.where(lane < LANES - 2, turn(here, -2, 1), turn(high[r], -1, 1))
        minus = jnp.where(lane > 1, turn(here, 2, 1), turn(low[r], 1, 1))
        return (
            2.0 * here
            - opposite
            + four_rate * here
            + (2.0 * here - plus - minus)
            + 4.0 * divergence
        )

    ends = (lane == 0) | (lane == LANES - 1)
    before = jnp.where(ends, extra, next_row(1, p[3]))
    inward = jnp.where(lane == 0, turn(extra, -1, 1), turn(extra, 1, 1))
    after = jnp.where(ends, inward, next_row(2, p[0]))
    padded = [before] + p + [after]
    slopes = [0.5 * (padded[x + 2] - padded[x]) for x in range(ROWS)]
    slopes += [0.5 * north_difference(p[x], low[x], high[x]) for x in range(ROWS)]
    matrix = back[...]
    slope = dot3(parts(matrix), parts(jnp.concatenate(slopes, axis=1)))
    lift = dot3(parts(0.5 * level_difference(matrix)), parts(jnp.concatenate(p, axis=1)))
    for x in range(ROWS):
        take = lambda values, i: values[:, i * LANES : (i + 1) * LANES]
        for f, change in ((0, take(slope, x)), (1, take(slope, ROWS + x)), (2, take(lift, x)), (3, None)):
            value = star[pl.ds((f * ROWS + x) * LEVELS, LEVELS), :]
            if change is not None:
                value = value - change
            out[pl.ds(f * LEVELS * ROWS + x, LEVELS, stride=ROWS), :] = value


def call(kernel, shapes, smem, args, name):
    vmem = pl.BlockSpec(memory_space=pltpu.VMEM)
    scalar = pl.BlockSpec(memory_space=pltpu.SMEM)
    return pl.pallas_call(
        kernel,
        out_shape=[jax.ShapeDtypeStruct(s, F32) for s in shapes],
        in_specs=[scalar] * smem + [vmem] * (len(args) - smem),
        out_specs=[vmem] * len(shapes),
        compiler_params=pltpu.CompilerParams(vmem_limit_bytes=32 * 1024 * 1024),
        name=name,
    )(*args)


def swap(values, axis, odd):
    count = lax.axis_size(axis)
    pairs = []
    for i in range(odd, count + odd, 2):
        pairs += [(i % count, (i + 1) % count), ((i + 1) % count, i % count)]
    return lax.ppermute(values, axis, pairs)


def exchange(values, axis, groups, rows):
    shaped = values.reshape(groups, 1, rows * values.shape[1])
    return lax.all_to_all(shaped, axis, 0, 0, tiled=True).reshape(values.shape)


def on_device(
    model_state, density, layer_in, layer_bias, layer_out, mode_forward, mode_back, mode_rate
):
    blocks = lax.axis_size("gx")
    total_east = blocks * ROWS
    place = jnp.stack([lax.axis_index("gx"), lax.axis_index("gy")]).astype(jnp.int32)
    state = model_state.reshape(4 * LEVELS * ROWS, LANES)
    basis, square = east_tables(total_east, blocks)
    forward_high, forward_low = split_table(basis)
    back_high, back_low = split_table(np.ascontiguousarray(basis.T))
    square_wide = np.ascontiguousarray(np.broadcast_to(square[:, None], (total_east, LANES)))
    square_row = np.ascontiguousarray(np.broadcast_to(square[None, :], (8, total_east)))

    x_even, x_odd, y_even, y_odd = call(
        edges_kernel,
        [(5 * LEVELS, LANES)] * 2 + [(16, LANES)] * 2,
        1,
        [place, state],
        "edges",
    )
    got_y_odd = swap(y_odd, "gy", 1)
    got_x_odd = swap(x_odd, "gx", 1)
    got_y_even = swap(y_even, "gy", 0)
    got_x_even = swap(x_even, "gx", 0)
    (inner,) = call(
        inner_kernel,
        [(16 * LEVELS, LANES)],
        0,
        [state, layer_in.T, layer_bias[:, None], layer_out.T],
        "inner",
    )
    zero = jnp.zeros((1,), F32)
    level_up = jnp.concatenate([0.5 * density[1:] / density[:-1], zero])
    level_down = jnp.concatenate([zero, 0.5 * density[:-1] / density[1:]])
    star, message = call(
        outer_kernel,
        [(16 * LEVELS, LANES), (blocks * (ROWS + 1), LANES)],
        1,
        [
            place,
            state,
            inner,
            got_x_even,
            got_x_odd,
            got_y_even,
            got_y_odd,
            level_up[:, None],
            level_down[:, None],
            mode_forward,
        ],
        "outer",
    )
    modal = exchange(message, "gx", blocks, ROWS + 1)
    local, moments = call(
        solve_kernel,
        [(total_east, LANES), (64, total_east)],
        2,
        [place, mode_rate, modal, forward_high, forward_low, square_wide],
        "solve",
    )
    moments = lax.all_to_all(
        moments.reshape(8, 8, total_east), "gy", 0, 0, tiled=True
    ).reshape(64, total_east)
    (reply,) = call(
        back_kernel,
        [(total_east * (ROWS + 1) // ROWS, LANES)],
        2,
        [place, mode_rate, local, moments, back_high, back_low, square_wide, square_row],
        "back",
    )
    pressure = exchange(reply, "gx", blocks, ROWS + 1)
    (out,) = call(
        final_kernel,
        [(4 * LEVELS * ROWS, LANES)],
        0,
        [pressure, message, star, mode_back, mode_rate[:, None]],
        "final",
    )
    return out.reshape(model_state.shape)


def solution(mesh):
    return jax.shard_map(
        on_device,
        mesh=mesh,
        in_specs=(P(None, None, "gx", "gy"), P(), P(), P(), P(), P(), P(), P()),
        out_specs=P(None, None, "gx", "gy"),
        check_vma=False,
    )
```

profile of v0, /device:TPU:1, one launch (start us, length us, event | category | flops | bytes accessed | tf_op | source)
XLA Modules:
  0.0 115.5 jit_solution(7501522005074702572)
XLA Ops:
  0.0 0.1 pad_add_fusion.place
  0.1 0.0 copy-start
  0.1 1.0 copy-done
  1.1 0.0 copy-start.1
  1.1 0.9 edges.1
  2.0 8.8 %collective-permute-start = (f32[320,128]{1,0:T(8,128)S(1)}, f32[320,128]{1,0:T(8,128)S(1)}, u32[]{:S(2)}, u32[]{:S(2)}) collective-permute-start(f32[320,128]{1,0:T(8,128)S(1)} %get-tuple-element.13), channel_id=1, source_target_pairs={{0,8},{8,0},{16,24},{24,16},{32,40},{40,32},{48,56},{56,48},{64,72... | collective-permute-start | bytes 491528 | tf_op jit(solution)/shard_map/ppermute | solution.py:379
  10.8 1.9 %collective-permute-start.1 = (f32[320,128]{1,0:T(8,128)S(1)}, f32[320,128]{1,0:T(8,128)S(1)}, u32[]{:S(2)}, u32[]{:S(2)}) collective-permute-start(f32[320,128]{1,0:T(8,128)S(1)} %get-tuple-element.14), channel_id=1, source_target_pairs={{8,16},{16,8},{24,32},{32,24},{40,48},{48,40},{56,64},{64,56},{72,... | collective-permute-start | bytes 491528 | tf_op jit(solution)/shard_map/ppermute | solution.py:379
  12.8 0.0 copy-start.12
  12.8 1.9 %collective-permute-start.2 = (f32[16,128]{1,0:T(8,128)S(1)}, f32[16,128]{1,0:T(8,128)S(1)}, u32[]{:S(2)}, u32[]{:S(2)}) collective-permute-start(f32[16,128]{1,0:T(8,128)S(1)} %get-tuple-element.15), channel_id=1, source_target_pairs={{0,1},{1,0},{2,3},{3,2},{4,5},{5,4},{6,7},{7,6},{8,9},{9,8},{10,11... | collective-permute-start | bytes 24584 | tf_op jit(solution)/shard_map/ppermute | solution.py:379
  14.7 13.6 %collective-permute-start.3 = (f32[16,128]{1,0:T(8,128)S(1)}, f32[16,128]{1,0:T(8,128)S(1)}, u32[]{:S(2)}, u32[]{:S(2)}) collective-permute-start(f32[16,128]{1,0:T(8,128)S(1)} %get-tuple-element.16), channel_id=1, source_target_pairs={{1,2},{2,1},{3,4},{4,3},{5,6},{6,5},{7,0},{0,7},{9,10},{10,9},{11,... | collective-permute-start | bytes 24584 | tf_op jit(solution)/shard_map/ppermute | solution.py:379
  28.3 0.0 copy-done.12
  28.3 0.1 multiply_divide_fusion
  28.4 0.1 maximum_bitcast_fusion
  28.5 0.1 copy.29.level_up
  28.6 0.1 copy.30.level_down
  28.7 1.0 copy.26
  29.7 0.0 copy-start.13
  29.7 0.7 copy-done.13
  30.4 0.0 copy-start.11
  30.4 0.1 copy.28.bias
  30.5 0.7 copy-done.11
  31.2 0.1 copy.27
  31.3 0.0 copy-done.1
  31.3 0.0 copy-start.7
  31.3 0.6 inner.1
  31.9 0.0 collective-permute-done.2.y_even
  31.9 0.0 collective-permute-done.3.y_odd
  32.0 0.0 collective-permute-done.x_even
  32.0 0.0 collective-permute-done.1.x_odd
  32.0 0.1 copy-done.7
  32.1 0.0 copy-start.4
  32.1 1.3 %outer.1 = (f32[1024,128]{1,0:T(8,128)S(1)}, f32[320,128]{1,0:T(8,128)S(1)}) custom-call(s32[2]{0:T(128)S(1)} %pad_add_fusion.place, f32[1024,128]{1,0:T(8,128)S(1)} %bitcast.20, f32[1024,128]{1,0:T(8,128)S(1)} %inner.1, f32[320,128]{1,0:T(8,128)S(1)} %collective-permute-done.x_even, f32[320,128]{1,0:T(8,128)S(1)} %collective-permute-done.1.x_odd, ...), custom_call_target="tpu_custom_call" | custom-call | tf_op jit(solution)/shard_map/outer/pallas_call | solution.py:364
  33.4 0.0 copy-start.2
  33.4 0.0 copy-start.3
  33.4 28.2 %all_to_all.15 = f32[64,1,640]{2,1,0:T(1,128)S(1)} all-to-all(f32[64,1,640]{2,1,0:T(1,128)S(1)} %bitcast.22), channel_id=1, replica_groups=mesh['gx'=64,'gy'=8] {'gx'}, dimensions={0} | all-to-all | bytes 327680 | tf_op jit(solution)/shard_map/all_to_all | solution.py:384
  61.6 0.0 copy-start.10
  61.6 0.0 copy-done.4
  61.6 0.0 copy-done.2
  61.6 0.0 copy-done.3
  61.6 0.6 copy-done.10
  62.3 0.0 copy-start.6
  62.3 0.0 copy-start.9
  62.3 1.6 %solve.1 = (f32[256,128]{1,0:T(8,128)S(1)}, f32[64,256]{1,0:T(8,128)S(1)}) custom-call(s32[2]{0:T(128)S(1)} %pad_add_fusion.place, f32[64]{0:T(128)S(1)} %copy-done.10, f32[320,128]{1,0:T(8,128)S(1)} %bitcast.21, bf16[256,256]{1,0:T(8,128)(2,1)S(1)} %copy-done.3, bf16[256,256]{1,0:T(8,128)(2,1)S(1)} %copy-done.4, f32[256,128]{1,0:T(8,128)S(1)} %copy-done.2), custom_call_target="tpu_custom_call" | custom-call | tf_op jit(solution)/shard_map/solve/pallas_call | solution.py:364
  63.9 0.0 copy-start.5
  63.9 24.7 %all_to_all.16 = f32[8,8,256]{2,1,0:T(8,128)S(1)} all-to-all(f32[8,8,256]{2,1,0:T(8,128)S(1)} %bitcast.27), channel_id=1, replica_groups=mesh['gx'=64,'gy'=8] {'gy'}, dimensions={0} | all-to-all | bytes 131072 | tf_op jit(solution)/shard_map/all_to_all | solution.py:447
  88.6 0.0 copy-done.6
  88.6 0.0 copy-done.9
  88.6 0.0 copy-done.5
  88.6 2.0 %back.2 = f32[320,128]{1,0:T(8,128)} custom-call(s32[2]{0:T(128)S(1)} %pad_add_fusion.place, f32[64]{0:T(128)S(1)} %copy-done.10, f32[256,128]{1,0:T(8,128)S(1)} %get-tuple-element.18.local, f32[64,256]{1,0:T(8,128)S(1)} %bitcast.25, bf16[256,256]{1,0:T(8,128)(2,1)S(1)} %copy-done.5, bf16[256,256]{1,0:T(8,128)(2,1)S(1)} %copy-done.6, ...), custom_call_target="tpu_custom_call" | custom-call | tf_op jit(solution)/shard_map/back/pallas_call | solution.py:364
  90.6 7.9 %all-to-all-start.2 = ((f32[64,1,640]{2,1,0:T(1,128)}), f32[64,1,640]{2,1,0:T(1,128)S(1)}, u32[]{:S(2)}, u32[]{:S(2)}) async-start(f32[64,1,640]{2,1,0:T(1,128)} %bitcast.12), calls=%async_computation.2 | async-start | bytes 327680 | tf_op jit(solution)/shard_map/all_to_all | solution.py:384
  98.5 0.0 copy-start.8
  98.5 0.1 copy.33.rate
  98.6 15.5 %all-to-all-done.2 = f32[64,1,640]{2,1,0:T(1,128)S(1)} async-done(((f32[64,1,640]{2,1,0:T(1,128)}), f32[64,1,640]{2,1,0:T(1,128)S(1)}, u32[]{:S(2)}, u32[]{:S(2)}) %all-to-all-start.2) | async-done | bytes 163872 | tf_op jit(solution)/shard_map/all_to_all | solution.py:384
  114.1 0.0 copy-done.8
  114.1 1.4 %final.1 = f32[1024,128]{1,0:T(8,128)} custom-call(f32[320,128]{1,0:T(8,128)S(1)} %bitcast.23, f32[320,128]{1,0:T(8,128)S(1)} %get-tuple-element.17.sent, f32[1024,128]{1,0:T(8,128)S(1)} %get-tuple-element.20.star, f32[64,64]{1,0:T(8,128)S(1)} %copy-done.8, f32[64,1]{1,0:T(8,128)S(1)} %copy.33.rate), custom_call_target="tpu_custom_call" | custom-call | tf_op jit(solution)/shard_map/final/pallas_call | solution.py:364
Async XLA Ops:
  0.1 1.0 copy-start
  1.1 30.2 %copy-start.1 = (f32[4,64,4,128]{3,2,1,0:T(4,128)S(1)}, f32[4,64,4,128]{3,2,1,0:T(4,128)}, u32[]{:S(2)}) copy-start(f32[4,64,4,128]{3,2,1,0:T(4,128)} %param.14) | copy-start | bytes 1572868
  2.0 29.9 %collective-permute-start = (f32[320,128]{1,0:T(8,128)S(1)}, f32[320,128]{1,0:T(8,128)S(1)}, u32[]{:S(2)}, u32[]{:S(2)}) collective-permute-start(f32[320,128]{1,0:T(8,128)S(1)} %get-tuple-element.13), channel_id=1, source_target_pairs={{0,8},{8,0},{16,24},{24,16},{32,40},{40,32},{48,56},{56,48},{64,72... | collective-permute-start | bytes 491528 | tf_op jit(solution)/shard_map/ppermute | solution.py:379
  10.8 21.1 %collective-permute-start.1 = (f32[320,128]{1,0:T(8,128)S(1)}, f32[320,128]{1,0:T(8,128)S(1)}, u32[]{:S(2)}, u32[]{:S(2)}) collective-permute-start(f32[320,128]{1,0:T(8,128)S(1)} %get-tuple-element.14), channel_id=1, source_target_pairs={{8,16},{16,8},{24,32},{32,24},{40,48},{48,40},{56,64},{64,56},{72,... | collective-permute-start | bytes 491528 | tf_op jit(solution)/shard_map/ppermute | solution.py:379
  12.8 15.5 %copy-start.12 = (f32[64]{0:T(128)S(1)}, f32[64]{0:T(128)}, u32[]{:S(2)}) copy-start(f32[64]{0:T(128)} %param.15) | copy-start | bytes 772
  12.8 19.2 %collective-permute-start.2 = (f32[16,128]{1,0:T(8,128)S(1)}, f32[16,128]{1,0:T(8,128)S(1)}, u32[]{:S(2)}, u32[]{:S(2)}) collective-permute-start(f32[16,128]{1,0:T(8,128)S(1)} %get-tuple-element.15), channel_id=1, source_target_pairs={{0,1},{1,0},{2,3},{3,2},{4,5},{5,4},{6,7},{7,6},{8,9},{9,8},{10,11... | collective-permute-start | bytes 24584 | tf_op jit(solution)/shard_map/ppermute | solution.py:379
  14.7 17.2 %collective-permute-start.3 = (f32[16,128]{1,0:T(8,128)S(1)}, f32[16,128]{1,0:T(8,128)S(1)}, u32[]{:S(2)}, u32[]{:S(2)}) collective-permute-start(f32[16,128]{1,0:T(8,128)S(1)} %get-tuple-element.16), channel_id=1, source_target_pairs={{1,2},{2,1},{3,4},{4,3},{5,6},{6,5},{7,0},{0,7},{9,10},{10,9},{11,... | collective-permute-start | bytes 24584 | tf_op jit(solution)/shard_map/ppermute | solution.py:379
  29.7 0.7 copy-start.13
  30.4 0.8 copy-start.11
  31.3 0.8 copy-start.7
  32.1 29.5 %copy-start.4 = (bf16[256,256]{1,0:T(8,128)(2,1)S(1)}, bf16[256,256]{1,0:T(8,128)(2,1)}, u32[]{:S(2)}) copy-start(bf16[256,256]{1,0:T(8,128)(2,1)} %constant.26.clone.basis_low) | copy-start | bytes 393220
  33.4 28.2 %copy-start.2 = (f32[256,128]{1,0:T(8,128)S(1)}, f32[256,128]{1,0:T(8,128)}, u32[]{:S(2)}) copy-start(f32[256,128]{1,0:T(8,128)} %constant.27.clone.square) | copy-start | bytes 393220
  33.4 28.2 %copy-start.3 = (bf16[256,256]{1,0:T(8,128)(2,1)S(1)}, bf16[256,256]{1,0:T(8,128)(2,1)}, u32[]{:S(2)}) copy-start(bf16[256,256]{1,0:T(8,128)(2,1)} %constant.25.clone.basis_high) | copy-start | bytes 393220
  61.6 0.7 copy-start.10
  62.3 26.3 %copy-start.6 = (bf16[256,256]{1,0:T(8,128)(2,1)S(1)}, bf16[256,256]{1,0:T(8,128)(2,1)}, u32[]{:S(2)}) copy-start(bf16[256,256]{1,0:T(8,128)(2,1)} %constant.29.clone.basis_low) | copy-start | bytes 393220
  62.3 26.3 %copy-start.9 = (f32[8,256]{1,0:T(8,128)S(1)}, f32[8,256]{1,0:T(8,128)}, u32[]{:S(2)}) copy-start(f32[8,256]{1,0:T(8,128)} %constant.30.clone.square_row) | copy-start | bytes 24580
  63.9 24.7 %copy-start.5 = (bf16[256,256]{1,0:T(8,128)(2,1)S(1)}, bf16[256,256]{1,0:T(8,128)(2,1)}, u32[]{:S(2)}) copy-start(bf16[256,256]{1,0:T(8,128)(2,1)} %constant.28.clone.basis_high) | copy-start | bytes 393220
  90.6 23.5 %all-to-all-start.2 = ((f32[64,1,640]{2,1,0:T(1,128)}), f32[64,1,640]{2,1,0:T(1,128)S(1)}, u32[]{:S(2)}, u32[]{:S(2)}) async-start(f32[64,1,640]{2,1,0:T(1,128)} %bitcast.12), calls=%async_computation.2 | async-start | bytes 327680 | tf_op jit(solution)/shard_map/all_to_all | solution.py:384
  98.5 15.6 %copy-start.8 = (f32[64,64]{1,0:T(8,128)S(1)}, f32[64,64]{1,0:T(8,128)}, u32[]{:S(2)}) copy-start(f32[64,64]{1,0:T(8,128)} %back.3) | copy-start | bytes 49156
where the time goes:
time: 116 us; the launch traced here: 115 us
  blocking collectives  52.8 us (46%)
  starting transfers between devices  34.1 us (29%)
  waiting for transfers between devices  15.5 us (13%)
  Pallas kernels  7.92 us (7%)
  local copies, waits for them, and re-layouts  4.74 us (4%)
    all_to_all x1, blocking collectives, exchange(): return lax.all_to_all(shaped, axis, 0, 0, tiled=True).reshape(values.shape)  28.2 us
    ppermute x4, starting transfers between devices, swap(): return lax.ppermute(values, axis, pairs)  26.2 us
    all_to_all x1, blocking collectives, on_device(): lax.all_to_all(moments.reshape(8, 8, total_east), 'gy', 0, 0, tiled=True)  24.7 us
    all_to_all x1, waiting for transfers between devices, exchange(): return lax.all_to_all(shaped, axis, 0, 0, tiled=True).reshape(values.shape)  15.5 us
    pallas_call x6, Pallas kernels, call(): pl.pallas_call(kernel, out_shape=[jax.ShapeDtypeStruct(s, F32) for s in s...  7.92 us
    all_to_all x1, starting transfers between devices, exchange(): return lax.all_to_all(shaped, axis, 0, 0, tiled=True).reshape(values.shape)  7.88 us
    unnamed x30, local copies, waits for them, and re-layouts  4.32 us
  transfers between devices with their start and end apart: 5, of which 1 were waited for; matrix products, arithmetic and copies ran while one was open for 1% of the time, Pallas kernels for 1%

commit v1 on v0

--- a/solution.py
+++ b/solution.py
@@ -32,8 +32,7 @@
     basis = np.where((k <= total // 2)[:, None], np.cos(angle), np.sin(angle))
     scale = np.where((k == 0) | (k == total // 2), 1.0, math.sqrt(2.0)) / math.sqrt(total)
     basis = basis * scale[:, None]
-    square = np.sin(2.0 * math.pi * k / total) ** 2
-    square[total // 2] = 0.0
+    square = np.sin(math.pi * k / total) ** 2
     return basis, square.astype(np.float32)
 
 
@@ -178,20 +177,19 @@
 
     padded = [east_star(0, plane(state, 0, 0))] + whole[0] + [east_star(1, plane(state, 0, ROWS - 1))]
     divergence = []
-    extra = jnp.where(lane == 0, -0.5 * side_u[ROWS - 1], 0.0)
-    extra = jnp.where(lane == LANES - 1, -0.5 * side_u[ROWS - 1], extra)
-    extra = jnp.where(lane == 1, 0.5 * turn(side_u[0], 1, 1), extra)
-    extra = jnp.where(lane == LANES - 2, 0.5 * turn(side_u[0], -1, 1), extra)
+    extra = [-0.5 * side_u[ROWS - 1], 0.5 * side_u[0]]
     up, down = level_up[...], level_down[...]
     for x in range(ROWS):
         v, w = whole[1][x], whole[2][x]
         upright = up * turn(w, -1, 0) - down * turn(w, 1, 0)
         divergence.append(0.5 * (padded[x + 2] - padded[x]) + 0.5 * north_difference(v) + upright)
-        extra = jnp.where(lane == LOW + x, 0.5 * turn(v, LOW + x, 1), extra)
-        extra = jnp.where(lane == HIGH + x, -0.5 * turn(v, HIGH + x + 1, 1), extra)
-    modal = dot3(parts(forward[...]), parts(jnp.concatenate(divergence + [extra], axis=1)))
-    for r in range(ROWS + 1):
-        message[pl.ds(r, LEVELS, stride=ROWS + 1), :] = modal[:, r * LANES : (r + 1) * LANES]
+        low, high = LOW + x // 2, HIGH + x // 2
+        value = jnp.where(lane == low, 0.5 * turn(v, low, 1), extra[x % 2])
+        extra[x % 2] = jnp.where(lane == high, -0.5 * turn(v, high + 1, 1), value)
+    pieces = [divergence[0], divergence[2], extra[0], divergence[1], divergence[3], extra[1]]
+    modal = dot3(parts(forward[...]), parts(jnp.concatenate(pieces, axis=1)))
+    for i in range(6):
+        message[pl.ds(i, LEVELS, stride=6), :] = modal[:, i * LANES : (i + 1) * LANES]
 
 
 def decay(rate, square):
@@ -217,26 +215,29 @@
 
 
 def solve_kernel(place, rates, received, basis_high, basis_low, square, local, moments):
-    blocks = received.shape[0] // (ROWS + 1)
-    size = blocks * ROWS
+    blocks = received.shape[0] // 6
+    half_size = blocks * 2
+    size = half_size * 2
     lane = lane_of((blocks, LANES))
-    rows = [received[pl.ds(r, blocks, stride=ROWS + 1), :] for r in range(ROWS + 1)]
-    extra = rows[ROWS]
     ends = (lane == 0) | (lane == LANES - 1)
-    rows[0] = rows[0] + jnp.where(ends, turn(extra, 1, 0), 0.0)
-    inward = jnp.where(lane == 0, turn(extra, -1, 1), turn(extra, 1, 1))
-    rows[ROWS - 1] = rows[ROWS - 1] + jnp.where(ends, turn(inward, -1, 0), 0.0)
-    outside = []
-    for r in range(ROWS):
-        value = jnp.where((lane == 0), turn(extra, -(HIGH + r), 1), 0.0)
-        value = jnp.where((lane == 1), turn(extra, 1 - (LOW + r), 1), value)
-        value = jnp.where((lane == 2), turn(extra, 2 - (HIGH + r), 1), value)
-        outside.append(jnp.where((lane == 3), turn(extra, 3 - (LOW + r), 1), value))
-    right = jnp.concatenate(
-        [jnp.concatenate(rows[:ROWS], axis=0), jnp.concatenate(outside, axis=0)], axis=1
-    )
+    even = place[1] < 4
+    inside, outside = [], [None, None]
+    for h in range(2):
+        first, second, extra = (received[pl.ds(3 * h + j, blocks, stride=6), :] for j in range(3))
+        first = first + jnp.where(ends & even, turn(extra, 1, 0), 0.0)
+        second = second + jnp.where(ends & ~even, turn(extra, -1, 0), 0.0)
+        inside.append(jnp.concatenate([first, second], axis=0))
+        for r in range(2):
+            value = jnp.zeros_like(extra) if outside[r] is None else outside[r]
+            for i in range(4):
+                at = 4 * h + i
+                value = jnp.where(lane == at, turn(extra, at - (HIGH, LOW)[i % 2] - r, 1), value)
+            outside[r] = value
+    right = jnp.concatenate(inside + [jnp.concatenate(outside, axis=0)], axis=1)
     spectral = dot3((basis_high[...], basis_low[...]), parts(right))
-    source, ext = spectral[:, :LANES], spectral[:, LANES:]
+    source = jnp.concatenate([spectral[:, :LANES], spectral[:, LANES : 2 * LANES]], axis=0)
+    ext = spectral[:, 2 * LANES :]
+    ext = jnp.concatenate([ext, turn(ext, -4, 1)], axis=0)
 
     rate = rates[place[0]]
     _, _, rho = decay(rate, square[...])
@@ -259,29 +260,31 @@
     column = jnp.where(lane < 2, turn(rho * ahead, 2, 1), turn(rho * behind, 2, 1)) + ext * weight
     column = jnp.where(lane < 4, column, 0.0)
     across = jnp.transpose(column)[:8]
-    for j in range(8):
+    for j in range(4):
         moments[pl.ds(j * 8, 8), :] = across
 
 
 def back_kernel(place, rates, local, moments, basis_high, basis_low, square, square_row, message):
     size = local.shape[0]
-    blocks = size // ROWS
+    half_size = size // 2
+    blocks = half_size // 2
     rate = rates[place[0]]
-    mine = place[1]
+    even = place[1] < 4
+    mine = place[1] & 3
     root, inverse, rho = decay(rate, square_row[...])
     r64 = squarings(rho, 6)[6]
     r128 = r64 * r64
     r256 = r128 * r128
     row = row_of((8, size))
     carry = jnp.zeros((8, size), F32)
-    for j in range(8):
-        from_low = (mine - j - 1) & 7
-        from_high = (j - mine - 1) & 7
-        exponent = jnp.where(row < 2, from_low, from_high)
-        weight = jnp.where((exponent & 1) != 0, r64, 1.0)
-        weight = weight * jnp.where((exponent & 2) != 0, r128, 1.0)
-        weight = weight * jnp.where((exponent & 4) != 0, r256, 1.0)
-        carry = carry + weight * moments[pl.ds(j * 8, 8), :]
+    for j in range(4):
+        theirs = moments[pl.ds(j * 8, 8), :]
+        for offset, values in ((-1, theirs), (3, turn(theirs, half_size, 1))):
+            exponent = jnp.where(row < 2, (mine - j + offset) & 7, (j - mine + offset) & 7)
+            weight = jnp.where((exponent & 1) != 0, r64, 1.0)
+            weight = weight * jnp.where((exponent & 2) != 0, r128, 1.0)
+            weight = weight * jnp.where((exponent & 4) != 0, r256, 1.0)
+            carry = carry + weight * values
     carry = carry / (1.0 - r256 * r256)
     own = moments[pl.ds(pl.multiple_of(mine * 8, 8), 8), :]
     scale = -1.0 / root[0:1]
@@ -300,35 +303,37 @@
     total = total + lane_powers(powers, 63 - half) * jnp.where(odd, spread(3), spread(2))
     total = -total / root
     ext = jnp.where((lane == 4) | (lane == 5), columns, 0.0)
+    ext = ext[:half_size] + turn(ext[half_size:], 2, 1)
     pressure = dot3(
-        (basis_high[...], basis_low[...]), parts(jnp.concatenate([total, ext], axis=1))
+        (basis_high[...], basis_low[...]),
+        parts(jnp.concatenate([total[:half_size], total[half_size:], ext], axis=1)),
     )
     lane = lane_of((blocks, LANES))
-    inside = [pressure[r * blocks : (r + 1) * blocks, :LANES] for r in range(ROWS)]
-    left = turn(inside[ROWS - 1], 1, 0)
-    right = turn(inside[0], -1, 0)
-    extra = jnp.where((lane == 0) | (lane == LANES - 1), left, 0.0)
-    extra = jnp.where(lane == 1, turn(right, 1, 1), extra)
-    extra = jnp.where(lane == LANES - 2, turn(right, -1, 1), extra)
-    for r in range(ROWS):
-        outside = pressure[r * blocks : (r + 1) * blocks, LANES:]
-        extra = jnp.where(lane == HIGH + r, turn(outside, HIGH + r - 4, 1), extra)
-        extra = jnp.where(lane == LOW + r, turn(outside, LOW + r - 5, 1), extra)
-        message[pl.ds(r, blocks, stride=ROWS + 1), :] = inside[r]
-    message[pl.ds(ROWS, blocks, stride=ROWS + 1), :] = extra
+    ends = (lane == 0) | (lane == LANES - 1)
+    outside = [pressure[r * blocks : (r + 1) * blocks, 2 * LANES :] for r in range(2)]
+    for h in range(2):
+        span = slice(h * LANES, (h + 1) * LANES)
+        first, second = pressure[:blocks, span], pressure[blocks:, span]
+        extra = jnp.where(ends, jnp.where(even, turn(first, -1, 0), turn(second, 1, 0)), 0.0)
+        for r in range(2):
+            extra = jnp.where(lane == HIGH + r, turn(outside[r], HIGH + r - 4 - 2 * h, 1), extra)
+            extra = jnp.where(lane == LOW + r, turn(outside[r], LOW + r - 5 - 2 * h, 1), extra)
+        for j, value in enumerate((first, second, extra)):
+            message[pl.ds(3 * h + j, blocks, stride=6), :] = value
 
 
 def final_kernel(received, sent, star, back, rate, out):
     lane = lane_of((LEVELS, LANES))
-    p = [received[pl.ds(r, LEVELS, stride=ROWS + 1), :] for r in range(ROWS)]
-    extra = received[pl.ds(ROWS, LEVELS, stride=ROWS + 1), :]
-    low = [turn(extra, -(LOW + r), 1) for r in range(ROWS)]
-    high = [turn(extra, LANES - 1 - (HIGH + r), 1) for r in range(ROWS)]
+    row_at = lambda ref, r: ref[pl.ds(3 * (r % 2) + r // 2, LEVELS, stride=6), :]
+    p = [row_at(received, r) for r in range(ROWS)]
+    extra = [row_at(received, 4), row_at(received, 5)]
+    low = [turn(extra[r % 2], -(LOW + r // 2), 1) for r in range(ROWS)]
+    high = [turn(extra[r % 2], LANES - 1 - (HIGH + r // 2), 1) for r in range(ROWS)]
     four_rate = 4.0 * rate[...]
 
     def next_row(r, opposite):
         here = p[r]
-        divergence = sent[pl.ds(r, LEVELS, stride=ROWS + 1), :]
+        divergence = row_at(sent, r)
         plus = jnp.where(lane < LANES - 2, turn(here, -2, 1), turn(high[r], -1, 1))
         minus = jnp.where(lane > 1, turn(here, 2, 1), turn(low[r], 1, 1))
         return (
@@ -340,9 +345,8 @@
         )
 
     ends = (lane == 0) | (lane == LANES - 1)
-    before = jnp.where(ends, extra, next_row(1, p[3]))
-    inward = jnp.where(lane == 0, turn(extra, -1, 1), turn(extra, 1, 1))
-    after = jnp.where(ends, inward, next_row(2, p[0]))
+    before = jnp.where(ends, extra[1], next_row(1, p[3]))
+    after = jnp.where(ends, extra[0], next_row(2, p[0]))
     padded = [before] + p + [after]
     slopes = [0.5 * (padded[x + 2] - padded[x]) for x in range(ROWS)]
     slopes += [0.5 * north_difference(p[x], low[x], high[x]) for x in range(ROWS)]
@@ -379,9 +383,15 @@
     return lax.ppermute(values, axis, pairs)
 
 
-def exchange(values, axis, groups, rows):
-    shaped = values.reshape(groups, 1, rows * values.shape[1])
-    return lax.all_to_all(shaped, axis, 0, 0, tiled=True).reshape(values.shape)
+def exchange(values):
+    count_x, count_y = lax.axis_size("gx"), lax.axis_size("gy")
+    near = count_y // 2
+    groups = [[i * count_y + h * near + y for i in range(count_x) for h in range(2)] for y in range(near)]
+    shaped = values.reshape(2 * count_x, 1, values.size // (2 * count_x))
+    moved = lax.all_to_all(
+        shaped, ("gx", "gy"), 0, 0, tiled=True, axis_index_groups=groups
+    )
+    return moved.reshape(values.shape)
 
 
 def on_device(
@@ -391,7 +401,8 @@
     total_east = blocks * ROWS
     place = jnp.stack([lax.axis_index("gx"), lax.axis_index("gy")]).astype(jnp.int32)
     state = model_state.reshape(4 * LEVELS * ROWS, LANES)
-    basis, square = east_tables(total_east, blocks)
+    basis, square = east_tables(total_east // 2, blocks)
+    square = np.concatenate([square, square])
     forward_high, forward_low = split_table(basis)
     back_high, back_low = split_table(np.ascontiguousarray(basis.T))
     square_wide = np.ascontiguousarray(np.broadcast_to(square[:, None], (total_east, LANES)))
@@ -420,7 +431,7 @@
     level_down = jnp.concatenate([zero, 0.5 * density[:-1] / density[1:]])
     star, message = call(
         outer_kernel,
-        [(16 * LEVELS, LANES), (blocks * (ROWS + 1), LANES)],
+        [(16 * LEVELS, LANES), (blocks * 6, LANES)],
         1,
         [
             place,
@@ -436,25 +447,30 @@
         ],
         "outer",
     )
-    modal = exchange(message, "gx", blocks, ROWS + 1)
+    modal = exchange(message)
     local, moments = call(
         solve_kernel,
-        [(total_east, LANES), (64, total_east)],
+        [(total_east, LANES), (32, total_east)],
         2,
         [place, mode_rate, modal, forward_high, forward_low, square_wide],
         "solve",
     )
     moments = lax.all_to_all(
-        moments.reshape(8, 8, total_east), "gy", 0, 0, tiled=True
-    ).reshape(64, total_east)
+        moments.reshape(4, 8, total_east),
+        "gy",
+        0,
+        0,
+        tiled=True,
+        axis_index_groups=[[0, 1, 2, 3], [4, 5, 6, 7]],
+    ).reshape(32, total_east)
     (reply,) = call(
         back_kernel,
-        [(total_east * (ROWS + 1) // ROWS, LANES)],
+        [(blocks * 6, LANES)],
         2,
         [place, mode_rate, local, moments, back_high, back_low, square_wide, square_row],
         "back",
     )
-    pressure = exchange(reply, "gx", blocks, ROWS + 1)
+    pressure = exchange(reply)
     (out,) = call(
         final_kernel,
         [(4 * LEVELS * ROWS, LANES)],

time: 116 us -> 113 us (0.974)
  blocking collectives: 52.8 us -> 45.4 us
  waiting for transfers between devices: 15.5 us -> 20 us
    all_to_all x2, blocking collectives: 52.8 us -> 45.4 us  [the longest x1 38 us: exchange(): lax.all_to_all(shaped, ('gx', 'gy'), 0, 0, tiled=True, axis_index_groups=...]
    all_to_all x1, waiting for transfers between devices: 15.5 us -> 20 us  [exchange(): lax.all_to_all(shaped, ('gx', 'gy'), 0, 0, tiled=True, axis_index_groups=...]
  transfers between devices with their start and end apart: 5 -> 5, of which waited for: 1 -> 1; matrix products, arithmetic and copies ran while one was open for 1% -> 2% of each run, Pallas kernels for 1% -> 1%
where the time goes in v1:
time: 113 us; the launch traced here: 112 us
  blocking collectives  45.4 us (40%)
  starting transfers between devices  33.8 us (30%)
  waiting for transfers between devices  20 us (18%)
  Pallas kernels  7.81 us (7%)
  local copies, waits for them, and re-layouts  4.75 us (4%)
    all_to_all x1, blocking collectives, exchange(): lax.all_to_all(shaped, ('gx', 'gy'), 0, 0, tiled=True, axis_index_groups=...  38 us
    ppermute x4, starting transfers between devices, swap(): return lax.ppermute(values, axis, pairs)  26.2 us
    all_to_all x1, waiting for transfers between devices, exchange(): lax.all_to_all(shaped, ('gx', 'gy'), 0, 0, tiled=True, axis_index_groups=...  20 us
    pallas_call x6, Pallas kernels, call(): pl.pallas_call(kernel, out_shape=[jax.ShapeDtypeStruct(s, F32) for s in s...  7.81 us
    all_to_all x1, starting transfers between devices, exchange(): lax.all_to_all(shaped, ('gx', 'gy'), 0, 0, tiled=True, axis_index_groups=...  7.6 us
    all_to_all x1, blocking collectives, on_device(): lax.all_to_all(moments.reshape(4, 8, total_east), 'gy', 0, 0, tiled=True,...  7.4 us
    unnamed x30, local copies, waits for them, and re-layouts  4.33 us
  transfers between devices with their start and end apart: 5, of which 1 were waited for; matrix products, arithmetic and copies ran while one was open for 2% of the time, Pallas kernels for 1%

profile of v1, /device:TPU:1, one launch (start us, length us, event | category | flops | bytes accessed | tf_op | source)
XLA Modules:
  0.0 112.2 jit_solution(4475981686881503776)
XLA Ops:
  0.0 0.1 pad_add_fusion.place
  0.1 0.0 copy-start
  0.1 1.0 copy-done
  1.1 0.0 copy-start.1
  1.1 0.9 edges.1
  2.0 8.8 %collective-permute-start = (f32[320,128]{1,0:T(8,128)S(1)}, f32[320,128]{1,0:T(8,128)S(1)}, u32[]{:S(2)}, u32[]{:S(2)}) collective-permute-start(f32[320,128]{1,0:T(8,128)S(1)} %get-tuple-element.13), channel_id=1, source_target_pairs={{0,8},{8,0},{16,24},{24,16},{32,40},{40,32},{48,56},{56,48},{64,72... | collective-permute-start | bytes 491528 | tf_op jit(solution)/shard_map/ppermute | solution.py:383
  10.8 1.9 %collective-permute-start.1 = (f32[320,128]{1,0:T(8,128)S(1)}, f32[320,128]{1,0:T(8,128)S(1)}, u32[]{:S(2)}, u32[]{:S(2)}) collective-permute-start(f32[320,128]{1,0:T(8,128)S(1)} %get-tuple-element.14), channel_id=1, source_target_pairs={{8,16},{16,8},{24,32},{32,24},{40,48},{48,40},{56,64},{64,56},{72,... | collective-permute-start | bytes 491528 | tf_op jit(solution)/shard_map/ppermute | solution.py:383
  12.8 0.0 copy-start.12
  12.8 1.9 %collective-permute-start.2 = (f32[16,128]{1,0:T(8,128)S(1)}, f32[16,128]{1,0:T(8,128)S(1)}, u32[]{:S(2)}, u32[]{:S(2)}) collective-permute-start(f32[16,128]{1,0:T(8,128)S(1)} %get-tuple-element.15), channel_id=1, source_target_pairs={{0,1},{1,0},{2,3},{3,2},{4,5},{5,4},{6,7},{7,6},{8,9},{9,8},{10,11... | collective-permute-start | bytes 24584 | tf_op jit(solution)/shard_map/ppermute | solution.py:383
  14.7 13.6 %collective-permute-start.3 = (f32[16,128]{1,0:T(8,128)S(1)}, f32[16,128]{1,0:T(8,128)S(1)}, u32[]{:S(2)}, u32[]{:S(2)}) collective-permute-start(f32[16,128]{1,0:T(8,128)S(1)} %get-tuple-element.16), channel_id=1, source_target_pairs={{1,2},{2,1},{3,4},{4,3},{5,6},{6,5},{7,0},{0,7},{9,10},{10,9},{11,... | collective-permute-start | bytes 24584 | tf_op jit(solution)/shard_map/ppermute | solution.py:383
  28.3 0.0 copy-done.12
  28.3 0.1 multiply_divide_fusion
  28.4 0.1 maximum_bitcast_fusion
  28.5 0.1 copy.29.level_up
  28.6 0.1 copy.30.level_down
  28.7 1.0 copy.26
  29.7 0.0 copy-start.13
  29.7 0.7 copy-done.13
  30.4 0.0 copy-start.11
  30.4 0.1 copy.28.bias
  30.5 0.7 copy-done.11
  31.2 0.1 copy.27
  31.3 0.0 copy-done.1
  31.3 0.0 copy-start.3
  31.3 0.6 inner.1
  31.9 0.0 collective-permute-done.2.y_even
  31.9 0.0 collective-permute-done.3.y_odd
  32.0 0.0 collective-permute-done.x_even
  32.0 0.0 collective-permute-done.1.x_odd
  32.0 0.1 copy-done.3
  32.1 1.3 %outer.1 = (f32[1024,128]{1,0:T(8,128)S(1)}, f32[384,128]{1,0:T(8,128)S(1)}) custom-call(s32[2]{0:T(128)S(1)} %pad_add_fusion.place, f32[1024,128]{1,0:T(8,128)S(1)} %bitcast.20, f32[1024,128]{1,0:T(8,128)S(1)} %inner.1, f32[320,128]{1,0:T(8,128)S(1)} %collective-permute-done.x_even, f32[320,128]{1,0:T(8,128)S(1)} %collective-permute-done.1.x_odd, ...), custom_call_target="tpu_custom_call" | custom-call | tf_op jit(solution)/shard_map/outer/pallas_call | solution.py:368
  33.4 0.0 copy-start.2
  33.4 0.0 copy-start.7
  33.4 0.0 copy-start.8
  33.4 38.0 %all_to_all.15 = f32[128,1,384]{2,1,0:T(1,128)S(1)} all-to-all(f32[128,1,384]{2,1,0:T(1,128)S(1)} %bitcast.22), channel_id=1, replica_groups={{0,4,8,12,16,20,24,28,32,36,40,44,48,52,56,60,64,68,72,76,80,84,88,92,9..., dimensions={0} | all-to-all | bytes 393216 | tf_op jit(solution)/shard_map/all_to_all | solution.py:391
  71.4 0.0 copy-start.10
  71.4 0.0 copy-done.2
  71.4 0.0 copy-done.7
  71.5 0.0 copy-done.8
  71.5 0.6 copy-done.10
  72.1 0.0 copy-start.9
  72.1 1.6 %solve.1 = (f32[256,128]{1,0:T(8,128)S(1)}, f32[32,256]{1,0:T(8,128)S(1)}) custom-call(s32[2]{0:T(128)S(1)} %pad_add_fusion.place, f32[64]{0:T(128)S(1)} %copy-done.10, f32[384,128]{1,0:T(8,128)S(1)} %bitcast.21, bf16[128,128]{1,0:T(8,128)(2,1)S(1)} %copy-done.7, bf16[128,128]{1,0:T(8,128)(2,1)S(1)} %copy-done.8, f32[256,128]{1,0:T(8,128)S(1)} %copy-done.2), custom_call_target="tpu_custom_call" | custom-call | tf_op jit(solution)/shard_map/solve/pallas_call | solution.py:368
  73.7 0.0 copy-start.5
  73.7 0.0 copy-start.6
  73.7 7.4 %all_to_all.16 = f32[4,8,256]{2,1,0:T(8,128)S(1)} all-to-all(f32[4,8,256]{2,1,0:T(8,128)S(1)} %bitcast.27), channel_id=1, replica_groups={{0,1,2,3},{4,5,6,7},{8,9,10,11},{12,13,14,15},{16,17,18,19},{20,21,22,2..., dimensions={0} | all-to-all | bytes 65536 | tf_op jit(solution)/shard_map/all_to_all | solution.py:458
  81.1 0.0 copy-done.9
  81.1 0.0 copy-done.5
  81.1 0.0 copy-done.6
  81.1 2.0 %back.2 = f32[384,128]{1,0:T(8,128)} custom-call(s32[2]{0:T(128)S(1)} %pad_add_fusion.place, f32[64]{0:T(128)S(1)} %copy-done.10, f32[256,128]{1,0:T(8,128)S(1)} %get-tuple-element.18.local, f32[32,256]{1,0:T(8,128)S(1)} %bitcast.26, bf16[128,128]{1,0:T(8,128)(2,1)S(1)} %copy-done.5, bf16[128,128]{1,0:T(8,128)(2,1)S(1)} %copy-done.6, ...), custom_call_target="tpu_custom_call" | custom-call | tf_op jit(solution)/shard_map/back/pallas_call | solution.py:368
  83.1 7.6 %all-to-all-start.2 = ((f32[128,1,384]{2,1,0:T(1,128)}), f32[128,1,384]{2,1,0:T(1,128)S(1)}, u32[]{:S(2)}, u32[]{:S(2)}) async-start(f32[128,1,384]{2,1,0:T(1,128)} %bitcast.12), calls=%async_computation.2 | async-start | bytes 393216 | tf_op jit(solution)/shard_map/all_to_all | solution.py:391
  90.7 0.0 copy-start.4
  90.7 0.1 copy.33.rate
  90.8 20.0 %all-to-all-done.2 = f32[128,1,384]{2,1,0:T(1,128)S(1)} async-done(((f32[128,1,384]{2,1,0:T(1,128)}), f32[128,1,384]{2,1,0:T(1,128)S(1)}, u32[]{:S(2)}, u32[]{:S(2)}) %all-to-all-start.2) | async-done | bytes 196640 | tf_op jit(solution)/shard_map/all_to_all | solution.py:391
  110.8 0.0 copy-done.4
  110.8 1.4 %final.1 = f32[1024,128]{1,0:T(8,128)} custom-call(f32[384,128]{1,0:T(8,128)S(1)} %bitcast.23, f32[384,128]{1,0:T(8,128)S(1)} %get-tuple-element.17.sent, f32[1024,128]{1,0:T(8,128)S(1)} %get-tuple-element.20.star, f32[64,64]{1,0:T(8,128)S(1)} %copy-done.4, f32[64,1]{1,0:T(8,128)S(1)} %copy.33.rate), custom_call_target="tpu_custom_call" | custom-call | tf_op jit(solution)/shard_map/final/pallas_call | solution.py:368
Async XLA Ops:
  0.1 1.0 copy-start
  1.1 30.2 %copy-start.1 = (f32[4,64,4,128]{3,2,1,0:T(4,128)S(1)}, f32[4,64,4,128]{3,2,1,0:T(4,128)}, u32[]{:S(2)}) copy-start(f32[4,64,4,128]{3,2,1,0:T(4,128)} %param.14) | copy-start | bytes 1572868
  2.0 29.9 %collective-permute-start = (f32[320,128]{1,0:T(8,128)S(1)}, f32[320,128]{1,0:T(8,128)S(1)}, u32[]{:S(2)}, u32[]{:S(2)}) collective-permute-start(f32[320,128]{1,0:T(8,128)S(1)} %get-tuple-element.13), channel_id=1, source_target_pairs={{0,8},{8,0},{16,24},{24,16},{32,40},{40,32},{48,56},{56,48},{64,72... | collective-permute-start | bytes 491528 | tf_op jit(solution)/shard_map/ppermute | solution.py:383
  10.8 21.1 %collective-permute-start.1 = (f32[320,128]{1,0:T(8,128)S(1)}, f32[320,128]{1,0:T(8,128)S(1)}, u32[]{:S(2)}, u32[]{:S(2)}) collective-permute-start(f32[320,128]{1,0:T(8,128)S(1)} %get-tuple-element.14), channel_id=1, source_target_pairs={{8,16},{16,8},{24,32},{32,24},{40,48},{48,40},{56,64},{64,56},{72,... | collective-permute-start | bytes 491528 | tf_op jit(solution)/shard_map/ppermute | solution.py:383
  12.8 15.5 %copy-start.12 = (f32[64]{0:T(128)S(1)}, f32[64]{0:T(128)}, u32[]{:S(2)}) copy-start(f32[64]{0:T(128)} %param.15) | copy-start | bytes 772
  12.8 19.2 %collective-permute-start.2 = (f32[16,128]{1,0:T(8,128)S(1)}, f32[16,128]{1,0:T(8,128)S(1)}, u32[]{:S(2)}, u32[]{:S(2)}) collective-permute-start(f32[16,128]{1,0:T(8,128)S(1)} %get-tuple-element.15), channel_id=1, source_target_pairs={{0,1},{1,0},{2,3},{3,2},{4,5},{5,4},{6,7},{7,6},{8,9},{9,8},{10,11... | collective-permute-start | bytes 24584 | tf_op jit(solution)/shard_map/ppermute | solution.py:383
  14.7 17.2 %collective-permute-start.3 = (f32[16,128]{1,0:T(8,128)S(1)}, f32[16,128]{1,0:T(8,128)S(1)}, u32[]{:S(2)}, u32[]{:S(2)}) collective-permute-start(f32[16,128]{1,0:T(8,128)S(1)} %get-tuple-element.16), channel_id=1, source_target_pairs={{1,2},{2,1},{3,4},{4,3},{5,6},{6,5},{7,0},{0,7},{9,10},{10,9},{11,... | collective-permute-start | bytes 24584 | tf_op jit(solution)/shard_map/ppermute | solution.py:383
  29.7 0.7 copy-start.13
  30.4 0.8 copy-start.11
  31.3 0.8 copy-start.3
  33.4 38.0 %copy-start.2 = (f32[256,128]{1,0:T(8,128)S(1)}, f32[256,128]{1,0:T(8,128)}, u32[]{:S(2)}) copy-start(f32[256,128]{1,0:T(8,128)} %constant.27.clone.square) | copy-start | bytes 393220
  33.4 38.0 %copy-start.7 = (bf16[128,128]{1,0:T(8,128)(2,1)S(1)}, bf16[128,128]{1,0:T(8,128)(2,1)}, u32[]{:S(2)}) copy-start(bf16[128,128]{1,0:T(8,128)(2,1)} %constant.25.clone.basis_high) | copy-start | bytes 98308
  33.4 38.0 %copy-start.8 = (bf16[128,128]{1,0:T(8,128)(2,1)S(1)}, bf16[128,128]{1,0:T(8,128)(2,1)}, u32[]{:S(2)}) copy-start(bf16[128,128]{1,0:T(8,128)(2,1)} %constant.26.clone.basis_low) | copy-start | bytes 98308
  71.4 0.7 copy-start.10
  72.1 9.0 %copy-start.9 = (f32[8,256]{1,0:T(8,128)S(1)}, f32[8,256]{1,0:T(8,128)}, u32[]{:S(2)}) copy-start(f32[8,256]{1,0:T(8,128)} %constant.30.clone.square_row) | copy-start | bytes 24580
  73.7 7.4 %copy-start.5 = (bf16[128,128]{1,0:T(8,128)(2,1)S(1)}, bf16[128,128]{1,0:T(8,128)(2,1)}, u32[]{:S(2)}) copy-start(bf16[128,128]{1,0:T(8,128)(2,1)} %constant.28.clone.basis_high) | copy-start | bytes 98308
  73.7 7.4 %copy-start.6 = (bf16[128,128]{1,0:T(8,128)(2,1)S(1)}, bf16[128,128]{1,0:T(8,128)(2,1)}, u32[]{:S(2)}) copy-start(bf16[128,128]{1,0:T(8,128)(2,1)} %constant.29.clone.basis_low) | copy-start | bytes 98308
  83.1 27.7 %all-to-all-start.2 = ((f32[128,1,384]{2,1,0:T(1,128)}), f32[128,1,384]{2,1,0:T(1,128)S(1)}, u32[]{:S(2)}, u32[]{:S(2)}) async-start(f32[128,1,384]{2,1,0:T(1,128)} %bitcast.12), calls=%async_computation.2 | async-start | bytes 393216 | tf_op jit(solution)/shard_map/all_to_all | solution.py:391
  90.7 20.1 %copy-start.4 = (f32[64,64]{1,0:T(8,128)S(1)}, f32[64,64]{1,0:T(8,128)}, u32[]{:S(2)}) copy-start(f32[64,64]{1,0:T(8,128)} %back.3) | copy-start | bytes 49156

commit v2 on v1

--- a/solution.py
+++ b/solution.py
@@ -76,6 +76,10 @@
 
 def plane(ref, field, x):
     return ref[pl.ds(field * LEVELS * ROWS + x, LEVELS, stride=ROWS), :]
+
+
+def far_both(gx, gy):
+    return ((gx % 16 == 0) | (gx % 16 == 15)) & ((gy % 4 == 0) | (gy % 4 == 3))
 
 
 def edges_kernel(place, state, x_even, x_odd, y_even, y_odd):
@@ -99,6 +103,7 @@
     low, high = flat[0:16], flat[16:32]
     y_even[...] = jnp.where(even_y, high, low)
     y_odd[...] = jnp.where(even_y, low, high)
+    x_even[pl.ds(5 * LEVELS, 16), :] = jnp.where(even_y, low, high)
 
 
 def inner_kernel(state, layer_in, bias, layer_out, star):
@@ -132,7 +137,19 @@
 
 
 def outer_kernel(
-    place, state, inner, x_even, x_odd, y_even, y_odd, level_up, level_down, forward, star, message
+    place,
+    state,
+    inner,
+    x_even,
+    x_odd,
+    y_even,
+    y_odd,
+    relayed,
+    level_up,
+    level_down,
+    forward,
+    star,
+    message,
 ):
     even_x = place[0] % 2 == 0
     even_y = place[1] % 2 == 0
@@ -144,8 +161,9 @@
         second = x_odd[pl.ds(slot * LEVELS, LEVELS), :]
         return jnp.where(even_x, second, first), jnp.where(even_x, first, second)
 
-    low_y = jnp.where(even_y, y_odd[...], y_even[...])
-    high_y = jnp.where(even_y, y_even[...], y_odd[...])
+    other = jnp.where(far_both(place[0], place[1]), relayed[...], y_odd[0:16, :])
+    low_y = jnp.where(even_y, other, y_even[...])
+    high_y = jnp.where(even_y, y_even[...], other)
     columns = jnp.transpose(jnp.concatenate([low_y, high_y, jnp.zeros((96, LANES), F32)], axis=0))
     columns = columns[:LEVELS]
     outer_x = [beyond(slot) for slot in range(5)]
@@ -383,6 +401,28 @@
     return lax.ppermute(values, axis, pairs)
 
 
+def swap_odd_y(values):
+    count_x, count_y = lax.axis_size("gx"), lax.axis_size("gy")
+    pairs = []
+    for i in range(count_x):
+        for j in range(1, count_y + 1, 2):
+            one, two = j % count_y, (j + 1) % count_y
+            if not far_both(i, one):
+                pairs += [(i * count_y + one, i * count_y + two), (i * count_y + two, i * count_y + one)]
+    return lax.ppermute(values, ("gx", "gy"), pairs)
+
+
+def hand_over(values):
+    count_x, count_y = lax.axis_size("gx"), lax.axis_size("gy")
+    pairs = [
+        ((i ^ 1) * count_y + j, i * count_y + j)
+        for i in range(count_x)
+        for j in range(count_y)
+        if far_both(i, j)
+    ]
+    return lax.ppermute(values, ("gx", "gy"), pairs)
+
+
 def exchange(values):
     count_x, count_y = lax.axis_size("gx"), lax.axis_size("gy")
     near = count_y // 2
@@ -410,15 +450,17 @@
 
     x_even, x_odd, y_even, y_odd = call(
         edges_kernel,
-        [(5 * LEVELS, LANES)] * 2 + [(16, LANES)] * 2,
+        [(5 * LEVELS + 16, LANES), (5 * LEVELS, LANES)] + [(16, LANES)] * 2,
         1,
         [place, state],
         "edges",
     )
-    got_y_odd = swap(y_odd, "gy", 1)
+    got_x_even = swap(x_even, "gx", 0)
+    y_both = jnp.concatenate([y_odd, got_x_even[5 * LEVELS :]], axis=0)
+    y_both, x_odd, y_even = lax.optimization_barrier((y_both, x_odd, y_even))
+    got_y_odd = swap_odd_y(y_both)
     got_x_odd = swap(x_odd, "gx", 1)
     got_y_even = swap(y_even, "gy", 0)
-    got_x_even = swap(x_even, "gx", 0)
     (inner,) = call(
         inner_kernel,
         [(16 * LEVELS, LANES)],
@@ -426,6 +468,8 @@
         [state, layer_in.T, layer_bias[:, None], layer_out.T],
         "inner",
     )
+    inner, got_y_odd = lax.optimization_barrier((inner, got_y_odd))
+    relayed = hand_over(got_y_odd[16:])
     zero = jnp.zeros((1,), F32)
     level_up = jnp.concatenate([0.5 * density[1:] / density[:-1], zero])
     level_down = jnp.concatenate([zero, 0.5 * density[:-1] / density[1:]])
@@ -441,6 +485,7 @@
             got_x_odd,
             got_y_even,
             got_y_odd,
+            relayed,
             level_up[:, None],
             level_down[:, None],
             mode_forward,

time: 113 us -> 107 us (0.947)
  blocking collectives: 45.4 us -> 36.7 us
  waiting for transfers between devices: 20 us -> 21.9 us
  starting transfers between devices: 33.8 us -> 35.1 us
    ppermute x0 -> x2, starting transfers between devices: none -> 13.9 us  [the longest x1 12.6 us: swap_odd_y(): return lax.ppermute(values, ('gx', 'gy'), pairs)]
    ppermute x4 -> x3, starting transfers between devices: 26.2 us -> 13.9 us  [swap(): return lax.ppermute(values, axis, pairs)]
    all_to_all x1, blocking collectives: 38 us -> 29.9 us  [exchange(): lax.all_to_all(shaped, ('gx', 'gy'), 0, 0, tiled=True, axis_index_groups=...]
    ppermute x4 -> x3, waiting for transfers between devices: 0.01 us -> 1.9 us  [swap(): return lax.ppermute(values, axis, pairs)]
  transfers between devices with their start and end apart: 5 -> 6, of which waited for: 1 -> 3; matrix products, arithmetic and copies ran while one was open for 2% -> 2% of each run, Pallas kernels for 1% -> 1%
where the time goes in v2:
time: 107 us
  blocking collectives  36.7 us (34%)
  starting transfers between devices  35.1 us (33%)
  waiting for transfers between devices  21.9 us (20%)
  Pallas kernels  7.82 us (7%)
  local copies, waits for them, and re-layouts  4.64 us (4%)
    all_to_all x1, blocking collectives, exchange(): lax.all_to_all(shaped, ('gx', 'gy'), 0, 0, tiled=True, axis_index_groups=...  29.9 us
    all_to_all x1, waiting for transfers between devices, exchange(): lax.all_to_all(shaped, ('gx', 'gy'), 0, 0, tiled=True, axis_index_groups=...  20 us
    ppermute x3, starting transfers between devices, swap(): return lax.ppermute(values, axis, pairs)  13.9 us
    ppermute x1, starting transfers between devices, swap_odd_y(): return lax.ppermute(values, ('gx', 'gy'), pairs)  12.6 us
    pallas_call x6, Pallas kernels, call(): pl.pallas_call(kernel, out_shape=[jax.ShapeDtypeStruct(s, F32) for s in s...  7.82 us
    all_to_all x1, starting transfers between devices, exchange(): lax.all_to_all(shaped, ('gx', 'gy'), 0, 0, tiled=True, axis_index_groups=...  7.32 us
    all_to_all x1, blocking collectives, on_device(): lax.all_to_all(moments.reshape(4, 8, total_east), 'gy', 0, 0, tiled=True,...  6.82 us
    unnamed x30, local copies, waits for them, and re-layouts  4.22 us
  transfers between devices with their start and end apart: 6, of which 3 were waited for; matrix products, arithmetic and copies ran while one was open for 2% of the time, Pallas kernels for 1%

profile of v2, /device:TPU:1, one launch (start us, length us, event | category | flops | bytes accessed | tf_op | source)
XLA Modules:
  0.0 106.6 jit_solution(3464499288620073364)
XLA Ops:
  0.0 0.1 pad_add_fusion.place
  0.1 0.0 copy-start
  0.1 1.0 copy-done
  1.1 0.0 copy-start.1
  1.1 0.9 edges.1
  2.0 8.8 %collective-permute-start = (f32[336,128]{1,0:T(8,128)S(1)}, f32[336,128]{1,0:T(8,128)S(1)}, u32[]{:S(2)}, u32[]{:S(2)}) collective-permute-start(f32[336,128]{1,0:T(8,128)S(1)} %get-tuple-element.19), channel_id=1, source_target_pairs={{0,8},{8,0},{16,24},{24,16},{32,40},{40,32},{48,56},{56,48},{64,72... | collective-permute-start | bytes 516104 | tf_op jit(solution)/shard_map/ppermute | solution.py:401
  10.8 1.0 collective-permute-done.x_even
  11.9 0.0 copy-start.12
  11.9 12.6 %collective-permute-start.1 = (f32[32,128]{1,0:T(8,128)S(1)}, f32[32,128]{1,0:T(8,128)S(1)}, u32[]{:S(2)}, u32[]{:S(2)}) collective-permute-start(f32[32,128]{1,0:T(8,128)S(1)} %pad_maximum_fusion), channel_id=1, source_target_pairs={{1,2},{2,1},{5,6},{6,5},{9,10},{10,9},{11,12},{12,11},{13,14},{14,... | collective-permute-start | bytes 49160 | tf_op jit(solution)/shard_map/ppermute | solution.py:412
  24.5 3.2 %collective-permute-start.2 = (f32[320,128]{1,0:T(8,128)S(1)}, f32[320,128]{1,0:T(8,128)S(1)}, u32[]{:S(2)}, u32[]{:S(2)}) collective-permute-start(f32[320,128]{1,0:T(8,128)S(1)} %get-tuple-element.24), channel_id=1, source_target_pairs={{8,16},{16,8},{24,32},{32,24},{40,48},{48,40},{56,64},{64,56},{72,... | collective-permute-start | bytes 491528 | tf_op jit(solution)/shard_map/ppermute | solution.py:401
  27.7 0.0 copy-done.12
  27.7 0.1 multiply_divide_fusion
  27.8 1.0 copy.26
  28.8 0.0 copy-start.13
  28.8 0.7 copy-done.13
  29.5 0.0 copy-start.11
  29.5 0.1 copy.28.bias
  29.6 0.7 copy-done.11
  30.3 0.1 copy.27
  30.4 0.0 copy-done.1
  30.4 0.6 inner.1
  31.0 1.9 %collective-permute-start.3 = (f32[16,128]{1,0:T(8,128)S(1)}, f32[16,128]{1,0:T(8,128)S(1)}, u32[]{:S(2)}, u32[]{:S(2)}) collective-permute-start(f32[16,128]{1,0:T(8,128)S(1)} %get-tuple-element.25), channel_id=1, source_target_pairs={{0,1},{1,0},{2,3},{3,2},{4,5},{5,4},{6,7},{7,6},{8,9},{9,8},{10,11... | collective-permute-start | bytes 24584 | tf_op jit(solution)/shard_map/ppermute | solution.py:401
  33.0 0.0 collective-permute-done.1.y_odd
  33.0 1.3 %collective-permute-start.4 = (f32[16,128]{1,0:T(8,128)S(1)}, f32[16,128]{1,0:T(8,128)S(1)}, u32[]{:S(2)}, u32[]{:S(2)}) collective-permute-start(f32[16,128]{1,0:T(8,128)S(1)} %slice.15), channel_id=1, source_target_pairs={{8,0},{11,3},{12,4},{15,7},{112,120},{115,123},{116,124},{119,127}... | collective-permute-start | bytes 24584 | tf_op jit(solution)/shard_map/ppermute | solution.py:423
  34.3 0.1 maximum_bitcast_fusion
  34.4 0.0 copy-start.3
  34.4 0.1 copy.29.level_up
  34.5 0.1 copy.30.level_down
  34.6 0.9 collective-permute-done.3.y_even
  35.4 0.0 collective-permute-done.4.relayed
  35.4 0.0 collective-permute-done.2.x_odd
  35.4 0.0 copy-done.3
  35.5 1.3 %outer.1 = (f32[1024,128]{1,0:T(8,128)S(1)}, f32[384,128]{1,0:T(8,128)S(1)}) custom-call(s32[2]{0:T(128)S(1)} %pad_add_fusion.place, f32[1024,128]{1,0:T(8,128)S(1)} %bitcast.20, f32[1024,128]{1,0:T(8,128)S(1)} %inner.1, f32[336,128]{1,0:T(8,128)S(1)} %collective-permute-done.x_even, f32[320,128]{1,0:T(8,128)S(1)} %collective-permute-done.2.x_odd, ...), custom_call_target="tpu_custom_call" | custom-call | tf_op jit(solution)/shard_map/outer/pallas_call | solution.py:386
  36.8 0.0 copy-start.2
  36.8 0.0 copy-start.7
  36.8 0.0 copy-start.8
  36.8 29.9 %all_to_all.15 = f32[128,1,384]{2,1,0:T(1,128)S(1)} all-to-all(f32[128,1,384]{2,1,0:T(1,128)S(1)} %bitcast.22), channel_id=1, replica_groups={{0,4,8,12,16,20,24,28,32,36,40,44,48,52,56,60,64,68,72,76,80,84,88,92,9..., dimensions={0} | all-to-all | bytes 393216 | tf_op jit(solution)/shard_map/all_to_all | solution.py:431
  66.7 0.0 copy-start.10
  66.7 0.0 copy-done.2
  66.7 0.0 copy-done.7
  66.7 0.0 copy-done.8
  66.7 0.6 copy-done.10
  67.4 0.0 copy-start.9
  67.4 1.6 %solve.1 = (f32[256,128]{1,0:T(8,128)S(1)}, f32[32,256]{1,0:T(8,128)S(1)}) custom-call(s32[2]{0:T(128)S(1)} %pad_add_fusion.place, f32[64]{0:T(128)S(1)} %copy-done.10, f32[384,128]{1,0:T(8,128)S(1)} %bitcast.21, bf16[128,128]{1,0:T(8,128)(2,1)S(1)} %copy-done.7, bf16[128,128]{1,0:T(8,128)(2,1)S(1)} %copy-done.8, f32[256,128]{1,0:T(8,128)S(1)} %copy-done.2), custom_call_target="tpu_custom_call" | custom-call | tf_op jit(solution)/shard_map/solve/pallas_call | solution.py:386
  68.9 0.0 copy-start.5
  68.9 0.0 copy-start.6
  69.0 6.8 %all_to_all.16 = f32[4,8,256]{2,1,0:T(8,128)S(1)} all-to-all(f32[4,8,256]{2,1,0:T(8,128)S(1)} %bitcast.27), channel_id=1, replica_groups={{0,1,2,3},{4,5,6,7},{8,9,10,11},{12,13,14,15},{16,17,18,19},{20,21,22,2..., dimensions={0} | all-to-all | bytes 65536 | tf_op jit(solution)/shard_map/all_to_all | solution.py:503
  75.8 0.0 copy-done.9
  75.8 0.0 copy-done.5
  75.8 0.0 copy-done.6
  75.8 2.0 %back.2 = f32[384,128]{1,0:T(8,128)} custom-call(s32[2]{0:T(128)S(1)} %pad_add_fusion.place, f32[64]{0:T(128)S(1)} %copy-done.10, f32[256,128]{1,0:T(8,128)S(1)} %get-tuple-element.28.local, f32[32,256]{1,0:T(8,128)S(1)} %bitcast.26, bf16[128,128]{1,0:T(8,128)(2,1)S(1)} %copy-done.5, bf16[128,128]{1,0:T(8,128)(2,1)S(1)} %copy-done.6, ...), custom_call_target="tpu_custom_call" | custom-call | tf_op jit(solution)/shard_map/back/pallas_call | solution.py:386
  77.8 7.3 %all-to-all-start.2 = ((f32[128,1,384]{2,1,0:T(1,128)}), f32[128,1,384]{2,1,0:T(1,128)S(1)}, u32[]{:S(2)}, u32[]{:S(2)}) async-start(f32[128,1,384]{2,1,0:T(1,128)} %bitcast.12), calls=%async_computation.2 | async-start | bytes 393216 | tf_op jit(solution)/shard_map/all_to_all | solution.py:431
  85.1 0.0 copy-start.4
  85.1 0.1 copy.33.rate
  85.2 20.0 %all-to-all-done.2 = f32[128,1,384]{2,1,0:T(1,128)S(1)} async-done(((f32[128,1,384]{2,1,0:T(1,128)}), f32[128,1,384]{2,1,0:T(1,128)S(1)}, u32[]{:S(2)}, u32[]{:S(2)}) %all-to-all-start.2) | async-done | bytes 196640 | tf_op jit(solution)/shard_map/all_to_all | solution.py:431
  105.2 0.0 copy-done.4
  105.2 1.4 %final.1 = f32[1024,128]{1,0:T(8,128)} custom-call(f32[384,128]{1,0:T(8,128)S(1)} %bitcast.23, f32[384,128]{1,0:T(8,128)S(1)} %get-tuple-element.27.sent, f32[1024,128]{1,0:T(8,128)S(1)} %get-tuple-element.30.star, f32[64,64]{1,0:T(8,128)S(1)} %copy-done.4, f32[64,1]{1,0:T(8,128)S(1)} %copy.33.rate), custom_call_target="tpu_custom_call" | custom-call | tf_op jit(solution)/shard_map/final/pallas_call | solution.py:386
  (3 shorter events, 0.0 us)
Async XLA Ops:
  0.1 1.0 copy-start
  1.1 29.3 %copy-start.1 = (f32[4,64,4,128]{3,2,1,0:T(4,128)S(1)}, f32[4,64,4,128]{3,2,1,0:T(4,128)}, u32[]{:S(2)}) copy-start(f32[4,64,4,128]{3,2,1,0:T(4,128)} %param.14) | copy-start | bytes 1572868
  2.0 9.8 %collective-permute-start = (f32[336,128]{1,0:T(8,128)S(1)}, f32[336,128]{1,0:T(8,128)S(1)}, u32[]{:S(2)}, u32[]{:S(2)}) collective-permute-start(f32[336,128]{1,0:T(8,128)S(1)} %get-tuple-element.19), channel_id=1, source_target_pairs={{0,8},{8,0},{16,24},{24,16},{32,40},{40,32},{48,56},{56,48},{64,72... | collective-permute-start | bytes 516104 | tf_op jit(solution)/shard_map/ppermute | solution.py:401
  11.9 15.8 %copy-start.12 = (f32[64]{0:T(128)S(1)}, f32[64]{0:T(128)}, u32[]{:S(2)}) copy-start(f32[64]{0:T(128)} %param.15) | copy-start | bytes 772
  11.9 21.1 %collective-permute-start.1 = (f32[32,128]{1,0:T(8,128)S(1)}, f32[32,128]{1,0:T(8,128)S(1)}, u32[]{:S(2)}, u32[]{:S(2)}) collective-permute-start(f32[32,128]{1,0:T(8,128)S(1)} %pad_maximum_fusion), channel_id=1, source_target_pairs={{1,2},{2,1},{5,6},{6,5},{9,10},{10,9},{11,12},{12,11},{13,14},{14,... | collective-permute-start | bytes 49160 | tf_op jit(solution)/shard_map/ppermute | solution.py:412
  24.5 10.9 %collective-permute-start.2 = (f32[320,128]{1,0:T(8,128)S(1)}, f32[320,128]{1,0:T(8,128)S(1)}, u32[]{:S(2)}, u32[]{:S(2)}) collective-permute-start(f32[320,128]{1,0:T(8,128)S(1)} %get-tuple-element.24), channel_id=1, source_target_pairs={{8,16},{16,8},{24,32},{32,24},{40,48},{48,40},{56,64},{64,56},{72,... | collective-permute-start | bytes 491528 | tf_op jit(solution)/shard_map/ppermute | solution.py:401
  28.8 0.7 copy-start.13
  29.5 0.8 copy-start.11
  31.0 4.4 %collective-permute-start.3 = (f32[16,128]{1,0:T(8,128)S(1)}, f32[16,128]{1,0:T(8,128)S(1)}, u32[]{:S(2)}, u32[]{:S(2)}) collective-permute-start(f32[16,128]{1,0:T(8,128)S(1)} %get-tuple-element.25), channel_id=1, source_target_pairs={{0,1},{1,0},{2,3},{3,2},{4,5},{5,4},{6,7},{7,6},{8,9},{9,8},{10,11... | collective-permute-start | bytes 24584 | tf_op jit(solution)/shard_map/ppermute | solution.py:401
  33.0 2.4 %collective-permute-start.4 = (f32[16,128]{1,0:T(8,128)S(1)}, f32[16,128]{1,0:T(8,128)S(1)}, u32[]{:S(2)}, u32[]{:S(2)}) collective-permute-start(f32[16,128]{1,0:T(8,128)S(1)} %slice.15), channel_id=1, source_target_pairs={{8,0},{11,3},{12,4},{15,7},{112,120},{115,123},{116,124},{119,127}... | collective-permute-start | bytes 24584 | tf_op jit(solution)/shard_map/ppermute | solution.py:423
  34.4 1.1 %copy-start.3 = (f32[64,64]{1,0:T(8,128)S(1)}, f32[64,64]{1,0:T(8,128)}, u32[]{:S(2)}) copy-start(f32[64,64]{1,0:T(8,128)} %forward.1) | copy-start | bytes 49156
  36.8 29.9 %copy-start.2 = (f32[256,128]{1,0:T(8,128)S(1)}, f32[256,128]{1,0:T(8,128)}, u32[]{:S(2)}) copy-start(f32[256,128]{1,0:T(8,128)} %constant.27.clone.square) | copy-start | bytes 393220
  36.8 29.9 %copy-start.7 = (bf16[128,128]{1,0:T(8,128)(2,1)S(1)}, bf16[128,128]{1,0:T(8,128)(2,1)}, u32[]{:S(2)}) copy-start(bf16[128,128]{1,0:T(8,128)(2,1)} %constant.25.clone.basis_high) | copy-start | bytes 98308
  36.8 29.9 %copy-start.8 = (bf16[128,128]{1,0:T(8,128)(2,1)S(1)}, bf16[128,128]{1,0:T(8,128)(2,1)}, u32[]{:S(2)}) copy-start(bf16[128,128]{1,0:T(8,128)(2,1)} %constant.26.clone.basis_low) | copy-start | bytes 98308
  66.7 0.7 copy-start.10
  67.4 8.4 %copy-start.9 = (f32[8,256]{1,0:T(8,128)S(1)}, f32[8,256]{1,0:T(8,128)}, u32[]{:S(2)}) copy-start(f32[8,256]{1,0:T(8,128)} %constant.30.clone.square_row) | copy-start | bytes 24580
  68.9 6.8 %copy-start.5 = (bf16[128,128]{1,0:T(8,128)(2,1)S(1)}, bf16[128,128]{1,0:T(8,128)(2,1)}, u32[]{:S(2)}) copy-start(bf16[128,128]{1,0:T(8,128)(2,1)} %constant.28.clone.basis_high) | copy-start | bytes 98308
  68.9 6.8 %copy-start.6 = (bf16[128,128]{1,0:T(8,128)(2,1)S(1)}, bf16[128,128]{1,0:T(8,128)(2,1)}, u32[]{:S(2)}) copy-start(bf16[128,128]{1,0:T(8,128)(2,1)} %constant.29.clone.basis_low) | copy-start | bytes 98308
  77.8 27.4 %all-to-all-start.2 = ((f32[128,1,384]{2,1,0:T(1,128)}), f32[128,1,384]{2,1,0:T(1,128)S(1)}, u32[]{:S(2)}, u32[]{:S(2)}) async-start(f32[128,1,384]{2,1,0:T(1,128)} %bitcast.12), calls=%async_computation.2 | async-start | bytes 393216 | tf_op jit(solution)/shard_map/all_to_all | solution.py:431
  85.1 20.1 %copy-start.4 = (f32[64,64]{1,0:T(8,128)S(1)}, f32[64,64]{1,0:T(8,128)}, u32[]{:S(2)}) copy-start(f32[64,64]{1,0:T(8,128)} %back.3) | copy-start | bytes 49156

commit v3 on v2

--- a/solution.py
+++ b/solution.py
@@ -75,30 +75,31 @@
 
 
 def plane(ref, field, x):
-    return ref[pl.ds(field * LEVELS * ROWS + x, LEVELS, stride=ROWS), :]
+    return ref[pl.ds((field * ROWS + x) * LEVELS, LEVELS), :]
 
 
 def far_both(gx, gy):
     return ((gx % 16 == 0) | (gx % 16 == 15)) & ((gy % 4 == 0) | (gy % 4 == 3))
 
 
-def edges_kernel(place, state, x_even, x_odd, y_even, y_odd):
+def edges_kernel(place, state, planes, x_even, x_odd, y_even, y_odd):
     even_x = place[0] % 2 == 0
     even_y = place[1] % 2 == 0
-    for slot, (field, depth) in enumerate(((0, 0), (1, 0), (2, 0), (3, 0), (0, 1))):
-        low = plane(state, field, depth)
-        high = plane(state, field, ROWS - 1 - depth)
-        span = pl.ds(slot * LEVELS, LEVELS)
-        x_even[span, :] = jnp.where(even_x, high, low)
-        x_odd[span, :] = jnp.where(even_x, low, high)
+    size = LEVELS * ROWS
     lane = lane_of((LEVELS, LANES))
     gathered = jnp.zeros((LEVELS, LANES), F32)
     for field in range(4):
+        values = [state[pl.ds(field * size + x, LEVELS, stride=ROWS), :] for x in range(ROWS)]
         for x in range(ROWS):
-            values = plane(state, field, x)
             slot = field * ROWS + x
-            gathered = jnp.where(lane == slot, turn(values, slot, 1), gathered)
-            gathered = jnp.where(lane == 16 + slot, turn(values, 17 + slot, 1), gathered)
+            planes[pl.ds(slot * LEVELS, LEVELS), :] = values[x]
+            gathered = jnp.where(lane == slot, turn(values[x], slot, 1), gathered)
+            gathered = jnp.where(lane == 16 + slot, turn(values[x], 17 + slot, 1), gathered)
+        for slot, depth in ((field, 0), (4, 1)) if field == 0 else ((field, 0),):
+            span = pl.ds(slot * LEVELS, LEVELS)
+            low, high = values[depth], values[ROWS - 1 - depth]
+            x_even[span, :] = jnp.where(even_x, high, low)
+            x_odd[span, :] = jnp.where(even_x, low, high)
     flat = jnp.transpose(jnp.concatenate([gathered, jnp.zeros_like(gathered)], axis=0))
     low, high = flat[0:16], flat[16:32]
     y_even[...] = jnp.where(even_y, high, low)
@@ -106,19 +107,62 @@
     x_even[pl.ds(5 * LEVELS, 16), :] = jnp.where(even_y, low, high)
 
 
-def inner_kernel(state, layer_in, bias, layer_out, star):
+def column_of(row):
+    return jnp.transpose(jnp.broadcast_to(row, (LANES, LANES)))
+
+
+def inner_kernel(
+    place,
+    state,
+    vectors,
+    bias,
+    square,
+    square_row,
+    layer_in,
+    layer_out,
+    star,
+    by_level,
+    by_wave,
+    by_block,
+):
     fields = [[plane(state, f, x) for x in range(ROWS)] for f in range(4)]
-    columns = jnp.concatenate(
-        [jnp.concatenate([fields[f][x] for f in range(4)], axis=0).astype(BF16) for x in range(ROWS)],
-        axis=1,
-    )
-    before = jnp.dot(layer_in[...], columns, preferred_element_type=F32) + bias[...]
-    hidden = (before * (1.0 / (1.0 + jnp.exp(-before)))).astype(BF16)
-    forcing = jnp.dot(layer_out[...], hidden, preferred_element_type=F32)
+    tall = column_of(vectors[...])
+    rate, density = tall[:LEVELS], tall[LEVELS:]
+    row = row_of((LEVELS, LANES))
+    by_level[pl.ds(0, LEVELS), :] = rate
+    by_level[pl.ds(LEVELS, LEVELS), :] = jnp.where(
+        row < LEVELS - 1, 0.5 * turn(density, -1, 0) / density, 0.0
+    )
+    by_level[pl.ds(2 * LEVELS, LEVELS), :] = jnp.where(row > 0, 0.5 * turn(density, 1, 0) / density, 0.0)
+    own = by_level[pl.ds(place[0], 1), :]
+
+    root, _, rho = decay(own, square[...])
+    powers = squarings(rho, 6)
+    half = lane_of((LANES, LANES)) >> 1
+    rising = lane_powers(powers, half)
+    falling = lane_powers(powers, 63 - half)
+    for i, value in enumerate(powers + [rising, falling, -1.0 / root]):
+        by_wave[pl.ds(i * LANES, LANES), :] = value
+
+    root, inverse, rho = decay(jnp.concatenate([own, own], axis=1), square_row[...])
+    r64 = squarings(rho, 6)[6]
+    r128 = r64 * r64
+    r256 = r128 * r128
+    images = 1.0 / (1.0 - r256 * r256)
+    mine = place[1] & 3
+    row = row_of(rho.shape)
+    for j in range(4):
+        for i, offset in enumerate((-1, 3)):
+            exponent = jnp.where(row < 2, (mine - j + offset) & 7, (j - mine + offset) & 7)
+            weight = jnp.where((exponent & 1) != 0, r64, 1.0)
+            weight = weight * jnp.where((exponent & 2) != 0, r128, 1.0)
+            weight = weight * jnp.where((exponent & 4) != 0, r256, 1.0)
+            by_block[pl.ds((2 * j + i) * 8, 8), :] = weight * images
+    scale = -1.0 / root
+    by_block[pl.ds(64, 8), :] = jnp.where(row == 0, scale, jnp.where(row == 1, scale * r64, scale * inverse))
+
     for x in range(ROWS):
         u, v, w, th = (fields[f][x] for f in range(4))
-        span = slice(x * LANES, (x + 1) * LANES)
-        heating, lift = forcing[:LEVELS, span], forcing[LEVELS:, span]
         for f in range(4):
             here = fields[f][x]
             change = v * north_difference(here) + w * level_difference(here)
@@ -130,10 +174,24 @@
                 change = change + u * (fields[f][x + 1] - fields[f][x - 1])
             value = here - 0.1 * change
             if f == 2:
-                value = value + 0.2 * (0.5 * th + lift)
-            if f == 3:
-                value = value + 0.2 * heating
+                value = value + 0.1 * th
             star[pl.ds((f * ROWS + x) * LEVELS, LEVELS), :] = value
+
+    columns = jnp.concatenate(
+        [jnp.concatenate([fields[f][x] for f in range(4)], axis=0).astype(BF16) for x in range(ROWS)],
+        axis=1,
+    )
+    first = (((0,), (0,)), ((), ()))
+    shift = jnp.concatenate([column_of(bias[:, :LANES]), column_of(bias[:, LANES:])], axis=0)
+    before = lax.dot_general(layer_in[...], columns, first, preferred_element_type=F32)
+    before = before + jnp.concatenate([shift] * ROWS, axis=1)
+    hidden = (before * (1.0 / (1.0 + jnp.exp(-before)))).astype(BF16)
+    forcing = lax.dot_general(layer_out[...], hidden, first, preferred_element_type=F32)
+    for x in range(ROWS):
+        span = slice(x * LANES, (x + 1) * LANES)
+        for f, part in ((2, forcing[LEVELS:, span]), (3, forcing[:LEVELS, span])):
+            at = pl.ds((f * ROWS + x) * LEVELS, LEVELS)
+            star[at, :] = star[at, :] + 0.2 * part
 
 
 def outer_kernel(
@@ -145,8 +203,7 @@
     y_even,
     y_odd,
     relayed,
-    level_up,
-    level_down,
+    by_level,
     forward,
     star,
     message,
@@ -196,7 +253,7 @@
     padded = [east_star(0, plane(state, 0, 0))] + whole[0] + [east_star(1, plane(state, 0, ROWS - 1))]
     divergence = []
     extra = [-0.5 * side_u[ROWS - 1], 0.5 * side_u[0]]
-    up, down = level_up[...], level_down[...]
+    up, down = by_level[pl.ds(LEVELS, LEVELS), :], by_level[pl.ds(2 * LEVELS, LEVELS), :]
     for x in range(ROWS):
         v, w = whole[1][x], whole[2][x]
         upright = up * turn(w, -1, 0) - down * turn(w, 1, 0)
@@ -232,7 +289,7 @@
     return product
 
 
-def solve_kernel(place, rates, received, basis_high, basis_low, square, local, moments):
+def solve_kernel(place, received, basis_high, basis_low, by_wave, local, moments):
     blocks = received.shape[0] // 6
     half_size = blocks * 2
     size = half_size * 2
@@ -257,22 +314,19 @@
     ext = spectral[:, 2 * LANES :]
     ext = jnp.concatenate([ext, turn(ext, -4, 1)], axis=0)
 
-    rate = rates[place[0]]
-    _, _, rho = decay(rate, square[...])
-    powers = squarings(rho, 6)
+    wave = lambda i: jnp.concatenate([by_wave[pl.ds(i * LANES, LANES), :]] * 2, axis=0)
+    powers = [wave(i) for i in range(7)]
+    rho = powers[0]
     lane = lane_of((size, LANES))
     ahead, behind = source, source
     for bit in range(6):
         shift = 2 << bit
         ahead = ahead + powers[bit] * jnp.where(lane >= shift, turn(ahead, shift, 1), 0.0)
         behind = behind + powers[bit] * jnp.where(lane < LANES - shift, turn(behind, -shift, 1), 0.0)
-    half = lane >> 1
-    rising = lane_powers(powers, half)
-    falling = lane_powers(powers, 63 - half)
     odd = (lane & 1) != 0
     first = jnp.broadcast_to(ext[:, 0:1], (size, LANES))
     second = jnp.broadcast_to(ext[:, 1:2], (size, LANES))
-    border = rho * jnp.where(odd, rising * second, falling * first)
+    border = rho * jnp.where(odd, wave(7) * second, wave(8) * first)
     local[...] = ahead + behind - source + border
     weight = jnp.where((lane == 1) | (lane == 2), powers[6] * rho, 1.0)
     column = jnp.where(lane < 2, turn(rho * ahead, 2, 1), turn(rho * behind, 2, 1)) + ext * weight
@@ -282,44 +336,31 @@
         moments[pl.ds(j * 8, 8), :] = across
 
 
-def back_kernel(place, rates, local, moments, basis_high, basis_low, square, square_row, message):
+def back_kernel(place, local, moments, basis_high, basis_low, by_wave, by_block, message):
     size = local.shape[0]
     half_size = size // 2
     blocks = half_size // 2
-    rate = rates[place[0]]
     even = place[1] < 4
     mine = place[1] & 3
-    root, inverse, rho = decay(rate, square_row[...])
-    r64 = squarings(rho, 6)[6]
-    r128 = r64 * r64
-    r256 = r128 * r128
-    row = row_of((8, size))
     carry = jnp.zeros((8, size), F32)
     for j in range(4):
         theirs = moments[pl.ds(j * 8, 8), :]
-        for offset, values in ((-1, theirs), (3, turn(theirs, half_size, 1))):
-            exponent = jnp.where(row < 2, (mine - j + offset) & 7, (j - mine + offset) & 7)
-            weight = jnp.where((exponent & 1) != 0, r64, 1.0)
-            weight = weight * jnp.where((exponent & 2) != 0, r128, 1.0)
-            weight = weight * jnp.where((exponent & 4) != 0, r256, 1.0)
-            carry = carry + weight * values
-    carry = carry / (1.0 - r256 * r256)
+        carry = carry + by_block[pl.ds(16 * j, 8), :] * theirs
+        carry = carry + by_block[pl.ds(16 * j + 8, 8), :] * turn(theirs, half_size, 1)
     own = moments[pl.ds(pl.multiple_of(mine * 8, 8), 8), :]
-    scale = -1.0 / root[0:1]
-    after = scale * (own[0:1] + carry[0:1] * r64[0:1] + carry[2:3] * inverse[0:1])
-    before = scale * (own[3:4] + carry[3:4] * r64[0:1] + carry[1:2] * inverse[0:1])
+    scale, by_r64, by_inverse = (by_block[pl.ds(64 + i, 1), :] for i in range(3))
+    after = scale * own[0:1] + by_r64 * carry[0:1] + by_inverse * carry[2:3]
+    before = scale * own[3:4] + by_r64 * carry[3:4] + by_inverse * carry[1:2]
     stacked = jnp.concatenate([carry[0:4], after, before, jnp.zeros((LANES - 6, size), F32)], axis=0)
     columns = jnp.transpose(stacked)
 
-    root, _, rho = decay(rate, square[...])
-    powers = squarings(rho, 5)
+    wave = lambda i: jnp.concatenate([by_wave[pl.ds(i * LANES, LANES), :]] * 2, axis=0)
     lane = lane_of((size, LANES))
-    half = lane >> 1
     odd = (lane & 1) != 0
     spread = lambda i: jnp.broadcast_to(columns[:, i : i + 1], (size, LANES))
-    total = local[...] + lane_powers(powers, half) * jnp.where(odd, spread(1), spread(0))
-    total = total + lane_powers(powers, 63 - half) * jnp.where(odd, spread(3), spread(2))
-    total = -total / root
+    total = local[...] + wave(7) * jnp.where(odd, spread(1), spread(0))
+    total = total + wave(8) * jnp.where(odd, spread(3), spread(2))
+    total = total * wave(9)
     ext = jnp.where((lane == 4) | (lane == 5), columns, 0.0)
     ext = ext[:half_size] + turn(ext[half_size:], 2, 1)
     pressure = dot3(
@@ -340,14 +381,14 @@
             message[pl.ds(3 * h + j, blocks, stride=6), :] = value
 
 
-def final_kernel(received, sent, star, back, rate, out):
+def final_kernel(received, sent, star, back, by_level, out):
     lane = lane_of((LEVELS, LANES))
     row_at = lambda ref, r: ref[pl.ds(3 * (r % 2) + r // 2, LEVELS, stride=6), :]
     p = [row_at(received, r) for r in range(ROWS)]
     extra = [row_at(received, 4), row_at(received, 5)]
     low = [turn(extra[r % 2], -(LOW + r // 2), 1) for r in range(ROWS)]
     high = [turn(extra[r % 2], LANES - 1 - (HIGH + r // 2), 1) for r in range(ROWS)]
-    four_rate = 4.0 * rate[...]
+    four_rate = 4.0 * by_level[pl.ds(0, LEVELS), :]
 
     def next_row(r, opposite):
         here = p[r]
@@ -380,16 +421,17 @@
             out[pl.ds(f * LEVELS * ROWS + x, LEVELS, stride=ROWS), :] = value
 
 
-def call(kernel, shapes, smem, args, name):
+def call(kernel, shapes, args, name, scalars=1, cost=None):
     vmem = pl.BlockSpec(memory_space=pltpu.VMEM)
     scalar = pl.BlockSpec(memory_space=pltpu.SMEM)
     return pl.pallas_call(
         kernel,
         out_shape=[jax.ShapeDtypeStruct(s, F32) for s in shapes],
-        in_specs=[scalar] * smem + [vmem] * (len(args) - smem),
+        in_specs=[scalar] * scalars + [vmem] * (len(args) - scalars),
         out_specs=[vmem] * len(shapes),
         compiler_params=pltpu.CompilerParams(vmem_limit_bytes=32 * 1024 * 1024),
         name=name,
+        cost_estimate=cost,
     )(*args)
 
 
@@ -442,16 +484,14 @@
     place = jnp.stack([lax.axis_index("gx"), lax.axis_index("gy")]).astype(jnp.int32)
     state = model_state.reshape(4 * LEVELS * ROWS, LANES)
     basis, square = east_tables(total_east // 2, blocks)
-    square = np.concatenate([square, square])
     forward_high, forward_low = split_table(basis)
     back_high, back_low = split_table(np.ascontiguousarray(basis.T))
-    square_wide = np.ascontiguousarray(np.broadcast_to(square[:, None], (total_east, LANES)))
-    square_row = np.ascontiguousarray(np.broadcast_to(square[None, :], (8, total_east)))
-
-    x_even, x_odd, y_even, y_odd = call(
+    square_wide = np.ascontiguousarray(np.broadcast_to(square[:, None], (total_east // 2, LANES)))
+    square_row = np.ascontiguousarray(np.broadcast_to(np.concatenate([square, square]), (8, total_east)))
+
+    planes, x_even, x_odd, y_even, y_odd = call(
         edges_kernel,
-        [(5 * LEVELS + 16, LANES), (5 * LEVELS, LANES)] + [(16, LANES)] * 2,
-        1,
+        [(16 * LEVELS, LANES)] + [(5 * LEVELS + 16, LANES), (5 * LEVELS, LANES)] + [(16, LANES)] * 2,
         [place, state],
         "edges",
     )
@@ -461,33 +501,37 @@
     got_y_odd = swap_odd_y(y_both)
     got_x_odd = swap(x_odd, "gx", 1)
     got_y_even = swap(y_even, "gy", 0)
-    (inner,) = call(
+    inner, by_level, by_wave, by_block = call(
         inner_kernel,
-        [(16 * LEVELS, LANES)],
-        0,
-        [state, layer_in.T, layer_bias[:, None], layer_out.T],
+        [(16 * LEVELS, LANES), (3 * LEVELS, LANES), (10 * LANES, LANES), (72, total_east)],
+        [
+            place,
+            planes,
+            jnp.concatenate([mode_rate, density])[None, :],
+            layer_bias[None, :],
+            square_wide,
+            square_row,
+            layer_in,
+            layer_out,
+        ],
         "inner",
+        cost=pl.CostEstimate(flops=10**10, transcendentals=0, bytes_accessed=2**24),
     )
     inner, got_y_odd = lax.optimization_barrier((inner, got_y_odd))
     relayed = hand_over(got_y_odd[16:])
-    zero = jnp.zeros((1,), F32)
-    level_up = jnp.concatenate([0.5 * density[1:] / density[:-1], zero])
-    level_down = jnp.concatenate([zero, 0.5 * density[:-1] / density[1:]])
     star, message = call(
         outer_kernel,
         [(16 * LEVELS, LANES), (blocks * 6, LANES)],
-        1,
         [
             place,
-            state,
+            planes,
             inner,
             got_x_even,
             got_x_odd,
             got_y_even,
             got_y_odd,
             relayed,
-            level_up[:, None],
-            level_down[:, None],
+            by_level,
             mode_forward,
         ],
         "outer",
@@ -496,8 +540,7 @@
     local, moments = call(
         solve_kernel,
         [(total_east, LANES), (32, total_east)],
-        2,
-        [place, mode_rate, modal, forward_high, forward_low, square_wide],
+        [place, modal, forward_high, forward_low, by_wave],
         "solve",
     )
     moments = lax.all_to_all(
@@ -511,17 +554,16 @@
     (reply,) = call(
         back_kernel,
         [(blocks * 6, LANES)],
-        2,
-        [place, mode_rate, local, moments, back_high, back_low, square_wide, square_row],
+        [place, local, moments, back_high, back_low, by_wave, by_block],
         "back",
     )
     pressure = exchange(reply)
     (out,) = call(
         final_kernel,
         [(4 * LEVELS * ROWS, LANES)],
-        0,
-        [pressure, message, star, mode_back, mode_rate[:, None]],
+        [pressure, message, star, mode_back, by_level],
         "final",
+        scalars=0,
     )
     return out.reshape(model_state.shape)
 

time: 107 us -> 106 us (level)
  blocking collectives: 36.7 us -> 65.1 us
  waiting for transfers between devices: 21.9 us -> 2.08 us
  starting transfers between devices: 35.1 us -> 27.9 us
  local copies, waits for them, and re-layouts: 4.64 us -> 1.73 us
    all_to_all x1 -> x2, blocking collectives: 29.9 us -> 57.5 us  [exchange(): lax.all_to_all(shaped, ('gx', 'gy'), 0, 0, tiled=True, axis_index_groups=...]
    all_to_all x1 -> x0, waiting for transfers between devices: 20 us -> none  [exchange(): lax.all_to_all(shaped, ('gx', 'gy'), 0, 0, tiled=True, axis_index_groups=...]
    all_to_all x1 -> x0, starting transfers between devices: 7.32 us -> none  [exchange(): lax.all_to_all(shaped, ('gx', 'gy'), 0, 0, tiled=True, axis_index_groups=...]
    unnamed x30 -> x28, local copies, waits for them, and re-layouts: 4.22 us -> 1.73 us
  transfers between devices with their start and end apart: 6 -> 5, of which waited for: 3 -> 2; matrix products, arithmetic and copies ran while one was open for 2% -> 0% of each run, Pallas kernels for 1% -> 1%
where the time goes in v3:
time: 106 us; the launch traced here: 105 us
  blocking collectives  65.1 us (61%)
  starting transfers between devices  27.9 us (26%)
  Pallas kernels  7.88 us (7%)
  waiting for transfers between devices  2.08 us (2%)
  local copies, waits for them, and re-layouts  1.73 us (2%)
    all_to_all x2, blocking collectives, exchange(): lax.all_to_all(shaped, ('gx', 'gy'), 0, 0, tiled=True, axis_index_groups=...  57.5 us
    ppermute x3, starting transfers between devices, swap(): return lax.ppermute(values, axis, pairs)  14 us
    ppermute x1, starting transfers between devices, swap_odd_y(): return lax.ppermute(values, ('gx', 'gy'), pairs)  12.6 us
    pallas_call x6, Pallas kernels, call(): pl.pallas_call(kernel, out_shape=[jax.ShapeDtypeStruct(s, F32) for s in s...  7.88 us
    all_to_all x1, blocking collectives, on_device(): lax.all_to_all(moments.reshape(4, 8, total_east), 'gy', 0, 0, tiled=True,...  7.6 us
  transfers between devices with their start and end apart: 5, of which 2 were waited for; matrix products, arithmetic and copies ran while one was open for 0% of the time, Pallas kernels for 1%

profile of v3, /device:TPU:1, one launch (start us, length us, event | category | flops | bytes accessed | tf_op | source)
XLA Modules:
  0.0 105.0 jit_solution(5370069288606648748)
XLA Ops:
  0.0 0.1 pad_add_fusion.place
  0.1 0.0 copy-start
  0.1 1.0 copy-done
  1.1 0.0 copy-start.7
  1.1 0.0 copy-start.8
  1.1 0.0 copy-start.10
  1.1 0.9 edges.1
  2.0 0.0 copy-start.12
  2.0 0.0 copy-start.13
  2.1 8.9 %collective-permute-start = (f32[336,128]{1,0:T(8,128)S(1)}, f32[336,128]{1,0:T(8,128)S(1)}, u32[]{:S(2)}, u32[]{:S(2)}) collective-permute-start(f32[336,128]{1,0:T(8,128)S(1)} %get-tuple-element.26), channel_id=1, source_target_pairs={{0,8},{8,0},{16,24},{24,16},{32,40},{40,32},{48,56},{56,48},{64,72... | collective-permute-start | bytes 516104 | tf_op jit(solution)/shard_map/ppermute | solution.py:443
  11.0 0.0 copy-done.12
  11.0 0.0 copy-done.13
  11.0 0.1 maximum_bitcast_fusion.vectors
  11.1 0.9 collective-permute-done.x_even
  12.0 0.0 copy-start.11
  12.0 12.6 %collective-permute-start.1 = (f32[32,128]{1,0:T(8,128)S(1)}, f32[32,128]{1,0:T(8,128)S(1)}, u32[]{:S(2)}, u32[]{:S(2)}) collective-permute-start(f32[32,128]{1,0:T(8,128)S(1)} %pad_maximum_fusion), channel_id=1, source_target_pairs={{1,2},{2,1},{5,6},{6,5},{9,10},{10,9},{11,12},{12,11},{13,14},{14,... | collective-permute-start | bytes 49160 | tf_op jit(solution)/shard_map/ppermute | solution.py:454
  24.7 3.2 %collective-permute-start.2 = (f32[320,128]{1,0:T(8,128)S(1)}, f32[320,128]{1,0:T(8,128)S(1)}, u32[]{:S(2)}, u32[]{:S(2)}) collective-permute-start(f32[320,128]{1,0:T(8,128)S(1)} %get-tuple-element.31), channel_id=1, source_target_pairs={{8,16},{16,8},{24,32},{32,24},{40,48},{48,40},{56,64},{64,56},{72,... | collective-permute-start | bytes 491528 | tf_op jit(solution)/shard_map/ppermute | solution.py:443
  27.8 0.0 copy-start.9
  27.9 0.0 copy-done.7
  27.9 0.0 copy-done.8
  27.9 0.0 copy-done.10
  27.9 0.0 copy-done.11
  27.9 0.6 copy-done.9
  28.5 0.0 copy-start.1
  28.5 1.4 %inner.1 = (f32[1024,128]{1,0:T(8,128)S(1)}, f32[192,128]{1,0:T(8,128)S(1)}, f32[1280,128]{1,0:T(8,128)S(1)}, f32[72,256]{1,0:T(8,128)S(1)}) custom-call(s32[2]{0:T(128)S(1)} %pad_add_fusion.place, f32[1024,128]{1,0:T(8,128)S(1)} %get-tuple-element.23.state, f32[1,128]{1,0:T(1,128)S(1)} %maximum_bitcast_fusion.vectors, f32[1,256]{1,0:T(1,128)S(1)} %bitcast.20, ...), custom_call_target="tpu_custom_call" | custom-call | flops 10000000000 | bytes 16777216 | tf_op jit(solution)/shard_map/inner/pallas_call | solution.py:427
  30.0 1.9 %collective-permute-start.3 = (f32[16,128]{1,0:T(8,128)S(1)}, f32[16,128]{1,0:T(8,128)S(1)}, u32[]{:S(2)}, u32[]{:S(2)}) collective-permute-start(f32[16,128]{1,0:T(8,128)S(1)} %get-tuple-element.32), channel_id=1, source_target_pairs={{0,1},{1,0},{2,3},{3,2},{4,5},{5,4},{6,7},{7,6},{8,9},{9,8},{10,11... | collective-permute-start | bytes 24584 | tf_op jit(solution)/shard_map/ppermute | solution.py:443
  31.9 0.0 collective-permute-done.1.y_odd
  31.9 1.3 %collective-permute-start.4 = (f32[16,128]{1,0:T(8,128)S(1)}, f32[16,128]{1,0:T(8,128)S(1)}, u32[]{:S(2)}, u32[]{:S(2)}) collective-permute-start(f32[16,128]{1,0:T(8,128)S(1)} %slice.7), channel_id=1, source_target_pairs={{8,0},{11,3},{12,4},{15,7},{112,120},{115,123},{116,124},{119,127}... | collective-permute-start | bytes 24584 | tf_op jit(solution)/shard_map/ppermute | solution.py:465
  33.2 1.1 %collective-permute-done.3.y_even = f32[16,128]{1,0:T(8,128)S(1)} collective-permute-done((f32[16,128]{1,0:T(8,128)S(1)}, f32[16,128]{1,0:T(8,128)S(1)}, u32[]{:S(2)}, u32[]{:S(2)}) %collective-permute-start.3) | collective-permute-done | bytes 8224 | tf_op jit(solution)/shard_map/ppermute | solution.py:443
  34.3 0.0 collective-permute-done.4.relayed
  34.4 0.0 collective-permute-done.2.x_odd
  34.4 0.0 copy-done.1
  34.4 1.3 %outer.1 = (f32[1024,128]{1,0:T(8,128)S(1)}, f32[384,128]{1,0:T(8,128)S(1)}) custom-call(s32[2]{0:T(128)S(1)} %pad_add_fusion.place, f32[1024,128]{1,0:T(8,128)S(1)} %get-tuple-element.23.state, f32[1024,128]{1,0:T(8,128)S(1)} %get-tuple-element.30.inner, f32[336,128]{1,0:T(8,128)S(1)} %collective-permute-done.x_even, ...), custom_call_target="tpu_custom_call" | custom-call | tf_op jit(solution)/shard_map/outer/pallas_call | solution.py:427
  35.7 0.0 copy-start.5
  35.7 0.0 copy-start.6
  35.7 29.9 %all_to_all.15 = f32[128,1,384]{2,1,0:T(1,128)S(1)} all-to-all(f32[128,1,384]{2,1,0:T(1,128)S(1)} %bitcast.13), channel_id=1, replica_groups={{0,4,8,12,16,20,24,28,32,36,40,44,48,52,56,60,64,68,72,76,80,84,88,92,9..., dimensions={0} | all-to-all | bytes 393216 | tf_op jit(solution)/shard_map/all_to_all | solution.py:473
  65.6 0.0 copy-done.5
  65.6 0.0 copy-done.6
  65.6 1.6 %solve.1 = (f32[256,128]{1,0:T(8,128)S(1)}, f32[32,256]{1,0:T(8,128)S(1)}) custom-call(s32[2]{0:T(128)S(1)} %pad_add_fusion.place, f32[384,128]{1,0:T(8,128)S(1)} %bitcast.15, bf16[128,128]{1,0:T(8,128)(2,1)S(1)} %copy-done.6, bf16[128,128]{1,0:T(8,128)(2,1)S(1)} %copy-done.5, f32[1280,128]{1,0:T(8,128)S(1)} %get-tuple-element.36.by_wave), custom_call_target="tpu_custom_call" | custom-call | tf_op jit(solution)/shard_map/solve/pallas_call | solution.py:427
  67.2 0.0 copy-start.3
  67.2 0.0 copy-start.4
  67.2 7.6 %all_to_all.16 = f32[4,8,256]{2,1,0:T(8,128)S(1)} all-to-all(f32[4,8,256]{2,1,0:T(8,128)S(1)} %bitcast.19), channel_id=1, replica_groups={{0,1,2,3},{4,5,6,7},{8,9,10,11},{12,13,14,15},{16,17,18,19},{20,21,22,2..., dimensions={0} | all-to-all | bytes 65536 | tf_op jit(solution)/shard_map/all_to_all | solution.py:546
  74.8 0.0 copy-done.3
  74.8 0.0 copy-done.4
  74.8 1.3 %back.2 = f32[384,128]{1,0:T(8,128)S(1)} custom-call(s32[2]{0:T(128)S(1)} %pad_add_fusion.place, f32[256,128]{1,0:T(8,128)S(1)} %get-tuple-element.37.local, f32[32,256]{1,0:T(8,128)S(1)} %bitcast.18, bf16[128,128]{1,0:T(8,128)(2,1)S(1)} %copy-done.4, bf16[128,128]{1,0:T(8,128)(2,1)S(1)} %copy-done.3, f32[1280,128]{1,0:T(8,128)S(1)} %get-tuple-element.36.by_wave, ...), custom_call_target="tpu_custom_call" | custom-call | tf_op jit(solution)/shard_map/back/pallas_call | solution.py:427
  76.1 0.0 copy-start.2
  76.1 27.5 %all_to_all.17 = f32[128,1,384]{2,1,0:T(1,128)S(1)} all-to-all(f32[128,1,384]{2,1,0:T(1,128)S(1)} %bitcast.16), channel_id=1, replica_groups={{0,4,8,12,16,20,24,28,32,36,40,44,48,52,56,60,64,68,72,76,80,84,88,92,9..., dimensions={0} | all-to-all | bytes 393216 | tf_op jit(solution)/shard_map/all_to_all | solution.py:473
  103.7 0.0 copy-done.2
  103.7 1.4 %final.1 = f32[1024,128]{1,0:T(8,128)} custom-call(f32[384,128]{1,0:T(8,128)S(1)} %bitcast.14, f32[384,128]{1,0:T(8,128)S(1)} %get-tuple-element.35.sent, f32[1024,128]{1,0:T(8,128)S(1)} %get-tuple-element.40.star, f32[64,64]{1,0:T(8,128)S(1)} %copy-done.2, f32[192,128]{1,0:T(8,128)S(1)} %get-tuple-element.34.by_level), custom_call_target="tpu_custom_call" | custom-call | tf_op jit(solution)/shard_map/final/pallas_call | solution.py:427
  (3 shorter events, 0.0 us)
Async XLA Ops:
  0.1 1.0 copy-start
  1.1 26.7 %copy-start.7 = (bf16[256,256]{1,0:T(8,128)(2,1)S(1)}, bf16[256,256]{1,0:T(8,128)(2,1)}, u32[]{:S(2)}) copy-start(bf16[256,256]{1,0:T(8,128)(2,1)} %layer_in.1) | copy-start | bytes 393220
  1.1 26.7 %copy-start.8 = (bf16[256,128]{1,0:T(8,128)(2,1)S(1)}, bf16[256,128]{1,0:T(8,128)(2,1)}, u32[]{:S(2)}) copy-start(bf16[256,128]{1,0:T(8,128)(2,1)} %layer_out.1) | copy-start | bytes 196612
  1.1 26.8 %copy-start.10 = (f32[128,128]{1,0:T(8,128)S(1)}, f32[128,128]{1,0:T(8,128)}, u32[]{:S(2)}) copy-start(f32[128,128]{1,0:T(8,128)} %constant.21.clone.square) | copy-start | bytes 196612
  2.0 8.9 %copy-start.12 = (f32[64]{0:T(128)S(1)}, f32[64]{0:T(128)}, u32[]{:S(2)}) copy-start(f32[64]{0:T(128)} %param.15) | copy-start | bytes 772
  2.0 8.9 %copy-start.13 = (f32[64]{0:T(128)S(1)}, f32[64]{0:T(128)}, u32[]{:S(2)}) copy-start(f32[64]{0:T(128)} %param.21) | copy-start | bytes 772
  2.1 9.9 %collective-permute-start = (f32[336,128]{1,0:T(8,128)S(1)}, f32[336,128]{1,0:T(8,128)S(1)}, u32[]{:S(2)}, u32[]{:S(2)}) collective-permute-start(f32[336,128]{1,0:T(8,128)S(1)} %get-tuple-element.26), channel_id=1, source_target_pairs={{0,8},{8,0},{16,24},{24,16},{32,40},{40,32},{48,56},{56,48},{64,72... | collective-permute-start | bytes 516104 | tf_op jit(solution)/shard_map/ppermute | solution.py:443
  12.0 15.9 %copy-start.11 = (f32[8,256]{1,0:T(8,128)S(1)}, f32[8,256]{1,0:T(8,128)}, u32[]{:S(2)}) copy-start(f32[8,256]{1,0:T(8,128)} %constant.22.clone.square_row) | copy-start | bytes 24580
  12.0 19.9 %collective-permute-start.1 = (f32[32,128]{1,0:T(8,128)S(1)}, f32[32,128]{1,0:T(8,128)S(1)}, u32[]{:S(2)}, u32[]{:S(2)}) collective-permute-start(f32[32,128]{1,0:T(8,128)S(1)} %pad_maximum_fusion), channel_id=1, source_target_pairs={{1,2},{2,1},{5,6},{6,5},{9,10},{10,9},{11,12},{12,11},{13,14},{14,... | collective-permute-start | bytes 49160 | tf_op jit(solution)/shard_map/ppermute | solution.py:454
  24.7 9.7 %collective-permute-start.2 = (f32[320,128]{1,0:T(8,128)S(1)}, f32[320,128]{1,0:T(8,128)S(1)}, u32[]{:S(2)}, u32[]{:S(2)}) collective-permute-start(f32[320,128]{1,0:T(8,128)S(1)} %get-tuple-element.31), channel_id=1, source_target_pairs={{8,16},{16,8},{24,32},{32,24},{40,48},{48,40},{56,64},{64,56},{72,... | collective-permute-start | bytes 491528 | tf_op jit(solution)/shard_map/ppermute | solution.py:443
  27.8 0.7 copy-start.9
  28.5 5.8 %copy-start.1 = (f32[64,64]{1,0:T(8,128)S(1)}, f32[64,64]{1,0:T(8,128)}, u32[]{:S(2)}) copy-start(f32[64,64]{1,0:T(8,128)} %forward.1) | copy-start | bytes 49156
  30.0 4.4 %collective-permute-start.3 = (f32[16,128]{1,0:T(8,128)S(1)}, f32[16,128]{1,0:T(8,128)S(1)}, u32[]{:S(2)}, u32[]{:S(2)}) collective-permute-start(f32[16,128]{1,0:T(8,128)S(1)} %get-tuple-element.32), channel_id=1, source_target_pairs={{0,1},{1,0},{2,3},{3,2},{4,5},{5,4},{6,7},{7,6},{8,9},{9,8},{10,11... | collective-permute-start | bytes 24584 | tf_op jit(solution)/shard_map/ppermute | solution.py:443
  31.9 2.4 %collective-permute-start.4 = (f32[16,128]{1,0:T(8,128)S(1)}, f32[16,128]{1,0:T(8,128)S(1)}, u32[]{:S(2)}, u32[]{:S(2)}) collective-permute-start(f32[16,128]{1,0:T(8,128)S(1)} %slice.7), channel_id=1, source_target_pairs={{8,0},{11,3},{12,4},{15,7},{112,120},{115,123},{116,124},{119,127}... | collective-permute-start | bytes 24584 | tf_op jit(solution)/shard_map/ppermute | solution.py:465
  35.7 30.0 %copy-start.5 = (bf16[128,128]{1,0:T(8,128)(2,1)S(1)}, bf16[128,128]{1,0:T(8,128)(2,1)}, u32[]{:S(2)}) copy-start(bf16[128,128]{1,0:T(8,128)(2,1)} %constant.24.clone.basis_low) | copy-start | bytes 98308
  35.7 29.9 %copy-start.6 = (bf16[128,128]{1,0:T(8,128)(2,1)S(1)}, bf16[128,128]{1,0:T(8,128)(2,1)}, u32[]{:S(2)}) copy-start(bf16[128,128]{1,0:T(8,128)(2,1)} %constant.23.clone.basis_high) | copy-start | bytes 98308
  67.2 7.6 %copy-start.3 = (bf16[128,128]{1,0:T(8,128)(2,1)S(1)}, bf16[128,128]{1,0:T(8,128)(2,1)}, u32[]{:S(2)}) copy-start(bf16[128,128]{1,0:T(8,128)(2,1)} %constant.26.clone.basis_low) | copy-start | bytes 98308
  67.2 7.6 %copy-start.4 = (bf16[128,128]{1,0:T(8,128)(2,1)S(1)}, bf16[128,128]{1,0:T(8,128)(2,1)}, u32[]{:S(2)}) copy-start(bf16[128,128]{1,0:T(8,128)(2,1)} %constant.25.clone.basis_high) | copy-start | bytes 98308
  76.1 27.6 %copy-start.2 = (f32[64,64]{1,0:T(8,128)S(1)}, f32[64,64]{1,0:T(8,128)}, u32[]{:S(2)}) copy-start(f32[64,64]{1,0:T(8,128)} %back.3) | copy-start | bytes 49156

commit v4 on v3

--- a/solution.py
+++ b/solution.py
@@ -82,7 +82,7 @@
     return ((gx % 16 == 0) | (gx % 16 == 15)) & ((gy % 4 == 0) | (gy % 4 == 3))
 
 
-def edges_kernel(place, state, planes, x_even, x_odd, y_even, y_odd):
+def edges_kernel(place, state, planes, x_even, x_odd, y_even, y_odd, flat):
     even_x = place[0] % 2 == 0
     even_y = place[1] % 2 == 0
     size = LEVELS * ROWS
@@ -93,18 +93,17 @@
         for x in range(ROWS):
             slot = field * ROWS + x
             planes[pl.ds(slot * LEVELS, LEVELS), :] = values[x]
-            gathered = jnp.where(lane == slot, turn(values[x], slot, 1), gathered)
-            gathered = jnp.where(lane == 16 + slot, turn(values[x], 17 + slot, 1), gathered)
+            gathered = jnp.where(lane >> 1 == slot, turn(values[x], 2 * slot + 1, 1), gathered)
         for slot, depth in ((field, 0), (4, 1)) if field == 0 else ((field, 0),):
             span = pl.ds(slot * LEVELS, LEVELS)
             low, high = values[depth], values[ROWS - 1 - depth]
             x_even[span, :] = jnp.where(even_x, high, low)
             x_odd[span, :] = jnp.where(even_x, low, high)
-    flat = jnp.transpose(jnp.concatenate([gathered, jnp.zeros_like(gathered)], axis=0))
-    low, high = flat[0:16], flat[16:32]
+    flat[...] = jnp.transpose(jnp.concatenate([gathered, jnp.zeros_like(gathered)], axis=0))
+    high, low = flat[pl.ds(0, 16, stride=2), :], flat[pl.ds(1, 16, stride=2), :]
     y_even[...] = jnp.where(even_y, high, low)
     y_odd[...] = jnp.where(even_y, low, high)
-    x_even[pl.ds(5 * LEVELS, 16), :] = jnp.where(even_y, low, high)
+    x_even[pl.ds(5 * LEVELS, 16), :] = jnp.zeros((16, LANES), F32)
 
 
 def column_of(row):
@@ -112,21 +111,15 @@
 
 
 def inner_kernel(
-    place,
     state,
     vectors,
-    bias,
-    square,
-    square_row,
     layer_in,
     layer_out,
     star,
     by_level,
-    by_wave,
-    by_block,
 ):
     fields = [[plane(state, f, x) for x in range(ROWS)] for f in range(4)]
-    tall = column_of(vectors[...])
+    tall = column_of(vectors[:, :LANES])
     rate, density = tall[:LEVELS], tall[LEVELS:]
     row = row_of((LEVELS, LANES))
     by_level[pl.ds(0, LEVELS), :] = rate
@@ -134,6 +127,55 @@
         row < LEVELS - 1, 0.5 * turn(density, -1, 0) / density, 0.0
     )
     by_level[pl.ds(2 * LEVELS, LEVELS), :] = jnp.where(row > 0, 0.5 * turn(density, 1, 0) / density, 0.0)
+    for x in range(ROWS):
+        u, v, w, th = (fields[f][x] for f in range(4))
+        for f in range(4):
+            here = fields[f][x]
+            change = v * north_difference(here) + w * level_difference(here)
+            if x == 0:
+                change = change + u * fields[f][1]
+            elif x == ROWS - 1:
+                change = change - u * fields[f][x - 1]
+            else:
+                change = change + u * (fields[f][x + 1] - fields[f][x - 1])
+            value = here - 0.1 * change
+            if f == 2:
+                value = value + 0.1 * th
+            star[pl.ds((f * ROWS + x) * LEVELS, LEVELS), :] = value
+
+    columns = jnp.concatenate(
+        [jnp.concatenate([fields[f][x] for f in range(4)], axis=0).astype(BF16) for x in range(ROWS)],
+        axis=1,
+    )
+    first = (((0,), (0,)), ((), ()))
+    shift = [column_of(vectors[:, i * LANES : (i + 1) * LANES]) for i in (1, 2)]
+    shift = jnp.concatenate(shift, axis=0)
+    before = lax.dot_general(layer_in[...], columns, first, preferred_element_type=F32)
+    before = before + jnp.concatenate([shift] * ROWS, axis=1)
+    hidden = (before * (1.0 / (1.0 + jnp.exp(-before)))).astype(BF16)
+    forcing = lax.dot_general(layer_out[...], hidden, first, preferred_element_type=F32)
+    for x in range(ROWS):
+        span = slice(x * LANES, (x + 1) * LANES)
+        for f, part in ((2, forcing[LEVELS:, span]), (3, forcing[:LEVELS, span])):
+            at = pl.ds((f * ROWS + x) * LEVELS, LEVELS)
+            star[at, :] = star[at, :] + 0.2 * part
+
+
+def side_terms(state, edge, low):
+    u, v, w = (edge[pl.ds(f * LEVELS, LEVELS), :] for f in range(3))
+    second = edge[pl.ds(4 * LEVELS, LEVELS), :]
+    own = jnp.where(low, plane(state, 0, 0), plane(state, 0, ROWS - 1))
+    sign = jnp.where(low, 0.1, -0.1)
+    adds = [sign * own * edge[pl.ds(f * LEVELS, LEVELS), :] for f in range(4)]
+    along = u * (own - second)
+    beyond = u - (sign * along + 0.1 * (v * north_difference(u) + w * level_difference(u)))
+    return adds, beyond
+
+
+def side_kernel(place, state, x_odd, by_level, square, square_row, terms, by_wave, by_block):
+    adds, beyond = side_terms(state, x_odd, place[0] % 2 == 0)
+    for i, value in enumerate(adds + [beyond]):
+        terms[pl.ds(i * LEVELS, LEVELS), :] = value
     own = by_level[pl.ds(place[0], 1), :]
 
     root, _, rho = decay(own, square[...])
@@ -161,96 +203,57 @@
     scale = -1.0 / root
     by_block[pl.ds(64, 8), :] = jnp.where(row == 0, scale, jnp.where(row == 1, scale * r64, scale * inverse))
 
-    for x in range(ROWS):
-        u, v, w, th = (fields[f][x] for f in range(4))
-        for f in range(4):
-            here = fields[f][x]
-            change = v * north_difference(here) + w * level_difference(here)
-            if x == 0:
-                change = change + u * fields[f][1]
-            elif x == ROWS - 1:
-                change = change - u * fields[f][x - 1]
-            else:
-                change = change + u * (fields[f][x + 1] - fields[f][x - 1])
-            value = here - 0.1 * change
-            if f == 2:
-                value = value + 0.1 * th
-            star[pl.ds((f * ROWS + x) * LEVELS, LEVELS), :] = value
-
-    columns = jnp.concatenate(
-        [jnp.concatenate([fields[f][x] for f in range(4)], axis=0).astype(BF16) for x in range(ROWS)],
-        axis=1,
-    )
-    first = (((0,), (0,)), ((), ()))
-    shift = jnp.concatenate([column_of(bias[:, :LANES]), column_of(bias[:, LANES:])], axis=0)
-    before = lax.dot_general(layer_in[...], columns, first, preferred_element_type=F32)
-    before = before + jnp.concatenate([shift] * ROWS, axis=1)
-    hidden = (before * (1.0 / (1.0 + jnp.exp(-before)))).astype(BF16)
-    forcing = lax.dot_general(layer_out[...], hidden, first, preferred_element_type=F32)
-    for x in range(ROWS):
-        span = slice(x * LANES, (x + 1) * LANES)
-        for f, part in ((2, forcing[LEVELS:, span]), (3, forcing[:LEVELS, span])):
-            at = pl.ds((f * ROWS + x) * LEVELS, LEVELS)
-            star[at, :] = star[at, :] + 0.2 * part
-
 
 def outer_kernel(
     place,
     state,
     inner,
+    odd_terms,
     x_even,
-    x_odd,
     y_even,
     y_odd,
-    relayed,
     by_level,
     forward,
     star,
     message,
+    flat,
 ):
     even_x = place[0] % 2 == 0
     even_y = place[1] % 2 == 0
     shape = (LEVELS, LANES)
     lane = lane_of(shape)
 
-    def beyond(slot):
-        first = x_even[pl.ds(slot * LEVELS, LEVELS), :]
-        second = x_odd[pl.ds(slot * LEVELS, LEVELS), :]
-        return jnp.where(even_x, second, first), jnp.where(even_x, first, second)
-
-    other = jnp.where(far_both(place[0], place[1]), relayed[...], y_odd[0:16, :])
-    low_y = jnp.where(even_y, other, y_even[...])
-    high_y = jnp.where(even_y, y_even[...], other)
-    columns = jnp.transpose(jnp.concatenate([low_y, high_y, jnp.zeros((96, LANES), F32)], axis=0))
-    columns = columns[:LEVELS]
-    outer_x = [beyond(slot) for slot in range(5)]
-
+    relayed = x_even[pl.ds(5 * LEVELS, 16), :]
+    other = jnp.where(far_both(place[0], place[1]), relayed, y_odd[0:16, :])
+    flat[...] = jnp.zeros((LANES, LANES), F32)
+    flat[pl.ds(0, 16, stride=2), :] = jnp.where(even_y, y_even[...], other)
+    flat[pl.ds(1, 16, stride=2), :] = jnp.where(even_y, other, y_even[...])
+    columns = jnp.transpose(flat[...])[:LEVELS]
+    even_adds, even_beyond = side_terms(state, x_even, ~even_x)
+    odd_adds = [odd_terms[pl.ds(f * LEVELS, LEVELS), :] for f in range(4)]
+    odd_beyond = odd_terms[pl.ds(4 * LEVELS, LEVELS), :]
+
+    end_sign = jnp.where(lane == 0, 0.1, jnp.where(lane == LANES - 1, -0.1, 0.0))
     whole = [[None] * ROWS for _ in range(4)]
     side_u = [None] * ROWS
     for x in range(ROWS):
-        u, v = plane(state, 0, x), plane(state, 1, x)
+        v = plane(state, 1, x)
         for f in range(4):
             slot = f * ROWS + x
-            side = jnp.where(lane == 0, turn(columns, -slot, 1), 0.0)
-            side = jnp.where(lane == LANES - 1, -turn(columns, LANES - 1 - 16 - slot, 1), side)
-            side = 0.1 * v * side
+            side = end_sign * v * turn(columns, -(2 * slot + 1), 1)
             if f == 0:
                 side_u[x] = side
             value = inner[pl.ds(slot * LEVELS, LEVELS), :] + side
             if x == 0:
-                value = value + 0.1 * u * outer_x[f][0]
+                value = value + jnp.where(even_x, odd_adds[f], even_adds[f])
             if x == ROWS - 1:
-                value = value - 0.1 * u * outer_x[f][1]
+                value = value + jnp.where(even_x, even_adds[f], odd_adds[f])
             whole[f][x] = value
             star[pl.ds(slot * LEVELS, LEVELS), :] = value
 
-    def east_star(which, neighbour):
-        u, v, w = (outer_x[f][which] for f in range(3))
-        second = outer_x[4][which]
-        along = (neighbour - second) if which == 0 else (second - neighbour)
-        return u - 0.1 * (u * along + v * north_difference(u) + w * level_difference(u))
-
-    padded = [east_star(0, plane(state, 0, 0))] + whole[0] + [east_star(1, plane(state, 0, ROWS - 1))]
+    low_beyond = jnp.where(even_x, odd_beyond, even_beyond)
+    high_beyond = jnp.where(even_x, even_beyond, odd_beyond)
+    padded = [low_beyond] + whole[0] + [high_beyond]
     divergence = []
     extra = [-0.5 * side_u[ROWS - 1], 0.5 * side_u[0]]
     up, down = by_level[pl.ds(LEVELS, LEVELS), :], by_level[pl.ds(2 * LEVELS, LEVELS), :]
@@ -421,7 +424,7 @@
             out[pl.ds(f * LEVELS * ROWS + x, LEVELS, stride=ROWS), :] = value
 
 
-def call(kernel, shapes, args, name, scalars=1, cost=None):
+def call(kernel, shapes, args, name, scalars=1, scratch=(), cost=None):
     vmem = pl.BlockSpec(memory_space=pltpu.VMEM)
     scalar = pl.BlockSpec(memory_space=pltpu.SMEM)
     return pl.pallas_call(
@@ -429,6 +432,7 @@
         out_shape=[jax.ShapeDtypeStruct(s, F32) for s in shapes],
         in_specs=[scalar] * scalars + [vmem] * (len(args) - scalars),
         out_specs=[vmem] * len(shapes),
+        scratch_shapes=[pltpu.VMEM(s, F32) for s in scratch],
         compiler_params=pltpu.CompilerParams(vmem_limit_bytes=32 * 1024 * 1024),
         name=name,
         cost_estimate=cost,
@@ -451,17 +455,6 @@
             one, two = j % count_y, (j + 1) % count_y
             if not far_both(i, one):
                 pairs += [(i * count_y + one, i * count_y + two), (i * count_y + two, i * count_y + one)]
-    return lax.ppermute(values, ("gx", "gy"), pairs)
-
-
-def hand_over(values):
-    count_x, count_y = lax.axis_size("gx"), lax.axis_size("gy")
-    pairs = [
-        ((i ^ 1) * count_y + j, i * count_y + j)
-        for i in range(count_x)
-        for j in range(count_y)
-        if far_both(i, j)
-    ]
     return lax.ppermute(values, ("gx", "gy"), pairs)
 
 
@@ -494,31 +487,36 @@
         [(16 * LEVELS, LANES)] + [(5 * LEVELS + 16, LANES), (5 * LEVELS, LANES)] + [(16, LANES)] * 2,
         [place, state],
         "edges",
-    )
-    got_x_even = swap(x_even, "gx", 0)
-    y_both = jnp.concatenate([y_odd, got_x_even[5 * LEVELS :]], axis=0)
+        scratch=[(LANES, LANES)],
+    )
+    y_both = jnp.concatenate([y_odd, swap(y_odd, "gx", 0)], axis=0)
     y_both, x_odd, y_even = lax.optimization_barrier((y_both, x_odd, y_even))
     got_y_odd = swap_odd_y(y_both)
     got_x_odd = swap(x_odd, "gx", 1)
-    got_y_even = swap(y_even, "gy", 0)
-    inner, by_level, by_wave, by_block = call(
+    inner, by_level = call(
         inner_kernel,
-        [(16 * LEVELS, LANES), (3 * LEVELS, LANES), (10 * LANES, LANES), (72, total_east)],
+        [(16 * LEVELS, LANES), (3 * LEVELS, LANES)],
         [
-            place,
             planes,
-            jnp.concatenate([mode_rate, density])[None, :],
-            layer_bias[None, :],
-            square_wide,
-            square_row,
+            jnp.concatenate([mode_rate, density, layer_bias])[None, :],
             layer_in,
             layer_out,
         ],
         "inner",
+        scalars=0,
         cost=pl.CostEstimate(flops=10**10, transcendentals=0, bytes_accessed=2**24),
     )
-    inner, got_y_odd = lax.optimization_barrier((inner, got_y_odd))
-    relayed = hand_over(got_y_odd[16:])
+    inner, y_even = lax.optimization_barrier((inner, y_even))
+    got_y_even = swap(y_even, "gy", 0)
+    inner, got_y_odd, got_y_even = lax.optimization_barrier((inner, got_y_odd, got_y_even))
+    got_x_even = swap(x_even.at[5 * LEVELS :].set(got_y_odd[16:]), "gx", 0)
+    odd_terms, by_wave, by_block = call(
+        side_kernel,
+        [(5 * LEVELS, LANES), (10 * LANES, LANES), (72, total_east)],
+        [place, planes, got_x_odd, by_level, square_wide, square_row],
+        "side",
+        cost=pl.CostEstimate(flops=10**11, transcendentals=0, bytes_accessed=2**27),
+    )
     star, message = call(
         outer_kernel,
         [(16 * LEVELS, LANES), (blocks * 6, LANES)],
@@ -526,15 +524,15 @@
             place,
             planes,
             inner,
+            odd_terms,
             got_x_even,
-            got_x_odd,
             got_y_even,
             got_y_odd,
-            relayed,
             by_level,
             mode_forward,
         ],
         "outer",
+        scratch=[(LANES, LANES)],
     )
     modal = exchange(message)
     local, moments = call(

time: 106 us -> 109 us (1.028)
  blocking collectives: 65.1 us -> 68.6 us
    all_to_all x2, blocking collectives: 57.5 us -> 61.8 us  [exchange(): lax.all_to_all(shaped, ('gx', 'gy'), 0, 0, tiled=True, axis_index_groups=...]
    ppermute x3 -> x4, starting transfers between devices: 14 us -> 15.9 us  [swap(): return lax.ppermute(values, axis, pairs)]
    ppermute x1 -> x0, starting transfers between devices: 1.29 us -> none  [hand_over(): return lax.ppermute(values, ('gx', 'gy'), pairs)]
    pallas_call x6 -> x7, Pallas kernels: 7.88 us -> 7.67 us  [call(): pl.pallas_call(kernel, out_shape=[jax.ShapeDtypeStruct(s, F32) for s in s...]
    ppermute x3 -> x4, waiting for transfers between devices: 2.07 us -> 2.2 us  [swap(): return lax.ppermute(values, axis, pairs)]
where the time goes in v4:
time: 109 us; the launch traced here: 108 us
  blocking collectives  68.6 us (63%)
  starting transfers between devices  28.4 us (26%)
  Pallas kernels  7.67 us (7%)
  waiting for transfers between devices  2.2 us (2%)
  local copies, waits for them, and re-layouts  1.12 us (1%)
    all_to_all x2, blocking collectives, exchange(): lax.all_to_all(shaped, ('gx', 'gy'), 0, 0, tiled=True, axis_index_groups=...  61.8 us
    ppermute x4, starting transfers between devices, swap(): return lax.ppermute(values, axis, pairs)  15.9 us
    ppermute x1, starting transfers between devices, swap_odd_y(): return lax.ppermute(values, ('gx', 'gy'), pairs)  12.5 us
    pallas_call x7, Pallas kernels, call(): pl.pallas_call(kernel, out_shape=[jax.ShapeDtypeStruct(s, F32) for s in s...  7.67 us
    all_to_all x1, blocking collectives, on_device(): lax.all_to_all(moments.reshape(4, 8, total_east), 'gy', 0, 0, tiled=True,...  6.79 us
    ppermute x4, waiting for transfers between devices, swap(): return lax.ppermute(values, axis, pairs)  2.2 us
  transfers between devices with their start and end apart: 5, of which 2 were waited for; matrix products, arithmetic and copies ran while one was open for 0% of the time, Pallas kernels for 1%

profile of v4, /device:TPU:1, one launch (start us, length us, event | category | flops | bytes accessed | tf_op | source)
XLA Modules:
  0.0 108.4 jit_solution(10140169722621170111)
XLA Ops:
  0.0 0.1 pad_add_fusion.place
  0.1 0.0 copy-start
  0.1 1.0 copy-done
  1.1 0.0 copy-start.13
  1.1 0.0 copy-start.7
  1.1 0.0 copy-start.8
  1.1 0.8 edges.1
  1.9 0.0 copy-start.11
  2.0 0.0 copy-start.12
  2.0 8.9 %collective-permute-start = (f32[16,128]{1,0:T(8,128)S(1)}, f32[16,128]{1,0:T(8,128)S(1)}, u32[]{:S(2)}, u32[]{:S(2)}) collective-permute-start(f32[16,128]{1,0:T(8,128)S(1)} %get-tuple-element.41), channel_id=1, source_target_pairs={{0,8},{8,0},{16,24},{24,16},{32,40},{40,32},{48,56},{56,48},{64,72... | collective-permute-start | bytes 24584 | tf_op jit(solution)/shard_map/ppermute | solution.py:447
  10.9 0.0 copy-done.13
  10.9 0.0 copy-done.11
  10.9 0.0 copy-done.12
  10.9 0.1 pad_maximum_fusion.1
  11.0 0.7 collective-permute-done
  11.7 12.5 %collective-permute-start.1 = (f32[32,128]{1,0:T(8,128)S(1)}, f32[32,128]{1,0:T(8,128)S(1)}, u32[]{:S(2)}, u32[]{:S(2)}) collective-permute-start(f32[32,128]{1,0:T(8,128)S(1)} %pad_maximum_fusion), channel_id=1, source_target_pairs={{1,2},{2,1},{5,6},{6,5},{9,10},{10,9},{11,12},{12,11},{13,14},{14,... | collective-permute-start | bytes 49160 | tf_op jit(solution)/shard_map/ppermute | solution.py:458
  24.2 0.0 copy-done.7
  24.2 0.0 copy-done.8
  24.2 0.0 copy-start.9
  24.3 0.7 inner.1
  25.0 1.9 %collective-permute-start.2 = (f32[16,128]{1,0:T(8,128)S(1)}, f32[16,128]{1,0:T(8,128)S(1)}, u32[]{:S(2)}, u32[]{:S(2)}) collective-permute-start(f32[16,128]{1,0:T(8,128)S(1)} %get-tuple-element.47), channel_id=1, source_target_pairs={{0,1},{1,0},{2,3},{3,2},{4,5},{5,4},{6,7},{7,6},{8,9},{9,8},{10,11... | collective-permute-start | bytes 24584 | tf_op jit(solution)/shard_map/ppermute | solution.py:447
  26.9 3.2 %collective-permute-start.3 = (f32[320,128]{1,0:T(8,128)S(1)}, f32[320,128]{1,0:T(8,128)S(1)}, u32[]{:S(2)}, u32[]{:S(2)}) collective-permute-start(f32[320,128]{1,0:T(8,128)S(1)} %get-tuple-element.49), channel_id=1, source_target_pairs={{8,16},{16,8},{24,32},{32,24},{40,48},{48,40},{56,64},{64,56},{72,... | collective-permute-start | bytes 491528 | tf_op jit(solution)/shard_map/ppermute | solution.py:447
  30.1 0.0 collective-permute-done.2.y_even
  30.1 0.0 collective-permute-done.1.y_odd
  30.1 0.0 copy-start.10
  30.1 1.9 %collective-permute-start.4 = (f32[336,128]{1,0:T(8,128)S(1)}, f32[336,128]{1,0:T(8,128)S(1)}, u32[]{:S(2)}, u32[]{:S(2)}) collective-permute-start(f32[336,128]{1,0:T(8,128)S(1)} %slice_dynamic-update-slice_fusion), channel_id=1, source_target_pairs={{0,8},{8,0},{16,24},{24,16},{32,40},{40,32},{48,56},{56,48},{64,72... | collective-permute-start | bytes 516104 | tf_op jit(solution)/shard_map/ppermute | solution.py:447
  32.1 1.5 %collective-permute-done.3.x_odd = f32[320,128]{1,0:T(8,128)S(1)} collective-permute-done((f32[320,128]{1,0:T(8,128)S(1)}, f32[320,128]{1,0:T(8,128)S(1)}, u32[]{:S(2)}, u32[]{:S(2)}) %collective-permute-start.3) | collective-permute-done | bytes 163872 | tf_op jit(solution)/shard_map/ppermute | solution.py:447
  33.6 0.0 copy-done.9
  33.6 0.0 copy-done.10
  33.6 0.0 copy-start.1
  33.6 0.7 side.1
  34.3 0.0 collective-permute-done.4.x_even
  34.3 0.0 copy-done.1
  34.3 1.1 %outer.1 = (f32[1024,128]{1,0:T(8,128)S(1)}, f32[384,128]{1,0:T(8,128)S(1)}) custom-call(s32[2]{0:T(128)S(1)} %pad_add_fusion.place, f32[1024,128]{1,0:T(8,128)S(1)} %get-tuple-element.39.state, f32[1024,128]{1,0:T(8,128)S(1)} %get-tuple-element.48.inner, f32[320,128]{1,0:T(8,128)S(1)} %get-tuple-element.51.odd_terms, ...), custom_call_target="tpu_custom_call" | custom-call | tf_op jit(solution)/shard_map/outer/pallas_call | solution.py:430
  35.5 0.0 copy-start.5
  35.5 0.0 copy-start.6
  35.5 34.5 %all_to_all.15 = f32[128,1,384]{2,1,0:T(1,128)S(1)} all-to-all(f32[128,1,384]{2,1,0:T(1,128)S(1)} %bitcast.10), channel_id=1, replica_groups={{0,4,8,12,16,20,24,28,32,36,40,44,48,52,56,60,64,68,72,76,80,84,88,92,9..., dimensions={0} | all-to-all | bytes 393216 | tf_op jit(solution)/shard_map/all_to_all | solution.py:466
  70.1 0.0 copy-done.5
  70.1 0.0 copy-done.6
  70.1 1.6 %solve.1 = (f32[256,128]{1,0:T(8,128)S(1)}, f32[32,256]{1,0:T(8,128)S(1)}) custom-call(s32[2]{0:T(128)S(1)} %pad_add_fusion.place, f32[384,128]{1,0:T(8,128)S(1)} %bitcast.12, bf16[128,128]{1,0:T(8,128)(2,1)S(1)} %copy-done.6, bf16[128,128]{1,0:T(8,128)(2,1)S(1)} %copy-done.5, f32[1280,128]{1,0:T(8,128)S(1)} %get-tuple-element.56.by_wave), custom_call_target="tpu_custom_call" | custom-call | tf_op jit(solution)/shard_map/solve/pallas_call | solution.py:430
  71.6 0.0 copy-start.3
  71.6 0.0 copy-start.4
  71.6 6.8 %all_to_all.16 = f32[4,8,256]{2,1,0:T(8,128)S(1)} all-to-all(f32[4,8,256]{2,1,0:T(8,128)S(1)} %bitcast.16), channel_id=1, replica_groups={{0,1,2,3},{4,5,6,7},{8,9,10,11},{12,13,14,15},{16,17,18,19},{20,21,22,2..., dimensions={0} | all-to-all | bytes 65536 | tf_op jit(solution)/shard_map/all_to_all | solution.py:544
  78.4 0.0 copy-done.3
  78.4 0.0 copy-done.4
  78.4 1.3 %back.2 = f32[384,128]{1,0:T(8,128)S(1)} custom-call(s32[2]{0:T(128)S(1)} %pad_add_fusion.place, f32[256,128]{1,0:T(8,128)S(1)} %get-tuple-element.57.local, f32[32,256]{1,0:T(8,128)S(1)} %bitcast.15, bf16[128,128]{1,0:T(8,128)(2,1)S(1)} %copy-done.4, bf16[128,128]{1,0:T(8,128)(2,1)S(1)} %copy-done.3, f32[1280,128]{1,0:T(8,128)S(1)} %get-tuple-element.56.by_wave, ...), custom_call_target="tpu_custom_call" | custom-call | tf_op jit(solution)/shard_map/back/pallas_call | solution.py:430
  79.7 0.0 copy-start.2
  79.8 27.2 %all_to_all.17 = f32[128,1,384]{2,1,0:T(1,128)S(1)} all-to-all(f32[128,1,384]{2,1,0:T(1,128)S(1)} %bitcast.13), channel_id=1, replica_groups={{0,4,8,12,16,20,24,28,32,36,40,44,48,52,56,60,64,68,72,76,80,84,88,92,9..., dimensions={0} | all-to-all | bytes 393216 | tf_op jit(solution)/shard_map/all_to_all | solution.py:466
  107.0 0.0 copy-done.2
  107.0 1.4 %final.1 = f32[1024,128]{1,0:T(8,128)} custom-call(f32[384,128]{1,0:T(8,128)S(1)} %bitcast.11, f32[384,128]{1,0:T(8,128)S(1)} %get-tuple-element.55.sent, f32[1024,128]{1,0:T(8,128)S(1)} %get-tuple-element.60.star, f32[64,64]{1,0:T(8,128)S(1)} %copy-done.2, f32[192,128]{1,0:T(8,128)S(1)} %get-tuple-element.50.by_level), custom_call_target="tpu_custom_call" | custom-call | tf_op jit(solution)/shard_map/final/pallas_call | solution.py:430
  (3 shorter events, 0.0 us)
Async XLA Ops:
  0.1 1.0 copy-start
  1.1 9.8 %copy-start.13 = (f32[64]{0:T(128)S(1)}, f32[64]{0:T(128)}, u32[]{:S(2)}) copy-start(f32[64]{0:T(128)} %param.23) | copy-start | bytes 772
  1.1 23.1 %copy-start.7 = (bf16[256,256]{1,0:T(8,128)(2,1)S(1)}, bf16[256,256]{1,0:T(8,128)(2,1)}, u32[]{:S(2)}) copy-start(bf16[256,256]{1,0:T(8,128)(2,1)} %layer_in.1) | copy-start | bytes 393220
  1.1 23.1 %copy-start.8 = (bf16[256,128]{1,0:T(8,128)(2,1)S(1)}, bf16[256,128]{1,0:T(8,128)(2,1)}, u32[]{:S(2)}) copy-start(bf16[256,128]{1,0:T(8,128)(2,1)} %layer_out.1) | copy-start | bytes 196612
  1.9 9.0 %copy-start.11 = (f32[256]{0:T(256)S(1)}, f32[256]{0:T(256)}, u32[]{:S(2)}) copy-start(f32[256]{0:T(256)} %param.19) | copy-start | bytes 3076
  2.0 9.0 %copy-start.12 = (f32[64]{0:T(128)S(1)}, f32[64]{0:T(128)}, u32[]{:S(2)}) copy-start(f32[64]{0:T(128)} %param.17) | copy-start | bytes 772
  2.0 9.7 %collective-permute-start = (f32[16,128]{1,0:T(8,128)S(1)}, f32[16,128]{1,0:T(8,128)S(1)}, u32[]{:S(2)}, u32[]{:S(2)}) collective-permute-start(f32[16,128]{1,0:T(8,128)S(1)} %get-tuple-element.41), channel_id=1, source_target_pairs={{0,8},{8,0},{16,24},{24,16},{32,40},{40,32},{48,56},{56,48},{64,72... | collective-permute-start | bytes 24584 | tf_op jit(solution)/shard_map/ppermute | solution.py:447
  11.7 18.4 %collective-permute-start.1 = (f32[32,128]{1,0:T(8,128)S(1)}, f32[32,128]{1,0:T(8,128)S(1)}, u32[]{:S(2)}, u32[]{:S(2)}) collective-permute-start(f32[32,128]{1,0:T(8,128)S(1)} %pad_maximum_fusion), channel_id=1, source_target_pairs={{1,2},{2,1},{5,6},{6,5},{9,10},{10,9},{11,12},{12,11},{13,14},{14,... | collective-permute-start | bytes 49160 | tf_op jit(solution)/shard_map/ppermute | solution.py:458
  24.2 9.3 %copy-start.9 = (f32[128,128]{1,0:T(8,128)S(1)}, f32[128,128]{1,0:T(8,128)}, u32[]{:S(2)}) copy-start(f32[128,128]{1,0:T(8,128)} %constant.50.clone.square) | copy-start | bytes 196612
  25.0 5.1 %collective-permute-start.2 = (f32[16,128]{1,0:T(8,128)S(1)}, f32[16,128]{1,0:T(8,128)S(1)}, u32[]{:S(2)}, u32[]{:S(2)}) collective-permute-start(f32[16,128]{1,0:T(8,128)S(1)} %get-tuple-element.47), channel_id=1, source_target_pairs={{0,1},{1,0},{2,3},{3,2},{4,5},{5,4},{6,7},{7,6},{8,9},{9,8},{10,11... | collective-permute-start | bytes 24584 | tf_op jit(solution)/shard_map/ppermute | solution.py:447
  26.9 6.6 %collective-permute-start.3 = (f32[320,128]{1,0:T(8,128)S(1)}, f32[320,128]{1,0:T(8,128)S(1)}, u32[]{:S(2)}, u32[]{:S(2)}) collective-permute-start(f32[320,128]{1,0:T(8,128)S(1)} %get-tuple-element.49), channel_id=1, source_target_pairs={{8,16},{16,8},{24,32},{32,24},{40,48},{48,40},{56,64},{64,56},{72,... | collective-permute-start | bytes 491528 | tf_op jit(solution)/shard_map/ppermute | solution.py:447
  30.1 3.5 %copy-start.10 = (f32[8,256]{1,0:T(8,128)S(1)}, f32[8,256]{1,0:T(8,128)}, u32[]{:S(2)}) copy-start(f32[8,256]{1,0:T(8,128)} %constant.51.clone.square_row) | copy-start | bytes 24580
  30.1 4.2 %collective-permute-start.4 = (f32[336,128]{1,0:T(8,128)S(1)}, f32[336,128]{1,0:T(8,128)S(1)}, u32[]{:S(2)}, u32[]{:S(2)}) collective-permute-start(f32[336,128]{1,0:T(8,128)S(1)} %slice_dynamic-update-slice_fusion), channel_id=1, source_target_pairs={{0,8},{8,0},{16,24},{24,16},{32,40},{40,32},{48,56},{56,48},{64,72... | collective-permute-start | bytes 516104 | tf_op jit(solution)/shard_map/ppermute | solution.py:447
  33.6 0.8 copy-start.1
  35.5 34.6 %copy-start.5 = (bf16[128,128]{1,0:T(8,128)(2,1)S(1)}, bf16[128,128]{1,0:T(8,128)(2,1)}, u32[]{:S(2)}) copy-start(bf16[128,128]{1,0:T(8,128)(2,1)} %constant.53.clone.basis_low) | copy-start | bytes 98308
  35.5 34.6 %copy-start.6 = (bf16[128,128]{1,0:T(8,128)(2,1)S(1)}, bf16[128,128]{1,0:T(8,128)(2,1)}, u32[]{:S(2)}) copy-start(bf16[128,128]{1,0:T(8,128)(2,1)} %constant.52.clone.basis_high) | copy-start | bytes 98308
  71.6 6.8 %copy-start.3 = (bf16[128,128]{1,0:T(8,128)(2,1)S(1)}, bf16[128,128]{1,0:T(8,128)(2,1)}, u32[]{:S(2)}) copy-start(bf16[128,128]{1,0:T(8,128)(2,1)} %constant.55.clone.basis_low) | copy-start | bytes 98308
  71.6 6.8 %copy-start.4 = (bf16[128,128]{1,0:T(8,128)(2,1)S(1)}, bf16[128,128]{1,0:T(8,128)(2,1)}, u32[]{:S(2)}) copy-start(bf16[128,128]{1,0:T(8,128)(2,1)} %constant.54.clone.basis_high) | copy-start | bytes 98308
  79.7 27.3 %copy-start.2 = (f32[64,64]{1,0:T(8,128)S(1)}, f32[64,64]{1,0:T(8,128)}, u32[]{:S(2)}) copy-start(f32[64,64]{1,0:T(8,128)} %back.3) | copy-start | bytes 49156

commit v5 on v4

--- a/solution.py
+++ b/solution.py
@@ -82,14 +82,14 @@
     return ((gx % 16 == 0) | (gx % 16 == 15)) & ((gy % 4 == 0) | (gy % 4 == 3))
 
 
-def edges_kernel(place, state, planes, x_even, x_odd, y_even, y_odd, flat):
+def edges_kernel(place, state_u, state_v, state_w, state_th, planes, x_even, x_odd, y_even, y_odd, flat):
     even_x = place[0] % 2 == 0
     even_y = place[1] % 2 == 0
-    size = LEVELS * ROWS
+    states = (state_u, state_v, state_w, state_th)
     lane = lane_of((LEVELS, LANES))
     gathered = jnp.zeros((LEVELS, LANES), F32)
     for field in range(4):
-        values = [state[pl.ds(field * size + x, LEVELS, stride=ROWS), :] for x in range(ROWS)]
+        values = [states[field][pl.ds(x, LEVELS, stride=ROWS), :] for x in range(ROWS)]
         for x in range(ROWS):
             slot = field * ROWS + x
             planes[pl.ds(slot * LEVELS, LEVELS), :] = values[x]
@@ -103,7 +103,7 @@
     high, low = flat[pl.ds(0, 16, stride=2), :], flat[pl.ds(1, 16, stride=2), :]
     y_even[...] = jnp.where(even_y, high, low)
     y_odd[...] = jnp.where(even_y, low, high)
-    x_even[pl.ds(5 * LEVELS, 16), :] = jnp.zeros((16, LANES), F32)
+    x_even[pl.ds(5 * LEVELS, 16), :] = jnp.where(even_y, low, high)
 
 
 def column_of(row):
@@ -172,22 +172,27 @@
     return adds, beyond
 
 
-def side_kernel(place, state, x_odd, by_level, square, square_row, terms, by_wave, by_block):
+def side_kernel(place, state, x_odd, by_level, square_row, terms, by_row, by_wave, by_block):
     adds, beyond = side_terms(state, x_odd, place[0] % 2 == 0)
     for i, value in enumerate(adds + [beyond]):
         terms[pl.ds(i * LEVELS, LEVELS), :] = value
     own = by_level[pl.ds(place[0], 1), :]
 
-    root, _, rho = decay(own, square[...])
+    both = jnp.concatenate([own, own], axis=1)
+    root, inverse, rho = decay(both, square_row[...])
     powers = squarings(rho, 6)
-    half = lane_of((LANES, LANES)) >> 1
-    rising = lane_powers(powers, half)
-    falling = lane_powers(powers, 63 - half)
-    for i, value in enumerate(powers + [rising, falling, -1.0 / root]):
-        by_wave[pl.ds(i * LANES, LANES), :] = value
-
-    root, inverse, rho = decay(jnp.concatenate([own, own], axis=1), square_row[...])
-    r64 = squarings(rho, 6)[6]
+    for i, value in enumerate(powers + [powers[6] * rho, -1.0 / root]):
+        by_row[pl.ds(8 * i, 8), :] = value
+    half = row_of((LANES, LANES)) >> 1
+    odd = (row_of((LANES, LANES)) & 1) != 0
+    narrow = [jnp.broadcast_to(value[0:1, :LANES], (LANES, LANES)) for value in powers[:6]]
+    rising = lane_powers(narrow, half)
+    falling = lane_powers(narrow, 63 - half)
+    by_wave[pl.ds(0, LANES), :] = rising
+    by_wave[pl.ds(LANES, LANES), :] = falling
+    by_wave[pl.ds(2 * LANES, LANES), :] = narrow[0] * jnp.where(odd, rising, falling)
+
+    r64 = powers[6]
     r128 = r64 * r64
     r256 = r128 * r128
     images = 1.0 / (1.0 - r256 * r256)
@@ -212,6 +217,7 @@
     x_even,
     y_even,
     y_odd,
+    relayed,
     by_level,
     forward,
     star,
@@ -223,8 +229,7 @@
     shape = (LEVELS, LANES)
     lane = lane_of(shape)
 
-    relayed = x_even[pl.ds(5 * LEVELS, 16), :]
-    other = jnp.where(far_both(place[0], place[1]), relayed, y_odd[0:16, :])
+    other = jnp.where(far_both(place[0], place[1]), relayed[...], y_odd[0:16, :])
     flat[...] = jnp.zeros((LANES, LANES), F32)
     flat[pl.ds(0, 16, stride=2), :] = jnp.where(even_y, y_even[...], other)
     flat[pl.ds(1, 16, stride=2), :] = jnp.where(even_y, other, y_even[...])
@@ -292,84 +297,98 @@
     return product
 
 
-def solve_kernel(place, received, basis_high, basis_low, by_wave, local, moments):
+def shifted(values, shift):
+    size = values.shape[0]
+    if shift % 8 == 0:
+        zeros = jnp.zeros((abs(shift), values.shape[1]), F32)
+        if shift > 0:
+            return jnp.concatenate([zeros, values[:-shift]], axis=0)
+        return jnp.concatenate([values[-shift:], zeros], axis=0)
+    row = row_of(values.shape)
+    inside = row >= shift if shift > 0 else row < size + shift
+    return jnp.where(inside, turn(values, shift, 0), 0.0)
+
+
+def by_parity(even, odd):
+    shape = (8, even.shape[1])
+    tile = jnp.where((row_of(shape) & 1) != 0, jnp.broadcast_to(odd, shape), jnp.broadcast_to(even, shape))
+    return jnp.concatenate([tile] * (LANES // 8), axis=0)
+
+
+def halves(values):
+    return jnp.concatenate([values, values], axis=1)
+
+
+def solve_kernel(place, received, basis_high, basis_low, by_row, by_wave, local, moments):
     blocks = received.shape[0] // 6
-    half_size = blocks * 2
-    size = half_size * 2
     lane = lane_of((blocks, LANES))
     ends = (lane == 0) | (lane == LANES - 1)
     even = place[1] < 4
-    inside, outside = [], [None, None]
+    inside, outside = [], [jnp.zeros((blocks, LANES), F32)] * 2
     for h in range(2):
         first, second, extra = (received[pl.ds(3 * h + j, blocks, stride=6), :] for j in range(3))
         first = first + jnp.where(ends & even, turn(extra, 1, 0), 0.0)
         second = second + jnp.where(ends & ~even, turn(extra, -1, 0), 0.0)
         inside.append(jnp.concatenate([first, second], axis=0))
         for r in range(2):
-            value = jnp.zeros_like(extra) if outside[r] is None else outside[r]
-            for i in range(4):
-                at = 4 * h + i
-                value = jnp.where(lane == at, turn(extra, at - (HIGH, LOW)[i % 2] - r, 1), value)
-            outside[r] = value
-    right = jnp.concatenate(inside + [jnp.concatenate(outside, axis=0)], axis=1)
-    spectral = dot3((basis_high[...], basis_low[...]), parts(right))
-    source = jnp.concatenate([spectral[:, :LANES], spectral[:, LANES : 2 * LANES]], axis=0)
-    ext = spectral[:, 2 * LANES :]
-    ext = jnp.concatenate([ext, turn(ext, -4, 1)], axis=0)
-
-    wave = lambda i: jnp.concatenate([by_wave[pl.ds(i * LANES, LANES), :]] * 2, axis=0)
-    powers = [wave(i) for i in range(7)]
-    rho = powers[0]
-    lane = lane_of((size, LANES))
+            for i, start in enumerate((HIGH, LOW)):
+                at = 2 * h + i
+                outside[r] = jnp.where(lane == at, turn(extra, at - start - r, 1), outside[r])
+    right = parts(jnp.concatenate(inside + [jnp.concatenate(outside, axis=0)], axis=1))
+    first = (((0,), (0,)), ((), ()))
+    dot = lambda a, b: lax.dot_general(a, b[...], first, preferred_element_type=F32)
+    spectral = dot(right[0], basis_high) + (dot(right[0], basis_low) + dot(right[1], basis_high))
+    source = jnp.concatenate([spectral[:LANES], spectral[LANES : 2 * LANES]], axis=1)
+    ext = spectral[2 * LANES : 2 * LANES + 8]
+    high = jnp.concatenate([ext[0:1], ext[2:3]], axis=1)
+    low = jnp.concatenate([ext[1:2], ext[3:4]], axis=1)
+
+    power = lambda i: by_row[pl.ds(8 * i, 1), :]
     ahead, behind = source, source
     for bit in range(6):
-        shift = 2 << bit
-        ahead = ahead + powers[bit] * jnp.where(lane >= shift, turn(ahead, shift, 1), 0.0)
-        behind = behind + powers[bit] * jnp.where(lane < LANES - shift, turn(behind, -shift, 1), 0.0)
-    odd = (lane & 1) != 0
-    first = jnp.broadcast_to(ext[:, 0:1], (size, LANES))
-    second = jnp.broadcast_to(ext[:, 1:2], (size, LANES))
-    border = rho * jnp.where(odd, wave(7) * second, wave(8) * first)
+        ahead = ahead + power(bit) * shifted(ahead, 2 << bit)
+        behind = behind + power(bit) * shifted(behind, -(2 << bit))
+    border = halves(by_wave[pl.ds(2 * LANES, LANES), :]) * by_parity(high, low)
     local[...] = ahead + behind - source + border
-    weight = jnp.where((lane == 1) | (lane == 2), powers[6] * rho, 1.0)
-    column = jnp.where(lane < 2, turn(rho * ahead, 2, 1), turn(rho * behind, 2, 1)) + ext * weight
-    column = jnp.where(lane < 4, column, 0.0)
-    across = jnp.transpose(column)[:8]
+    rho, r65 = power(0), power(7)
+    across = [
+        rho * ahead[LANES - 2 : LANES - 1] + high,
+        rho * ahead[LANES - 1 :] + r65 * low,
+        rho * behind[0:1] + r65 * high,
+        rho * behind[1:2] + low,
+        jnp.zeros((4, source.shape[1]), F32),
+    ]
+    across = jnp.concatenate(across, axis=0)
     for j in range(4):
         moments[pl.ds(j * 8, 8), :] = across
 
 
-def back_kernel(place, local, moments, basis_high, basis_low, by_wave, by_block, message):
-    size = local.shape[0]
-    half_size = size // 2
-    blocks = half_size // 2
+def back_kernel(place, local, moments, basis_high, basis_low, by_row, by_wave, by_block, message):
+    width = local.shape[1]
+    blocks = basis_high.shape[0] // 2
     even = place[1] < 4
     mine = place[1] & 3
-    carry = jnp.zeros((8, size), F32)
+    carry = jnp.zeros((8, width), F32)
     for j in range(4):
         theirs = moments[pl.ds(j * 8, 8), :]
-        carry = carry + by_block[pl.ds(16 * j, 8), :] * theirs
-        carry = carry + by_block[pl.ds(16 * j + 8, 8), :] * turn(theirs, half_size, 1)
+        swapped = jnp.concatenate([theirs[:, LANES:], theirs[:, :LANES]], axis=1)
+        carry = carry + by_block[pl.ds(16 * j, 8), :] * theirs + by_block[pl.ds(16 * j + 8, 8), :] * swapped
     own = moments[pl.ds(pl.multiple_of(mine * 8, 8), 8), :]
     scale, by_r64, by_inverse = (by_block[pl.ds(64 + i, 1), :] for i in range(3))
     after = scale * own[0:1] + by_r64 * carry[0:1] + by_inverse * carry[2:3]
     before = scale * own[3:4] + by_r64 * carry[3:4] + by_inverse * carry[1:2]
-    stacked = jnp.concatenate([carry[0:4], after, before, jnp.zeros((LANES - 6, size), F32)], axis=0)
-    columns = jnp.transpose(stacked)
-
-    wave = lambda i: jnp.concatenate([by_wave[pl.ds(i * LANES, LANES), :]] * 2, axis=0)
-    lane = lane_of((size, LANES))
-    odd = (lane & 1) != 0
-    spread = lambda i: jnp.broadcast_to(columns[:, i : i + 1], (size, LANES))
-    total = local[...] + wave(7) * jnp.where(odd, spread(1), spread(0))
-    total = total + wave(8) * jnp.where(odd, spread(3), spread(2))
-    total = total * wave(9)
-    ext = jnp.where((lane == 4) | (lane == 5), columns, 0.0)
-    ext = ext[:half_size] + turn(ext[half_size:], 2, 1)
-    pressure = dot3(
-        (basis_high[...], basis_low[...]),
-        parts(jnp.concatenate([total[:half_size], total[half_size:], ext], axis=1)),
-    )
+    total = local[...] + halves(by_wave[pl.ds(0, LANES), :]) * by_parity(carry[0:1], carry[1:2])
+    total = total + halves(by_wave[pl.ds(LANES, LANES), :]) * by_parity(carry[2:3], carry[3:4])
+    total = total * scale
+    pieces = [total[:, :LANES], total[:, LANES:]]
+    for h in range(2):
+        span = slice(h * LANES, (h + 1) * LANES)
+        pieces += [after[:, span], before[:, span]]
+    pieces.append(jnp.zeros((LANES - 4, LANES), F32))
+    right = parts(jnp.concatenate(pieces, axis=0))
+    last = (((1,), (1,)), ((), ()))
+    dot = lambda a, b: lax.dot_general(a[...], b, last, preferred_element_type=F32)
+    pressure = dot(basis_high, right[0]) + (dot(basis_high, right[1]) + dot(basis_low, right[0]))
     lane = lane_of((blocks, LANES))
     ends = (lane == 0) | (lane == LANES - 1)
     outside = [pressure[r * blocks : (r + 1) * blocks, 2 * LANES :] for r in range(2)]
@@ -378,13 +397,26 @@
         first, second = pressure[:blocks, span], pressure[blocks:, span]
         extra = jnp.where(ends, jnp.where(even, turn(first, -1, 0), turn(second, 1, 0)), 0.0)
         for r in range(2):
-            extra = jnp.where(lane == HIGH + r, turn(outside[r], HIGH + r - 4 - 2 * h, 1), extra)
-            extra = jnp.where(lane == LOW + r, turn(outside[r], LOW + r - 5 - 2 * h, 1), extra)
+            extra = jnp.where(lane == HIGH + r, turn(outside[r], HIGH + r - 2 * h, 1), extra)
+            extra = jnp.where(lane == LOW + r, turn(outside[r], LOW + r - 1 - 2 * h, 1), extra)
         for j, value in enumerate((first, second, extra)):
             message[pl.ds(3 * h + j, blocks, stride=6), :] = value
 
 
-def final_kernel(received, sent, star, back, by_level, out):
+def final_kernel(received, sent, star, back, by_level, out, held, sent_out):
+    size = LEVELS * ROWS
+    span = lambda f: pl.ds(f * size, size)
+    copies = [pltpu.make_async_copy(held.at[span(f), :], out.at[span(f), :], sent_out.at[f]) for f in range(4)]
+
+    def put(f, changes):
+        for x in range(ROWS):
+            value = star[pl.ds((f * ROWS + x) * LEVELS, LEVELS), :]
+            if changes is not None:
+                value = value - changes[:, x * LANES : (x + 1) * LANES]
+            held[pl.ds(f * size + x, LEVELS, stride=ROWS), :] = value
+        copies[f].start()
+
+    put(3, None)
     lane = lane_of((LEVELS, LANES))
     row_at = lambda ref, r: ref[pl.ds(3 * (r % 2) + r // 2, LEVELS, stride=6), :]
     p = [row_at(received, r) for r in range(ROWS)]
@@ -410,29 +442,26 @@
     before = jnp.where(ends, extra[1], next_row(1, p[3]))
     after = jnp.where(ends, extra[0], next_row(2, p[0]))
     padded = [before] + p + [after]
-    slopes = [0.5 * (padded[x + 2] - padded[x]) for x in range(ROWS)]
-    slopes += [0.5 * north_difference(p[x], low[x], high[x]) for x in range(ROWS)]
     matrix = back[...]
-    slope = dot3(parts(matrix), parts(jnp.concatenate(slopes, axis=1)))
-    lift = dot3(parts(0.5 * level_difference(matrix)), parts(jnp.concatenate(p, axis=1)))
-    for x in range(ROWS):
-        take = lambda values, i: values[:, i * LANES : (i + 1) * LANES]
-        for f, change in ((0, take(slope, x)), (1, take(slope, ROWS + x)), (2, take(lift, x)), (3, None)):
-            value = star[pl.ds((f * ROWS + x) * LEVELS, LEVELS), :]
-            if change is not None:
-                value = value - change
-            out[pl.ds(f * LEVELS * ROWS + x, LEVELS, stride=ROWS), :] = value
-
-
-def call(kernel, shapes, args, name, scalars=1, scratch=(), cost=None):
+    joined = lambda values: parts(jnp.concatenate(values, axis=1))
+    put(2, dot3(parts(0.5 * level_difference(matrix)), joined(p)))
+    matrix = parts(matrix)
+    put(1, dot3(matrix, joined([0.5 * north_difference(p[x], low[x], high[x]) for x in range(ROWS)])))
+    put(0, dot3(matrix, joined([0.5 * (padded[x + 2] - padded[x]) for x in range(ROWS)])))
+    for copy in copies:
+        copy.wait()
+
+
+def call(kernel, shapes, args, name, scalars=1, scratch=(), cost=None, copies=0):
     vmem = pl.BlockSpec(memory_space=pltpu.VMEM)
     scalar = pl.BlockSpec(memory_space=pltpu.SMEM)
     return pl.pallas_call(
         kernel,
         out_shape=[jax.ShapeDtypeStruct(s, F32) for s in shapes],
         in_specs=[scalar] * scalars + [vmem] * (len(args) - scalars),
-        out_specs=[vmem] * len(shapes),
-        scratch_shapes=[pltpu.VMEM(s, F32) for s in scratch],
+        out_specs=[pl.BlockSpec(memory_space=pl.ANY) if copies else vmem] * len(shapes),
+        scratch_shapes=[pltpu.VMEM(s, F32) for s in scratch]
+        + ([pltpu.SemaphoreType.DMA((copies,))] if copies else []),
         compiler_params=pltpu.CompilerParams(vmem_limit_bytes=32 * 1024 * 1024),
         name=name,
         cost_estimate=cost,
@@ -458,6 +487,17 @@
     return lax.ppermute(values, ("gx", "gy"), pairs)
 
 
+def hand_over(values):
+    count_x, count_y = lax.axis_size("gx"), lax.axis_size("gy")
+    pairs = [
+        ((i ^ 1) * count_y + j, i * count_y + j)
+        for i in range(count_x)
+        for j in range(count_y)
+        if far_both(i, j)
+    ]
+    return lax.ppermute(values, ("gx", "gy"), pairs)
+
+
 def exchange(values):
     count_x, count_y = lax.axis_size("gx"), lax.axis_size("gy")
     near = count_y // 2
@@ -475,24 +515,24 @@
     blocks = lax.axis_size("gx")
     total_east = blocks * ROWS
     place = jnp.stack([lax.axis_index("gx"), lax.axis_index("gy")]).astype(jnp.int32)
-    state = model_state.reshape(4 * LEVELS * ROWS, LANES)
+    state = [model_state[f].reshape(LEVELS * ROWS, LANES) for f in range(4)]
     basis, square = east_tables(total_east // 2, blocks)
-    forward_high, forward_low = split_table(basis)
-    back_high, back_low = split_table(np.ascontiguousarray(basis.T))
-    square_wide = np.ascontiguousarray(np.broadcast_to(square[:, None], (total_east // 2, LANES)))
+    basis_high, basis_low = split_table(np.ascontiguousarray(basis.T))
     square_row = np.ascontiguousarray(np.broadcast_to(np.concatenate([square, square]), (8, total_east)))
 
     planes, x_even, x_odd, y_even, y_odd = call(
         edges_kernel,
         [(16 * LEVELS, LANES)] + [(5 * LEVELS + 16, LANES), (5 * LEVELS, LANES)] + [(16, LANES)] * 2,
-        [place, state],
+        [place, *state],
         "edges",
         scratch=[(LANES, LANES)],
     )
-    y_both = jnp.concatenate([y_odd, swap(y_odd, "gx", 0)], axis=0)
+    got_x_even = swap(x_even, "gx", 0)
+    y_both = jnp.concatenate([y_odd, got_x_even[5 * LEVELS :]], axis=0)
     y_both, x_odd, y_even = lax.optimization_barrier((y_both, x_odd, y_even))
     got_y_odd = swap_odd_y(y_both)
     got_x_odd = swap(x_odd, "gx", 1)
+    got_y_even = swap(y_even, "gy", 0)
     inner, by_level = call(
         inner_kernel,
         [(16 * LEVELS, LANES), (3 * LEVELS, LANES)],
@@ -506,14 +546,12 @@
         scalars=0,
         cost=pl.CostEstimate(flops=10**10, transcendentals=0, bytes_accessed=2**24),
     )
-    inner, y_even = lax.optimization_barrier((inner, y_even))
-    got_y_even = swap(y_even, "gy", 0)
-    inner, got_y_odd, got_y_even = lax.optimization_barrier((inner, got_y_odd, got_y_even))
-    got_x_even = swap(x_even.at[5 * LEVELS :].set(got_y_odd[16:]), "gx", 0)
-    odd_terms, by_wave, by_block = call(
+    inner, got_y_odd = lax.optimization_barrier((inner, got_y_odd))
+    relayed = hand_over(got_y_odd[16:])
+    odd_terms, by_row, by_wave, by_block = call(
         side_kernel,
-        [(5 * LEVELS, LANES), (10 * LANES, LANES), (72, total_east)],
-        [place, planes, got_x_odd, by_level, square_wide, square_row],
+        [(5 * LEVELS, LANES), (72, total_east), (3 * LANES, LANES), (72, total_east)],
+        [place, planes, got_x_odd, by_level, square_row],
         "side",
         cost=pl.CostEstimate(flops=10**11, transcendentals=0, bytes_accessed=2**27),
     )
@@ -528,6 +566,7 @@
             got_x_even,
             got_y_even,
             got_y_odd,
+            relayed,
             by_level,
             mode_forward,
         ],
@@ -537,8 +576,8 @@
     modal = exchange(message)
     local, moments = call(
         solve_kernel,
-        [(total_east, LANES), (32, total_east)],
-        [place, modal, forward_high, forward_low, by_wave],
+        [(LANES, total_east), (32, total_east)],
+        [place, modal, basis_high, basis_low, by_row, by_wave],
         "solve",
     )
     moments = lax.all_to_all(
@@ -552,7 +591,7 @@
     (reply,) = call(
         back_kernel,
         [(blocks * 6, LANES)],
-        [place, local, moments, back_high, back_low, by_wave, by_block],
+        [place, local, moments, basis_high, basis_low, by_row, by_wave, by_block],
         "back",
     )
     pressure = exchange(reply)
@@ -562,6 +601,8 @@
         [pressure, message, star, mode_back, by_level],
         "final",
         scalars=0,
+        scratch=[(4 * LEVELS * ROWS, LANES)],
+        copies=4,
     )
     return out.reshape(model_state.shape)
 

time: 109 us -> 105 us (0.963)
  blocking collectives: 68.6 us -> 66.8 us
  Pallas kernels: 7.67 us -> 6.57 us
    all_to_all x2, blocking collectives: 61.8 us -> 59.7 us  [exchange(): lax.all_to_all(shaped, ('gx', 'gy'), 0, 0, tiled=True, axis_index_groups=...]
    ppermute x4 -> x3, starting transfers between devices: 15.9 us -> 14 us  [swap(): return lax.ppermute(values, axis, pairs)]
    ppermute x0 -> x1, starting transfers between devices: none -> 1.29 us  [hand_over(): return lax.ppermute(values, ('gx', 'gy'), pairs)]
    slice x0 -> x3, local copies, waits for them, and re-layouts: none -> 1.13 us  [the longest x1 1.13 us: on_device(): state = [model_state[f].reshape(LEVELS * ROWS, LANES) for f in range(4)]]
    pallas_call x7, Pallas kernels: 7.67 us -> 6.57 us  [call(): pl.pallas_call(kernel, out_shape=[jax.ShapeDtypeStruct(s, F32) for s in s...]
    ppermute x4 -> x3, waiting for transfers between devices: 2.2 us -> 1.28 us  [swap(): return lax.ppermute(values, axis, pairs)]
where the time goes in v5:
time: 105 us; the launch traced here: 104 us
  blocking collectives  66.8 us (64%)
  starting transfers between devices  27.8 us (26%)
  Pallas kernels  6.57 us (6%)
  waiting for transfers between devices  1.28 us (1%)
  local copies, waits for them, and re-layouts  1.19 us (1%)
    all_to_all x2, blocking collectives, exchange(): lax.all_to_all(shaped, ('gx', 'gy'), 0, 0, tiled=True, axis_index_groups=...  59.7 us
    ppermute x3, starting transfers between devices, swap(): return lax.ppermute(values, axis, pairs)  14 us
    ppermute x1, starting transfers between devices, swap_odd_y(): return lax.ppermute(values, ('gx', 'gy'), pairs)  12.5 us
    all_to_all x1, blocking collectives, on_device(): lax.all_to_all(moments.reshape(4, 8, total_east), 'gy', 0, 0, tiled=True,...  7.15 us
    pallas_call x7, Pallas kernels, call(): pl.pallas_call(kernel, out_shape=[jax.ShapeDtypeStruct(s, F32) for s in s...  6.57 us
  transfers between devices with their start and end apart: 5, of which 2 were waited for; matrix products, arithmetic and copies ran while one was open for 0% of the time, Pallas kernels for 1%

profile of v5, /device:TPU:1, one launch (start us, length us, event | category | flops | bytes accessed | tf_op | source)
XLA Modules:
  0.0 104.1 jit_solution(1968838875699167866)
XLA Ops:
  0.0 1.1 %fusion = (f32[1,64,4,128]{3,2,1,0:T(4,128)S(1)}, f32[1,64,4,128]{3,2,1,0:T(4,128)S(1)}, f32[1,64,4,128]{3,2,1,0:T(4,128)S(1)}, f32[1,64,4,128]{3,2,1,0:T(4,128)S(1)}) fusion(f32[4,64,4,128]{3,2,1,0:T(4,128)} %param.11), kind=kLoop, calls=%fused_computation.3 | loop fusion | bytes 1048576 | tf_op jit(solution)/shard_map/slice | solution.py:518
  1.1 0.1 pad_add_fusion.place
  1.2 0.0 copy-start.7
  1.2 0.0 copy-start.8
  1.2 0.0 copy-start.9
  1.2 0.0 copy-start.4
  1.2 0.8 edges.1
  2.0 0.0 copy-start.5
  2.1 8.9 %collective-permute-start = (f32[336,128]{1,0:T(8,128)S(1)}, f32[336,128]{1,0:T(8,128)S(1)}, u32[]{:S(2)}, u32[]{:S(2)}) collective-permute-start(f32[336,128]{1,0:T(8,128)S(1)} %get-tuple-element.28), channel_id=1, source_target_pairs={{0,8},{8,0},{16,24},{24,16},{32,40},{40,32},{48,56},{56,48},{64,72... | collective-permute-start | bytes 516104 | tf_op jit(solution)/shard_map/ppermute | solution.py:476
  11.0 0.0 copy-done.7
  11.0 0.0 copy-done.8
  11.0 0.0 copy-done.9
  11.0 0.1 pad_maximum_fusion.1
  11.1 0.9 collective-permute-done.x_even
  12.0 12.5 %collective-permute-start.1 = (f32[32,128]{1,0:T(8,128)S(1)}, f32[32,128]{1,0:T(8,128)S(1)}, u32[]{:S(2)}, u32[]{:S(2)}) collective-permute-start(f32[32,128]{1,0:T(8,128)S(1)} %pad_maximum_fusion), channel_id=1, source_target_pairs={{1,2},{2,1},{5,6},{6,5},{9,10},{10,9},{11,12},{12,11},{13,14},{14,... | collective-permute-start | bytes 49160 | tf_op jit(solution)/shard_map/ppermute | solution.py:487
  24.5 3.2 %collective-permute-start.2 = (f32[320,128]{1,0:T(8,128)S(1)}, f32[320,128]{1,0:T(8,128)S(1)}, u32[]{:S(2)}, u32[]{:S(2)}) collective-permute-start(f32[320,128]{1,0:T(8,128)S(1)} %get-tuple-element.33), channel_id=1, source_target_pairs={{8,16},{16,8},{24,32},{32,24},{40,48},{48,40},{56,64},{64,56},{72,... | collective-permute-start | bytes 491528 | tf_op jit(solution)/shard_map/ppermute | solution.py:476
  27.7 0.0 copy-done.4
  27.7 0.0 copy-done.5
  27.7 0.7 inner.1
  28.5 1.9 %collective-permute-start.3 = (f32[16,128]{1,0:T(8,128)S(1)}, f32[16,128]{1,0:T(8,128)S(1)}, u32[]{:S(2)}, u32[]{:S(2)}) collective-permute-start(f32[16,128]{1,0:T(8,128)S(1)} %get-tuple-element.36), channel_id=1, source_target_pairs={{0,1},{1,0},{2,3},{3,2},{4,5},{5,4},{6,7},{7,6},{8,9},{9,8},{10,11... | collective-permute-start | bytes 24584 | tf_op jit(solution)/shard_map/ppermute | solution.py:476
  30.4 0.0 collective-permute-done.1.y_odd
  30.4 0.0 copy-start.6
  30.4 1.3 %collective-permute-start.4 = (f32[16,128]{1,0:T(8,128)S(1)}, f32[16,128]{1,0:T(8,128)S(1)}, u32[]{:S(2)}, u32[]{:S(2)}) collective-permute-start(f32[16,128]{1,0:T(8,128)S(1)} %slice.23), channel_id=1, source_target_pairs={{8,0},{11,3},{12,4},{15,7},{112,120},{115,123},{116,124},{119,127}... | collective-permute-start | bytes 24584 | tf_op jit(solution)/shard_map/ppermute | solution.py:498
  31.7 0.0 collective-permute-done.2.x_odd
  31.8 0.0 copy-done.6
  31.8 0.0 copy-start.2
  31.8 0.7 side.1
  32.5 0.4 collective-permute-done.3.y_even
  32.9 0.0 collective-permute-done.4.relayed
  32.9 0.0 copy-done.2
  32.9 1.1 %outer.1 = (f32[1024,128]{1,0:T(8,128)S(1)}, f32[384,128]{1,0:T(8,128)S(1)}) custom-call(s32[2]{0:T(128)S(1)} %pad_add_fusion.place, f32[1024,128]{1,0:T(8,128)S(1)} %get-tuple-element.25.state, f32[1024,128]{1,0:T(8,128)S(1)} %get-tuple-element.32.inner, f32[320,128]{1,0:T(8,128)S(1)} %get-tuple-element.35.odd_terms, ...), custom_call_target="tpu_custom_call" | custom-call | tf_op jit(solution)/shard_map/outer/pallas_call | solution.py:458
  34.0 0.0 copy-start
  34.0 0.0 copy-start.1
  34.1 32.2 %all_to_all.15 = f32[128,1,384]{2,1,0:T(1,128)S(1)} all-to-all(f32[128,1,384]{2,1,0:T(1,128)S(1)} %bitcast.13), channel_id=1, replica_groups={{0,4,8,12,16,20,24,28,32,36,40,44,48,52,56,60,64,68,72,76,80,84,88,92,9..., dimensions={0} | all-to-all | bytes 393216 | tf_op jit(solution)/shard_map/all_to_all | solution.py:506
  66.2 0.0 copy-done
  66.2 0.0 copy-done.1
  66.2 1.0 solve.1
  67.3 7.1 %all_to_all.16 = f32[4,8,256]{2,1,0:T(8,128)S(1)} all-to-all(f32[4,8,256]{2,1,0:T(8,128)S(1)} %bitcast.22), channel_id=1, replica_groups={{0,1,2,3},{4,5,6,7},{8,9,10,11},{12,13,14,15},{16,17,18,19},{20,21,22,2..., dimensions={0} | all-to-all | bytes 65536 | tf_op jit(solution)/shard_map/all_to_all | solution.py:583
  74.4 0.9 back.2
  75.3 0.0 copy-start.3
  75.3 27.5 %all_to_all.17 = f32[128,1,384]{2,1,0:T(1,128)S(1)} all-to-all(f32[128,1,384]{2,1,0:T(1,128)S(1)} %bitcast.16), channel_id=1, replica_groups={{0,4,8,12,16,20,24,28,32,36,40,44,48,52,56,60,64,68,72,76,80,84,88,92,9..., dimensions={0} | all-to-all | bytes 393216 | tf_op jit(solution)/shard_map/all_to_all | solution.py:506
  102.9 0.0 copy-done.3
  102.9 1.2 %final.1 = f32[1024,128]{1,0:T(8,128)} custom-call(f32[384,128]{1,0:T(8,128)S(1)} %bitcast.14, f32[384,128]{1,0:T(8,128)S(1)} %get-tuple-element.38.sent, f32[1024,128]{1,0:T(8,128)S(1)} %get-tuple-element.44.star, f32[64,64]{1,0:T(8,128)S(1)} %copy-done.3, f32[192,128]{1,0:T(8,128)S(1)} %get-tuple-element.34.by_level), custom_call_target="tpu_custom_call" | custom-call | tf_op jit(solution)/shard_map/final/pallas_call | solution.py:458
  (4 shorter events, 0.0 us)
Async XLA Ops:
  1.2 9.8 %copy-start.7 = (f32[256]{0:T(256)S(1)}, f32[256]{0:T(256)}, u32[]{:S(2)}) copy-start(f32[256]{0:T(256)} %param.14) | copy-start | bytes 3076
  1.2 9.8 %copy-start.8 = (f32[64]{0:T(128)S(1)}, f32[64]{0:T(128)}, u32[]{:S(2)}) copy-start(f32[64]{0:T(128)} %param.12) | copy-start | bytes 772
  1.2 9.8 %copy-start.9 = (f32[64]{0:T(128)S(1)}, f32[64]{0:T(128)}, u32[]{:S(2)}) copy-start(f32[64]{0:T(128)} %param.18) | copy-start | bytes 772
  1.2 26.5 %copy-start.4 = (bf16[256,256]{1,0:T(8,128)(2,1)S(1)}, bf16[256,256]{1,0:T(8,128)(2,1)}, u32[]{:S(2)}) copy-start(bf16[256,256]{1,0:T(8,128)(2,1)} %layer_in.1) | copy-start | bytes 393220
  2.0 25.7 %copy-start.5 = (bf16[256,128]{1,0:T(8,128)(2,1)S(1)}, bf16[256,128]{1,0:T(8,128)(2,1)}, u32[]{:S(2)}) copy-start(bf16[256,128]{1,0:T(8,128)(2,1)} %layer_out.1) | copy-start | bytes 196612
  2.1 9.9 %collective-permute-start = (f32[336,128]{1,0:T(8,128)S(1)}, f32[336,128]{1,0:T(8,128)S(1)}, u32[]{:S(2)}, u32[]{:S(2)}) collective-permute-start(f32[336,128]{1,0:T(8,128)S(1)} %get-tuple-element.28), channel_id=1, source_target_pairs={{0,8},{8,0},{16,24},{24,16},{32,40},{40,32},{48,56},{56,48},{64,72... | collective-permute-start | bytes 516104 | tf_op jit(solution)/shard_map/ppermute | solution.py:476
  12.0 18.4 %collective-permute-start.1 = (f32[32,128]{1,0:T(8,128)S(1)}, f32[32,128]{1,0:T(8,128)S(1)}, u32[]{:S(2)}, u32[]{:S(2)}) collective-permute-start(f32[32,128]{1,0:T(8,128)S(1)} %pad_maximum_fusion), channel_id=1, source_target_pairs={{1,2},{2,1},{5,6},{6,5},{9,10},{10,9},{11,12},{12,11},{13,14},{14,... | collective-permute-start | bytes 49160 | tf_op jit(solution)/shard_map/ppermute | solution.py:487
  24.5 7.2 %collective-permute-start.2 = (f32[320,128]{1,0:T(8,128)S(1)}, f32[320,128]{1,0:T(8,128)S(1)}, u32[]{:S(2)}, u32[]{:S(2)}) collective-permute-start(f32[320,128]{1,0:T(8,128)S(1)} %get-tuple-element.33), channel_id=1, source_target_pairs={{8,16},{16,8},{24,32},{32,24},{40,48},{48,40},{56,64},{64,56},{72,... | collective-permute-start | bytes 491528 | tf_op jit(solution)/shard_map/ppermute | solution.py:476
  28.5 4.4 %collective-permute-start.3 = (f32[16,128]{1,0:T(8,128)S(1)}, f32[16,128]{1,0:T(8,128)S(1)}, u32[]{:S(2)}, u32[]{:S(2)}) collective-permute-start(f32[16,128]{1,0:T(8,128)S(1)} %get-tuple-element.36), channel_id=1, source_target_pairs={{0,1},{1,0},{2,3},{3,2},{4,5},{5,4},{6,7},{7,6},{8,9},{9,8},{10,11... | collective-permute-start | bytes 24584 | tf_op jit(solution)/shard_map/ppermute | solution.py:476
  30.4 1.3 %copy-start.6 = (f32[8,256]{1,0:T(8,128)S(1)}, f32[8,256]{1,0:T(8,128)}, u32[]{:S(2)}) copy-start(f32[8,256]{1,0:T(8,128)} %constant.15.clone.square_row) | copy-start | bytes 24580
  30.4 2.4 %collective-permute-start.4 = (f32[16,128]{1,0:T(8,128)S(1)}, f32[16,128]{1,0:T(8,128)S(1)}, u32[]{:S(2)}, u32[]{:S(2)}) collective-permute-start(f32[16,128]{1,0:T(8,128)S(1)} %slice.23), channel_id=1, source_target_pairs={{8,0},{11,3},{12,4},{15,7},{112,120},{115,123},{116,124},{119,127}... | collective-permute-start | bytes 24584 | tf_op jit(solution)/shard_map/ppermute | solution.py:498
  31.8 1.1 %copy-start.2 = (f32[64,64]{1,0:T(8,128)S(1)}, f32[64,64]{1,0:T(8,128)}, u32[]{:S(2)}) copy-start(f32[64,64]{1,0:T(8,128)} %forward.1) | copy-start | bytes 49156
  34.0 32.2 %copy-start = (bf16[128,128]{1,0:T(8,128)(2,1)S(1)}, bf16[128,128]{1,0:T(8,128)(2,1)}, u32[]{:S(2)}) copy-start(bf16[128,128]{1,0:T(8,128)(2,1)} %constant.17.clone.basis_low) | copy-start | bytes 98308
  34.0 32.2 %copy-start.1 = (bf16[128,128]{1,0:T(8,128)(2,1)S(1)}, bf16[128,128]{1,0:T(8,128)(2,1)}, u32[]{:S(2)}) copy-start(bf16[128,128]{1,0:T(8,128)(2,1)} %constant.16.clone.basis_high) | copy-start | bytes 98308
  75.3 27.5 %copy-start.3 = (f32[64,64]{1,0:T(8,128)S(1)}, f32[64,64]{1,0:T(8,128)}, u32[]{:S(2)}) copy-start(f32[64,64]{1,0:T(8,128)} %back.3) | copy-start | bytes 49156

commit v6 on v5

--- a/solution.py
+++ b/solution.py
@@ -101,7 +101,8 @@
             x_odd[span, :] = jnp.where(even_x, low, high)
     flat[...] = jnp.transpose(jnp.concatenate([gathered, jnp.zeros_like(gathered)], axis=0))
     high, low = flat[pl.ds(0, 16, stride=2), :], flat[pl.ds(1, 16, stride=2), :]
-    y_even[...] = jnp.where(even_y, high, low)
+    y_even[0:16, :] = jnp.where(even_y, high, low)
+    y_even[16:32, :] = jnp.zeros((16, LANES), F32)
     y_odd[...] = jnp.where(even_y, low, high)
     x_even[pl.ds(5 * LEVELS, 16), :] = jnp.where(even_y, low, high)
 
@@ -111,12 +112,17 @@
 
 
 def inner_kernel(
+    place,
     state,
     vectors,
+    square_row,
     layer_in,
     layer_out,
     star,
     by_level,
+    by_row,
+    by_wave,
+    by_block,
 ):
     fields = [[plane(state, f, x) for x in range(ROWS)] for f in range(4)]
     tall = column_of(vectors[:, :LANES])
@@ -127,6 +133,38 @@
         row < LEVELS - 1, 0.5 * turn(density, -1, 0) / density, 0.0
     )
     by_level[pl.ds(2 * LEVELS, LEVELS), :] = jnp.where(row > 0, 0.5 * turn(density, 1, 0) / density, 0.0)
+    own = by_level[pl.ds(place[0], 1), :]
+
+    both = jnp.concatenate([own, own], axis=1)
+    root, inverse, rho = decay(both, square_row[...])
+    powers = squarings(rho, 6)
+    for i, value in enumerate(powers + [powers[6] * rho, -1.0 / root]):
+        by_row[pl.ds(8 * i, 8), :] = value
+    half = row_of((LANES, LANES)) >> 1
+    odd = (row_of((LANES, LANES)) & 1) != 0
+    narrow = [jnp.broadcast_to(value[0:1, :LANES], (LANES, LANES)) for value in powers[:6]]
+    rising = lane_powers(narrow, half)
+    falling = lane_powers(narrow, 63 - half)
+    by_wave[pl.ds(0, LANES), :] = rising
+    by_wave[pl.ds(LANES, LANES), :] = falling
+    by_wave[pl.ds(2 * LANES, LANES), :] = narrow[0] * jnp.where(odd, rising, falling)
+
+    r64 = powers[6]
+    r128 = r64 * r64
+    r256 = r128 * r128
+    images = 1.0 / (1.0 - r256 * r256)
+    mine = place[1] & 3
+    row = row_of(rho.shape)
+    for j in range(4):
+        for i, offset in enumerate((-1, 3)):
+            exponent = jnp.where(row < 2, (mine - j + offset) & 7, (j - mine + offset) & 7)
+            weight = jnp.where((exponent & 1) != 0, r64, 1.0)
+            weight = weight * jnp.where((exponent & 2) != 0, r128, 1.0)
+            weight = weight * jnp.where((exponent & 4) != 0, r256, 1.0)
+            by_block[pl.ds((2 * j + i) * 8, 8), :] = weight * images
+    scale = -1.0 / root
+    by_block[pl.ds(64, 8), :] = jnp.where(row == 0, scale, jnp.where(row == 1, scale * r64, scale * inverse))
+
     for x in range(ROWS):
         u, v, w, th = (fields[f][x] for f in range(4))
         for f in range(4):
@@ -172,49 +210,12 @@
     return adds, beyond
 
 
-def side_kernel(place, state, x_odd, by_level, square_row, terms, by_row, by_wave, by_block):
-    adds, beyond = side_terms(state, x_odd, place[0] % 2 == 0)
-    for i, value in enumerate(adds + [beyond]):
-        terms[pl.ds(i * LEVELS, LEVELS), :] = value
-    own = by_level[pl.ds(place[0], 1), :]
-
-    both = jnp.concatenate([own, own], axis=1)
-    root, inverse, rho = decay(both, square_row[...])
-    powers = squarings(rho, 6)
-    for i, value in enumerate(powers + [powers[6] * rho, -1.0 / root]):
-        by_row[pl.ds(8 * i, 8), :] = value
-    half = row_of((LANES, LANES)) >> 1
-    odd = (row_of((LANES, LANES)) & 1) != 0
-    narrow = [jnp.broadcast_to(value[0:1, :LANES], (LANES, LANES)) for value in powers[:6]]
-    rising = lane_powers(narrow, half)
-    falling = lane_powers(narrow, 63 - half)
-    by_wave[pl.ds(0, LANES), :] = rising
-    by_wave[pl.ds(LANES, LANES), :] = falling
-    by_wave[pl.ds(2 * LANES, LANES), :] = narrow[0] * jnp.where(odd, rising, falling)
-
-    r64 = powers[6]
-    r128 = r64 * r64
-    r256 = r128 * r128
-    images = 1.0 / (1.0 - r256 * r256)
-    mine = place[1] & 3
-    row = row_of(rho.shape)
-    for j in range(4):
-        for i, offset in enumerate((-1, 3)):
-            exponent = jnp.where(row < 2, (mine - j + offset) & 7, (j - mine + offset) & 7)
-            weight = jnp.where((exponent & 1) != 0, r64, 1.0)
-            weight = weight * jnp.where((exponent & 2) != 0, r128, 1.0)
-            weight = weight * jnp.where((exponent & 4) != 0, r256, 1.0)
-            by_block[pl.ds((2 * j + i) * 8, 8), :] = weight * images
-    scale = -1.0 / root
-    by_block[pl.ds(64, 8), :] = jnp.where(row == 0, scale, jnp.where(row == 1, scale * r64, scale * inverse))
-
-
 def outer_kernel(
     place,
     state,
     inner,
-    odd_terms,
     x_even,
+    x_odd,
     y_even,
     y_odd,
     relayed,
@@ -229,15 +230,13 @@
     shape = (LEVELS, LANES)
     lane = lane_of(shape)
 
-    other = jnp.where(far_both(place[0], place[1]), relayed[...], y_odd[0:16, :])
+    other = jnp.where(far_both(place[0], place[1]), relayed[16:32, :], y_odd[0:16, :])
     flat[...] = jnp.zeros((LANES, LANES), F32)
-    flat[pl.ds(0, 16, stride=2), :] = jnp.where(even_y, y_even[...], other)
-    flat[pl.ds(1, 16, stride=2), :] = jnp.where(even_y, other, y_even[...])
+    flat[pl.ds(0, 16, stride=2), :] = jnp.where(even_y, y_even[0:16, :], other)
+    flat[pl.ds(1, 16, stride=2), :] = jnp.where(even_y, other, y_even[0:16, :])
     columns = jnp.transpose(flat[...])[:LEVELS]
     even_adds, even_beyond = side_terms(state, x_even, ~even_x)
-    odd_adds = [odd_terms[pl.ds(f * LEVELS, LEVELS), :] for f in range(4)]
-    odd_beyond = odd_terms[pl.ds(4 * LEVELS, LEVELS), :]
-
+    odd_adds, odd_beyond = side_terms(state, x_odd, even_x)
     end_sign = jnp.where(lane == 0, 0.1, jnp.where(lane == LANES - 1, -0.1, 0.0))
     whole = [[None] * ROWS for _ in range(4)]
     side_u = [None] * ROWS
@@ -522,7 +521,7 @@
 
     planes, x_even, x_odd, y_even, y_odd = call(
         edges_kernel,
-        [(16 * LEVELS, LANES)] + [(5 * LEVELS + 16, LANES), (5 * LEVELS, LANES)] + [(16, LANES)] * 2,
+        [(16 * LEVELS, LANES), (5 * LEVELS + 16, LANES), (5 * LEVELS, LANES), (32, LANES), (16, LANES)],
         [place, *state],
         "edges",
         scratch=[(LANES, LANES)],
@@ -532,29 +531,24 @@
     y_both, x_odd, y_even = lax.optimization_barrier((y_both, x_odd, y_even))
     got_y_odd = swap_odd_y(y_both)
     got_x_odd = swap(x_odd, "gx", 1)
-    got_y_even = swap(y_even, "gy", 0)
-    inner, by_level = call(
+    inner, by_level, by_row, by_wave, by_block = call(
         inner_kernel,
-        [(16 * LEVELS, LANES), (3 * LEVELS, LANES)],
+        [(16 * LEVELS, LANES), (3 * LEVELS, LANES), (72, total_east), (3 * LANES, LANES), (72, total_east)],
         [
+            place,
             planes,
             jnp.concatenate([mode_rate, density, layer_bias])[None, :],
+            square_row,
             layer_in,
             layer_out,
         ],
         "inner",
-        scalars=0,
         cost=pl.CostEstimate(flops=10**10, transcendentals=0, bytes_accessed=2**24),
     )
+    inner, y_even = lax.optimization_barrier((inner, y_even))
+    got_y_even = swap(y_even, "gy", 0)
     inner, got_y_odd = lax.optimization_barrier((inner, got_y_odd))
-    relayed = hand_over(got_y_odd[16:])
-    odd_terms, by_row, by_wave, by_block = call(
-        side_kernel,
-        [(5 * LEVELS, LANES), (72, total_east), (3 * LANES, LANES), (72, total_east)],
-        [place, planes, got_x_odd, by_level, square_row],
-        "side",
-        cost=pl.CostEstimate(flops=10**11, transcendentals=0, bytes_accessed=2**27),
-    )
+    relayed = hand_over(got_y_odd)
     star, message = call(
         outer_kernel,
         [(16 * LEVELS, LANES), (blocks * 6, LANES)],
@@ -562,8 +556,8 @@
             place,
             planes,
             inner,
-            odd_terms,
             got_x_even,
+            got_x_odd,
             got_y_even,
             got_y_odd,
             relayed,

time: 105 us -> 104 us (level)
  blocking collectives: 66.8 us -> 65.5 us
    all_to_all x2, blocking collectives: 59.7 us -> 58 us  [exchange(): lax.all_to_all(shaped, ('gx', 'gy'), 0, 0, tiled=True, axis_index_groups=...]
    pallas_call x7 -> x6, Pallas kernels: 6.57 us -> 6.52 us  [call(): pl.pallas_call(kernel, out_shape=[jax.ShapeDtypeStruct(s, F32) for s in s...]
where the time goes in v6:
time: 104 us
  blocking collectives  65.5 us (63%)
  starting transfers between devices  27.8 us (27%)
  Pallas kernels  6.52 us (6%)
  waiting for transfers between devices  2.16 us (2%)
  local copies, waits for them, and re-layouts  1.19 us (1%)
    all_to_all x2, blocking collectives, exchange(): lax.all_to_all(shaped, ('gx', 'gy'), 0, 0, tiled=True, axis_index_groups=...  58 us
    ppermute x3, starting transfers between devices, swap(): return lax.ppermute(values, axis, pairs)  14 us
    ppermute x1, starting transfers between devices, swap_odd_y(): return lax.ppermute(values, ('gx', 'gy'), pairs)  12.5 us
    all_to_all x1, blocking collectives, on_device(): lax.all_to_all(moments.reshape(4, 8, total_east), 'gy', 0, 0, tiled=True,...  7.49 us
    pallas_call x6, Pallas kernels, call(): pl.pallas_call(kernel, out_shape=[jax.ShapeDtypeStruct(s, F32) for s in s...  6.52 us
    ppermute x3, waiting for transfers between devices, swap(): return lax.ppermute(values, axis, pairs)  2.15 us
  transfers between devices with their start and end apart: 5, of which 2 were waited for; matrix products, arithmetic and copies ran while one was open for 0% of the time, Pallas kernels for 1%

profile of v6, /device:TPU:1, one launch (start us, length us, event | category | flops | bytes accessed | tf_op | source)
XLA Modules:
  0.0 103.6 jit_solution(11422038399864389696)
XLA Ops:
  0.0 1.1 %fusion = (f32[1,64,4,128]{3,2,1,0:T(4,128)S(1)}, f32[1,64,4,128]{3,2,1,0:T(4,128)S(1)}, f32[1,64,4,128]{3,2,1,0:T(4,128)S(1)}, f32[1,64,4,128]{3,2,1,0:T(4,128)S(1)}) fusion(f32[4,64,4,128]{3,2,1,0:T(4,128)} %param.11), kind=kLoop, calls=%fused_computation.3 | loop fusion | bytes 1048576 | tf_op jit(solution)/shard_map/slice | solution.py:517
  1.1 0.1 pad_add_fusion.place
  1.2 0.0 copy-start.7
  1.2 0.0 copy-start.8
  1.2 0.0 copy-start.9
  1.2 0.0 copy-start.4
  1.2 0.0 copy-start.6
  1.2 0.8 edges.1
  2.1 0.0 copy-start.5
  2.1 8.9 %collective-permute-start = (f32[336,128]{1,0:T(8,128)S(1)}, f32[336,128]{1,0:T(8,128)S(1)}, u32[]{:S(2)}, u32[]{:S(2)}) collective-permute-start(f32[336,128]{1,0:T(8,128)S(1)} %get-tuple-element.29), channel_id=1, source_target_pairs={{0,8},{8,0},{16,24},{24,16},{32,40},{40,32},{48,56},{56,48},{64,72... | collective-permute-start | bytes 516104 | tf_op jit(solution)/shard_map/ppermute | solution.py:475
  11.0 0.0 copy-done.7
  11.0 0.0 copy-done.8
  11.0 0.0 copy-done.9
  11.0 0.1 pad_maximum_fusion.1
  11.1 0.9 collective-permute-done.x_even
  12.0 12.5 %collective-permute-start.1 = (f32[32,128]{1,0:T(8,128)S(1)}, f32[32,128]{1,0:T(8,128)S(1)}, u32[]{:S(2)}, u32[]{:S(2)}) collective-permute-start(f32[32,128]{1,0:T(8,128)S(1)} %pad_maximum_fusion), channel_id=1, source_target_pairs={{1,2},{2,1},{5,6},{6,5},{9,10},{10,9},{11,12},{12,11},{13,14},{14,... | collective-permute-start | bytes 49160 | tf_op jit(solution)/shard_map/ppermute | solution.py:486
  24.5 3.2 %collective-permute-start.2 = (f32[320,128]{1,0:T(8,128)S(1)}, f32[320,128]{1,0:T(8,128)S(1)}, u32[]{:S(2)}, u32[]{:S(2)}) collective-permute-start(f32[320,128]{1,0:T(8,128)S(1)} %get-tuple-element.36), channel_id=1, source_target_pairs={{8,16},{16,8},{24,32},{32,24},{40,48},{48,40},{56,64},{64,56},{72,... | collective-permute-start | bytes 491528 | tf_op jit(solution)/shard_map/ppermute | solution.py:475
  27.7 0.0 copy-done.4
  27.7 0.0 copy-done.6
  27.7 0.0 copy-done.5
  27.8 0.0 copy-start.2
  27.8 1.4 %inner.1 = (f32[1024,128]{1,0:T(8,128)S(1)}, f32[192,128]{1,0:T(8,128)S(1)}, f32[72,256]{1,0:T(8,128)S(1)}, f32[384,128]{1,0:T(8,128)S(1)}, f32[72,256]{1,0:T(8,128)S(1)}) custom-call(s32[2]{0:T(128)S(1)} %pad_add_fusion.place, f32[1024,128]{1,0:T(8,128)S(1)} %get-tuple-element.26.state, f32[1,384]{1,0:T(1,128)S(1)} %broadcast_in_dim.3.vectors, ...), custom_call_target="tpu_custom_call" | custom-call | flops 10000000000 | bytes 16777216 | tf_op jit(solution)/shard_map/inner/pallas_call | solution.py:457
  29.2 1.9 %collective-permute-start.3 = (f32[32,128]{1,0:T(8,128)S(1)}, f32[32,128]{1,0:T(8,128)S(1)}, u32[]{:S(2)}, u32[]{:S(2)}) collective-permute-start(f32[32,128]{1,0:T(8,128)S(1)} %get-tuple-element.37), channel_id=1, source_target_pairs={{0,1},{1,0},{2,3},{3,2},{4,5},{5,4},{6,7},{7,6},{8,9},{9,8},{10,11... | collective-permute-start | bytes 49160 | tf_op jit(solution)/shard_map/ppermute | solution.py:475
  31.1 0.0 collective-permute-done.1.y_odd
  31.1 1.3 %collective-permute-start.4 = (f32[32,128]{1,0:T(8,128)S(1)}, f32[32,128]{1,0:T(8,128)S(1)}, u32[]{:S(2)}, u32[]{:S(2)}) collective-permute-start(f32[32,128]{1,0:T(8,128)S(1)} %collective-permute-done.1.y_odd), channel_id=1, source_target_pairs={{8,0},{11,3},{12,4},{15,7},{112,120},{115,123},{116,124},{119,127}... | collective-permute-start | bytes 49160 | tf_op jit(solution)/shard_map/ppermute | solution.py:497
  32.4 1.2 %collective-permute-done.3.y_even = f32[32,128]{1,0:T(8,128)S(1)} collective-permute-done((f32[32,128]{1,0:T(8,128)S(1)}, f32[32,128]{1,0:T(8,128)S(1)}, u32[]{:S(2)}, u32[]{:S(2)}) %collective-permute-start.3) | collective-permute-done | bytes 16416 | tf_op jit(solution)/shard_map/ppermute | solution.py:475
  33.7 0.0 collective-permute-done.4.relayed
  33.7 0.0 collective-permute-done.2.x_odd
  33.7 0.0 copy-done.2
  33.7 1.1 %outer.1 = (f32[1024,128]{1,0:T(8,128)S(1)}, f32[384,128]{1,0:T(8,128)S(1)}) custom-call(s32[2]{0:T(128)S(1)} %pad_add_fusion.place, f32[1024,128]{1,0:T(8,128)S(1)} %get-tuple-element.26.state, f32[1024,128]{1,0:T(8,128)S(1)} %get-tuple-element.35.inner, f32[336,128]{1,0:T(8,128)S(1)} %collective-permute-done.x_even, ...), custom_call_target="tpu_custom_call" | custom-call | tf_op jit(solution)/shard_map/outer/pallas_call | solution.py:457
  34.8 0.0 copy-start
  34.9 0.0 copy-start.1
  34.9 30.5 %all_to_all.15 = f32[128,1,384]{2,1,0:T(1,128)S(1)} all-to-all(f32[128,1,384]{2,1,0:T(1,128)S(1)} %bitcast.13), channel_id=1, replica_groups={{0,4,8,12,16,20,24,28,32,36,40,44,48,52,56,60,64,68,72,76,80,84,88,92,9..., dimensions={0} | all-to-all | bytes 393216 | tf_op jit(solution)/shard_map/all_to_all | solution.py:505
  65.3 0.0 copy-done
  65.4 0.0 copy-done.1
  65.4 1.0 solve.1
  66.4 7.5 %all_to_all.16 = f32[4,8,256]{2,1,0:T(8,128)S(1)} all-to-all(f32[4,8,256]{2,1,0:T(8,128)S(1)} %bitcast.22), channel_id=1, replica_groups={{0,1,2,3},{4,5,6,7},{8,9,10,11},{12,13,14,15},{16,17,18,19},{20,21,22,2..., dimensions={0} | all-to-all | bytes 65536 | tf_op jit(solution)/shard_map/all_to_all | solution.py:577
  73.9 0.9 back.2
  74.8 0.0 copy-start.3
  74.8 27.5 %all_to_all.17 = f32[128,1,384]{2,1,0:T(1,128)S(1)} all-to-all(f32[128,1,384]{2,1,0:T(1,128)S(1)} %bitcast.16), channel_id=1, replica_groups={{0,4,8,12,16,20,24,28,32,36,40,44,48,52,56,60,64,68,72,76,80,84,88,92,9..., dimensions={0} | all-to-all | bytes 393216 | tf_op jit(solution)/shard_map/all_to_all | solution.py:505
  102.3 0.0 copy-done.3
  102.4 1.2 %final.1 = f32[1024,128]{1,0:T(8,128)} custom-call(f32[384,128]{1,0:T(8,128)S(1)} %bitcast.14, f32[384,128]{1,0:T(8,128)S(1)} %get-tuple-element.40.sent, f32[1024,128]{1,0:T(8,128)S(1)} %get-tuple-element.46.star, f32[64,64]{1,0:T(8,128)S(1)} %copy-done.3, f32[192,128]{1,0:T(8,128)S(1)} %get-tuple-element.39.by_level), custom_call_target="tpu_custom_call" | custom-call | tf_op jit(solution)/shard_map/final/pallas_call | solution.py:457
  (3 shorter events, 0.0 us)
Async XLA Ops:
  1.2 9.8 %copy-start.7 = (f32[256]{0:T(256)S(1)}, f32[256]{0:T(256)}, u32[]{:S(2)}) copy-start(f32[256]{0:T(256)} %param.14) | copy-start | bytes 3076
  1.2 9.8 %copy-start.8 = (f32[64]{0:T(128)S(1)}, f32[64]{0:T(128)}, u32[]{:S(2)}) copy-start(f32[64]{0:T(128)} %param.12) | copy-start | bytes 772
  1.2 9.8 %copy-start.9 = (f32[64]{0:T(128)S(1)}, f32[64]{0:T(128)}, u32[]{:S(2)}) copy-start(f32[64]{0:T(128)} %param.18) | copy-start | bytes 772
  1.2 26.5 %copy-start.4 = (bf16[256,256]{1,0:T(8,128)(2,1)S(1)}, bf16[256,256]{1,0:T(8,128)(2,1)}, u32[]{:S(2)}) copy-start(bf16[256,256]{1,0:T(8,128)(2,1)} %layer_in.1) | copy-start | bytes 393220
  1.2 26.5 %copy-start.6 = (f32[8,256]{1,0:T(8,128)S(1)}, f32[8,256]{1,0:T(8,128)}, u32[]{:S(2)}) copy-start(f32[8,256]{1,0:T(8,128)} %constant.15.clone.square_row) | copy-start | bytes 24580
  2.1 25.7 %copy-start.5 = (bf16[256,128]{1,0:T(8,128)(2,1)S(1)}, bf16[256,128]{1,0:T(8,128)(2,1)}, u32[]{:S(2)}) copy-start(bf16[256,128]{1,0:T(8,128)(2,1)} %layer_out.1) | copy-start | bytes 196612
  2.1 9.9 %collective-permute-start = (f32[336,128]{1,0:T(8,128)S(1)}, f32[336,128]{1,0:T(8,128)S(1)}, u32[]{:S(2)}, u32[]{:S(2)}) collective-permute-start(f32[336,128]{1,0:T(8,128)S(1)} %get-tuple-element.29), channel_id=1, source_target_pairs={{0,8},{8,0},{16,24},{24,16},{32,40},{40,32},{48,56},{56,48},{64,72... | collective-permute-start | bytes 516104 | tf_op jit(solution)/shard_map/ppermute | solution.py:475
  12.0 19.1 %collective-permute-start.1 = (f32[32,128]{1,0:T(8,128)S(1)}, f32[32,128]{1,0:T(8,128)S(1)}, u32[]{:S(2)}, u32[]{:S(2)}) collective-permute-start(f32[32,128]{1,0:T(8,128)S(1)} %pad_maximum_fusion), channel_id=1, source_target_pairs={{1,2},{2,1},{5,6},{6,5},{9,10},{10,9},{11,12},{12,11},{13,14},{14,... | collective-permute-start | bytes 49160 | tf_op jit(solution)/shard_map/ppermute | solution.py:486
  24.5 9.1 %collective-permute-start.2 = (f32[320,128]{1,0:T(8,128)S(1)}, f32[320,128]{1,0:T(8,128)S(1)}, u32[]{:S(2)}, u32[]{:S(2)}) collective-permute-start(f32[320,128]{1,0:T(8,128)S(1)} %get-tuple-element.36), channel_id=1, source_target_pairs={{8,16},{16,8},{24,32},{32,24},{40,48},{48,40},{56,64},{64,56},{72,... | collective-permute-start | bytes 491528 | tf_op jit(solution)/shard_map/ppermute | solution.py:475
  27.8 5.9 %copy-start.2 = (f32[64,64]{1,0:T(8,128)S(1)}, f32[64,64]{1,0:T(8,128)}, u32[]{:S(2)}) copy-start(f32[64,64]{1,0:T(8,128)} %forward.1) | copy-start | bytes 49156
  29.2 4.5 %collective-permute-start.3 = (f32[32,128]{1,0:T(8,128)S(1)}, f32[32,128]{1,0:T(8,128)S(1)}, u32[]{:S(2)}, u32[]{:S(2)}) collective-permute-start(f32[32,128]{1,0:T(8,128)S(1)} %get-tuple-element.37), channel_id=1, source_target_pairs={{0,1},{1,0},{2,3},{3,2},{4,5},{5,4},{6,7},{7,6},{8,9},{9,8},{10,11... | collective-permute-start | bytes 49160 | tf_op jit(solution)/shard_map/ppermute | solution.py:475
  31.1 2.5 %collective-permute-start.4 = (f32[32,128]{1,0:T(8,128)S(1)}, f32[32,128]{1,0:T(8,128)S(1)}, u32[]{:S(2)}, u32[]{:S(2)}) collective-permute-start(f32[32,128]{1,0:T(8,128)S(1)} %collective-permute-done.1.y_odd), channel_id=1, source_target_pairs={{8,0},{11,3},{12,4},{15,7},{112,120},{115,123},{116,124},{119,127}... | collective-permute-start | bytes 49160 | tf_op jit(solution)/shard_map/ppermute | solution.py:497
  34.8 30.5 %copy-start = (bf16[128,128]{1,0:T(8,128)(2,1)S(1)}, bf16[128,128]{1,0:T(8,128)(2,1)}, u32[]{:S(2)}) copy-start(bf16[128,128]{1,0:T(8,128)(2,1)} %constant.17.clone.basis_low) | copy-start | bytes 98308
  34.9 30.5 %copy-start.1 = (bf16[128,128]{1,0:T(8,128)(2,1)S(1)}, bf16[128,128]{1,0:T(8,128)(2,1)}, u32[]{:S(2)}) copy-start(bf16[128,128]{1,0:T(8,128)(2,1)} %constant.16.clone.basis_high) | copy-start | bytes 98308
  74.8 27.6 %copy-start.3 = (f32[64,64]{1,0:T(8,128)S(1)}, f32[64,64]{1,0:T(8,128)}, u32[]{:S(2)}) copy-start(f32[64,64]{1,0:T(8,128)} %back.3) | copy-start | bytes 49156

commit v7 on v6

--- a/solution.py
+++ b/solution.py
@@ -36,6 +36,10 @@
     return basis, square.astype(np.float32)
 
 
+def position():
+    return lax.axis_index("gx"), lax.axis_index("gy")
+
+
 def lane_of(shape):
     return lax.broadcasted_iota(jnp.int32, shape, len(shape) - 1)
 
@@ -82,7 +86,8 @@
     return ((gx % 16 == 0) | (gx % 16 == 15)) & ((gy % 4 == 0) | (gy % 4 == 3))
 
 
-def edges_kernel(place, state_u, state_v, state_w, state_th, planes, x_even, x_odd, y_even, y_odd, flat):
+def edges_kernel(state_u, state_v, state_w, state_th, planes, x_even, x_odd, y_even, y_odd, flat):
+    place = position()
     even_x = place[0] % 2 == 0
     even_y = place[1] % 2 == 0
     states = (state_u, state_v, state_w, state_th)
@@ -112,7 +117,6 @@
 
 
 def inner_kernel(
-    place,
     state,
     vectors,
     square_row,
@@ -124,6 +128,7 @@
     by_wave,
     by_block,
 ):
+    place = position()
     fields = [[plane(state, f, x) for x in range(ROWS)] for f in range(4)]
     tall = column_of(vectors[:, :LANES])
     rate, density = tall[:LEVELS], tall[LEVELS:]
@@ -211,7 +216,6 @@
 
 
 def outer_kernel(
-    place,
     state,
     inner,
     x_even,
@@ -225,6 +229,7 @@
     message,
     flat,
 ):
+    place = position()
     even_x = place[0] % 2 == 0
     even_y = place[1] % 2 == 0
     shape = (LEVELS, LANES)
@@ -318,7 +323,8 @@
     return jnp.concatenate([values, values], axis=1)
 
 
-def solve_kernel(place, received, basis_high, basis_low, by_row, by_wave, local, moments):
+def solve_kernel(received, basis_high, basis_low, by_row, by_wave, local, moments):
+    place = position()
     blocks = received.shape[0] // 6
     lane = lane_of((blocks, LANES))
     ends = (lane == 0) | (lane == LANES - 1)
@@ -362,7 +368,8 @@
         moments[pl.ds(j * 8, 8), :] = across
 
 
-def back_kernel(place, local, moments, basis_high, basis_low, by_row, by_wave, by_block, message):
+def back_kernel(local, moments, basis_high, basis_low, by_row, by_wave, by_block, message):
+    place = position()
     width = local.shape[1]
     blocks = basis_high.shape[0] // 2
     even = place[1] < 4
@@ -451,13 +458,12 @@
         copy.wait()
 
 
-def call(kernel, shapes, args, name, scalars=1, scratch=(), cost=None, copies=0):
+def call(kernel, shapes, args, name, scratch=(), cost=None, copies=0):
     vmem = pl.BlockSpec(memory_space=pltpu.VMEM)
-    scalar = pl.BlockSpec(memory_space=pltpu.SMEM)
     return pl.pallas_call(
         kernel,
         out_shape=[jax.ShapeDtypeStruct(s, F32) for s in shapes],
-        in_specs=[scalar] * scalars + [vmem] * (len(args) - scalars),
+        in_specs=[vmem] * len(args),
         out_specs=[pl.BlockSpec(memory_space=pl.ANY) if copies else vmem] * len(shapes),
         scratch_shapes=[pltpu.VMEM(s, F32) for s in scratch]
         + ([pltpu.SemaphoreType.DMA((copies,))] if copies else []),
@@ -513,7 +519,6 @@
 ):
     blocks = lax.axis_size("gx")
     total_east = blocks * ROWS
-    place = jnp.stack([lax.axis_index("gx"), lax.axis_index("gy")]).astype(jnp.int32)
     state = [model_state[f].reshape(LEVELS * ROWS, LANES) for f in range(4)]
     basis, square = east_tables(total_east // 2, blocks)
     basis_high, basis_low = split_table(np.ascontiguousarray(basis.T))
@@ -522,7 +527,7 @@
     planes, x_even, x_odd, y_even, y_odd = call(
         edges_kernel,
         [(16 * LEVELS, LANES), (5 * LEVELS + 16, LANES), (5 * LEVELS, LANES), (32, LANES), (16, LANES)],
-        [place, *state],
+        [*state],
         "edges",
         scratch=[(LANES, LANES)],
     )
@@ -535,7 +540,6 @@
         inner_kernel,
         [(16 * LEVELS, LANES), (3 * LEVELS, LANES), (72, total_east), (3 * LANES, LANES), (72, total_east)],
         [
-            place,
             planes,
             jnp.concatenate([mode_rate, density, layer_bias])[None, :],
             square_row,
@@ -553,7 +557,6 @@
         outer_kernel,
         [(16 * LEVELS, LANES), (blocks * 6, LANES)],
         [
-            place,
             planes,
             inner,
             got_x_even,
@@ -571,7 +574,7 @@
     local, moments = call(
         solve_kernel,
         [(LANES, total_east), (32, total_east)],
-        [place, modal, basis_high, basis_low, by_row, by_wave],
+        [modal, basis_high, basis_low, by_row, by_wave],
         "solve",
     )
     moments = lax.all_to_all(
@@ -585,7 +588,7 @@
     (reply,) = call(
         back_kernel,
         [(blocks * 6, LANES)],
-        [place, local, moments, basis_high, basis_low, by_row, by_wave, by_block],
+        [local, moments, basis_high, basis_low, by_row, by_wave, by_block],
         "back",
     )
     pressure = exchange(reply)
@@ -594,7 +597,6 @@
         [(4 * LEVELS * ROWS, LANES)],
         [pressure, message, star, mode_back, by_level],
         "final",
-        scalars=0,
         scratch=[(4 * LEVELS * ROWS, LANES)],
         copies=4,
     )

time: 104 us -> 102 us (0.981)
  Pallas kernels: 6.52 us -> 3.81 us
    pallas_call x6, Pallas kernels: 6.52 us -> 3.81 us  [call(): pl.pallas_call(kernel, out_shape=[jax.ShapeDtypeStruct(s, F32) for s in s...]
where the time goes in v7:
time: 102 us; the launch traced here: 101 us
  blocking collectives  66.1 us (65%)
  starting transfers between devices  27.8 us (27%)
  Pallas kernels  3.81 us (4%)
  waiting for transfers between devices  2.16 us (2%)
  local copies, waits for them, and re-layouts  1.2 us (1%)
    all_to_all x2, blocking collectives, exchange(): lax.all_to_all(shaped, ('gx', 'gy'), 0, 0, tiled=True, axis_index_groups=...  58.6 us
    ppermute x3, starting transfers between devices, swap(): return lax.ppermute(values, axis, pairs)  14 us
    ppermute x1, starting transfers between devices, swap_odd_y(): return lax.ppermute(values, ('gx', 'gy'), pairs)  12.5 us
    all_to_all x1, blocking collectives, on_device(): lax.all_to_all(moments.reshape(4, 8, total_east), 'gy', 0, 0, tiled=True,...  7.49 us
    pallas_call x6, Pallas kernels, call(): pl.pallas_call(kernel, out_shape=[jax.ShapeDtypeStruct(s, F32) for s in s...  3.81 us
    ppermute x3, waiting for transfers between devices, swap(): return lax.ppermute(values, axis, pairs)  2.15 us
  transfers between devices with their start and end apart: 5, of which 2 were waited for; matrix products, arithmetic and copies ran while one was open for 0% of the time, Pallas kernels for 1%

profile of v7, /device:TPU:1, one launch (start us, length us, event | category | flops | bytes accessed | tf_op | source)
XLA Modules:
  0.0 101.3 jit_solution(17223726340384103393)
XLA Ops:
  0.0 1.1 %fusion = (f32[1,64,4,128]{3,2,1,0:T(4,128)S(1)}, f32[1,64,4,128]{3,2,1,0:T(4,128)S(1)}, f32[1,64,4,128]{3,2,1,0:T(4,128)S(1)}, f32[1,64,4,128]{3,2,1,0:T(4,128)S(1)}) fusion(f32[4,64,4,128]{3,2,1,0:T(4,128)} %param.11), kind=kLoop, calls=%fused_computation.2 | loop fusion | bytes 1048576 | tf_op jit(solution)/shard_map/slice | solution.py:522
  1.1 0.0 copy-start.7
  1.1 0.0 copy-start.8
  1.2 0.0 copy-start.9
  1.2 0.0 copy-start.4
  1.2 0.0 copy-start.6
  1.2 0.3 edges.1
  1.5 0.0 copy-start.5
  1.5 8.9 %collective-permute-start = (f32[336,128]{1,0:T(8,128)S(1)}, f32[336,128]{1,0:T(8,128)S(1)}, u32[]{:S(2)}, u32[]{:S(2)}) collective-permute-start(f32[336,128]{1,0:T(8,128)S(1)} %get-tuple-element.29), channel_id=1, source_target_pairs={{0,8},{8,0},{16,24},{24,16},{32,40},{40,32},{48,56},{56,48},{64,72... | collective-permute-start | bytes 516104 | tf_op jit(solution)/shard_map/ppermute | solution.py:481
  10.4 0.0 copy-done.7
  10.4 0.0 copy-done.8
  10.4 0.0 copy-done.9
  10.4 0.1 pad_maximum_fusion.1
  10.5 0.9 collective-permute-done.x_even
  11.4 12.5 %collective-permute-start.1 = (f32[32,128]{1,0:T(8,128)S(1)}, f32[32,128]{1,0:T(8,128)S(1)}, u32[]{:S(2)}, u32[]{:S(2)}) collective-permute-start(f32[32,128]{1,0:T(8,128)S(1)} %pad_maximum_fusion), channel_id=1, source_target_pairs={{1,2},{2,1},{5,6},{6,5},{9,10},{10,9},{11,12},{12,11},{13,14},{14,... | collective-permute-start | bytes 49160 | tf_op jit(solution)/shard_map/ppermute | solution.py:492
  24.0 3.2 %collective-permute-start.2 = (f32[320,128]{1,0:T(8,128)S(1)}, f32[320,128]{1,0:T(8,128)S(1)}, u32[]{:S(2)}, u32[]{:S(2)}) collective-permute-start(f32[320,128]{1,0:T(8,128)S(1)} %get-tuple-element.36), channel_id=1, source_target_pairs={{8,16},{16,8},{24,32},{32,24},{40,48},{48,40},{56,64},{64,56},{72,... | collective-permute-start | bytes 491528 | tf_op jit(solution)/shard_map/ppermute | solution.py:481
  27.1 0.0 copy-done.4
  27.2 0.0 copy-done.6
  27.2 0.0 copy-done.5
  27.2 0.0 copy-start.2
  27.2 0.9 inner.1
  28.1 1.9 %collective-permute-start.3 = (f32[32,128]{1,0:T(8,128)S(1)}, f32[32,128]{1,0:T(8,128)S(1)}, u32[]{:S(2)}, u32[]{:S(2)}) collective-permute-start(f32[32,128]{1,0:T(8,128)S(1)} %get-tuple-element.37), channel_id=1, source_target_pairs={{0,1},{1,0},{2,3},{3,2},{4,5},{5,4},{6,7},{7,6},{8,9},{9,8},{10,11... | collective-permute-start | bytes 49160 | tf_op jit(solution)/shard_map/ppermute | solution.py:481
  30.0 0.0 collective-permute-done.1.y_odd
  30.0 1.3 %collective-permute-start.4 = (f32[32,128]{1,0:T(8,128)S(1)}, f32[32,128]{1,0:T(8,128)S(1)}, u32[]{:S(2)}, u32[]{:S(2)}) collective-permute-start(f32[32,128]{1,0:T(8,128)S(1)} %collective-permute-done.1.y_odd), channel_id=1, source_target_pairs={{8,0},{11,3},{12,4},{15,7},{112,120},{115,123},{116,124},{119,127}... | collective-permute-start | bytes 49160 | tf_op jit(solution)/shard_map/ppermute | solution.py:503
  31.3 1.2 %collective-permute-done.3.y_even = f32[32,128]{1,0:T(8,128)S(1)} collective-permute-done((f32[32,128]{1,0:T(8,128)S(1)}, f32[32,128]{1,0:T(8,128)S(1)}, u32[]{:S(2)}, u32[]{:S(2)}) %collective-permute-start.3) | collective-permute-done | bytes 16416 | tf_op jit(solution)/shard_map/ppermute | solution.py:481
  32.5 0.0 collective-permute-done.4.relayed
  32.5 0.0 collective-permute-done.2.x_odd
  32.5 0.0 copy-done.2
  32.6 0.6 outer.1
  33.2 0.0 copy-start
  33.2 0.0 copy-start.1
  33.2 31.0 %all_to_all.15 = f32[128,1,384]{2,1,0:T(1,128)S(1)} all-to-all(f32[128,1,384]{2,1,0:T(1,128)S(1)} %bitcast.11), channel_id=1, replica_groups={{0,4,8,12,16,20,24,28,32,36,40,44,48,52,56,60,64,68,72,76,80,84,88,92,9..., dimensions={0} | all-to-all | bytes 393216 | tf_op jit(solution)/shard_map/all_to_all | solution.py:511
  64.2 0.0 copy-done
  64.2 0.0 copy-done.1
  64.2 0.5 solve.1
  64.7 7.5 %all_to_all.16 = f32[4,8,256]{2,1,0:T(8,128)S(1)} all-to-all(f32[4,8,256]{2,1,0:T(8,128)S(1)} %bitcast.20), channel_id=1, replica_groups={{0,1,2,3},{4,5,6,7},{8,9,10,11},{12,13,14,15},{16,17,18,19},{20,21,22,2..., dimensions={0} | all-to-all | bytes 65536 | tf_op jit(solution)/shard_map/all_to_all | solution.py:580
  72.2 0.4 back.2
  72.6 0.0 copy-start.3
  72.6 27.5 %all_to_all.17 = f32[128,1,384]{2,1,0:T(1,128)S(1)} all-to-all(f32[128,1,384]{2,1,0:T(1,128)S(1)} %bitcast.14), channel_id=1, replica_groups={{0,4,8,12,16,20,24,28,32,36,40,44,48,52,56,60,64,68,72,76,80,84,88,92,9..., dimensions={0} | all-to-all | bytes 393216 | tf_op jit(solution)/shard_map/all_to_all | solution.py:511
  100.1 0.0 copy-done.3
  100.1 1.2 %final.1 = f32[1024,128]{1,0:T(8,128)} custom-call(f32[384,128]{1,0:T(8,128)S(1)} %bitcast.12, f32[384,128]{1,0:T(8,128)S(1)} %get-tuple-element.40.sent, f32[1024,128]{1,0:T(8,128)S(1)} %get-tuple-element.46.star, f32[64,64]{1,0:T(8,128)S(1)} %copy-done.3, f32[192,128]{1,0:T(8,128)S(1)} %get-tuple-element.39.by_level), custom_call_target="tpu_custom_call" | custom-call | tf_op jit(solution)/shard_map/final/pallas_call | solution.py:463
  (3 shorter events, 0.0 us)
Async XLA Ops:
  1.1 9.3 %copy-start.7 = (f32[256]{0:T(256)S(1)}, f32[256]{0:T(256)}, u32[]{:S(2)}) copy-start(f32[256]{0:T(256)} %param.14) | copy-start | bytes 3076
  1.1 9.3 %copy-start.8 = (f32[64]{0:T(128)S(1)}, f32[64]{0:T(128)}, u32[]{:S(2)}) copy-start(f32[64]{0:T(128)} %param.12) | copy-start | bytes 772
  1.2 9.3 %copy-start.9 = (f32[64]{0:T(128)S(1)}, f32[64]{0:T(128)}, u32[]{:S(2)}) copy-start(f32[64]{0:T(128)} %param.18) | copy-start | bytes 772
  1.2 26.0 %copy-start.4 = (bf16[256,256]{1,0:T(8,128)(2,1)S(1)}, bf16[256,256]{1,0:T(8,128)(2,1)}, u32[]{:S(2)}) copy-start(bf16[256,256]{1,0:T(8,128)(2,1)} %layer_in.1) | copy-start | bytes 393220
  1.2 26.0 %copy-start.6 = (f32[8,256]{1,0:T(8,128)S(1)}, f32[8,256]{1,0:T(8,128)}, u32[]{:S(2)}) copy-start(f32[8,256]{1,0:T(8,128)} %constant.6.clone.square_row) | copy-start | bytes 24580
  1.5 25.7 %copy-start.5 = (bf16[256,128]{1,0:T(8,128)(2,1)S(1)}, bf16[256,128]{1,0:T(8,128)(2,1)}, u32[]{:S(2)}) copy-start(bf16[256,128]{1,0:T(8,128)(2,1)} %layer_out.1) | copy-start | bytes 196612
  1.5 9.9 %collective-permute-start = (f32[336,128]{1,0:T(8,128)S(1)}, f32[336,128]{1,0:T(8,128)S(1)}, u32[]{:S(2)}, u32[]{:S(2)}) collective-permute-start(f32[336,128]{1,0:T(8,128)S(1)} %get-tuple-element.29), channel_id=1, source_target_pairs={{0,8},{8,0},{16,24},{24,16},{32,40},{40,32},{48,56},{56,48},{64,72... | collective-permute-start | bytes 516104 | tf_op jit(solution)/shard_map/ppermute | solution.py:481
  11.4 18.6 %collective-permute-start.1 = (f32[32,128]{1,0:T(8,128)S(1)}, f32[32,128]{1,0:T(8,128)S(1)}, u32[]{:S(2)}, u32[]{:S(2)}) collective-permute-start(f32[32,128]{1,0:T(8,128)S(1)} %pad_maximum_fusion), channel_id=1, source_target_pairs={{1,2},{2,1},{5,6},{6,5},{9,10},{10,9},{11,12},{12,11},{13,14},{14,... | collective-permute-start | bytes 49160 | tf_op jit(solution)/shard_map/ppermute | solution.py:492
  24.0 8.6 %collective-permute-start.2 = (f32[320,128]{1,0:T(8,128)S(1)}, f32[320,128]{1,0:T(8,128)S(1)}, u32[]{:S(2)}, u32[]{:S(2)}) collective-permute-start(f32[320,128]{1,0:T(8,128)S(1)} %get-tuple-element.36), channel_id=1, source_target_pairs={{8,16},{16,8},{24,32},{32,24},{40,48},{48,40},{56,64},{64,56},{72,... | collective-permute-start | bytes 491528 | tf_op jit(solution)/shard_map/ppermute | solution.py:481
  27.2 5.4 %copy-start.2 = (f32[64,64]{1,0:T(8,128)S(1)}, f32[64,64]{1,0:T(8,128)}, u32[]{:S(2)}) copy-start(f32[64,64]{1,0:T(8,128)} %forward.1) | copy-start | bytes 49156
  28.1 4.5 %collective-permute-start.3 = (f32[32,128]{1,0:T(8,128)S(1)}, f32[32,128]{1,0:T(8,128)S(1)}, u32[]{:S(2)}, u32[]{:S(2)}) collective-permute-start(f32[32,128]{1,0:T(8,128)S(1)} %get-tuple-element.37), channel_id=1, source_target_pairs={{0,1},{1,0},{2,3},{3,2},{4,5},{5,4},{6,7},{7,6},{8,9},{9,8},{10,11... | collective-permute-start | bytes 49160 | tf_op jit(solution)/shard_map/ppermute | solution.py:481
  30.0 2.5 %collective-permute-start.4 = (f32[32,128]{1,0:T(8,128)S(1)}, f32[32,128]{1,0:T(8,128)S(1)}, u32[]{:S(2)}, u32[]{:S(2)}) collective-permute-start(f32[32,128]{1,0:T(8,128)S(1)} %collective-permute-done.1.y_odd), channel_id=1, source_target_pairs={{8,0},{11,3},{12,4},{15,7},{112,120},{115,123},{116,124},{119,127}... | collective-permute-start | bytes 49160 | tf_op jit(solution)/shard_map/ppermute | solution.py:503
  33.2 31.1 %copy-start = (bf16[128,128]{1,0:T(8,128)(2,1)S(1)}, bf16[128,128]{1,0:T(8,128)(2,1)}, u32[]{:S(2)}) copy-start(bf16[128,128]{1,0:T(8,128)(2,1)} %constant.8.clone.basis_low) | copy-start | bytes 98308
  33.2 31.0 %copy-start.1 = (bf16[128,128]{1,0:T(8,128)(2,1)S(1)}, bf16[128,128]{1,0:T(8,128)(2,1)}, u32[]{:S(2)}) copy-start(bf16[128,128]{1,0:T(8,128)(2,1)} %constant.7.clone.basis_high) | copy-start | bytes 98308
  72.6 27.6 %copy-start.3 = (f32[64,64]{1,0:T(8,128)S(1)}, f32[64,64]{1,0:T(8,128)}, u32[]{:S(2)}) copy-start(f32[64,64]{1,0:T(8,128)} %back.3) | copy-start | bytes 49156

commit v8 on v7

--- a/solution.py
+++ b/solution.py
@@ -16,6 +16,7 @@
 LANES = 128
 LOW = 16
 HIGH = 32
+OTHER = 48
 
 
 def split_table(table):
@@ -107,7 +108,6 @@
     flat[...] = jnp.transpose(jnp.concatenate([gathered, jnp.zeros_like(gathered)], axis=0))
     high, low = flat[pl.ds(0, 16, stride=2), :], flat[pl.ds(1, 16, stride=2), :]
     y_even[0:16, :] = jnp.where(even_y, high, low)
-    y_even[16:32, :] = jnp.zeros((16, LANES), F32)
     y_odd[...] = jnp.where(even_y, low, high)
     x_even[pl.ds(5 * LEVELS, 16), :] = jnp.where(even_y, low, high)
 
@@ -205,11 +205,10 @@
 
 
 def side_terms(state, edge, low):
-    u, v, w = (edge[pl.ds(f * LEVELS, LEVELS), :] for f in range(3))
-    second = edge[pl.ds(4 * LEVELS, LEVELS), :]
+    u, v, w, _, second = edge
     own = jnp.where(low, plane(state, 0, 0), plane(state, 0, ROWS - 1))
     sign = jnp.where(low, 0.1, -0.1)
-    adds = [sign * own * edge[pl.ds(f * LEVELS, LEVELS), :] for f in range(4)]
+    adds = [sign * own * value for value in edge[:4]]
     along = u * (own - second)
     beyond = u - (sign * along + 0.1 * (v * north_difference(u) + w * level_difference(u)))
     return adds, beyond
@@ -219,10 +218,10 @@
     state,
     inner,
     x_even,
-    x_odd,
+    x_far,
+    x_near,
     y_even,
     y_odd,
-    relayed,
     by_level,
     forward,
     star,
@@ -235,13 +234,20 @@
     shape = (LEVELS, LANES)
     lane = lane_of(shape)
 
-    other = jnp.where(far_both(place[0], place[1]), relayed[16:32, :], y_odd[0:16, :])
+    other = jnp.where(far_both(place[0], place[1]), 0.0, y_odd[0:16, :])
     flat[...] = jnp.zeros((LANES, LANES), F32)
     flat[pl.ds(0, 16, stride=2), :] = jnp.where(even_y, y_even[0:16, :], other)
     flat[pl.ds(1, 16, stride=2), :] = jnp.where(even_y, other, y_even[0:16, :])
+    low_side = place[1] % 4 == 0
+    scale = jnp.where(low_side, 0.1, -0.1) * jnp.where(far_both(place[0] ^ 1, place[1]), 1.0, 0.0)
+    theirs = x_even[pl.ds(5 * LEVELS + 4, 4), :]
+    flat[pl.ds(32, 16), :] = scale * jnp.concatenate([theirs] * 4, axis=0) * y_odd[16:32, :]
     columns = jnp.transpose(flat[...])[:LEVELS]
-    even_adds, even_beyond = side_terms(state, x_even, ~even_x)
-    odd_adds, odd_beyond = side_terms(state, x_odd, even_x)
+    spans = [pl.ds(i * LEVELS, LEVELS) for i in range(5)]
+    even_adds, even_beyond = side_terms(state, [x_even[at, :] for at in spans], ~even_x)
+    far_x = (place[0] % 16 == 0) | (place[0] % 16 == 15)
+    odd_edge = [jnp.where(far_x, x_far[at, :], x_near[at, :]) for at in spans]
+    odd_adds, odd_beyond = side_terms(state, odd_edge, even_x)
     end_sign = jnp.where(lane == 0, 0.1, jnp.where(lane == LANES - 1, -0.1, 0.0))
     whole = [[None] * ROWS for _ in range(4)]
     side_u = [None] * ROWS
@@ -264,8 +270,17 @@
     high_beyond = jnp.where(even_x, even_beyond, odd_beyond)
     padded = [low_beyond] + whole[0] + [high_beyond]
     divergence = []
-    extra = [-0.5 * side_u[ROWS - 1], 0.5 * side_u[0]]
     up, down = by_level[pl.ds(LEVELS, LEVELS), :], by_level[pl.ds(2 * LEVELS, LEVELS), :]
+    step = jnp.where(lane < 35, turn(columns, -1, 1), 0.0) - jnp.where(lane > 32, turn(columns, 1, 1), 0.0)
+    lifted = turn(columns, -8, 1)
+    step = 0.5 * step + up * turn(lifted, -1, 0) - down * turn(lifted, 1, 0)
+    left_out = jnp.where((lane >= 32) & (lane < 36), step, 0.0)
+    beside = jnp.where(low_side, 0.5, -0.5) * columns
+    left_out = jnp.where((lane >= 36) & (lane < 40), beside, left_out)
+    left_out = jnp.where(lane == 40, -0.5 * turn(columns, 5, 1), left_out)
+    left_out = jnp.where(lane == 41, 0.5 * turn(columns, 9, 1), left_out)
+    left_out = turn(left_out, OTHER - 32, 1)
+    extra = [left_out - 0.5 * side_u[ROWS - 1], left_out + 0.5 * side_u[0]]
     for x in range(ROWS):
         v, w = whole[1][x], whole[2][x]
         upright = up * turn(w, -1, 0) - down * turn(w, 1, 0)
@@ -329,16 +344,31 @@
     lane = lane_of((blocks, LANES))
     ends = (lane == 0) | (lane == LANES - 1)
     even = place[1] < 4
+    parity = jnp.where(even, 0, 1)
+    low_side = place[1] % 4 == 0
+    edge = jnp.where(low_side, 0, LANES - 1)
+    within = jnp.where(low_side, 1, LANES - 2)
+    row = row_of((blocks, LANES))
     inside, outside = [], [jnp.zeros((blocks, LANES), F32)] * 2
     for h in range(2):
         first, second, extra = (received[pl.ds(3 * h + j, blocks, stride=6), :] for j in range(3))
         first = first + jnp.where(ends & even, turn(extra, 1, 0), 0.0)
         second = second + jnp.where(ends & ~even, turn(extra, -1, 0), 0.0)
+        other = jnp.where(row % 16 == 0, turn(extra, -1, 0), jnp.where(row % 16 == 15, turn(extra, 1, 0), 0.0))
+        value = lambda i: jnp.sum(jnp.where(lane == OTHER + i + parity, other, 0.0), axis=1, keepdims=True)
+        beside = [value(4), value(6)]
+        corner = jnp.broadcast_to(value(8), (blocks, LANES))
+        first = first + jnp.where(lane == edge, value(0), jnp.where(lane == within, -beside[0], 0.0))
+        second = second + jnp.where(lane == edge, value(2), jnp.where(lane == within, -beside[1], 0.0))
+        first = first + jnp.where((lane == edge) & even, turn(corner, 1, 0), 0.0)
+        second = second + jnp.where((lane == edge) & ~even, turn(corner, -1, 0), 0.0)
         inside.append(jnp.concatenate([first, second], axis=0))
         for r in range(2):
             for i, start in enumerate((HIGH, LOW)):
                 at = 2 * h + i
                 outside[r] = jnp.where(lane == at, turn(extra, at - start - r, 1), outside[r])
+            at = 2 * h + jnp.where(low_side, 1, 0)
+            outside[r] = outside[r] + jnp.where(lane == at, beside[r], 0.0)
     right = parts(jnp.concatenate(inside + [jnp.concatenate(outside, axis=0)], axis=1))
     first = (((0,), (0,)), ((), ()))
     dot = lambda a, b: lax.dot_general(a, b[...], first, preferred_element_type=F32)
@@ -409,7 +439,40 @@
             message[pl.ds(3 * h + j, blocks, stride=6), :] = value
 
 
-def final_kernel(received, sent, star, back, by_level, out, held, sent_out):
+def mend_kernel(star, message, state, relayed, forward, whole, middle, flat):
+    place = position()
+    both = far_both(place[0], place[1])
+    whole[...] = star[...]
+    for i, r in enumerate((1, 2)):
+        middle[pl.ds(i * LEVELS, LEVELS), :] = message[pl.ds(3 * (r % 2) + r // 2, LEVELS, stride=6), :]
+
+    @pl.when(both)
+    def _():
+        lane = lane_of((LEVELS, LANES))
+        even_y = place[1] % 2 == 0
+        far = relayed[16:32, :]
+        flat[...] = jnp.zeros((LANES, LANES), F32)
+        flat[pl.ds(0, 16, stride=2), :] = jnp.where(even_y, 0.0, far)
+        flat[pl.ds(1, 16, stride=2), :] = jnp.where(even_y, far, 0.0)
+        columns = jnp.transpose(flat[...])[:LEVELS]
+        end_sign = jnp.where(lane == 0, 0.1, jnp.where(lane == LANES - 1, -0.1, 0.0))
+        steps = []
+        for x in range(ROWS):
+            v = plane(state, 1, x)
+            for f in range(4):
+                slot = f * ROWS + x
+                side = end_sign * v * turn(columns, -(2 * slot + 1), 1)
+                at = pl.ds(slot * LEVELS, LEVELS)
+                whole[at, :] = whole[at, :] + side
+                if f == 1 and x in (1, 2):
+                    steps.append(0.5 * north_difference(side))
+        modal = dot3(parts(forward[...]), parts(jnp.concatenate(steps, axis=1)))
+        for i in range(2):
+            at = pl.ds(i * LEVELS, LEVELS)
+            middle[at, :] = middle[at, :] + modal[:, i * LANES : (i + 1) * LANES]
+
+
+def final_kernel(received, middle, star, back, by_level, out, held, sent_out):
     size = LEVELS * ROWS
     span = lambda f: pl.ds(f * size, size)
     copies = [pltpu.make_async_copy(held.at[span(f), :], out.at[span(f), :], sent_out.at[f]) for f in range(4)]
@@ -433,7 +496,7 @@
 
     def next_row(r, opposite):
         here = p[r]
-        divergence = row_at(sent, r)
+        divergence = middle[pl.ds((r - 1) * LEVELS, LEVELS), :]
         plus = jnp.where(lane < LANES - 2, turn(here, -2, 1), turn(high[r], -1, 1))
         minus = jnp.where(lane > 1, turn(here, 2, 1), turn(low[r], 1, 1))
         return (
@@ -481,6 +544,16 @@
     return lax.ppermute(values, axis, pairs)
 
 
+def swap_odd_x(values, far):
+    count = lax.axis_size("gx")
+    pairs = []
+    for i in range(1, count + 1, 2):
+        one, two = i % count, (i + 1) % count
+        if (one % 16 == 15) == far:
+            pairs += [(one, two), (two, one)]
+    return lax.ppermute(values, "gx", pairs)
+
+
 def swap_odd_y(values):
     count_x, count_y = lax.axis_size("gx"), lax.axis_size("gy")
     pairs = []
@@ -526,16 +599,17 @@
 
     planes, x_even, x_odd, y_even, y_odd = call(
         edges_kernel,
-        [(16 * LEVELS, LANES), (5 * LEVELS + 16, LANES), (5 * LEVELS, LANES), (32, LANES), (16, LANES)],
+        [(16 * LEVELS, LANES), (5 * LEVELS + 16, LANES), (5 * LEVELS, LANES), (16, LANES), (16, LANES)],
         [*state],
         "edges",
         scratch=[(LANES, LANES)],
     )
     got_x_even = swap(x_even, "gx", 0)
+    got_x_far = swap_odd_x(x_odd, True)
     y_both = jnp.concatenate([y_odd, got_x_even[5 * LEVELS :]], axis=0)
     y_both, x_odd, y_even = lax.optimization_barrier((y_both, x_odd, y_even))
     got_y_odd = swap_odd_y(y_both)
-    got_x_odd = swap(x_odd, "gx", 1)
+    got_x_near = swap_odd_x(x_odd, False)
     inner, by_level, by_row, by_wave, by_block = call(
         inner_kernel,
         [(16 * LEVELS, LANES), (3 * LEVELS, LANES), (72, total_east), (3 * LANES, LANES), (72, total_east)],
@@ -551,8 +625,6 @@
     )
     inner, y_even = lax.optimization_barrier((inner, y_even))
     got_y_even = swap(y_even, "gy", 0)
-    inner, got_y_odd = lax.optimization_barrier((inner, got_y_odd))
-    relayed = hand_over(got_y_odd)
     star, message = call(
         outer_kernel,
         [(16 * LEVELS, LANES), (blocks * 6, LANES)],
@@ -560,10 +632,10 @@
             planes,
             inner,
             got_x_even,
-            got_x_odd,
+            got_x_far,
+            got_x_near,
             got_y_even,
             got_y_odd,
-            relayed,
             by_level,
             mode_forward,
         ],
@@ -576,6 +648,15 @@
         [(LANES, total_east), (32, total_east)],
         [modal, basis_high, basis_low, by_row, by_wave],
         "solve",
+    )
+    moments, got_y_odd = lax.optimization_barrier((moments, got_y_odd))
+    relayed = hand_over(got_y_odd)
+    whole, middle = call(
+        mend_kernel,
+        [(16 * LEVELS, LANES), (2 * LEVELS, LANES)],
+        [star, message, planes, relayed, mode_forward],
+        "mend",
+        scratch=[(LANES, LANES)],
     )
     moments = lax.all_to_all(
         moments.reshape(4, 8, total_east),
@@ -585,6 +666,7 @@
         tiled=True,
         axis_index_groups=[[0, 1, 2, 3], [4, 5, 6, 7]],
     ).reshape(32, total_east)
+    moments, whole, middle = lax.optimization_barrier((moments, whole, middle))
     (reply,) = call(
         back_kernel,
         [(blocks * 6, LANES)],
@@ -595,7 +677,7 @@
     (out,) = call(
         final_kernel,
         [(4 * LEVELS * ROWS, LANES)],
-        [pressure, message, star, mode_back, by_level],
+        [pressure, middle, whole, mode_back, by_level],
         "final",
         scratch=[(4 * LEVELS * ROWS, LANES)],
         copies=4,

time: 102 us -> 101 us (level)
  blocking collectives: 66.1 us -> 57.2 us
  starting transfers between devices: 27.8 us -> 32.4 us
  waiting for transfers between devices: 2.16 us -> 4.98 us
    all_to_all x1 -> x0, blocking collectives: 7.49 us -> none  [on_device(): lax.all_to_all(moments.reshape(4, 8, total_east), 'gy', 0, 0, tiled=True,...]
    ppermute x0 -> x2, starting transfers between devices: none -> 3.85 us  [swap_odd_x(): return lax.ppermute(values, 'gx', pairs)]
    all_to_all x0 -> x1, starting transfers between devices: none -> 3.26 us  [on_device(): lax.all_to_all(moments.reshape(4, 8, total_east), 'gy', 0, 0, tiled=True,...]
    ppermute x3 -> x2, starting transfers between devices: 14 us -> 10.8 us  [swap(): return lax.ppermute(values, axis, pairs)]
    all_to_all x0 -> x1, waiting for transfers between devices: none -> 1.47 us  [on_device(): lax.all_to_all(moments.reshape(4, 8, total_east), 'gy', 0, 0, tiled=True,...]
    all_to_all x2, blocking collectives: 58.6 us -> 57.2 us  [exchange(): lax.all_to_all(shaped, ('gx', 'gy'), 0, 0, tiled=True, axis_index_groups=...]
    pallas_call x6 -> x7, Pallas kernels: 3.81 us -> 4.58 us  [call(): pl.pallas_call(kernel, out_shape=[jax.ShapeDtypeStruct(s, F32) for s in s...]
    ppermute x3 -> x2, waiting for transfers between devices: 2.15 us -> 2.68 us  [swap(): return lax.ppermute(values, axis, pairs)]
  transfers between devices with their start and end apart: 5 -> 7, of which waited for: 2 -> 4; matrix products, arithmetic and copies ran while one was open for 0% -> 0% of each run, Pallas kernels for 1% -> 1%
where the time goes in v8:
time: 101 us
  blocking collectives  57.2 us (57%)
  starting transfers between devices  32.4 us (32%)
  waiting for transfers between devices  4.98 us (5%)
  Pallas kernels  4.58 us (5%)
  local copies, waits for them, and re-layouts  1.2 us (1%)
    all_to_all x2, blocking collectives, exchange(): lax.all_to_all(shaped, ('gx', 'gy'), 0, 0, tiled=True, axis_index_groups=...  57.2 us
    ppermute x1, starting transfers between devices, swap_odd_y(): return lax.ppermute(values, ('gx', 'gy'), pairs)  12.5 us
    ppermute x2, starting transfers between devices, swap(): return lax.ppermute(values, axis, pairs)  10.8 us
    pallas_call x7, Pallas kernels, call(): pl.pallas_call(kernel, out_shape=[jax.ShapeDtypeStruct(s, F32) for s in s...  4.58 us
    ppermute x2, starting transfers between devices, swap_odd_x(): return lax.ppermute(values, 'gx', pairs)  3.85 us
    all_to_all x1, starting transfers between devices, on_device(): lax.all_to_all(moments.reshape(4, 8, total_east), 'gy', 0, 0, tiled=True,...  3.26 us
    ppermute x2, waiting for transfers between devices, swap(): return lax.ppermute(values, axis, pairs)  2.68 us
  transfers between devices with their start and end apart: 7, of which 4 were waited for; matrix products, arithmetic and copies ran while one was open for 0% of the time, Pallas kernels for 1%

profile of v8, /device:TPU:1, one launch (start us, length us, event | category | flops | bytes accessed | tf_op | source)
XLA Modules:
  0.0 100.7 jit_solution(17650355971385783439)
XLA Ops:
  0.0 1.1 %fusion = (f32[1,64,4,128]{3,2,1,0:T(4,128)S(1)}, f32[1,64,4,128]{3,2,1,0:T(4,128)S(1)}, f32[1,64,4,128]{3,2,1,0:T(4,128)S(1)}, f32[1,64,4,128]{3,2,1,0:T(4,128)S(1)}) fusion(f32[4,64,4,128]{3,2,1,0:T(4,128)} %param.11), kind=kLoop, calls=%fused_computation.2 | loop fusion | bytes 1048576 | tf_op jit(solution)/shard_map/slice | solution.py:595
  1.1 0.0 copy-start.7
  1.1 0.0 copy-start.8
  1.2 0.0 copy-start.9
  1.2 0.0 copy-start.4
  1.2 0.0 copy-start.6
  1.2 0.3 edges.1
  1.5 0.0 copy-start.5
  1.5 8.9 %collective-permute-start = (f32[336,128]{1,0:T(8,128)S(1)}, f32[336,128]{1,0:T(8,128)S(1)}, u32[]{:S(2)}, u32[]{:S(2)}) collective-permute-start(f32[336,128]{1,0:T(8,128)S(1)} %get-tuple-element.34), channel_id=1, source_target_pairs={{0,8},{8,0},{16,24},{24,16},{32,40},{40,32},{48,56},{56,48},{64,72... | collective-permute-start | bytes 516104 | tf_op jit(solution)/shard_map/ppermute | solution.py:544
  10.4 0.7 collective-permute-start.1
  11.1 0.0 copy-done.7
  11.1 0.0 copy-done.8
  11.1 0.0 copy-done.9
  11.1 0.1 pad_maximum_fusion.1
  11.2 0.2 collective-permute-done.x_even
  11.4 12.5 %collective-permute-start.4 = (f32[32,128]{1,0:T(8,128)S(1)}, f32[32,128]{1,0:T(8,128)S(1)}, u32[]{:S(2)}, u32[]{:S(2)}) collective-permute-start(f32[32,128]{1,0:T(8,128)S(1)} %pad_maximum_fusion), channel_id=1, source_target_pairs={{1,2},{2,1},{5,6},{6,5},{9,10},{10,9},{11,12},{12,11},{13,14},{14,... | collective-permute-start | bytes 49160 | tf_op jit(solution)/shard_map/ppermute | solution.py:565
  24.0 3.2 %collective-permute-start.2 = (f32[320,128]{1,0:T(8,128)S(1)}, f32[320,128]{1,0:T(8,128)S(1)}, u32[]{:S(2)}, u32[]{:S(2)}) collective-permute-start(f32[320,128]{1,0:T(8,128)S(1)} %get-tuple-element.39), channel_id=1, source_target_pairs={{8,16},{16,8},{24,32},{32,24},{40,48},{48,40},{56,64},{64,56},{72,... | collective-permute-start | bytes 491528 | tf_op jit(solution)/shard_map/ppermute | solution.py:554
  27.1 0.0 copy-done.4
  27.2 0.0 copy-done.6
  27.2 0.0 copy-done.5
  27.2 0.0 copy-start.2
  27.2 0.8 inner.1
  28.0 1.9 %collective-permute-start.3 = (f32[16,128]{1,0:T(8,128)S(1)}, f32[16,128]{1,0:T(8,128)S(1)}, u32[]{:S(2)}, u32[]{:S(2)}) collective-permute-start(f32[16,128]{1,0:T(8,128)S(1)} %get-tuple-element.40), channel_id=1, source_target_pairs={{0,1},{1,0},{2,3},{3,2},{4,5},{5,4},{6,7},{7,6},{8,9},{9,8},{10,11... | collective-permute-start | bytes 24584 | tf_op jit(solution)/shard_map/ppermute | solution.py:544
  30.0 0.0 collective-permute-done.1.x_far
  30.0 2.5 %collective-permute-done.3.y_even = f32[16,128]{1,0:T(8,128)S(1)} collective-permute-done((f32[16,128]{1,0:T(8,128)S(1)}, f32[16,128]{1,0:T(8,128)S(1)}, u32[]{:S(2)}, u32[]{:S(2)}) %collective-permute-start.3) | collective-permute-done | bytes 8224 | tf_op jit(solution)/shard_map/ppermute | solution.py:544
  32.4 0.0 collective-permute-done.4.y_odd
  32.4 0.0 collective-permute-done.2.x_near
  32.4 0.0 copy-done.2
  32.4 0.7 outer.1
  33.1 0.0 copy-start
  33.1 0.0 copy-start.1
  33.1 29.8 %all_to_all.15 = f32[128,1,384]{2,1,0:T(1,128)S(1)} all-to-all(f32[128,1,384]{2,1,0:T(1,128)S(1)} %bitcast.11), channel_id=1, replica_groups={{0,4,8,12,16,20,24,28,32,36,40,44,48,52,56,60,64,68,72,76,80,84,88,92,9..., dimensions={0} | all-to-all | bytes 393216 | tf_op jit(solution)/shard_map/all_to_all | solution.py:584
  62.9 0.0 copy-done
  62.9 0.0 copy-done.1
  62.9 1.2 %solve.1 = (f32[128,256]{1,0:T(8,128)S(1)}, f32[32,256]{1,0:T(8,128)}) custom-call(f32[384,128]{1,0:T(8,128)S(1)} %bitcast.12, bf16[128,128]{1,0:T(8,128)(2,1)S(1)} %copy-done.1, bf16[128,128]{1,0:T(8,128)(2,1)S(1)} %copy-done, f32[72,256]{1,0:T(8,128)S(1)} %get-tuple-element.44.by_row, f32[384,128]{1,0:T(8,128)S(1)} %get-tuple-element.45.by_wave), custom_call_target="tpu_custom_call" | custom-call | tf_op jit(solution)/shard_map/solve/pallas_call | solution.py:526
  64.1 3.3 %all-to-all-start.1 = ((f32[4,8,256]{2,1,0:T(8,128)}), f32[4,8,256]{2,1,0:T(8,128)S(1)}, u32[]{:S(2)}, u32[]{:S(2)}) async-start(f32[4,8,256]{2,1,0:T(8,128)} %bitcast.6), calls=%async_computation.1 | async-start | bytes 65536 | tf_op jit(solution)/shard_map/all_to_all | solution.py:661
  67.4 1.9 %collective-permute-start.5 = (f32[32,128]{1,0:T(8,128)S(1)}, f32[32,128]{1,0:T(8,128)S(1)}, u32[]{:S(2)}, u32[]{:S(2)}) collective-permute-start(f32[32,128]{1,0:T(8,128)S(1)} %collective-permute-done.4.y_odd), channel_id=1, source_target_pairs={{8,0},{11,3},{12,4},{15,7},{112,120},{115,123},{116,124},{119,127}... | collective-permute-start | bytes 49160 | tf_op jit(solution)/shard_map/ppermute | solution.py:576
  69.3 0.8 collective-permute-done.5.relayed
  70.2 1.5 %all-to-all-done.1 = f32[4,8,256]{2,1,0:T(8,128)S(1)} async-done(((f32[4,8,256]{2,1,0:T(8,128)}), f32[4,8,256]{2,1,0:T(8,128)S(1)}, u32[]{:S(2)}, u32[]{:S(2)}) %all-to-all-start.1) | async-done | bytes 32800 | tf_op jit(solution)/shard_map/all_to_all | solution.py:661
  71.6 0.4 back.2
  72.0 0.0 copy-start.3
  72.0 27.5 %all_to_all.16 = f32[128,1,384]{2,1,0:T(1,128)S(1)} all-to-all(f32[128,1,384]{2,1,0:T(1,128)S(1)} %bitcast.13), channel_id=1, replica_groups={{0,4,8,12,16,20,24,28,32,36,40,44,48,52,56,60,64,68,72,76,80,84,88,92,9..., dimensions={0} | all-to-all | bytes 393216 | tf_op jit(solution)/shard_map/all_to_all | solution.py:584
  99.5 0.0 copy-done.3
  99.5 1.2 %final.1 = f32[1024,128]{1,0:T(8,128)} custom-call(f32[384,128]{1,0:T(8,128)S(1)} %bitcast.14, f32[128,128]{1,0:T(8,128)S(1)} %get-tuple-element.55.middle, f32[1024,128]{1,0:T(8,128)S(1)} %get-tuple-element.56.star, f32[64,64]{1,0:T(8,128)S(1)} %copy-done.3, f32[192,128]{1,0:T(8,128)S(1)} %get-tuple-element.42.by_level), custom_call_target="tpu_custom_call" | custom-call | tf_op jit(solution)/shard_map/final/pallas_call | solution.py:526
  (4 shorter events, 0.1 us)
Async XLA Ops:
  1.1 10.0 %copy-start.7 = (f32[256]{0:T(256)S(1)}, f32[256]{0:T(256)}, u32[]{:S(2)}) copy-start(f32[256]{0:T(256)} %param.14) | copy-start | bytes 3076
  1.1 10.0 %copy-start.8 = (f32[64]{0:T(128)S(1)}, f32[64]{0:T(128)}, u32[]{:S(2)}) copy-start(f32[64]{0:T(128)} %param.12) | copy-start | bytes 772
  1.2 10.0 %copy-start.9 = (f32[64]{0:T(128)S(1)}, f32[64]{0:T(128)}, u32[]{:S(2)}) copy-start(f32[64]{0:T(128)} %param.18) | copy-start | bytes 772
  1.2 26.0 %copy-start.4 = (bf16[256,256]{1,0:T(8,128)(2,1)S(1)}, bf16[256,256]{1,0:T(8,128)(2,1)}, u32[]{:S(2)}) copy-start(bf16[256,256]{1,0:T(8,128)(2,1)} %layer_in.1) | copy-start | bytes 393220
  1.2 26.0 %copy-start.6 = (f32[8,256]{1,0:T(8,128)S(1)}, f32[8,256]{1,0:T(8,128)}, u32[]{:S(2)}) copy-start(f32[8,256]{1,0:T(8,128)} %constant.6.clone.square_row) | copy-start | bytes 24580
  1.5 25.7 %copy-start.5 = (bf16[256,128]{1,0:T(8,128)(2,1)S(1)}, bf16[256,128]{1,0:T(8,128)(2,1)}, u32[]{:S(2)}) copy-start(bf16[256,128]{1,0:T(8,128)(2,1)} %layer_out.1) | copy-start | bytes 196612
  1.5 9.9 %collective-permute-start = (f32[336,128]{1,0:T(8,128)S(1)}, f32[336,128]{1,0:T(8,128)S(1)}, u32[]{:S(2)}, u32[]{:S(2)}) collective-permute-start(f32[336,128]{1,0:T(8,128)S(1)} %get-tuple-element.34), channel_id=1, source_target_pairs={{0,8},{8,0},{16,24},{24,16},{32,40},{40,32},{48,56},{56,48},{64,72... | collective-permute-start | bytes 516104 | tf_op jit(solution)/shard_map/ppermute | solution.py:544
  10.4 19.5 %collective-permute-start.1 = (f32[320,128]{1,0:T(8,128)S(1)}, f32[320,128]{1,0:T(8,128)S(1)}, u32[]{:S(2)}, u32[]{:S(2)}) collective-permute-start(f32[320,128]{1,0:T(8,128)S(1)} %get-tuple-element.39), channel_id=1, source_target_pairs={{120,128},{128,120},{248,256},{256,248},{376,384},{384,376},{504,0... | collective-permute-start | bytes 491528 | tf_op jit(solution)/shard_map/ppermute | solution.py:554
  11.4 21.0 %collective-permute-start.4 = (f32[32,128]{1,0:T(8,128)S(1)}, f32[32,128]{1,0:T(8,128)S(1)}, u32[]{:S(2)}, u32[]{:S(2)}) collective-permute-start(f32[32,128]{1,0:T(8,128)S(1)} %pad_maximum_fusion), channel_id=1, source_target_pairs={{1,2},{2,1},{5,6},{6,5},{9,10},{10,9},{11,12},{12,11},{13,14},{14,... | collective-permute-start | bytes 49160 | tf_op jit(solution)/shard_map/ppermute | solution.py:565
  24.0 8.5 %collective-permute-start.2 = (f32[320,128]{1,0:T(8,128)S(1)}, f32[320,128]{1,0:T(8,128)S(1)}, u32[]{:S(2)}, u32[]{:S(2)}) collective-permute-start(f32[320,128]{1,0:T(8,128)S(1)} %get-tuple-element.39), channel_id=1, source_target_pairs={{8,16},{16,8},{24,32},{32,24},{40,48},{48,40},{56,64},{64,56},{72,... | collective-permute-start | bytes 491528 | tf_op jit(solution)/shard_map/ppermute | solution.py:554
  27.2 5.3 %copy-start.2 = (f32[64,64]{1,0:T(8,128)S(1)}, f32[64,64]{1,0:T(8,128)}, u32[]{:S(2)}) copy-start(f32[64,64]{1,0:T(8,128)} %forward.3) | copy-start | bytes 49156
  28.0 4.4 %collective-permute-start.3 = (f32[16,128]{1,0:T(8,128)S(1)}, f32[16,128]{1,0:T(8,128)S(1)}, u32[]{:S(2)}, u32[]{:S(2)}) collective-permute-start(f32[16,128]{1,0:T(8,128)S(1)} %get-tuple-element.40), channel_id=1, source_target_pairs={{0,1},{1,0},{2,3},{3,2},{4,5},{5,4},{6,7},{7,6},{8,9},{9,8},{10,11... | collective-permute-start | bytes 24584 | tf_op jit(solution)/shard_map/ppermute | solution.py:544
  33.1 29.8 %copy-start = (bf16[128,128]{1,0:T(8,128)(2,1)S(1)}, bf16[128,128]{1,0:T(8,128)(2,1)}, u32[]{:S(2)}) copy-start(bf16[128,128]{1,0:T(8,128)(2,1)} %constant.8.clone.basis_low) | copy-start | bytes 98308
  33.1 29.8 %copy-start.1 = (bf16[128,128]{1,0:T(8,128)(2,1)S(1)}, bf16[128,128]{1,0:T(8,128)(2,1)}, u32[]{:S(2)}) copy-start(bf16[128,128]{1,0:T(8,128)(2,1)} %constant.7.clone.basis_high) | copy-start | bytes 98308
  64.1 7.6 %all-to-all-start.1 = ((f32[4,8,256]{2,1,0:T(8,128)}), f32[4,8,256]{2,1,0:T(8,128)S(1)}, u32[]{:S(2)}, u32[]{:S(2)}) async-start(f32[4,8,256]{2,1,0:T(8,128)} %bitcast.6), calls=%async_computation.1 | async-start | bytes 65536 | tf_op jit(solution)/shard_map/all_to_all | solution.py:661
  67.4 2.8 %collective-permute-start.5 = (f32[32,128]{1,0:T(8,128)S(1)}, f32[32,128]{1,0:T(8,128)S(1)}, u32[]{:S(2)}, u32[]{:S(2)}) collective-permute-start(f32[32,128]{1,0:T(8,128)S(1)} %collective-permute-done.4.y_odd), channel_id=1, source_target_pairs={{8,0},{11,3},{12,4},{15,7},{112,120},{115,123},{116,124},{119,127}... | collective-permute-start | bytes 49160 | tf_op jit(solution)/shard_map/ppermute | solution.py:576
  72.0 27.5 %copy-start.3 = (f32[64,64]{1,0:T(8,128)S(1)}, f32[64,64]{1,0:T(8,128)}, u32[]{:S(2)}) copy-start(f32[64,64]{1,0:T(8,128)} %back.3) | copy-start | bytes 49156

commit v9 on v8

--- a/solution.py
+++ b/solution.py
@@ -116,20 +116,8 @@
     return jnp.transpose(jnp.broadcast_to(row, (LANES, LANES)))
 
 
-def inner_kernel(
-    state,
-    vectors,
-    square_row,
-    layer_in,
-    layer_out,
-    star,
-    by_level,
-    by_row,
-    by_wave,
-    by_block,
-):
+def tables_kernel(vectors, square_row, by_level, by_row, by_wave, by_block):
     place = position()
-    fields = [[plane(state, f, x) for x in range(ROWS)] for f in range(4)]
     tall = column_of(vectors[:, :LANES])
     rate, density = tall[:LEVELS], tall[LEVELS:]
     row = row_of((LEVELS, LANES))
@@ -170,6 +158,9 @@
     scale = -1.0 / root
     by_block[pl.ds(64, 8), :] = jnp.where(row == 0, scale, jnp.where(row == 1, scale * r64, scale * inverse))
 
+
+def inner_kernel(state, vectors, layer_in, layer_out, star):
+    fields = [[plane(state, f, x) for x in range(ROWS)] for f in range(4)]
     for x in range(ROWS):
         u, v, w, th = (fields[f][x] for f in range(4))
         for f in range(4):
@@ -222,6 +213,7 @@
     x_near,
     y_even,
     y_odd,
+    y_both,
     by_level,
     forward,
     star,
@@ -234,14 +226,16 @@
     shape = (LEVELS, LANES)
     lane = lane_of(shape)
 
-    other = jnp.where(far_both(place[0], place[1]), 0.0, y_odd[0:16, :])
+    helping = far_both(place[0] ^ 1, place[1])
+    other = jnp.where(helping, y_both[0:16, :], y_odd[...])
+    other = jnp.where(far_both(place[0], place[1]), 0.0, other)
     flat[...] = jnp.zeros((LANES, LANES), F32)
     flat[pl.ds(0, 16, stride=2), :] = jnp.where(even_y, y_even[0:16, :], other)
     flat[pl.ds(1, 16, stride=2), :] = jnp.where(even_y, other, y_even[0:16, :])
     low_side = place[1] % 4 == 0
-    scale = jnp.where(low_side, 0.1, -0.1) * jnp.where(far_both(place[0] ^ 1, place[1]), 1.0, 0.0)
+    scale = jnp.where(low_side, 0.1, -0.1) * jnp.where(helping, 1.0, 0.0)
     theirs = x_even[pl.ds(5 * LEVELS + 4, 4), :]
-    flat[pl.ds(32, 16), :] = scale * jnp.concatenate([theirs] * 4, axis=0) * y_odd[16:32, :]
+    flat[pl.ds(32, 16), :] = scale * jnp.concatenate([theirs] * 4, axis=0) * y_both[16:32, :]
     columns = jnp.transpose(flat[...])[:LEVELS]
     spans = [pl.ds(i * LEVELS, LEVELS) for i in range(5)]
     even_adds, even_beyond = side_terms(state, [x_even[at, :] for at in spans], ~even_x)
@@ -554,13 +548,13 @@
     return lax.ppermute(values, "gx", pairs)
 
 
-def swap_odd_y(values):
+def swap_odd_y(values, helping):
     count_x, count_y = lax.axis_size("gx"), lax.axis_size("gy")
     pairs = []
     for i in range(count_x):
         for j in range(1, count_y + 1, 2):
             one, two = j % count_y, (j + 1) % count_y
-            if not far_both(i, one):
+            if not far_both(i, one) and far_both(i ^ 1, one) == helping:
                 pairs += [(i * count_y + one, i * count_y + two), (i * count_y + two, i * count_y + one)]
     return lax.ppermute(values, ("gx", "gy"), pairs)
 
@@ -606,25 +600,29 @@
     )
     got_x_even = swap(x_even, "gx", 0)
     got_x_far = swap_odd_x(x_odd, True)
+    got_y_odd = swap_odd_y(y_odd, False)
     y_both = jnp.concatenate([y_odd, got_x_even[5 * LEVELS :]], axis=0)
     y_both, x_odd, y_even = lax.optimization_barrier((y_both, x_odd, y_even))
-    got_y_odd = swap_odd_y(y_both)
+    got_y_both = swap_odd_y(y_both, True)
     got_x_near = swap_odd_x(x_odd, False)
-    inner, by_level, by_row, by_wave, by_block = call(
+    vectors = jnp.concatenate([mode_rate, density, layer_bias])[None, :]
+    long = pl.CostEstimate(flops=10**10, transcendentals=0, bytes_accessed=2**24)
+    by_level, by_row, by_wave, by_block = call(
+        tables_kernel,
+        [(3 * LEVELS, LANES), (72, total_east), (3 * LANES, LANES), (72, total_east)],
+        [vectors, square_row],
+        "tables",
+        cost=long,
+    )
+    by_level, y_even = lax.optimization_barrier((by_level, y_even))
+    got_y_even = swap(y_even, "gy", 0)
+    (inner,) = call(
         inner_kernel,
-        [(16 * LEVELS, LANES), (3 * LEVELS, LANES), (72, total_east), (3 * LANES, LANES), (72, total_east)],
-        [
-            planes,
-            jnp.concatenate([mode_rate, density, layer_bias])[None, :],
-            square_row,
-            layer_in,
-            layer_out,
-        ],
+        [(16 * LEVELS, LANES)],
+        [planes, vectors, layer_in, layer_out],
         "inner",
-        cost=pl.CostEstimate(flops=10**10, transcendentals=0, bytes_accessed=2**24),
-    )
-    inner, y_even = lax.optimization_barrier((inner, y_even))
-    got_y_even = swap(y_even, "gy", 0)
+        cost=None,
+    )
     star, message = call(
         outer_kernel,
         [(16 * LEVELS, LANES), (blocks * 6, LANES)],
@@ -636,27 +634,29 @@
             got_x_near,
             got_y_even,
             got_y_odd,
+            got_y_both,
             by_level,
             mode_forward,
         ],
         "outer",
         scratch=[(LANES, LANES)],
     )
+    message, got_y_both = lax.optimization_barrier((message, got_y_both))
+    relayed = hand_over(got_y_both)
     modal = exchange(message)
-    local, moments = call(
-        solve_kernel,
-        [(LANES, total_east), (32, total_east)],
-        [modal, basis_high, basis_low, by_row, by_wave],
-        "solve",
-    )
-    moments, got_y_odd = lax.optimization_barrier((moments, got_y_odd))
-    relayed = hand_over(got_y_odd)
     whole, middle = call(
         mend_kernel,
         [(16 * LEVELS, LANES), (2 * LEVELS, LANES)],
         [star, message, planes, relayed, mode_forward],
         "mend",
         scratch=[(LANES, LANES)],
+    )
+    modal, whole, middle = lax.optimization_barrier((modal, whole, middle))
+    local, moments = call(
+        solve_kernel,
+        [(LANES, total_east), (32, total_east)],
+        [modal, basis_high, basis_low, by_row, by_wave],
+        "solve",
     )
     moments = lax.all_to_all(
         moments.reshape(4, 8, total_east),
@@ -666,7 +666,6 @@
         tiled=True,
         axis_index_groups=[[0, 1, 2, 3], [4, 5, 6, 7]],
     ).reshape(32, total_east)
-    moments, whole, middle = lax.optimization_barrier((moments, whole, middle))
     (reply,) = call(
         back_kernel,
         [(blocks * 6, LANES)],

time: 101 us -> 101 us (level)
  blocking collectives: 57.2 us -> 34.5 us
  waiting for transfers between devices: 4.98 us -> 18.1 us
  starting transfers between devices: 32.4 us -> 40.6 us
  Pallas kernels: 4.58 us -> 5.73 us
    all_to_all x2 -> x1, blocking collectives: 57.2 us -> 27.6 us  [exchange(): lax.all_to_all(shaped, ('gx', 'gy'), 0, 0, tiled=True, axis_index_groups=...]
    all_to_all x1, waiting for transfers between devices: 1.47 us -> 15.5 us  [exchange(): lax.all_to_all(shaped, ('gx', 'gy'), 0, 0, tiled=True, axis_index_groups=...]
    all_to_all x1, starting transfers between devices: 3.26 us -> 10.2 us  [exchange(): lax.all_to_all(shaped, ('gx', 'gy'), 0, 0, tiled=True, axis_index_groups=...]
    all_to_all x0 -> x1, blocking collectives: none -> 6.9 us  [on_device(): lax.all_to_all(moments.reshape(4, 8, total_east), 'gy', 0, 0, tiled=True,...]
    pallas_call x7 -> x8, Pallas kernels: 4.58 us -> 5.73 us  [call(): pl.pallas_call(kernel, out_shape=[jax.ShapeDtypeStruct(s, F32) for s in s...]
    ppermute x1 -> x2, starting transfers between devices: 12.5 us -> 13.4 us  [swap_odd_y(): return lax.ppermute(values, ('gx', 'gy'), pairs)]
  transfers between devices with their start and end apart: 7 -> 8, of which waited for: 4 -> 3; matrix products, arithmetic and copies ran while one was open for 0% -> 0% of each run, Pallas kernels for 1% -> 2%
where the time goes in v9:
time: 101 us; the launch traced here: 100 us
  starting transfers between devices  40.6 us (40%)
  blocking collectives  34.5 us (34%)
  waiting for transfers between devices  18.1 us (18%)
  Pallas kernels  5.73 us (6%)
  local copies, waits for them, and re-layouts  1.19 us (1%)
    all_to_all x1, blocking collectives, exchange(): lax.all_to_all(shaped, ('gx', 'gy'), 0, 0, tiled=True, axis_index_groups=...  27.6 us
    all_to_all x1, waiting for transfers between devices, exchange(): lax.all_to_all(shaped, ('gx', 'gy'), 0, 0, tiled=True, axis_index_groups=...  15.5 us
    ppermute x2, starting transfers between devices, swap_odd_y(): return lax.ppermute(values, ('gx', 'gy'), pairs)  13.4 us
    ppermute x2, starting transfers between devices, swap(): return lax.ppermute(values, axis, pairs)  10.7 us
    all_to_all x1, starting transfers between devices, exchange(): lax.all_to_all(shaped, ('gx', 'gy'), 0, 0, tiled=True, axis_index_groups=...  10.2 us
    all_to_all x1, blocking collectives, on_device(): lax.all_to_all(moments.reshape(4, 8, total_east), 'gy', 0, 0, tiled=True,...  6.9 us
    pallas_call x8, Pallas kernels, call(): pl.pallas_call(kernel, out_shape=[jax.ShapeDtypeStruct(s, F32) for s in s...  5.73 us
    ppermute x2, starting transfers between devices, swap_odd_x(): return lax.ppermute(values, 'gx', pairs)  3.5 us
  transfers between devices with their start and end apart: 8, of which 3 were waited for; matrix products, arithmetic and copies ran while one was open for 0% of the time, Pallas kernels for 2%

profile of v9, /device:TPU:1, one launch (start us, length us, event | category | flops | bytes accessed | tf_op | source)
XLA Modules:
  0.0 100.4 jit_solution(8940500614644102329)
XLA Ops:
  0.0 1.1 %fusion = (f32[1,64,4,128]{3,2,1,0:T(4,128)S(1)}, f32[1,64,4,128]{3,2,1,0:T(4,128)S(1)}, f32[1,64,4,128]{3,2,1,0:T(4,128)S(1)}, f32[1,64,4,128]{3,2,1,0:T(4,128)S(1)}) fusion(f32[4,64,4,128]{3,2,1,0:T(4,128)} %param.11), kind=kLoop, calls=%fused_computation.2 | loop fusion | bytes 1048576 | tf_op jit(solution)/shard_map/slice | solution.py:589
  1.1 0.3 edges.1
  1.4 8.8 %collective-permute-start = (f32[336,128]{1,0:T(8,128)S(1)}, f32[336,128]{1,0:T(8,128)S(1)}, u32[]{:S(2)}, u32[]{:S(2)}) collective-permute-start(f32[336,128]{1,0:T(8,128)S(1)} %get-tuple-element.31), channel_id=1, source_target_pairs={{0,8},{8,0},{16,24},{24,16},{32,40},{40,32},{48,56},{56,48},{64,72... | collective-permute-start | bytes 516104 | tf_op jit(solution)/shard_map/ppermute | solution.py:538
  10.2 0.0 copy-start.9
  10.2 0.0 copy-start.7
  10.2 0.0 copy-start.8
  10.2 0.8 collective-permute-start.4
  11.1 0.7 collective-permute-start.1
  11.7 0.0 copy-done.9
  11.7 0.0 copy-done.7
  11.7 0.0 copy-done.8
  11.8 0.1 pad_maximum_fusion.1
  11.8 0.0 collective-permute-done.x_even
  11.8 0.0 copy-start.6
  11.9 0.0 copy-start.2
  11.9 0.0 copy-start.4
  11.9 12.7 %collective-permute-start.5 = (f32[32,128]{1,0:T(8,128)S(1)}, f32[32,128]{1,0:T(8,128)S(1)}, u32[]{:S(2)}, u32[]{:S(2)}) collective-permute-start(f32[32,128]{1,0:T(8,128)S(1)} %pad_maximum_fusion), channel_id=1, source_target_pairs={{11,12},{12,11},{15,8},{8,15},{115,116},{116,115},{119,112},{112,1... | collective-permute-start | bytes 49160 | tf_op jit(solution)/shard_map/ppermute | solution.py:559
  24.6 2.8 %collective-permute-start.2 = (f32[320,128]{1,0:T(8,128)S(1)}, f32[320,128]{1,0:T(8,128)S(1)}, u32[]{:S(2)}, u32[]{:S(2)}) collective-permute-start(f32[320,128]{1,0:T(8,128)S(1)} %get-tuple-element.35), channel_id=1, source_target_pairs={{8,16},{16,8},{24,32},{32,24},{40,48},{48,40},{56,64},{64,56},{72,... | collective-permute-start | bytes 491528 | tf_op jit(solution)/shard_map/ppermute | solution.py:548
  27.4 0.0 copy-done.6
  27.4 0.3 tables.1
  27.7 1.9 %collective-permute-start.3 = (f32[16,128]{1,0:T(8,128)S(1)}, f32[16,128]{1,0:T(8,128)S(1)}, u32[]{:S(2)}, u32[]{:S(2)}) collective-permute-start(f32[16,128]{1,0:T(8,128)S(1)} %get-tuple-element.38), channel_id=1, source_target_pairs={{0,1},{1,0},{2,3},{3,2},{4,5},{5,4},{6,7},{7,6},{8,9},{9,8},{10,11... | collective-permute-start | bytes 24584 | tf_op jit(solution)/shard_map/ppermute | solution.py:538
  29.6 0.0 copy-done.2
  29.6 0.0 copy-done.4
  29.7 0.0 copy-start.3
  29.7 0.7 inner.1
  30.3 0.0 collective-permute-done.4.y_odd
  30.3 0.0 collective-permute-done.1.x_far
  30.4 1.7 %collective-permute-done.3.y_even = f32[16,128]{1,0:T(8,128)S(1)} collective-permute-done((f32[16,128]{1,0:T(8,128)S(1)}, f32[16,128]{1,0:T(8,128)S(1)}, u32[]{:S(2)}, u32[]{:S(2)}) %collective-permute-start.3) | collective-permute-done | bytes 8224 | tf_op jit(solution)/shard_map/ppermute | solution.py:538
  32.1 0.0 collective-permute-done.5.y_both
  32.1 0.0 collective-permute-done.2.x_near
  32.1 0.0 copy-done.3
  32.1 1.3 %outer.1 = (f32[1024,128]{1,0:T(8,128)S(1)}, f32[384,128]{1,0:T(8,128)}) custom-call(f32[1024,128]{1,0:T(8,128)S(1)} %get-tuple-element.30.state, f32[1024,128]{1,0:T(8,128)S(1)} %inner.1, f32[336,128]{1,0:T(8,128)S(1)} %collective-permute-done.x_even, f32[320,128]{1,0:T(8,128)S(1)} %collective-permute-done.1.x_far, ...), custom_call_target="tpu_custom_call" | custom-call | tf_op jit(solution)/shard_map/outer/pallas_call | solution.py:520
  33.5 10.2 %all-to-all-start = ((f32[128,1,384]{2,1,0:T(1,128)}), f32[128,1,384]{2,1,0:T(1,128)S(1)}, u32[]{:S(2)}, u32[]{:S(2)}) async-start(f32[128,1,384]{2,1,0:T(1,128)} %bitcast.4), calls=%async_computation | async-start | bytes 393216 | tf_op jit(solution)/shard_map/all_to_all | solution.py:578
  43.6 2.8 %collective-permute-start.6 = (f32[32,128]{1,0:T(8,128)S(1)}, f32[32,128]{1,0:T(8,128)S(1)}, u32[]{:S(2)}, u32[]{:S(2)}) collective-permute-start(f32[32,128]{1,0:T(8,128)S(1)} %collective-permute-done.5.y_both), channel_id=1, source_target_pairs={{8,0},{11,3},{12,4},{15,7},{112,120},{115,123},{116,124},{119,127}... | collective-permute-start | bytes 49160 | tf_op jit(solution)/shard_map/ppermute | solution.py:570
  46.4 0.8 collective-permute-done.6.relayed
  47.3 0.0 copy-start
  47.3 0.0 copy-start.1
  47.3 1.0 mend.1
  48.2 15.5 %all-to-all-done = f32[128,1,384]{2,1,0:T(1,128)S(1)} async-done(((f32[128,1,384]{2,1,0:T(1,128)}), f32[128,1,384]{2,1,0:T(1,128)S(1)}, u32[]{:S(2)}, u32[]{:S(2)}) %all-to-all-start) | async-done | bytes 196640 | tf_op jit(solution)/shard_map/all_to_all | solution.py:578
  63.7 0.0 copy-done
  63.7 0.0 copy-done.1
  63.7 0.6 solve.1
  64.3 6.9 %all_to_all.15 = f32[4,8,256]{2,1,0:T(8,128)S(1)} all-to-all(f32[4,8,256]{2,1,0:T(8,128)S(1)} %bitcast.19), channel_id=1, replica_groups={{0,1,2,3},{4,5,6,7},{8,9,10,11},{12,13,14,15},{16,17,18,19},{20,21,22,2..., dimensions={0} | all-to-all | bytes 65536 | tf_op jit(solution)/shard_map/all_to_all | solution.py:661
  71.2 0.4 back.2
  71.6 0.0 copy-start.5
  71.6 27.6 %all_to_all.16 = f32[128,1,384]{2,1,0:T(1,128)S(1)} all-to-all(f32[128,1,384]{2,1,0:T(1,128)S(1)} %bitcast.12), channel_id=1, replica_groups={{0,4,8,12,16,20,24,28,32,36,40,44,48,52,56,60,64,68,72,76,80,84,88,92,9..., dimensions={0} | all-to-all | bytes 393216 | tf_op jit(solution)/shard_map/all_to_all | solution.py:578
  99.2 0.0 copy-done.5
  99.2 1.2 %final.1 = f32[1024,128]{1,0:T(8,128)} custom-call(f32[384,128]{1,0:T(8,128)S(1)} %bitcast.13, f32[128,128]{1,0:T(8,128)S(1)} %get-tuple-element.53.middle, f32[1024,128]{1,0:T(8,128)S(1)} %get-tuple-element.54.star, f32[64,64]{1,0:T(8,128)S(1)} %copy-done.5, f32[192,128]{1,0:T(8,128)S(1)} %get-tuple-element.40.by_level), custom_call_target="tpu_custom_call" | custom-call | tf_op jit(solution)/shard_map/final/pallas_call | solution.py:520
  (3 shorter events, 0.0 us)
Async XLA Ops:
  1.4 10.4 %collective-permute-start = (f32[336,128]{1,0:T(8,128)S(1)}, f32[336,128]{1,0:T(8,128)S(1)}, u32[]{:S(2)}, u32[]{:S(2)}) collective-permute-start(f32[336,128]{1,0:T(8,128)S(1)} %get-tuple-element.31), channel_id=1, source_target_pairs={{0,8},{8,0},{16,24},{24,16},{32,40},{40,32},{48,56},{56,48},{64,72... | collective-permute-start | bytes 516104 | tf_op jit(solution)/shard_map/ppermute | solution.py:538
  10.2 1.5 %copy-start.9 = (f32[64]{0:T(128)S(1)}, f32[64]{0:T(128)}, u32[]{:S(2)}) copy-start(f32[64]{0:T(128)} %param.18) | copy-start | bytes 772
  10.2 1.5 %copy-start.7 = (f32[256]{0:T(256)S(1)}, f32[256]{0:T(256)}, u32[]{:S(2)}) copy-start(f32[256]{0:T(256)} %param.14) | copy-start | bytes 3076
  10.2 1.5 %copy-start.8 = (f32[64]{0:T(128)S(1)}, f32[64]{0:T(128)}, u32[]{:S(2)}) copy-start(f32[64]{0:T(128)} %param.12) | copy-start | bytes 772
  10.2 20.1 %collective-permute-start.4 = (f32[16,128]{1,0:T(8,128)S(1)}, f32[16,128]{1,0:T(8,128)S(1)}, u32[]{:S(2)}, u32[]{:S(2)}) collective-permute-start(f32[16,128]{1,0:T(8,128)S(1)} %get-tuple-element.33), channel_id=1, source_target_pairs={{1,2},{2,1},{5,6},{6,5},{9,10},{10,9},{13,14},{14,13},{17,18},{18,... | collective-permute-start | bytes 24584 | tf_op jit(solution)/shard_map/ppermute | solution.py:559
  11.1 19.3 %collective-permute-start.1 = (f32[320,128]{1,0:T(8,128)S(1)}, f32[320,128]{1,0:T(8,128)S(1)}, u32[]{:S(2)}, u32[]{:S(2)}) collective-permute-start(f32[320,128]{1,0:T(8,128)S(1)} %get-tuple-element.35), channel_id=1, source_target_pairs={{120,128},{128,120},{248,256},{256,248},{376,384},{384,376},{504,0... | collective-permute-start | bytes 491528 | tf_op jit(solution)/shard_map/ppermute | solution.py:548
  11.8 15.5 %copy-start.6 = (f32[8,256]{1,0:T(8,128)S(1)}, f32[8,256]{1,0:T(8,128)}, u32[]{:S(2)}) copy-start(f32[8,256]{1,0:T(8,128)} %constant.6.clone.square_row) | copy-start | bytes 24580
  11.9 17.8 %copy-start.2 = (bf16[256,256]{1,0:T(8,128)(2,1)S(1)}, bf16[256,256]{1,0:T(8,128)(2,1)}, u32[]{:S(2)}) copy-start(bf16[256,256]{1,0:T(8,128)(2,1)} %layer_in.1) | copy-start | bytes 393220
  11.9 17.8 %copy-start.4 = (bf16[256,128]{1,0:T(8,128)(2,1)S(1)}, bf16[256,128]{1,0:T(8,128)(2,1)}, u32[]{:S(2)}) copy-start(bf16[256,128]{1,0:T(8,128)(2,1)} %layer_out.1) | copy-start | bytes 196612
  11.9 20.2 %collective-permute-start.5 = (f32[32,128]{1,0:T(8,128)S(1)}, f32[32,128]{1,0:T(8,128)S(1)}, u32[]{:S(2)}, u32[]{:S(2)}) collective-permute-start(f32[32,128]{1,0:T(8,128)S(1)} %pad_maximum_fusion), channel_id=1, source_target_pairs={{11,12},{12,11},{15,8},{8,15},{115,116},{116,115},{119,112},{112,1... | collective-permute-start | bytes 49160 | tf_op jit(solution)/shard_map/ppermute | solution.py:559
  24.6 7.5 %collective-permute-start.2 = (f32[320,128]{1,0:T(8,128)S(1)}, f32[320,128]{1,0:T(8,128)S(1)}, u32[]{:S(2)}, u32[]{:S(2)}) collective-permute-start(f32[320,128]{1,0:T(8,128)S(1)} %get-tuple-element.35), channel_id=1, source_target_pairs={{8,16},{16,8},{24,32},{32,24},{40,48},{48,40},{56,64},{64,56},{72,... | collective-permute-start | bytes 491528 | tf_op jit(solution)/shard_map/ppermute | solution.py:548
  27.7 4.4 %collective-permute-start.3 = (f32[16,128]{1,0:T(8,128)S(1)}, f32[16,128]{1,0:T(8,128)S(1)}, u32[]{:S(2)}, u32[]{:S(2)}) collective-permute-start(f32[16,128]{1,0:T(8,128)S(1)} %get-tuple-element.38), channel_id=1, source_target_pairs={{0,1},{1,0},{2,3},{3,2},{4,5},{5,4},{6,7},{7,6},{8,9},{9,8},{10,11... | collective-permute-start | bytes 24584 | tf_op jit(solution)/shard_map/ppermute | solution.py:538
  29.7 2.5 %copy-start.3 = (f32[64,64]{1,0:T(8,128)S(1)}, f32[64,64]{1,0:T(8,128)}, u32[]{:S(2)}) copy-start(f32[64,64]{1,0:T(8,128)} %forward.3) | copy-start | bytes 49156
  33.5 30.3 %all-to-all-start = ((f32[128,1,384]{2,1,0:T(1,128)}), f32[128,1,384]{2,1,0:T(1,128)S(1)}, u32[]{:S(2)}, u32[]{:S(2)}) async-start(f32[128,1,384]{2,1,0:T(1,128)} %bitcast.4), calls=%async_computation | async-start | bytes 393216 | tf_op jit(solution)/shard_map/all_to_all | solution.py:578
  43.6 3.6 %collective-permute-start.6 = (f32[32,128]{1,0:T(8,128)S(1)}, f32[32,128]{1,0:T(8,128)S(1)}, u32[]{:S(2)}, u32[]{:S(2)}) collective-permute-start(f32[32,128]{1,0:T(8,128)S(1)} %collective-permute-done.5.y_both), channel_id=1, source_target_pairs={{8,0},{11,3},{12,4},{15,7},{112,120},{115,123},{116,124},{119,127}... | collective-permute-start | bytes 49160 | tf_op jit(solution)/shard_map/ppermute | solution.py:570
  47.3 16.5 %copy-start = (bf16[128,128]{1,0:T(8,128)(2,1)S(1)}, bf16[128,128]{1,0:T(8,128)(2,1)}, u32[]{:S(2)}) copy-start(bf16[128,128]{1,0:T(8,128)(2,1)} %constant.8.clone.basis_low) | copy-start | bytes 98308
  47.3 16.5 %copy-start.1 = (bf16[128,128]{1,0:T(8,128)(2,1)S(1)}, bf16[128,128]{1,0:T(8,128)(2,1)}, u32[]{:S(2)}) copy-start(bf16[128,128]{1,0:T(8,128)(2,1)} %constant.7.clone.basis_high) | copy-start | bytes 98308
  71.6 27.6 %copy-start.5 = (f32[64,64]{1,0:T(8,128)S(1)}, f32[64,64]{1,0:T(8,128)}, u32[]{:S(2)}) copy-start(f32[64,64]{1,0:T(8,128)} %back.3) | copy-start | bytes 49156

commit v10 on v9

--- a/solution.py
+++ b/solution.py
@@ -87,15 +87,15 @@
     return ((gx % 16 == 0) | (gx % 16 == 15)) & ((gy % 4 == 0) | (gy % 4 == 3))
 
 
-def edges_kernel(state_u, state_v, state_w, state_th, planes, x_even, x_odd, y_even, y_odd, flat):
+def edges_kernel(state, planes, x_even, x_odd, y_even, y_odd, flat):
     place = position()
     even_x = place[0] % 2 == 0
     even_y = place[1] % 2 == 0
-    states = (state_u, state_v, state_w, state_th)
+    size = LEVELS * ROWS
     lane = lane_of((LEVELS, LANES))
     gathered = jnp.zeros((LEVELS, LANES), F32)
     for field in range(4):
-        values = [states[field][pl.ds(x, LEVELS, stride=ROWS), :] for x in range(ROWS)]
+        values = [state[pl.ds(field * size + x, LEVELS, stride=ROWS), :] for x in range(ROWS)]
         for x in range(ROWS):
             slot = field * ROWS + x
             planes[pl.ds(slot * LEVELS, LEVELS), :] = values[x]
@@ -468,18 +468,22 @@
 
 def final_kernel(received, middle, star, back, by_level, out, held, sent_out):
     size = LEVELS * ROWS
-    span = lambda f: pl.ds(f * size, size)
-    copies = [pltpu.make_async_copy(held.at[span(f), :], out.at[span(f), :], sent_out.at[f]) for f in range(4)]
-
-    def put(f, changes):
-        for x in range(ROWS):
-            value = star[pl.ds((f * ROWS + x) * LEVELS, LEVELS), :]
-            if changes is not None:
-                value = value - changes[:, x * LANES : (x + 1) * LANES]
-            held[pl.ds(f * size + x, LEVELS, stride=ROWS), :] = value
-        copies[f].start()
-
-    put(3, None)
+    span = lambda i: pl.ds(i * size // 2, size // 2)
+    copies = [pltpu.make_async_copy(held.at[span(i), :], out.at[span(i), :], sent_out.at[i]) for i in range(8)]
+    some = LEVELS // 2
+
+    def put(f, matrix, right):
+        for half in range(2):
+            if right is not None:
+                changes = dot3(parts(matrix[half * some : (half + 1) * some]), right)
+            for x in range(ROWS):
+                value = star[pl.ds((f * ROWS + x) * LEVELS + half * some, some), :]
+                if right is not None:
+                    value = value - changes[:, x * LANES : (x + 1) * LANES]
+                held[pl.ds(f * size + half * some * ROWS + x, some, stride=ROWS), :] = value
+            copies[2 * f + half].start()
+
+    put(3, None, None)
     lane = lane_of((LEVELS, LANES))
     row_at = lambda ref, r: ref[pl.ds(3 * (r % 2) + r // 2, LEVELS, stride=6), :]
     p = [row_at(received, r) for r in range(ROWS)]
@@ -507,10 +511,9 @@
     padded = [before] + p + [after]
     matrix = back[...]
     joined = lambda values: parts(jnp.concatenate(values, axis=1))
-    put(2, dot3(parts(0.5 * level_difference(matrix)), joined(p)))
-    matrix = parts(matrix)
-    put(1, dot3(matrix, joined([0.5 * north_difference(p[x], low[x], high[x]) for x in range(ROWS)])))
-    put(0, dot3(matrix, joined([0.5 * (padded[x + 2] - padded[x]) for x in range(ROWS)])))
+    put(2, 0.5 * level_difference(matrix), joined(p))
+    put(1, matrix, joined([0.5 * north_difference(p[x], low[x], high[x]) for x in range(ROWS)]))
+    put(0, matrix, joined([0.5 * (padded[x + 2] - padded[x]) for x in range(ROWS)]))
     for copy in copies:
         copy.wait()
 
@@ -586,7 +589,7 @@
 ):
     blocks = lax.axis_size("gx")
     total_east = blocks * ROWS
-    state = [model_state[f].reshape(LEVELS * ROWS, LANES) for f in range(4)]
+    state = model_state.reshape(4 * LEVELS * ROWS, LANES)
     basis, square = east_tables(total_east // 2, blocks)
     basis_high, basis_low = split_table(np.ascontiguousarray(basis.T))
     square_row = np.ascontiguousarray(np.broadcast_to(np.concatenate([square, square]), (8, total_east)))
@@ -594,7 +597,7 @@
     planes, x_even, x_odd, y_even, y_odd = call(
         edges_kernel,
         [(16 * LEVELS, LANES), (5 * LEVELS + 16, LANES), (5 * LEVELS, LANES), (16, LANES), (16, LANES)],
-        [*state],
+        [state],
         "edges",
         scratch=[(LANES, LANES)],
     )
@@ -679,7 +682,7 @@
         [pressure, middle, whole, mode_back, by_level],
         "final",
         scratch=[(4 * LEVELS * ROWS, LANES)],
-        copies=4,
+        copies=8,
     )
     return out.reshape(model_state.shape)
 

time: 101 us -> 101 us (level)
    slice x1 -> x0, local copies, waits for them, and re-layouts: 1.13 us -> none  [on_device(): state = [model_state[f].reshape(LEVELS * ROWS, LANES) for f in range(4)]]
    unnamed x20 -> x22, local copies, waits for them, and re-layouts: 0.06 us -> 1.1 us
where the time goes in v10:
time: 101 us; the launch traced here: 100 us
  starting transfers between devices  40.6 us (40%)
  blocking collectives  34.5 us (34%)
  waiting for transfers between devices  18.1 us (18%)
  Pallas kernels  5.75 us (6%)
  local copies, waits for them, and re-layouts  1.11 us (1%)
    all_to_all x1, blocking collectives, exchange(): lax.all_to_all(shaped, ('gx', 'gy'), 0, 0, tiled=True, axis_index_groups=...  27.6 us
    all_to_all x1, waiting for transfers between devices, exchange(): lax.all_to_all(shaped, ('gx', 'gy'), 0, 0, tiled=True, axis_index_groups=...  15.5 us
    ppermute x2, starting transfers between devices, swap_odd_y(): return lax.ppermute(values, ('gx', 'gy'), pairs)  13.4 us
    ppermute x2, starting transfers between devices, swap(): return lax.ppermute(values, axis, pairs)  10.7 us
    all_to_all x1, starting transfers between devices, exchange(): lax.all_to_all(shaped, ('gx', 'gy'), 0, 0, tiled=True, axis_index_groups=...  10.2 us
    all_to_all x1, blocking collectives, on_device(): lax.all_to_all(moments.reshape(4, 8, total_east), 'gy', 0, 0, tiled=True,...  6.91 us
    pallas_call x8, Pallas kernels, call(): pl.pallas_call(kernel, out_shape=[jax.ShapeDtypeStruct(s, F32) for s in s...  5.75 us
    ppermute x2, starting transfers between devices, swap_odd_x(): return lax.ppermute(values, 'gx', pairs)  3.5 us
  transfers between devices with their start and end apart: 8, of which 3 were waited for; matrix products, arithmetic and copies ran while one was open for 0% of the time, Pallas kernels for 2%

profile of v10, /device:TPU:1, one launch (start us, length us, event | category | flops | bytes accessed | tf_op | source)
XLA Modules:
  0.0 100.3 jit_solution(12914004014828093482)
XLA Ops:
  0.0 0.0 copy-start
  0.0 1.0 %copy-done = f32[4,64,4,128]{3,2,1,0:T(4,128)S(1)} copy-done((f32[4,64,4,128]{3,2,1,0:T(4,128)S(1)}, f32[4,64,4,128]{3,2,1,0:T(4,128)}, u32[]{:S(2)}) %copy-start) | copy-done | bytes 524312
  1.0 0.3 edges.1
  1.3 8.8 %collective-permute-start = (f32[336,128]{1,0:T(8,128)S(1)}, f32[336,128]{1,0:T(8,128)S(1)}, u32[]{:S(2)}, u32[]{:S(2)}) collective-permute-start(f32[336,128]{1,0:T(8,128)S(1)} %get-tuple-element.31), channel_id=1, source_target_pairs={{0,8},{8,0},{16,24},{24,16},{32,40},{40,32},{48,56},{56,48},{64,72... | collective-permute-start | bytes 516104 | tf_op jit(solution)/shard_map/ppermute | solution.py:541
  10.1 0.0 copy-start.10
  10.1 0.0 copy-start.8
  10.1 0.0 copy-start.9
  10.2 0.8 collective-permute-start.4
  11.0 0.7 collective-permute-start.1
  11.6 0.0 copy-done.10
  11.6 0.0 copy-done.8
  11.7 0.0 copy-done.9
  11.7 0.1 pad_maximum_fusion.1
  11.7 0.0 collective-permute-done.x_even
  11.8 0.0 copy-start.7
  11.8 0.0 copy-start.3
  11.8 0.0 copy-start.5
  11.8 12.7 %collective-permute-start.5 = (f32[32,128]{1,0:T(8,128)S(1)}, f32[32,128]{1,0:T(8,128)S(1)}, u32[]{:S(2)}, u32[]{:S(2)}) collective-permute-start(f32[32,128]{1,0:T(8,128)S(1)} %pad_maximum_fusion), channel_id=1, source_target_pairs={{11,12},{12,11},{15,8},{8,15},{115,116},{116,115},{119,112},{112,1... | collective-permute-start | bytes 49160 | tf_op jit(solution)/shard_map/ppermute | solution.py:562
  24.5 2.8 %collective-permute-start.2 = (f32[320,128]{1,0:T(8,128)S(1)}, f32[320,128]{1,0:T(8,128)S(1)}, u32[]{:S(2)}, u32[]{:S(2)}) collective-permute-start(f32[320,128]{1,0:T(8,128)S(1)} %get-tuple-element.35), channel_id=1, source_target_pairs={{8,16},{16,8},{24,32},{32,24},{40,48},{48,40},{56,64},{64,56},{72,... | collective-permute-start | bytes 491528 | tf_op jit(solution)/shard_map/ppermute | solution.py:551
  27.3 0.0 copy-done.7
  27.3 0.3 tables.1
  27.6 1.9 %collective-permute-start.3 = (f32[16,128]{1,0:T(8,128)S(1)}, f32[16,128]{1,0:T(8,128)S(1)}, u32[]{:S(2)}, u32[]{:S(2)}) collective-permute-start(f32[16,128]{1,0:T(8,128)S(1)} %get-tuple-element.38), channel_id=1, source_target_pairs={{0,1},{1,0},{2,3},{3,2},{4,5},{5,4},{6,7},{7,6},{8,9},{9,8},{10,11... | collective-permute-start | bytes 24584 | tf_op jit(solution)/shard_map/ppermute | solution.py:541
  29.5 0.0 copy-done.3
  29.5 0.0 copy-done.5
  29.6 0.0 copy-start.4
  29.6 0.7 inner.1
  30.2 0.0 collective-permute-done.4.y_odd
  30.3 0.0 collective-permute-done.1.x_far
  30.3 1.7 %collective-permute-done.3.y_even = f32[16,128]{1,0:T(8,128)S(1)} collective-permute-done((f32[16,128]{1,0:T(8,128)S(1)}, f32[16,128]{1,0:T(8,128)S(1)}, u32[]{:S(2)}, u32[]{:S(2)}) %collective-permute-start.3) | collective-permute-done | bytes 8224 | tf_op jit(solution)/shard_map/ppermute | solution.py:541
  32.0 0.0 collective-permute-done.5.y_both
  32.0 0.0 collective-permute-done.2.x_near
  32.0 0.0 copy-done.4
  32.0 1.3 %outer.1 = (f32[1024,128]{1,0:T(8,128)S(1)}, f32[384,128]{1,0:T(8,128)}) custom-call(f32[1024,128]{1,0:T(8,128)S(1)} %get-tuple-element.30.state, f32[1024,128]{1,0:T(8,128)S(1)} %inner.1, f32[336,128]{1,0:T(8,128)S(1)} %collective-permute-done.x_even, f32[320,128]{1,0:T(8,128)S(1)} %collective-permute-done.1.x_far, ...), custom_call_target="tpu_custom_call" | custom-call | tf_op jit(solution)/shard_map/outer/pallas_call | solution.py:523
  33.4 10.2 %all-to-all-start = ((f32[128,1,384]{2,1,0:T(1,128)}), f32[128,1,384]{2,1,0:T(1,128)S(1)}, u32[]{:S(2)}, u32[]{:S(2)}) async-start(f32[128,1,384]{2,1,0:T(1,128)} %bitcast.1), calls=%async_computation | async-start | bytes 393216 | tf_op jit(solution)/shard_map/all_to_all | solution.py:581
  43.5 2.8 %collective-permute-start.6 = (f32[32,128]{1,0:T(8,128)S(1)}, f32[32,128]{1,0:T(8,128)S(1)}, u32[]{:S(2)}, u32[]{:S(2)}) collective-permute-start(f32[32,128]{1,0:T(8,128)S(1)} %collective-permute-done.5.y_both), channel_id=1, source_target_pairs={{8,0},{11,3},{12,4},{15,7},{112,120},{115,123},{116,124},{119,127}... | collective-permute-start | bytes 49160 | tf_op jit(solution)/shard_map/ppermute | solution.py:573
  46.3 0.8 collective-permute-done.6.relayed
  47.2 0.0 copy-start.1
  47.2 0.0 copy-start.2
  47.2 1.0 mend.1
  48.1 15.5 %all-to-all-done = f32[128,1,384]{2,1,0:T(1,128)S(1)} async-done(((f32[128,1,384]{2,1,0:T(1,128)}), f32[128,1,384]{2,1,0:T(1,128)S(1)}, u32[]{:S(2)}, u32[]{:S(2)}) %all-to-all-start) | async-done | bytes 196640 | tf_op jit(solution)/shard_map/all_to_all | solution.py:581
  63.6 0.0 copy-done.1
  63.6 0.0 copy-done.2
  63.6 0.6 solve.1
  64.2 6.9 %all_to_all.15 = f32[4,8,256]{2,1,0:T(8,128)S(1)} all-to-all(f32[4,8,256]{2,1,0:T(8,128)S(1)} %bitcast.13), channel_id=1, replica_groups={{0,1,2,3},{4,5,6,7},{8,9,10,11},{12,13,14,15},{16,17,18,19},{20,21,22,2..., dimensions={0} | all-to-all | bytes 65536 | tf_op jit(solution)/shard_map/all_to_all | solution.py:664
  71.2 0.4 back.2
  71.5 0.0 copy-start.6
  71.5 27.6 %all_to_all.16 = f32[128,1,384]{2,1,0:T(1,128)S(1)} all-to-all(f32[128,1,384]{2,1,0:T(1,128)S(1)} %bitcast.9), channel_id=1, replica_groups={{0,4,8,12,16,20,24,28,32,36,40,44,48,52,56,60,64,68,72,76,80,84,88,92,9..., dimensions={0} | all-to-all | bytes 393216 | tf_op jit(solution)/shard_map/all_to_all | solution.py:581
  99.1 0.0 copy-done.6
  99.1 1.2 %final.1 = f32[1024,128]{1,0:T(8,128)} custom-call(f32[384,128]{1,0:T(8,128)S(1)} %bitcast.10, f32[128,128]{1,0:T(8,128)S(1)} %get-tuple-element.53.middle, f32[1024,128]{1,0:T(8,128)S(1)} %get-tuple-element.54.star, f32[64,64]{1,0:T(8,128)S(1)} %copy-done.6, f32[192,128]{1,0:T(8,128)S(1)} %get-tuple-element.40.by_level), custom_call_target="tpu_custom_call" | custom-call | tf_op jit(solution)/shard_map/final/pallas_call | solution.py:523
  (3 shorter events, 0.0 us)
Async XLA Ops:
  0.0 1.0 %copy-start = (f32[4,64,4,128]{3,2,1,0:T(4,128)S(1)}, f32[4,64,4,128]{3,2,1,0:T(4,128)}, u32[]{:S(2)}) copy-start(f32[4,64,4,128]{3,2,1,0:T(4,128)} %param.11) | copy-start | bytes 1572868
  1.3 10.4 %collective-permute-start = (f32[336,128]{1,0:T(8,128)S(1)}, f32[336,128]{1,0:T(8,128)S(1)}, u32[]{:S(2)}, u32[]{:S(2)}) collective-permute-start(f32[336,128]{1,0:T(8,128)S(1)} %get-tuple-element.31), channel_id=1, source_target_pairs={{0,8},{8,0},{16,24},{24,16},{32,40},{40,32},{48,56},{56,48},{64,72... | collective-permute-start | bytes 516104 | tf_op jit(solution)/shard_map/ppermute | solution.py:541
  10.1 1.5 %copy-start.10 = (f32[64]{0:T(128)S(1)}, f32[64]{0:T(128)}, u32[]{:S(2)}) copy-start(f32[64]{0:T(128)} %param.18) | copy-start | bytes 772
  10.1 1.5 %copy-start.8 = (f32[256]{0:T(256)S(1)}, f32[256]{0:T(256)}, u32[]{:S(2)}) copy-start(f32[256]{0:T(256)} %param.14) | copy-start | bytes 3076
  10.1 1.5 %copy-start.9 = (f32[64]{0:T(128)S(1)}, f32[64]{0:T(128)}, u32[]{:S(2)}) copy-start(f32[64]{0:T(128)} %param.12) | copy-start | bytes 772
  10.2 20.1 %collective-permute-start.4 = (f32[16,128]{1,0:T(8,128)S(1)}, f32[16,128]{1,0:T(8,128)S(1)}, u32[]{:S(2)}, u32[]{:S(2)}) collective-permute-start(f32[16,128]{1,0:T(8,128)S(1)} %get-tuple-element.33), channel_id=1, source_target_pairs={{1,2},{2,1},{5,6},{6,5},{9,10},{10,9},{13,14},{14,13},{17,18},{18,... | collective-permute-start | bytes 24584 | tf_op jit(solution)/shard_map/ppermute | solution.py:562
  11.0 19.3 %collective-permute-start.1 = (f32[320,128]{1,0:T(8,128)S(1)}, f32[320,128]{1,0:T(8,128)S(1)}, u32[]{:S(2)}, u32[]{:S(2)}) collective-permute-start(f32[320,128]{1,0:T(8,128)S(1)} %get-tuple-element.35), channel_id=1, source_target_pairs={{120,128},{128,120},{248,256},{256,248},{376,384},{384,376},{504,0... | collective-permute-start | bytes 491528 | tf_op jit(solution)/shard_map/ppermute | solution.py:551
  11.8 15.5 %copy-start.7 = (f32[8,256]{1,0:T(8,128)S(1)}, f32[8,256]{1,0:T(8,128)}, u32[]{:S(2)}) copy-start(f32[8,256]{1,0:T(8,128)} %constant.6.clone.square_row) | copy-start | bytes 24580
  11.8 17.8 %copy-start.3 = (bf16[256,256]{1,0:T(8,128)(2,1)S(1)}, bf16[256,256]{1,0:T(8,128)(2,1)}, u32[]{:S(2)}) copy-start(bf16[256,256]{1,0:T(8,128)(2,1)} %layer_in.1) | copy-start | bytes 393220
  11.8 17.8 %copy-start.5 = (bf16[256,128]{1,0:T(8,128)(2,1)S(1)}, bf16[256,128]{1,0:T(8,128)(2,1)}, u32[]{:S(2)}) copy-start(bf16[256,128]{1,0:T(8,128)(2,1)} %layer_out.1) | copy-start | bytes 196612
  11.8 20.2 %collective-permute-start.5 = (f32[32,128]{1,0:T(8,128)S(1)}, f32[32,128]{1,0:T(8,128)S(1)}, u32[]{:S(2)}, u32[]{:S(2)}) collective-permute-start(f32[32,128]{1,0:T(8,128)S(1)} %pad_maximum_fusion), channel_id=1, source_target_pairs={{11,12},{12,11},{15,8},{8,15},{115,116},{116,115},{119,112},{112,1... | collective-permute-start | bytes 49160 | tf_op jit(solution)/shard_map/ppermute | solution.py:562
  24.5 7.5 %collective-permute-start.2 = (f32[320,128]{1,0:T(8,128)S(1)}, f32[320,128]{1,0:T(8,128)S(1)}, u32[]{:S(2)}, u32[]{:S(2)}) collective-permute-start(f32[320,128]{1,0:T(8,128)S(1)} %get-tuple-element.35), channel_id=1, source_target_pairs={{8,16},{16,8},{24,32},{32,24},{40,48},{48,40},{56,64},{64,56},{72,... | collective-permute-start | bytes 491528 | tf_op jit(solution)/shard_map/ppermute | solution.py:551
  27.6 4.4 %collective-permute-start.3 = (f32[16,128]{1,0:T(8,128)S(1)}, f32[16,128]{1,0:T(8,128)S(1)}, u32[]{:S(2)}, u32[]{:S(2)}) collective-permute-start(f32[16,128]{1,0:T(8,128)S(1)} %get-tuple-element.38), channel_id=1, source_target_pairs={{0,1},{1,0},{2,3},{3,2},{4,5},{5,4},{6,7},{7,6},{8,9},{9,8},{10,11... | collective-permute-start | bytes 24584 | tf_op jit(solution)/shard_map/ppermute | solution.py:541
  29.6 2.5 %copy-start.4 = (f32[64,64]{1,0:T(8,128)S(1)}, f32[64,64]{1,0:T(8,128)}, u32[]{:S(2)}) copy-start(f32[64,64]{1,0:T(8,128)} %forward.3) | copy-start | bytes 49156
  33.4 30.3 %all-to-all-start = ((f32[128,1,384]{2,1,0:T(1,128)}), f32[128,1,384]{2,1,0:T(1,128)S(1)}, u32[]{:S(2)}, u32[]{:S(2)}) async-start(f32[128,1,384]{2,1,0:T(1,128)} %bitcast.1), calls=%async_computation | async-start | bytes 393216 | tf_op jit(solution)/shard_map/all_to_all | solution.py:581
  43.5 3.6 %collective-permute-start.6 = (f32[32,128]{1,0:T(8,128)S(1)}, f32[32,128]{1,0:T(8,128)S(1)}, u32[]{:S(2)}, u32[]{:S(2)}) collective-permute-start(f32[32,128]{1,0:T(8,128)S(1)} %collective-permute-done.5.y_both), channel_id=1, source_target_pairs={{8,0},{11,3},{12,4},{15,7},{112,120},{115,123},{116,124},{119,127}... | collective-permute-start | bytes 49160 | tf_op jit(solution)/shard_map/ppermute | solution.py:573
  47.2 16.5 %copy-start.1 = (bf16[128,128]{1,0:T(8,128)(2,1)S(1)}, bf16[128,128]{1,0:T(8,128)(2,1)}, u32[]{:S(2)}) copy-start(bf16[128,128]{1,0:T(8,128)(2,1)} %constant.8.clone.basis_low) | copy-start | bytes 98308
  47.2 16.5 %copy-start.2 = (bf16[128,128]{1,0:T(8,128)(2,1)S(1)}, bf16[128,128]{1,0:T(8,128)(2,1)}, u32[]{:S(2)}) copy-start(bf16[128,128]{1,0:T(8,128)(2,1)} %constant.7.clone.basis_high) | copy-start | bytes 98308
  71.5 27.6 %copy-start.6 = (f32[64,64]{1,0:T(8,128)S(1)}, f32[64,64]{1,0:T(8,128)}, u32[]{:S(2)}) copy-start(f32[64,64]{1,0:T(8,128)} %back.3) | copy-start | bytes 49156

commit v11 on v10

--- a/solution.py
+++ b/solution.py
@@ -385,11 +385,10 @@
         rho * ahead[LANES - 1 :] + r65 * low,
         rho * behind[0:1] + r65 * high,
         rho * behind[1:2] + low,
-        jnp.zeros((4, source.shape[1]), F32),
     ]
     across = jnp.concatenate(across, axis=0)
     for j in range(4):
-        moments[pl.ds(j * 8, 8), :] = across
+        moments[pl.ds(j * 4, 4), :] = across
 
 
 def back_kernel(local, moments, basis_high, basis_low, by_row, by_wave, by_block, message):
@@ -398,12 +397,13 @@
     blocks = basis_high.shape[0] // 2
     even = place[1] < 4
     mine = place[1] & 3
-    carry = jnp.zeros((8, width), F32)
+    carry = jnp.zeros((4, width), F32)
+    own = jnp.zeros((4, width), F32)
     for j in range(4):
-        theirs = moments[pl.ds(j * 8, 8), :]
+        theirs = moments[pl.ds(j * 4, 4), :]
+        own = jnp.where(mine == j, theirs, own)
         swapped = jnp.concatenate([theirs[:, LANES:], theirs[:, :LANES]], axis=1)
-        carry = carry + by_block[pl.ds(16 * j, 8), :] * theirs + by_block[pl.ds(16 * j + 8, 8), :] * swapped
-    own = moments[pl.ds(pl.multiple_of(mine * 8, 8), 8), :]
+        carry = carry + by_block[pl.ds(16 * j, 4), :] * theirs + by_block[pl.ds(16 * j + 8, 4), :] * swapped
     scale, by_r64, by_inverse = (by_block[pl.ds(64 + i, 1), :] for i in range(3))
     after = scale * own[0:1] + by_r64 * carry[0:1] + by_inverse * carry[2:3]
     before = scale * own[3:4] + by_r64 * carry[3:4] + by_inverse * carry[1:2]
@@ -657,18 +657,18 @@
     modal, whole, middle = lax.optimization_barrier((modal, whole, middle))
     local, moments = call(
         solve_kernel,
-        [(LANES, total_east), (32, total_east)],
+        [(LANES, total_east), (16, total_east)],
         [modal, basis_high, basis_low, by_row, by_wave],
         "solve",
     )
     moments = lax.all_to_all(
-        moments.reshape(4, 8, total_east),
+        moments.reshape(4, 4, total_east),
         "gy",
         0,
         0,
         tiled=True,
         axis_index_groups=[[0, 1, 2, 3], [4, 5, 6, 7]],
-    ).reshape(32, total_east)
+    ).reshape(16, total_east)
     (reply,) = call(
         back_kernel,
         [(blocks * 6, LANES)],

time: 101 us -> 101 us (level)
  no operation moved by 1% of the time
where the time goes in v11:
time: 101 us; the launch traced here: 100 us
  starting transfers between devices  40.6 us (40%)
  blocking collectives  34.4 us (34%)
  waiting for transfers between devices  18.1 us (18%)
  Pallas kernels  5.75 us (6%)
  local copies, waits for them, and re-layouts  1.13 us (1%)
    all_to_all x1, blocking collectives, exchange(): lax.all_to_all(shaped, ('gx', 'gy'), 0, 0, tiled=True, axis_index_groups=...  27.6 us
    all_to_all x1, waiting for transfers between devices, exchange(): lax.all_to_all(shaped, ('gx', 'gy'), 0, 0, tiled=True, axis_index_groups=...  15.5 us
    ppermute x2, starting transfers between devices, swap_odd_y(): return lax.ppermute(values, ('gx', 'gy'), pairs)  13.4 us
    ppermute x2, starting transfers between devices, swap(): return lax.ppermute(values, axis, pairs)  10.7 us
    all_to_all x1, starting transfers between devices, exchange(): lax.all_to_all(shaped, ('gx', 'gy'), 0, 0, tiled=True, axis_index_groups=...  10.2 us
    all_to_all x1, blocking collectives, on_device(): lax.all_to_all(moments.reshape(4, 4, total_east), 'gy', 0, 0, tiled=True,...  6.82 us
    pallas_call x8, Pallas kernels, call(): pl.pallas_call(kernel, out_shape=[jax.ShapeDtypeStruct(s, F32) for s in s...  5.75 us
    ppermute x2, starting transfers between devices, swap_odd_x(): return lax.ppermute(values, 'gx', pairs)  3.5 us
  transfers between devices with their start and end apart: 8, of which 3 were waited for; matrix products, arithmetic and copies ran while one was open for 0% of the time, Pallas kernels for 2%

profile of v11, /device:TPU:1, one launch (start us, length us, event | category | flops | bytes accessed | tf_op | source)
XLA Modules:
  0.0 100.3 jit_solution(16795099123768066512)
XLA Ops:
  0.0 0.0 copy-start
  0.0 1.0 %copy-done = f32[4,64,4,128]{3,2,1,0:T(4,128)S(1)} copy-done((f32[4,64,4,128]{3,2,1,0:T(4,128)S(1)}, f32[4,64,4,128]{3,2,1,0:T(4,128)}, u32[]{:S(2)}) %copy-start) | copy-done | bytes 524312
  1.0 0.3 edges.1
  1.3 8.8 %collective-permute-start = (f32[336,128]{1,0:T(8,128)S(1)}, f32[336,128]{1,0:T(8,128)S(1)}, u32[]{:S(2)}, u32[]{:S(2)}) collective-permute-start(f32[336,128]{1,0:T(8,128)S(1)} %get-tuple-element.31), channel_id=1, source_target_pairs={{0,8},{8,0},{16,24},{24,16},{32,40},{40,32},{48,56},{56,48},{64,72... | collective-permute-start | bytes 516104 | tf_op jit(solution)/shard_map/ppermute | solution.py:541
  10.1 0.0 copy-start.10
  10.1 0.0 copy-start.8
  10.1 0.0 copy-start.9
  10.2 0.8 collective-permute-start.4
  11.0 0.7 collective-permute-start.1
  11.6 0.0 copy-done.10
  11.6 0.0 copy-done.8
  11.7 0.0 copy-done.9
  11.7 0.1 pad_maximum_fusion.1
  11.7 0.0 collective-permute-done.x_even
  11.8 0.0 copy-start.7
  11.8 0.0 copy-start.3
  11.8 0.0 copy-start.5
  11.8 12.7 %collective-permute-start.5 = (f32[32,128]{1,0:T(8,128)S(1)}, f32[32,128]{1,0:T(8,128)S(1)}, u32[]{:S(2)}, u32[]{:S(2)}) collective-permute-start(f32[32,128]{1,0:T(8,128)S(1)} %pad_maximum_fusion), channel_id=1, source_target_pairs={{11,12},{12,11},{15,8},{8,15},{115,116},{116,115},{119,112},{112,1... | collective-permute-start | bytes 49160 | tf_op jit(solution)/shard_map/ppermute | solution.py:562
  24.5 2.8 %collective-permute-start.2 = (f32[320,128]{1,0:T(8,128)S(1)}, f32[320,128]{1,0:T(8,128)S(1)}, u32[]{:S(2)}, u32[]{:S(2)}) collective-permute-start(f32[320,128]{1,0:T(8,128)S(1)} %get-tuple-element.35), channel_id=1, source_target_pairs={{8,16},{16,8},{24,32},{32,24},{40,48},{48,40},{56,64},{64,56},{72,... | collective-permute-start | bytes 491528 | tf_op jit(solution)/shard_map/ppermute | solution.py:551
  27.3 0.0 copy-done.7
  27.3 0.3 tables.1
  27.6 1.9 %collective-permute-start.3 = (f32[16,128]{1,0:T(8,128)S(1)}, f32[16,128]{1,0:T(8,128)S(1)}, u32[]{:S(2)}, u32[]{:S(2)}) collective-permute-start(f32[16,128]{1,0:T(8,128)S(1)} %get-tuple-element.38), channel_id=1, source_target_pairs={{0,1},{1,0},{2,3},{3,2},{4,5},{5,4},{6,7},{7,6},{8,9},{9,8},{10,11... | collective-permute-start | bytes 24584 | tf_op jit(solution)/shard_map/ppermute | solution.py:541
  29.5 0.0 copy-done.3
  29.5 0.0 copy-done.5
  29.6 0.0 copy-start.4
  29.6 0.7 inner.1
  30.2 0.0 collective-permute-done.4.y_odd
  30.3 0.0 collective-permute-done.1.x_far
  30.3 1.7 %collective-permute-done.3.y_even = f32[16,128]{1,0:T(8,128)S(1)} collective-permute-done((f32[16,128]{1,0:T(8,128)S(1)}, f32[16,128]{1,0:T(8,128)S(1)}, u32[]{:S(2)}, u32[]{:S(2)}) %collective-permute-start.3) | collective-permute-done | bytes 8224 | tf_op jit(solution)/shard_map/ppermute | solution.py:541
  32.0 0.0 collective-permute-done.5.y_both
  32.0 0.0 collective-permute-done.2.x_near
  32.0 0.0 copy-done.4
  32.0 1.3 %outer.1 = (f32[1024,128]{1,0:T(8,128)S(1)}, f32[384,128]{1,0:T(8,128)}) custom-call(f32[1024,128]{1,0:T(8,128)S(1)} %get-tuple-element.30.state, f32[1024,128]{1,0:T(8,128)S(1)} %inner.1, f32[336,128]{1,0:T(8,128)S(1)} %collective-permute-done.x_even, f32[320,128]{1,0:T(8,128)S(1)} %collective-permute-done.1.x_far, ...), custom_call_target="tpu_custom_call" | custom-call | tf_op jit(solution)/shard_map/outer/pallas_call | solution.py:523
  33.4 10.2 %all-to-all-start = ((f32[128,1,384]{2,1,0:T(1,128)}), f32[128,1,384]{2,1,0:T(1,128)S(1)}, u32[]{:S(2)}, u32[]{:S(2)}) async-start(f32[128,1,384]{2,1,0:T(1,128)} %bitcast.1), calls=%async_computation | async-start | bytes 393216 | tf_op jit(solution)/shard_map/all_to_all | solution.py:581
  43.5 2.8 %collective-permute-start.6 = (f32[32,128]{1,0:T(8,128)S(1)}, f32[32,128]{1,0:T(8,128)S(1)}, u32[]{:S(2)}, u32[]{:S(2)}) collective-permute-start(f32[32,128]{1,0:T(8,128)S(1)} %collective-permute-done.5.y_both), channel_id=1, source_target_pairs={{8,0},{11,3},{12,4},{15,7},{112,120},{115,123},{116,124},{119,127}... | collective-permute-start | bytes 49160 | tf_op jit(solution)/shard_map/ppermute | solution.py:573
  46.3 0.8 collective-permute-done.6.relayed
  47.2 0.0 copy-start.1
  47.2 0.0 copy-start.2
  47.2 1.0 mend.1
  48.1 15.5 %all-to-all-done = f32[128,1,384]{2,1,0:T(1,128)S(1)} async-done(((f32[128,1,384]{2,1,0:T(1,128)}), f32[128,1,384]{2,1,0:T(1,128)S(1)}, u32[]{:S(2)}, u32[]{:S(2)}) %all-to-all-start) | async-done | bytes 196640 | tf_op jit(solution)/shard_map/all_to_all | solution.py:581
  63.6 0.0 copy-done.1
  63.6 0.0 copy-done.2
  63.6 0.6 solve.1
  64.3 6.8 %all_to_all.15 = f32[4,4,256]{2,1,0:T(4,128)S(1)} all-to-all(f32[4,4,256]{2,1,0:T(4,128)S(1)} %reshape.27), channel_id=1, replica_groups={{0,1,2,3},{4,5,6,7},{8,9,10,11},{12,13,14,15},{16,17,18,19},{20,21,22,2..., dimensions={0} | all-to-all | bytes 32768 | tf_op jit(solution)/shard_map/all_to_all | solution.py:664
  71.1 0.4 back.2
  71.5 0.0 copy-start.6
  71.5 27.6 %all_to_all.16 = f32[128,1,384]{2,1,0:T(1,128)S(1)} all-to-all(f32[128,1,384]{2,1,0:T(1,128)S(1)} %bitcast.7), channel_id=1, replica_groups={{0,4,8,12,16,20,24,28,32,36,40,44,48,52,56,60,64,68,72,76,80,84,88,92,9..., dimensions={0} | all-to-all | bytes 393216 | tf_op jit(solution)/shard_map/all_to_all | solution.py:581
  99.1 0.0 copy-done.6
  99.1 1.2 %final.1 = f32[1024,128]{1,0:T(8,128)} custom-call(f32[384,128]{1,0:T(8,128)S(1)} %bitcast.8, f32[128,128]{1,0:T(8,128)S(1)} %get-tuple-element.53.middle, f32[1024,128]{1,0:T(8,128)S(1)} %get-tuple-element.54.star, f32[64,64]{1,0:T(8,128)S(1)} %copy-done.6, f32[192,128]{1,0:T(8,128)S(1)} %get-tuple-element.40.by_level), custom_call_target="tpu_custom_call" | custom-call | tf_op jit(solution)/shard_map/final/pallas_call | solution.py:523
  (5 shorter events, 0.0 us)
Async XLA Ops:
  0.0 1.0 %copy-start = (f32[4,64,4,128]{3,2,1,0:T(4,128)S(1)}, f32[4,64,4,128]{3,2,1,0:T(4,128)}, u32[]{:S(2)}) copy-start(f32[4,64,4,128]{3,2,1,0:T(4,128)} %param.11) | copy-start | bytes 1572868
  1.3 10.4 %collective-permute-start = (f32[336,128]{1,0:T(8,128)S(1)}, f32[336,128]{1,0:T(8,128)S(1)}, u32[]{:S(2)}, u32[]{:S(2)}) collective-permute-start(f32[336,128]{1,0:T(8,128)S(1)} %get-tuple-element.31), channel_id=1, source_target_pairs={{0,8},{8,0},{16,24},{24,16},{32,40},{40,32},{48,56},{56,48},{64,72... | collective-permute-start | bytes 516104 | tf_op jit(solution)/shard_map/ppermute | solution.py:541
  10.1 1.5 %copy-start.10 = (f32[64]{0:T(128)S(1)}, f32[64]{0:T(128)}, u32[]{:S(2)}) copy-start(f32[64]{0:T(128)} %param.18) | copy-start | bytes 772
  10.1 1.5 %copy-start.8 = (f32[256]{0:T(256)S(1)}, f32[256]{0:T(256)}, u32[]{:S(2)}) copy-start(f32[256]{0:T(256)} %param.14) | copy-start | bytes 3076
  10.1 1.5 %copy-start.9 = (f32[64]{0:T(128)S(1)}, f32[64]{0:T(128)}, u32[]{:S(2)}) copy-start(f32[64]{0:T(128)} %param.12) | copy-start | bytes 772
  10.2 20.1 %collective-permute-start.4 = (f32[16,128]{1,0:T(8,128)S(1)}, f32[16,128]{1,0:T(8,128)S(1)}, u32[]{:S(2)}, u32[]{:S(2)}) collective-permute-start(f32[16,128]{1,0:T(8,128)S(1)} %get-tuple-element.33), channel_id=1, source_target_pairs={{1,2},{2,1},{5,6},{6,5},{9,10},{10,9},{13,14},{14,13},{17,18},{18,... | collective-permute-start | bytes 24584 | tf_op jit(solution)/shard_map/ppermute | solution.py:562
  11.0 19.3 %collective-permute-start.1 = (f32[320,128]{1,0:T(8,128)S(1)}, f32[320,128]{1,0:T(8,128)S(1)}, u32[]{:S(2)}, u32[]{:S(2)}) collective-permute-start(f32[320,128]{1,0:T(8,128)S(1)} %get-tuple-element.35), channel_id=1, source_target_pairs={{120,128},{128,120},{248,256},{256,248},{376,384},{384,376},{504,0... | collective-permute-start | bytes 491528 | tf_op jit(solution)/shard_map/ppermute | solution.py:551
  11.8 15.5 %copy-start.7 = (f32[8,256]{1,0:T(8,128)S(1)}, f32[8,256]{1,0:T(8,128)}, u32[]{:S(2)}) copy-start(f32[8,256]{1,0:T(8,128)} %constant.6.clone.square_row) | copy-start | bytes 24580
  11.8 17.8 %copy-start.3 = (bf16[256,256]{1,0:T(8,128)(2,1)S(1)}, bf16[256,256]{1,0:T(8,128)(2,1)}, u32[]{:S(2)}) copy-start(bf16[256,256]{1,0:T(8,128)(2,1)} %layer_in.1) | copy-start | bytes 393220
  11.8 17.8 %copy-start.5 = (bf16[256,128]{1,0:T(8,128)(2,1)S(1)}, bf16[256,128]{1,0:T(8,128)(2,1)}, u32[]{:S(2)}) copy-start(bf16[256,128]{1,0:T(8,128)(2,1)} %layer_out.1) | copy-start | bytes 196612
  11.8 20.2 %collective-permute-start.5 = (f32[32,128]{1,0:T(8,128)S(1)}, f32[32,128]{1,0:T(8,128)S(1)}, u32[]{:S(2)}, u32[]{:S(2)}) collective-permute-start(f32[32,128]{1,0:T(8,128)S(1)} %pad_maximum_fusion), channel_id=1, source_target_pairs={{11,12},{12,11},{15,8},{8,15},{115,116},{116,115},{119,112},{112,1... | collective-permute-start | bytes 49160 | tf_op jit(solution)/shard_map/ppermute | solution.py:562
  24.5 7.5 %collective-permute-start.2 = (f32[320,128]{1,0:T(8,128)S(1)}, f32[320,128]{1,0:T(8,128)S(1)}, u32[]{:S(2)}, u32[]{:S(2)}) collective-permute-start(f32[320,128]{1,0:T(8,128)S(1)} %get-tuple-element.35), channel_id=1, source_target_pairs={{8,16},{16,8},{24,32},{32,24},{40,48},{48,40},{56,64},{64,56},{72,... | collective-permute-start | bytes 491528 | tf_op jit(solution)/shard_map/ppermute | solution.py:551
  27.6 4.4 %collective-permute-start.3 = (f32[16,128]{1,0:T(8,128)S(1)}, f32[16,128]{1,0:T(8,128)S(1)}, u32[]{:S(2)}, u32[]{:S(2)}) collective-permute-start(f32[16,128]{1,0:T(8,128)S(1)} %get-tuple-element.38), channel_id=1, source_target_pairs={{0,1},{1,0},{2,3},{3,2},{4,5},{5,4},{6,7},{7,6},{8,9},{9,8},{10,11... | collective-permute-start | bytes 24584 | tf_op jit(solution)/shard_map/ppermute | solution.py:541
  29.6 2.5 %copy-start.4 = (f32[64,64]{1,0:T(8,128)S(1)}, f32[64,64]{1,0:T(8,128)}, u32[]{:S(2)}) copy-start(f32[64,64]{1,0:T(8,128)} %forward.3) | copy-start | bytes 49156
  33.4 30.3 %all-to-all-start = ((f32[128,1,384]{2,1,0:T(1,128)}), f32[128,1,384]{2,1,0:T(1,128)S(1)}, u32[]{:S(2)}, u32[]{:S(2)}) async-start(f32[128,1,384]{2,1,0:T(1,128)} %bitcast.1), calls=%async_computation | async-start | bytes 393216 | tf_op jit(solution)/shard_map/all_to_all | solution.py:581
  43.5 3.6 %collective-permute-start.6 = (f32[32,128]{1,0:T(8,128)S(1)}, f32[32,128]{1,0:T(8,128)S(1)}, u32[]{:S(2)}, u32[]{:S(2)}) collective-permute-start(f32[32,128]{1,0:T(8,128)S(1)} %collective-permute-done.5.y_both), channel_id=1, source_target_pairs={{8,0},{11,3},{12,4},{15,7},{112,120},{115,123},{116,124},{119,127}... | collective-permute-start | bytes 49160 | tf_op jit(solution)/shard_map/ppermute | solution.py:573
  47.2 16.5 %copy-start.1 = (bf16[128,128]{1,0:T(8,128)(2,1)S(1)}, bf16[128,128]{1,0:T(8,128)(2,1)}, u32[]{:S(2)}) copy-start(bf16[128,128]{1,0:T(8,128)(2,1)} %constant.8.clone.basis_low) | copy-start | bytes 98308
  47.2 16.5 %copy-start.2 = (bf16[128,128]{1,0:T(8,128)(2,1)S(1)}, bf16[128,128]{1,0:T(8,128)(2,1)}, u32[]{:S(2)}) copy-start(bf16[128,128]{1,0:T(8,128)(2,1)} %constant.7.clone.basis_high) | copy-start | bytes 98308
  71.5 27.6 %copy-start.6 = (f32[64,64]{1,0:T(8,128)S(1)}, f32[64,64]{1,0:T(8,128)}, u32[]{:S(2)}) copy-start(f32[64,64]{1,0:T(8,128)} %back.3) | copy-start | bytes 49156

commit v12 on v11

--- a/solution.py
+++ b/solution.py
@@ -116,8 +116,20 @@
     return jnp.transpose(jnp.broadcast_to(row, (LANES, LANES)))
 
 
-def tables_kernel(vectors, square_row, by_level, by_row, by_wave, by_block):
+def inner_kernel(
+    state,
+    vectors,
+    square_row,
+    layer_in,
+    layer_out,
+    star,
+    by_level,
+    by_row,
+    by_wave,
+    by_block,
+):
     place = position()
+    fields = [[plane(state, f, x) for x in range(ROWS)] for f in range(4)]
     tall = column_of(vectors[:, :LANES])
     rate, density = tall[:LEVELS], tall[LEVELS:]
     row = row_of((LEVELS, LANES))
@@ -158,9 +170,6 @@
     scale = -1.0 / root
     by_block[pl.ds(64, 8), :] = jnp.where(row == 0, scale, jnp.where(row == 1, scale * r64, scale * inverse))
 
-
-def inner_kernel(state, vectors, layer_in, layer_out, star):
-    fields = [[plane(state, f, x) for x in range(ROWS)] for f in range(4)]
     for x in range(ROWS):
         u, v, w, th = (fields[f][x] for f in range(4))
         for f in range(4):
@@ -608,24 +617,21 @@
     y_both, x_odd, y_even = lax.optimization_barrier((y_both, x_odd, y_even))
     got_y_both = swap_odd_y(y_both, True)
     got_x_near = swap_odd_x(x_odd, False)
-    vectors = jnp.concatenate([mode_rate, density, layer_bias])[None, :]
-    long = pl.CostEstimate(flops=10**10, transcendentals=0, bytes_accessed=2**24)
-    by_level, by_row, by_wave, by_block = call(
-        tables_kernel,
-        [(3 * LEVELS, LANES), (72, total_east), (3 * LANES, LANES), (72, total_east)],
-        [vectors, square_row],
-        "tables",
-        cost=long,
-    )
-    by_level, y_even = lax.optimization_barrier((by_level, y_even))
+    inner, by_level, by_row, by_wave, by_block = call(
+        inner_kernel,
+        [(16 * LEVELS, LANES), (3 * LEVELS, LANES), (72, total_east), (3 * LANES, LANES), (72, total_east)],
+        [
+            planes,
+            jnp.concatenate([mode_rate, density, layer_bias])[None, :],
+            square_row,
+            layer_in,
+            layer_out,
+        ],
+        "inner",
+        cost=pl.CostEstimate(flops=10**10, transcendentals=0, bytes_accessed=2**24),
+    )
+    inner, y_even = lax.optimization_barrier((inner, y_even))
     got_y_even = swap(y_even, "gy", 0)
-    (inner,) = call(
-        inner_kernel,
-        [(16 * LEVELS, LANES)],
-        [planes, vectors, layer_in, layer_out],
-        "inner",
-        cost=None,
-    )
     star, message = call(
         outer_kernel,
         [(16 * LEVELS, LANES), (blocks * 6, LANES)],

time: 101 us -> 101 us (level)
    pallas_call x8 -> x7, Pallas kernels: 5.75 us -> 5.63 us  [call(): pl.pallas_call(kernel, out_shape=[jax.ShapeDtypeStruct(s, F32) for s in s...]
where the time goes in v12:
time: 101 us; the launch traced here: 100 us
  starting transfers between devices  40.5 us (40%)
  blocking collectives  33.9 us (34%)
  waiting for transfers between devices  18.8 us (19%)
  Pallas kernels  5.63 us (6%)
  local copies, waits for them, and re-layouts  1.12 us (1%)
    all_to_all x1, blocking collectives, exchange(): lax.all_to_all(shaped, ('gx', 'gy'), 0, 0, tiled=True, axis_index_groups=...  27.3 us
    all_to_all x1, waiting for transfers between devices, exchange(): lax.all_to_all(shaped, ('gx', 'gy'), 0, 0, tiled=True, axis_index_groups=...  15.5 us
    ppermute x2, starting transfers between devices, swap_odd_y(): return lax.ppermute(values, ('gx', 'gy'), pairs)  13.2 us
    ppermute x2, starting transfers between devices, swap(): return lax.ppermute(values, axis, pairs)  10.8 us
    all_to_all x1, starting transfers between devices, exchange(): lax.all_to_all(shaped, ('gx', 'gy'), 0, 0, tiled=True, axis_index_groups=...  10.2 us
    all_to_all x1, blocking collectives, on_device(): lax.all_to_all(moments.reshape(4, 4, total_east), 'gy', 0, 0, tiled=True,...  6.58 us
    pallas_call x7, Pallas kernels, call(): pl.pallas_call(kernel, out_shape=[jax.ShapeDtypeStruct(s, F32) for s in s...  5.63 us
    ppermute x2, starting transfers between devices, swap_odd_x(): return lax.ppermute(values, 'gx', pairs)  3.5 us
  transfers between devices with their start and end apart: 8, of which 3 were waited for; matrix products, arithmetic and copies ran while one was open for 0% of the time, Pallas kernels for 2%

profile of v12, /device:TPU:1, one launch (start us, length us, event | category | flops | bytes accessed | tf_op | source)
XLA Modules:
  0.0 100.2 jit_solution(14335102359174520172)
XLA Ops:
  0.0 0.0 copy-start
  0.0 1.0 %copy-done = f32[4,64,4,128]{3,2,1,0:T(4,128)S(1)} copy-done((f32[4,64,4,128]{3,2,1,0:T(4,128)S(1)}, f32[4,64,4,128]{3,2,1,0:T(4,128)}, u32[]{:S(2)}) %copy-start) | copy-done | bytes 524312
  1.0 0.0 copy-start.8
  1.0 0.0 copy-start.9
  1.0 0.0 copy-start.10
  1.0 0.0 copy-start.5
  1.1 0.0 copy-start.7
  1.1 0.3 edges.1
  1.3 0.0 copy-start.6
  1.4 8.9 %collective-permute-start = (f32[336,128]{1,0:T(8,128)S(1)}, f32[336,128]{1,0:T(8,128)S(1)}, u32[]{:S(2)}, u32[]{:S(2)}) collective-permute-start(f32[336,128]{1,0:T(8,128)S(1)} %get-tuple-element.34), channel_id=1, source_target_pairs={{0,8},{8,0},{16,24},{24,16},{32,40},{40,32},{48,56},{56,48},{64,72... | collective-permute-start | bytes 516104 | tf_op jit(solution)/shard_map/ppermute | solution.py:550
  10.3 0.7 collective-permute-start.4
  11.0 0.7 collective-permute-start.1
  11.6 0.0 copy-done.8
  11.6 0.0 copy-done.9
  11.7 0.0 copy-done.10
  11.7 0.1 pad_maximum_fusion.1
  11.7 0.0 collective-permute-done.x_even
  11.8 12.5 %collective-permute-start.5 = (f32[32,128]{1,0:T(8,128)S(1)}, f32[32,128]{1,0:T(8,128)S(1)}, u32[]{:S(2)}, u32[]{:S(2)}) collective-permute-start(f32[32,128]{1,0:T(8,128)S(1)} %pad_maximum_fusion), channel_id=1, source_target_pairs={{11,12},{12,11},{15,8},{8,15},{115,116},{116,115},{119,112},{112,1... | collective-permute-start | bytes 49160 | tf_op jit(solution)/shard_map/ppermute | solution.py:571
  24.3 2.8 %collective-permute-start.2 = (f32[320,128]{1,0:T(8,128)S(1)}, f32[320,128]{1,0:T(8,128)S(1)}, u32[]{:S(2)}, u32[]{:S(2)}) collective-permute-start(f32[320,128]{1,0:T(8,128)S(1)} %get-tuple-element.39), channel_id=1, source_target_pairs={{8,16},{16,8},{24,32},{32,24},{40,48},{48,40},{56,64},{64,56},{72,... | collective-permute-start | bytes 491528 | tf_op jit(solution)/shard_map/ppermute | solution.py:560
  27.1 0.0 copy-done.5
  27.1 0.0 copy-done.7
  27.1 0.0 copy-done.6
  27.2 0.0 copy-start.3
  27.2 0.8 inner.1
  28.0 1.9 %collective-permute-start.3 = (f32[16,128]{1,0:T(8,128)S(1)}, f32[16,128]{1,0:T(8,128)S(1)}, u32[]{:S(2)}, u32[]{:S(2)}) collective-permute-start(f32[16,128]{1,0:T(8,128)S(1)} %get-tuple-element.40), channel_id=1, source_target_pairs={{0,1},{1,0},{2,3},{3,2},{4,5},{5,4},{6,7},{7,6},{8,9},{9,8},{10,11... | collective-permute-start | bytes 24584 | tf_op jit(solution)/shard_map/ppermute | solution.py:550
  29.9 0.0 collective-permute-done.4.y_odd
  29.9 0.0 collective-permute-done.1.x_far
  29.9 2.4 %collective-permute-done.3.y_even = f32[16,128]{1,0:T(8,128)S(1)} collective-permute-done((f32[16,128]{1,0:T(8,128)S(1)}, f32[16,128]{1,0:T(8,128)S(1)}, u32[]{:S(2)}, u32[]{:S(2)}) %collective-permute-start.3) | collective-permute-done | bytes 8224 | tf_op jit(solution)/shard_map/ppermute | solution.py:550
  32.4 0.0 collective-permute-done.5.y_both
  32.4 0.0 collective-permute-done.2.x_near
  32.4 0.0 copy-done.3
  32.4 1.3 %outer.1 = (f32[1024,128]{1,0:T(8,128)S(1)}, f32[384,128]{1,0:T(8,128)}) custom-call(f32[1024,128]{1,0:T(8,128)S(1)} %get-tuple-element.31.state, f32[1024,128]{1,0:T(8,128)S(1)} %get-tuple-element.38.inner, f32[336,128]{1,0:T(8,128)S(1)} %collective-permute-done.x_even, f32[320,128]{1,0:T(8,128)S(1)} %collective-permute-done.1.x_far, ...), custom_call_target="tpu_custom_call" | custom-call | tf_op jit(solution)/shard_map/outer/pallas_call | solution.py:532
  33.7 10.2 %all-to-all-start = ((f32[128,1,384]{2,1,0:T(1,128)}), f32[128,1,384]{2,1,0:T(1,128)S(1)}, u32[]{:S(2)}, u32[]{:S(2)}) async-start(f32[128,1,384]{2,1,0:T(1,128)} %bitcast.1), calls=%async_computation | async-start | bytes 393216 | tf_op jit(solution)/shard_map/all_to_all | solution.py:590
  43.9 2.8 %collective-permute-start.6 = (f32[32,128]{1,0:T(8,128)S(1)}, f32[32,128]{1,0:T(8,128)S(1)}, u32[]{:S(2)}, u32[]{:S(2)}) collective-permute-start(f32[32,128]{1,0:T(8,128)S(1)} %collective-permute-done.5.y_both), channel_id=1, source_target_pairs={{8,0},{11,3},{12,4},{15,7},{112,120},{115,123},{116,124},{119,127}... | collective-permute-start | bytes 49160 | tf_op jit(solution)/shard_map/ppermute | solution.py:582
  46.7 0.8 collective-permute-done.6.relayed
  47.6 0.0 copy-start.1
  47.6 0.0 copy-start.2
  47.6 1.0 mend.1
  48.5 15.5 %all-to-all-done = f32[128,1,384]{2,1,0:T(1,128)S(1)} async-done(((f32[128,1,384]{2,1,0:T(1,128)}), f32[128,1,384]{2,1,0:T(1,128)S(1)}, u32[]{:S(2)}, u32[]{:S(2)}) %all-to-all-start) | async-done | bytes 196640 | tf_op jit(solution)/shard_map/all_to_all | solution.py:590
  64.0 0.0 copy-done.1
  64.0 0.0 copy-done.2
  64.0 0.6 solve.1
  64.7 6.6 %all_to_all.15 = f32[4,4,256]{2,1,0:T(4,128)S(1)} all-to-all(f32[4,4,256]{2,1,0:T(4,128)S(1)} %reshape.27), channel_id=1, replica_groups={{0,1,2,3},{4,5,6,7},{8,9,10,11},{12,13,14,15},{16,17,18,19},{20,21,22,2..., dimensions={0} | all-to-all | bytes 32768 | tf_op jit(solution)/shard_map/all_to_all | solution.py:670
  71.3 0.4 back.2
  71.6 0.0 copy-start.4
  71.7 27.3 %all_to_all.16 = f32[128,1,384]{2,1,0:T(1,128)S(1)} all-to-all(f32[128,1,384]{2,1,0:T(1,128)S(1)} %bitcast.7), channel_id=1, replica_groups={{0,4,8,12,16,20,24,28,32,36,40,44,48,52,56,60,64,68,72,76,80,84,88,92,9..., dimensions={0} | all-to-all | bytes 393216 | tf_op jit(solution)/shard_map/all_to_all | solution.py:590
  98.9 0.0 copy-done.4
  98.9 1.2 %final.1 = f32[1024,128]{1,0:T(8,128)} custom-call(f32[384,128]{1,0:T(8,128)S(1)} %bitcast.8, f32[128,128]{1,0:T(8,128)S(1)} %get-tuple-element.55.middle, f32[1024,128]{1,0:T(8,128)S(1)} %get-tuple-element.56.star, f32[64,64]{1,0:T(8,128)S(1)} %copy-done.4, f32[192,128]{1,0:T(8,128)S(1)} %get-tuple-element.42.by_level), custom_call_target="tpu_custom_call" | custom-call | tf_op jit(solution)/shard_map/final/pallas_call | solution.py:532
  (5 shorter events, 0.0 us)
Async XLA Ops:
  0.0 1.0 %copy-start = (f32[4,64,4,128]{3,2,1,0:T(4,128)S(1)}, f32[4,64,4,128]{3,2,1,0:T(4,128)}, u32[]{:S(2)}) copy-start(f32[4,64,4,128]{3,2,1,0:T(4,128)} %param.11) | copy-start | bytes 1572868
  1.0 10.6 %copy-start.8 = (f32[256]{0:T(256)S(1)}, f32[256]{0:T(256)}, u32[]{:S(2)}) copy-start(f32[256]{0:T(256)} %param.14) | copy-start | bytes 3076
  1.0 10.6 %copy-start.9 = (f32[64]{0:T(128)S(1)}, f32[64]{0:T(128)}, u32[]{:S(2)}) copy-start(f32[64]{0:T(128)} %param.12) | copy-start | bytes 772
  1.0 10.6 %copy-start.10 = (f32[64]{0:T(128)S(1)}, f32[64]{0:T(128)}, u32[]{:S(2)}) copy-start(f32[64]{0:T(128)} %param.18) | copy-start | bytes 772
  1.0 26.1 %copy-start.5 = (bf16[256,256]{1,0:T(8,128)(2,1)S(1)}, bf16[256,256]{1,0:T(8,128)(2,1)}, u32[]{:S(2)}) copy-start(bf16[256,256]{1,0:T(8,128)(2,1)} %layer_in.1) | copy-start | bytes 393220
  1.1 26.1 %copy-start.7 = (f32[8,256]{1,0:T(8,128)S(1)}, f32[8,256]{1,0:T(8,128)}, u32[]{:S(2)}) copy-start(f32[8,256]{1,0:T(8,128)} %constant.6.clone.square_row) | copy-start | bytes 24580
  1.3 25.8 %copy-start.6 = (bf16[256,128]{1,0:T(8,128)(2,1)S(1)}, bf16[256,128]{1,0:T(8,128)(2,1)}, u32[]{:S(2)}) copy-start(bf16[256,128]{1,0:T(8,128)(2,1)} %layer_out.1) | copy-start | bytes 196612
  1.4 10.4 %collective-permute-start = (f32[336,128]{1,0:T(8,128)S(1)}, f32[336,128]{1,0:T(8,128)S(1)}, u32[]{:S(2)}, u32[]{:S(2)}) collective-permute-start(f32[336,128]{1,0:T(8,128)S(1)} %get-tuple-element.34), channel_id=1, source_target_pairs={{0,8},{8,0},{16,24},{24,16},{32,40},{40,32},{48,56},{56,48},{64,72... | collective-permute-start | bytes 516104 | tf_op jit(solution)/shard_map/ppermute | solution.py:550
  10.3 19.6 %collective-permute-start.4 = (f32[16,128]{1,0:T(8,128)S(1)}, f32[16,128]{1,0:T(8,128)S(1)}, u32[]{:S(2)}, u32[]{:S(2)}) collective-permute-start(f32[16,128]{1,0:T(8,128)S(1)} %get-tuple-element.33), channel_id=1, source_target_pairs={{1,2},{2,1},{5,6},{6,5},{9,10},{10,9},{13,14},{14,13},{17,18},{18,... | collective-permute-start | bytes 24584 | tf_op jit(solution)/shard_map/ppermute | solution.py:571
  11.0 19.0 %collective-permute-start.1 = (f32[320,128]{1,0:T(8,128)S(1)}, f32[320,128]{1,0:T(8,128)S(1)}, u32[]{:S(2)}, u32[]{:S(2)}) collective-permute-start(f32[320,128]{1,0:T(8,128)S(1)} %get-tuple-element.39), channel_id=1, source_target_pairs={{120,128},{128,120},{248,256},{256,248},{376,384},{384,376},{504,0... | collective-permute-start | bytes 491528 | tf_op jit(solution)/shard_map/ppermute | solution.py:560
  11.8 20.6 %collective-permute-start.5 = (f32[32,128]{1,0:T(8,128)S(1)}, f32[32,128]{1,0:T(8,128)S(1)}, u32[]{:S(2)}, u32[]{:S(2)}) collective-permute-start(f32[32,128]{1,0:T(8,128)S(1)} %pad_maximum_fusion), channel_id=1, source_target_pairs={{11,12},{12,11},{15,8},{8,15},{115,116},{116,115},{119,112},{112,1... | collective-permute-start | bytes 49160 | tf_op jit(solution)/shard_map/ppermute | solution.py:571
  24.3 8.1 %collective-permute-start.2 = (f32[320,128]{1,0:T(8,128)S(1)}, f32[320,128]{1,0:T(8,128)S(1)}, u32[]{:S(2)}, u32[]{:S(2)}) collective-permute-start(f32[320,128]{1,0:T(8,128)S(1)} %get-tuple-element.39), channel_id=1, source_target_pairs={{8,16},{16,8},{24,32},{32,24},{40,48},{48,40},{56,64},{64,56},{72,... | collective-permute-start | bytes 491528 | tf_op jit(solution)/shard_map/ppermute | solution.py:560
  27.2 5.3 %copy-start.3 = (f32[64,64]{1,0:T(8,128)S(1)}, f32[64,64]{1,0:T(8,128)}, u32[]{:S(2)}) copy-start(f32[64,64]{1,0:T(8,128)} %forward.3) | copy-start | bytes 49156
  28.0 4.4 %collective-permute-start.3 = (f32[16,128]{1,0:T(8,128)S(1)}, f32[16,128]{1,0:T(8,128)S(1)}, u32[]{:S(2)}, u32[]{:S(2)}) collective-permute-start(f32[16,128]{1,0:T(8,128)S(1)} %get-tuple-element.40), channel_id=1, source_target_pairs={{0,1},{1,0},{2,3},{3,2},{4,5},{5,4},{6,7},{7,6},{8,9},{9,8},{10,11... | collective-permute-start | bytes 24584 | tf_op jit(solution)/shard_map/ppermute | solution.py:550
  33.7 30.3 %all-to-all-start = ((f32[128,1,384]{2,1,0:T(1,128)}), f32[128,1,384]{2,1,0:T(1,128)S(1)}, u32[]{:S(2)}, u32[]{:S(2)}) async-start(f32[128,1,384]{2,1,0:T(1,128)} %bitcast.1), calls=%async_computation | async-start | bytes 393216 | tf_op jit(solution)/shard_map/all_to_all | solution.py:590
  43.9 3.6 %collective-permute-start.6 = (f32[32,128]{1,0:T(8,128)S(1)}, f32[32,128]{1,0:T(8,128)S(1)}, u32[]{:S(2)}, u32[]{:S(2)}) collective-permute-start(f32[32,128]{1,0:T(8,128)S(1)} %collective-permute-done.5.y_both), channel_id=1, source_target_pairs={{8,0},{11,3},{12,4},{15,7},{112,120},{115,123},{116,124},{119,127}... | collective-permute-start | bytes 49160 | tf_op jit(solution)/shard_map/ppermute | solution.py:582
  47.6 16.5 %copy-start.1 = (bf16[128,128]{1,0:T(8,128)(2,1)S(1)}, bf16[128,128]{1,0:T(8,128)(2,1)}, u32[]{:S(2)}) copy-start(bf16[128,128]{1,0:T(8,128)(2,1)} %constant.8.clone.basis_low) | copy-start | bytes 98308
  47.6 16.5 %copy-start.2 = (bf16[128,128]{1,0:T(8,128)(2,1)S(1)}, bf16[128,128]{1,0:T(8,128)(2,1)}, u32[]{:S(2)}) copy-start(bf16[128,128]{1,0:T(8,128)(2,1)} %constant.7.clone.basis_high) | copy-start | bytes 98308
  71.6 27.3 %copy-start.4 = (f32[64,64]{1,0:T(8,128)S(1)}, f32[64,64]{1,0:T(8,128)}, u32[]{:S(2)}) copy-start(f32[64,64]{1,0:T(8,128)} %back.3) | copy-start | bytes 49156

commit v13 on v12

--- a/solution.py
+++ b/solution.py
@@ -650,17 +650,7 @@
         "outer",
         scratch=[(LANES, LANES)],
     )
-    message, got_y_both = lax.optimization_barrier((message, got_y_both))
-    relayed = hand_over(got_y_both)
     modal = exchange(message)
-    whole, middle = call(
-        mend_kernel,
-        [(16 * LEVELS, LANES), (2 * LEVELS, LANES)],
-        [star, message, planes, relayed, mode_forward],
-        "mend",
-        scratch=[(LANES, LANES)],
-    )
-    modal, whole, middle = lax.optimization_barrier((modal, whole, middle))
     local, moments = call(
         solve_kernel,
         [(LANES, total_east), (16, total_east)],
@@ -681,7 +671,16 @@
         [local, moments, basis_high, basis_low, by_row, by_wave, by_block],
         "back",
     )
+    reply, got_y_both = lax.optimization_barrier((reply, got_y_both))
+    relayed = hand_over(got_y_both)
     pressure = exchange(reply)
+    whole, middle = call(
+        mend_kernel,
+        [(16 * LEVELS, LANES), (2 * LEVELS, LANES)],
+        [star, message, planes, relayed, mode_forward],
+        "mend",
+        scratch=[(LANES, LANES)],
+    )
     (out,) = call(
         final_kernel,
         [(4 * LEVELS * ROWS, LANES)],

time: 101 us -> 101 us (level)
  starting transfers between devices: 40.5 us -> 37.6 us
  blocking collectives: 33.9 us -> 36.7 us
    all_to_all x1, starting transfers between devices: 10.2 us -> 7.31 us  [exchange(): lax.all_to_all(shaped, ('gx', 'gy'), 0, 0, tiled=True, axis_index_groups=...]
    all_to_all x1, blocking collectives: 27.3 us -> 30.1 us  [exchange(): lax.all_to_all(shaped, ('gx', 'gy'), 0, 0, tiled=True, axis_index_groups=...]
  transfers between devices with their start and end apart: 8 -> 8, of which waited for: 3 -> 3; matrix products, arithmetic and copies ran while one was open for 0% -> 0% of each run, Pallas kernels for 2% -> 1%
where the time goes in v13:
time: 101 us; the launch traced here: 100 us
  starting transfers between devices  37.6 us (37%)
  blocking collectives  36.7 us (36%)
  waiting for transfers between devices  19.7 us (20%)
  Pallas kernels  4.7 us (5%)
  local copies, waits for them, and re-layouts  1.12 us (1%)
    all_to_all x1, blocking collectives, exchange(): lax.all_to_all(shaped, ('gx', 'gy'), 0, 0, tiled=True, axis_index_groups=...  30.1 us
    all_to_all x1, waiting for transfers between devices, exchange(): lax.all_to_all(shaped, ('gx', 'gy'), 0, 0, tiled=True, axis_index_groups=...  16.4 us
    ppermute x2, starting transfers between devices, swap_odd_y(): return lax.ppermute(values, ('gx', 'gy'), pairs)  13.2 us
    ppermute x2, starting transfers between devices, swap(): return lax.ppermute(values, axis, pairs)  10.8 us
    all_to_all x1, starting transfers between devices, exchange(): lax.all_to_all(shaped, ('gx', 'gy'), 0, 0, tiled=True, axis_index_groups=...  7.31 us
    all_to_all x1, blocking collectives, on_device(): lax.all_to_all(moments.reshape(4, 4, total_east), 'gy', 0, 0, tiled=True,...  6.57 us
    pallas_call x7, Pallas kernels, call(): pl.pallas_call(kernel, out_shape=[jax.ShapeDtypeStruct(s, F32) for s in s...  4.7 us
    ppermute x2, starting transfers between devices, swap_odd_x(): return lax.ppermute(values, 'gx', pairs)  3.5 us
  transfers between devices with their start and end apart: 8, of which 3 were waited for; matrix products, arithmetic and copies ran while one was open for 0% of the time, Pallas kernels for 1%

profile of v13, /device:TPU:1, one launch (start us, length us, event | category | flops | bytes accessed | tf_op | source)
XLA Modules:
  0.0 100.1 jit_solution(17032735510541028335)
XLA Ops:
  0.0 0.0 copy-start
  0.0 1.0 %copy-done = f32[4,64,4,128]{3,2,1,0:T(4,128)S(1)} copy-done((f32[4,64,4,128]{3,2,1,0:T(4,128)S(1)}, f32[4,64,4,128]{3,2,1,0:T(4,128)}, u32[]{:S(2)}) %copy-start) | copy-done | bytes 524312
  1.0 0.0 copy-start.8
  1.0 0.0 copy-start.9
  1.0 0.0 copy-start.10
  1.0 0.0 copy-start.5
  1.1 0.0 copy-start.7
  1.1 0.3 edges.1
  1.3 0.0 copy-start.6
  1.4 8.9 %collective-permute-start = (f32[336,128]{1,0:T(8,128)S(1)}, f32[336,128]{1,0:T(8,128)S(1)}, u32[]{:S(2)}, u32[]{:S(2)}) collective-permute-start(f32[336,128]{1,0:T(8,128)S(1)} %get-tuple-element.31), channel_id=1, source_target_pairs={{0,8},{8,0},{16,24},{24,16},{32,40},{40,32},{48,56},{56,48},{64,72... | collective-permute-start | bytes 516104 | tf_op jit(solution)/shard_map/ppermute | solution.py:550
  10.3 0.7 collective-permute-start.4
  11.0 0.7 collective-permute-start.1
  11.6 0.0 copy-done.8
  11.6 0.0 copy-done.9
  11.7 0.0 copy-done.10
  11.7 0.1 pad_maximum_fusion.1
  11.7 0.0 collective-permute-done.x_even
  11.8 12.5 %collective-permute-start.5 = (f32[32,128]{1,0:T(8,128)S(1)}, f32[32,128]{1,0:T(8,128)S(1)}, u32[]{:S(2)}, u32[]{:S(2)}) collective-permute-start(f32[32,128]{1,0:T(8,128)S(1)} %pad_maximum_fusion), channel_id=1, source_target_pairs={{11,12},{12,11},{15,8},{8,15},{115,116},{116,115},{119,112},{112,1... | collective-permute-start | bytes 49160 | tf_op jit(solution)/shard_map/ppermute | solution.py:571
  24.3 2.8 %collective-permute-start.2 = (f32[320,128]{1,0:T(8,128)S(1)}, f32[320,128]{1,0:T(8,128)S(1)}, u32[]{:S(2)}, u32[]{:S(2)}) collective-permute-start(f32[320,128]{1,0:T(8,128)S(1)} %get-tuple-element.36), channel_id=1, source_target_pairs={{8,16},{16,8},{24,32},{32,24},{40,48},{48,40},{56,64},{64,56},{72,... | collective-permute-start | bytes 491528 | tf_op jit(solution)/shard_map/ppermute | solution.py:560
  27.1 0.0 copy-done.5
  27.1 0.0 copy-done.7
  27.1 0.0 copy-done.6
  27.2 0.0 copy-start.3
  27.2 0.8 inner.1
  28.0 1.9 %collective-permute-start.3 = (f32[16,128]{1,0:T(8,128)S(1)}, f32[16,128]{1,0:T(8,128)S(1)}, u32[]{:S(2)}, u32[]{:S(2)}) collective-permute-start(f32[16,128]{1,0:T(8,128)S(1)} %get-tuple-element.37), channel_id=1, source_target_pairs={{0,1},{1,0},{2,3},{3,2},{4,5},{5,4},{6,7},{7,6},{8,9},{9,8},{10,11... | collective-permute-start | bytes 24584 | tf_op jit(solution)/shard_map/ppermute | solution.py:550
  29.9 0.0 collective-permute-done.4.y_odd
  29.9 0.0 collective-permute-done.1.x_far
  29.9 2.4 %collective-permute-done.3.y_even = f32[16,128]{1,0:T(8,128)S(1)} collective-permute-done((f32[16,128]{1,0:T(8,128)S(1)}, f32[16,128]{1,0:T(8,128)S(1)}, u32[]{:S(2)}, u32[]{:S(2)}) %collective-permute-start.3) | collective-permute-done | bytes 8224 | tf_op jit(solution)/shard_map/ppermute | solution.py:550
  32.4 0.0 collective-permute-done.5.y_both
  32.4 0.0 collective-permute-done.2.x_near
  32.4 0.0 copy-done.3
  32.4 0.7 outer.1
  33.1 0.0 copy-start.1
  33.1 0.0 copy-start.2
  33.1 30.1 %all_to_all.15 = f32[128,1,384]{2,1,0:T(1,128)S(1)} all-to-all(f32[128,1,384]{2,1,0:T(1,128)S(1)} %bitcast.6), channel_id=1, replica_groups={{0,4,8,12,16,20,24,28,32,36,40,44,48,52,56,60,64,68,72,76,80,84,88,92,9..., dimensions={0} | all-to-all | bytes 393216 | tf_op jit(solution)/shard_map/all_to_all | solution.py:590
  63.2 0.0 copy-done.1
  63.2 0.0 copy-done.2
  63.2 0.6 solve.1
  63.8 6.6 %all_to_all.16 = f32[4,4,256]{2,1,0:T(4,128)S(1)} all-to-all(f32[4,4,256]{2,1,0:T(4,128)S(1)} %reshape.27), channel_id=1, replica_groups={{0,1,2,3},{4,5,6,7},{8,9,10,11},{12,13,14,15},{16,17,18,19},{20,21,22,2..., dimensions={0} | all-to-all | bytes 32768 | tf_op jit(solution)/shard_map/all_to_all | solution.py:660
  70.4 1.1 %back.2 = f32[384,128]{1,0:T(8,128)} custom-call(f32[128,256]{1,0:T(8,128)S(1)} %get-tuple-element.43.local, f32[16,256]{1,0:T(8,128)S(1)} %reshape.28.moments, bf16[128,128]{1,0:T(8,128)(2,1)S(1)} %copy-done.2, bf16[128,128]{1,0:T(8,128)(2,1)S(1)} %copy-done.1, f32[72,256]{1,0:T(8,128)S(1)} %get-tuple-element.41.by_row, ...), custom_call_target="tpu_custom_call" | custom-call | tf_op jit(solution)/shard_map/back/pallas_call | solution.py:532
  71.5 7.3 %all-to-all-start.2 = ((f32[128,1,384]{2,1,0:T(1,128)}), f32[128,1,384]{2,1,0:T(1,128)S(1)}, u32[]{:S(2)}, u32[]{:S(2)}) async-start(f32[128,1,384]{2,1,0:T(1,128)} %bitcast.3), calls=%async_computation.2 | async-start | bytes 393216 | tf_op jit(solution)/shard_map/all_to_all | solution.py:590
  78.8 2.8 %collective-permute-start.6 = (f32[32,128]{1,0:T(8,128)S(1)}, f32[32,128]{1,0:T(8,128)S(1)}, u32[]{:S(2)}, u32[]{:S(2)}) collective-permute-start(f32[32,128]{1,0:T(8,128)S(1)} %collective-permute-done.5.y_both), channel_id=1, source_target_pairs={{8,0},{11,3},{12,4},{15,7},{112,120},{115,123},{116,124},{119,127}... | collective-permute-start | bytes 49160 | tf_op jit(solution)/shard_map/ppermute | solution.py:582
  81.6 0.8 collective-permute-done.6.relayed
  82.4 0.0 copy-start.4
  82.5 16.4 %all-to-all-done.2 = f32[128,1,384]{2,1,0:T(1,128)S(1)} async-done(((f32[128,1,384]{2,1,0:T(1,128)}), f32[128,1,384]{2,1,0:T(1,128)S(1)}, u32[]{:S(2)}, u32[]{:S(2)}) %all-to-all-start.2) | async-done | bytes 196640 | tf_op jit(solution)/shard_map/all_to_all | solution.py:590
  98.9 0.0 copy-done.4
  98.9 1.2 %final.1 = f32[1024,128]{1,0:T(8,128)} custom-call(f32[384,128]{1,0:T(8,128)S(1)} %bitcast.8, f32[128,128]{1,0:T(8,128)S(1)} %get-tuple-element.49.middle, f32[1024,128]{1,0:T(8,128)S(1)} %get-tuple-element.50.star, f32[64,64]{1,0:T(8,128)S(1)} %copy-done.4, f32[192,128]{1,0:T(8,128)S(1)} %get-tuple-element.39.by_level), custom_call_target="tpu_custom_call" | custom-call | tf_op jit(solution)/shard_map/final/pallas_call | solution.py:532
  (6 shorter events, 0.1 us)
Async XLA Ops:
  0.0 1.0 %copy-start = (f32[4,64,4,128]{3,2,1,0:T(4,128)S(1)}, f32[4,64,4,128]{3,2,1,0:T(4,128)}, u32[]{:S(2)}) copy-start(f32[4,64,4,128]{3,2,1,0:T(4,128)} %param.11) | copy-start | bytes 1572868
  1.0 10.6 %copy-start.8 = (f32[256]{0:T(256)S(1)}, f32[256]{0:T(256)}, u32[]{:S(2)}) copy-start(f32[256]{0:T(256)} %param.14) | copy-start | bytes 3076
  1.0 10.6 %copy-start.9 = (f32[64]{0:T(128)S(1)}, f32[64]{0:T(128)}, u32[]{:S(2)}) copy-start(f32[64]{0:T(128)} %param.12) | copy-start | bytes 772
  1.0 10.6 %copy-start.10 = (f32[64]{0:T(128)S(1)}, f32[64]{0:T(128)}, u32[]{:S(2)}) copy-start(f32[64]{0:T(128)} %param.18) | copy-start | bytes 772
  1.0 26.1 %copy-start.5 = (bf16[256,256]{1,0:T(8,128)(2,1)S(1)}, bf16[256,256]{1,0:T(8,128)(2,1)}, u32[]{:S(2)}) copy-start(bf16[256,256]{1,0:T(8,128)(2,1)} %layer_in.1) | copy-start | bytes 393220
  1.1 26.1 %copy-start.7 = (f32[8,256]{1,0:T(8,128)S(1)}, f32[8,256]{1,0:T(8,128)}, u32[]{:S(2)}) copy-start(f32[8,256]{1,0:T(8,128)} %constant.6.clone.square_row) | copy-start | bytes 24580
  1.3 25.8 %copy-start.6 = (bf16[256,128]{1,0:T(8,128)(2,1)S(1)}, bf16[256,128]{1,0:T(8,128)(2,1)}, u32[]{:S(2)}) copy-start(bf16[256,128]{1,0:T(8,128)(2,1)} %layer_out.1) | copy-start | bytes 196612
  1.4 10.4 %collective-permute-start = (f32[336,128]{1,0:T(8,128)S(1)}, f32[336,128]{1,0:T(8,128)S(1)}, u32[]{:S(2)}, u32[]{:S(2)}) collective-permute-start(f32[336,128]{1,0:T(8,128)S(1)} %get-tuple-element.31), channel_id=1, source_target_pairs={{0,8},{8,0},{16,24},{24,16},{32,40},{40,32},{48,56},{56,48},{64,72... | collective-permute-start | bytes 516104 | tf_op jit(solution)/shard_map/ppermute | solution.py:550
  10.3 19.6 %collective-permute-start.4 = (f32[16,128]{1,0:T(8,128)S(1)}, f32[16,128]{1,0:T(8,128)S(1)}, u32[]{:S(2)}, u32[]{:S(2)}) collective-permute-start(f32[16,128]{1,0:T(8,128)S(1)} %get-tuple-element.30), channel_id=1, source_target_pairs={{1,2},{2,1},{5,6},{6,5},{9,10},{10,9},{13,14},{14,13},{17,18},{18,... | collective-permute-start | bytes 24584 | tf_op jit(solution)/shard_map/ppermute | solution.py:571
  11.0 19.0 %collective-permute-start.1 = (f32[320,128]{1,0:T(8,128)S(1)}, f32[320,128]{1,0:T(8,128)S(1)}, u32[]{:S(2)}, u32[]{:S(2)}) collective-permute-start(f32[320,128]{1,0:T(8,128)S(1)} %get-tuple-element.36), channel_id=1, source_target_pairs={{120,128},{128,120},{248,256},{256,248},{376,384},{384,376},{504,0... | collective-permute-start | bytes 491528 | tf_op jit(solution)/shard_map/ppermute | solution.py:560
  11.8 20.6 %collective-permute-start.5 = (f32[32,128]{1,0:T(8,128)S(1)}, f32[32,128]{1,0:T(8,128)S(1)}, u32[]{:S(2)}, u32[]{:S(2)}) collective-permute-start(f32[32,128]{1,0:T(8,128)S(1)} %pad_maximum_fusion), channel_id=1, source_target_pairs={{11,12},{12,11},{15,8},{8,15},{115,116},{116,115},{119,112},{112,1... | collective-permute-start | bytes 49160 | tf_op jit(solution)/shard_map/ppermute | solution.py:571
  24.3 8.1 %collective-permute-start.2 = (f32[320,128]{1,0:T(8,128)S(1)}, f32[320,128]{1,0:T(8,128)S(1)}, u32[]{:S(2)}, u32[]{:S(2)}) collective-permute-start(f32[320,128]{1,0:T(8,128)S(1)} %get-tuple-element.36), channel_id=1, source_target_pairs={{8,16},{16,8},{24,32},{32,24},{40,48},{48,40},{56,64},{64,56},{72,... | collective-permute-start | bytes 491528 | tf_op jit(solution)/shard_map/ppermute | solution.py:560
  27.2 5.2 %copy-start.3 = (f32[64,64]{1,0:T(8,128)S(1)}, f32[64,64]{1,0:T(8,128)}, u32[]{:S(2)}) copy-start(f32[64,64]{1,0:T(8,128)} %forward.3) | copy-start | bytes 49156
  28.0 4.4 %collective-permute-start.3 = (f32[16,128]{1,0:T(8,128)S(1)}, f32[16,128]{1,0:T(8,128)S(1)}, u32[]{:S(2)}, u32[]{:S(2)}) collective-permute-start(f32[16,128]{1,0:T(8,128)S(1)} %get-tuple-element.37), channel_id=1, source_target_pairs={{0,1},{1,0},{2,3},{3,2},{4,5},{5,4},{6,7},{7,6},{8,9},{9,8},{10,11... | collective-permute-start | bytes 24584 | tf_op jit(solution)/shard_map/ppermute | solution.py:550
  33.1 30.1 %copy-start.1 = (bf16[128,128]{1,0:T(8,128)(2,1)S(1)}, bf16[128,128]{1,0:T(8,128)(2,1)}, u32[]{:S(2)}) copy-start(bf16[128,128]{1,0:T(8,128)(2,1)} %constant.8.clone.basis_low) | copy-start | bytes 98308
  33.1 30.1 %copy-start.2 = (bf16[128,128]{1,0:T(8,128)(2,1)S(1)}, bf16[128,128]{1,0:T(8,128)(2,1)}, u32[]{:S(2)}) copy-start(bf16[128,128]{1,0:T(8,128)(2,1)} %constant.7.clone.basis_high) | copy-start | bytes 98308
  71.5 27.4 %all-to-all-start.2 = ((f32[128,1,384]{2,1,0:T(1,128)}), f32[128,1,384]{2,1,0:T(1,128)S(1)}, u32[]{:S(2)}, u32[]{:S(2)}) async-start(f32[128,1,384]{2,1,0:T(1,128)} %bitcast.3), calls=%async_computation.2 | async-start | bytes 393216 | tf_op jit(solution)/shard_map/all_to_all | solution.py:590
  78.8 3.6 %collective-permute-start.6 = (f32[32,128]{1,0:T(8,128)S(1)}, f32[32,128]{1,0:T(8,128)S(1)}, u32[]{:S(2)}, u32[]{:S(2)}) collective-permute-start(f32[32,128]{1,0:T(8,128)S(1)} %collective-permute-done.5.y_both), channel_id=1, source_target_pairs={{8,0},{11,3},{12,4},{15,7},{112,120},{115,123},{116,124},{119,127}... | collective-permute-start | bytes 49160 | tf_op jit(solution)/shard_map/ppermute | solution.py:582
  82.4 16.5 %copy-start.4 = (f32[64,64]{1,0:T(8,128)S(1)}, f32[64,64]{1,0:T(8,128)}, u32[]{:S(2)}) copy-start(f32[64,64]{1,0:T(8,128)} %back.3) | copy-start | bytes 49156

commit v14 on v13

--- a/solution.py
+++ b/solution.py
@@ -87,7 +87,7 @@
     return ((gx % 16 == 0) | (gx % 16 == 15)) & ((gy % 4 == 0) | (gy % 4 == 3))
 
 
-def edges_kernel(state, planes, x_even, x_odd, y_even, y_odd, flat):
+def edges_kernel(state, planes, x_even, x_odd, y_even, y_odd, y_pair, flat):
     place = position()
     even_x = place[0] % 2 == 0
     even_y = place[1] % 2 == 0
@@ -110,6 +110,8 @@
     y_even[0:16, :] = jnp.where(even_y, high, low)
     y_odd[...] = jnp.where(even_y, low, high)
     x_even[pl.ds(5 * LEVELS, 16), :] = jnp.where(even_y, low, high)
+    y_pair[0:16, :] = jnp.where(even_y, low, high)
+    y_pair[16:32, :] = jnp.zeros((16, LANES), F32)
 
 
 def column_of(row):
@@ -603,9 +605,9 @@
     basis_high, basis_low = split_table(np.ascontiguousarray(basis.T))
     square_row = np.ascontiguousarray(np.broadcast_to(np.concatenate([square, square]), (8, total_east)))
 
-    planes, x_even, x_odd, y_even, y_odd = call(
+    planes, x_even, x_odd, y_even, y_odd, y_pair = call(
         edges_kernel,
-        [(16 * LEVELS, LANES), (5 * LEVELS + 16, LANES), (5 * LEVELS, LANES), (16, LANES), (16, LANES)],
+        [(16 * LEVELS, LANES), (5 * LEVELS + 16, LANES), (5 * LEVELS, LANES), (16, LANES), (16, LANES), (32, LANES)],
         [state],
         "edges",
         scratch=[(LANES, LANES)],
@@ -613,7 +615,7 @@
     got_x_even = swap(x_even, "gx", 0)
     got_x_far = swap_odd_x(x_odd, True)
     got_y_odd = swap_odd_y(y_odd, False)
-    y_both = jnp.concatenate([y_odd, got_x_even[5 * LEVELS :]], axis=0)
+    y_both = y_pair.at[16:].set(got_x_even[5 * LEVELS :])
     y_both, x_odd, y_even = lax.optimization_barrier((y_both, x_odd, y_even))
     got_y_both = swap_odd_y(y_both, True)
     got_x_near = swap_odd_x(x_odd, False)

time: 101 us -> 101 us (level)
  no operation moved by 1% of the time
where the time goes in v14:
time: 101 us; the launch traced here: 100 us
  starting transfers between devices  37.6 us (37%)
  blocking collectives  36.7 us (36%)
  waiting for transfers between devices  19.7 us (20%)
  Pallas kernels  4.69 us (5%)
  local copies, waits for them, and re-layouts  1.12 us (1%)
    all_to_all x1, blocking collectives, exchange(): lax.all_to_all(shaped, ('gx', 'gy'), 0, 0, tiled=True, axis_index_groups=...  30.1 us
    all_to_all x1, waiting for transfers between devices, exchange(): lax.all_to_all(shaped, ('gx', 'gy'), 0, 0, tiled=True, axis_index_groups=...  16.4 us
    ppermute x2, starting transfers between devices, swap_odd_y(): return lax.ppermute(values, ('gx', 'gy'), pairs)  13.3 us
    ppermute x2, starting transfers between devices, swap(): return lax.ppermute(values, axis, pairs)  10.7 us
    all_to_all x1, starting transfers between devices, exchange(): lax.all_to_all(shaped, ('gx', 'gy'), 0, 0, tiled=True, axis_index_groups=...  7.31 us
    all_to_all x1, blocking collectives, on_device(): lax.all_to_all(moments.reshape(4, 4, total_east), 'gy', 0, 0, tiled=True,...  6.57 us
    pallas_call x7, Pallas kernels, call(): pl.pallas_call(kernel, out_shape=[jax.ShapeDtypeStruct(s, F32) for s in s...  4.69 us
    ppermute x2, starting transfers between devices, swap_odd_x(): return lax.ppermute(values, 'gx', pairs)  3.5 us
  transfers between devices with their start and end apart: 8, of which 3 were waited for; matrix products, arithmetic and copies ran while one was open for 0% of the time, Pallas kernels for 1%

profile of v14, /device:TPU:1, one launch (start us, length us, event | category | flops | bytes accessed | tf_op | source)
XLA Modules:
  0.0 100.1 jit_solution(13344926842625977455)
XLA Ops:
  0.0 0.0 copy-start
  0.0 1.0 %copy-done = f32[4,64,4,128]{3,2,1,0:T(4,128)S(1)} copy-done((f32[4,64,4,128]{3,2,1,0:T(4,128)S(1)}, f32[4,64,4,128]{3,2,1,0:T(4,128)}, u32[]{:S(2)}) %copy-start) | copy-done | bytes 524312
  1.0 0.0 copy-start.5
  1.0 0.0 copy-start.6
  1.0 0.3 edges.1
  1.3 8.8 %collective-permute-start = (f32[336,128]{1,0:T(8,128)S(1)}, f32[336,128]{1,0:T(8,128)S(1)}, u32[]{:S(2)}, u32[]{:S(2)}) collective-permute-start(f32[336,128]{1,0:T(8,128)S(1)} %get-tuple-element.44), channel_id=1, source_target_pairs={{0,8},{8,0},{16,24},{24,16},{32,40},{40,32},{48,56},{56,48},{64,72... | collective-permute-start | bytes 516104 | tf_op jit(solution)/shard_map/ppermute | solution.py:552
  10.1 0.0 copy-start.10
  10.1 0.0 copy-start.8
  10.1 0.0 copy-start.9
  10.2 0.8 collective-permute-start.4
  11.0 0.7 collective-permute-start.1
  11.6 0.0 copy-done.10
  11.7 0.0 copy-done.8
  11.7 0.0 copy-done.9
  11.7 0.1 pad_maximum_fusion
  11.8 0.0 collective-permute-done.x_even
  11.8 0.0 copy-start.7
  11.8 12.5 %collective-permute-start.5 = (f32[32,128]{1,0:T(8,128)S(1)}, f32[32,128]{1,0:T(8,128)S(1)}, u32[]{:S(2)}, u32[]{:S(2)}) collective-permute-start(f32[32,128]{1,0:T(8,128)S(1)} %slice_dynamic-update-slice_fusion), channel_id=1, source_target_pairs={{11,12},{12,11},{15,8},{8,15},{115,116},{116,115},{119,112},{112,1... | collective-permute-start | bytes 49160 | tf_op jit(solution)/shard_map/ppermute | solution.py:573
  24.3 2.8 %collective-permute-start.2 = (f32[320,128]{1,0:T(8,128)S(1)}, f32[320,128]{1,0:T(8,128)S(1)}, u32[]{:S(2)}, u32[]{:S(2)}) collective-permute-start(f32[320,128]{1,0:T(8,128)S(1)} %get-tuple-element.49), channel_id=1, source_target_pairs={{8,16},{16,8},{24,32},{32,24},{40,48},{48,40},{56,64},{64,56},{72,... | collective-permute-start | bytes 491528 | tf_op jit(solution)/shard_map/ppermute | solution.py:562
  27.1 0.0 copy-done.5
  27.1 0.0 copy-done.6
  27.1 0.0 copy-done.7
  27.2 0.0 copy-start.3
  27.2 0.8 inner.1
  28.0 1.9 %collective-permute-start.3 = (f32[16,128]{1,0:T(8,128)S(1)}, f32[16,128]{1,0:T(8,128)S(1)}, u32[]{:S(2)}, u32[]{:S(2)}) collective-permute-start(f32[16,128]{1,0:T(8,128)S(1)} %get-tuple-element.50), channel_id=1, source_target_pairs={{0,1},{1,0},{2,3},{3,2},{4,5},{5,4},{6,7},{7,6},{8,9},{9,8},{10,11... | collective-permute-start | bytes 24584 | tf_op jit(solution)/shard_map/ppermute | solution.py:552
  29.9 0.0 collective-permute-done.4.y_odd
  29.9 0.0 collective-permute-done.1.x_far
  29.9 2.4 %collective-permute-done.3.y_even = f32[16,128]{1,0:T(8,128)S(1)} collective-permute-done((f32[16,128]{1,0:T(8,128)S(1)}, f32[16,128]{1,0:T(8,128)S(1)}, u32[]{:S(2)}, u32[]{:S(2)}) %collective-permute-start.3) | collective-permute-done | bytes 8224 | tf_op jit(solution)/shard_map/ppermute | solution.py:552
  32.4 0.0 collective-permute-done.5.y_both
  32.4 0.0 collective-permute-done.2.x_near
  32.4 0.0 copy-done.3
  32.4 0.7 outer.1
  33.1 0.0 copy-start.1
  33.1 0.0 copy-start.2
  33.1 30.1 %all_to_all.15 = f32[128,1,384]{2,1,0:T(1,128)S(1)} all-to-all(f32[128,1,384]{2,1,0:T(1,128)S(1)} %bitcast.6), channel_id=1, replica_groups={{0,4,8,12,16,20,24,28,32,36,40,44,48,52,56,60,64,68,72,76,80,84,88,92,9..., dimensions={0} | all-to-all | bytes 393216 | tf_op jit(solution)/shard_map/all_to_all | solution.py:592
  63.2 0.0 copy-done.1
  63.2 0.0 copy-done.2
  63.2 0.6 solve.1
  63.8 6.6 %all_to_all.16 = f32[4,4,256]{2,1,0:T(4,128)S(1)} all-to-all(f32[4,4,256]{2,1,0:T(4,128)S(1)} %reshape.53), channel_id=1, replica_groups={{0,1,2,3},{4,5,6,7},{8,9,10,11},{12,13,14,15},{16,17,18,19},{20,21,22,2..., dimensions={0} | all-to-all | bytes 32768 | tf_op jit(solution)/shard_map/all_to_all | solution.py:662
  70.4 1.1 %back.2 = f32[384,128]{1,0:T(8,128)} custom-call(f32[128,256]{1,0:T(8,128)S(1)} %get-tuple-element.57.local, f32[16,256]{1,0:T(8,128)S(1)} %reshape.54.moments, bf16[128,128]{1,0:T(8,128)(2,1)S(1)} %copy-done.2, bf16[128,128]{1,0:T(8,128)(2,1)S(1)} %copy-done.1, f32[72,256]{1,0:T(8,128)S(1)} %get-tuple-element.55.by_row, ...), custom_call_target="tpu_custom_call" | custom-call | tf_op jit(solution)/shard_map/back/pallas_call | solution.py:534
  71.5 7.3 %all-to-all-start.2 = ((f32[128,1,384]{2,1,0:T(1,128)}), f32[128,1,384]{2,1,0:T(1,128)S(1)}, u32[]{:S(2)}, u32[]{:S(2)}) async-start(f32[128,1,384]{2,1,0:T(1,128)} %bitcast.3), calls=%async_computation.2 | async-start | bytes 393216 | tf_op jit(solution)/shard_map/all_to_all | solution.py:592
  78.8 2.8 %collective-permute-start.6 = (f32[32,128]{1,0:T(8,128)S(1)}, f32[32,128]{1,0:T(8,128)S(1)}, u32[]{:S(2)}, u32[]{:S(2)}) collective-permute-start(f32[32,128]{1,0:T(8,128)S(1)} %collective-permute-done.5.y_both), channel_id=1, source_target_pairs={{8,0},{11,3},{12,4},{15,7},{112,120},{115,123},{116,124},{119,127}... | collective-permute-start | bytes 49160 | tf_op jit(solution)/shard_map/ppermute | solution.py:584
  81.6 0.8 collective-permute-done.6.relayed
  82.4 0.0 copy-start.4
  82.5 16.4 %all-to-all-done.2 = f32[128,1,384]{2,1,0:T(1,128)S(1)} async-done(((f32[128,1,384]{2,1,0:T(1,128)}), f32[128,1,384]{2,1,0:T(1,128)S(1)}, u32[]{:S(2)}, u32[]{:S(2)}) %all-to-all-start.2) | async-done | bytes 196640 | tf_op jit(solution)/shard_map/all_to_all | solution.py:592
  98.9 0.0 copy-done.4
  98.9 1.2 %final.1 = f32[1024,128]{1,0:T(8,128)} custom-call(f32[384,128]{1,0:T(8,128)S(1)} %bitcast.8, f32[128,128]{1,0:T(8,128)S(1)} %get-tuple-element.63.middle, f32[1024,128]{1,0:T(8,128)S(1)} %get-tuple-element.64.star, f32[64,64]{1,0:T(8,128)S(1)} %copy-done.4, f32[192,128]{1,0:T(8,128)S(1)} %get-tuple-element.53.by_level), custom_call_target="tpu_custom_call" | custom-call | tf_op jit(solution)/shard_map/final/pallas_call | solution.py:534
  (5 shorter events, 0.1 us)
Async XLA Ops:
  0.0 1.0 %copy-start = (f32[4,64,4,128]{3,2,1,0:T(4,128)S(1)}, f32[4,64,4,128]{3,2,1,0:T(4,128)}, u32[]{:S(2)}) copy-start(f32[4,64,4,128]{3,2,1,0:T(4,128)} %param.13) | copy-start | bytes 1572868
  1.0 26.1 %copy-start.5 = (bf16[256,256]{1,0:T(8,128)(2,1)S(1)}, bf16[256,256]{1,0:T(8,128)(2,1)}, u32[]{:S(2)}) copy-start(bf16[256,256]{1,0:T(8,128)(2,1)} %layer_in.1) | copy-start | bytes 393220
  1.0 26.1 %copy-start.6 = (bf16[256,128]{1,0:T(8,128)(2,1)S(1)}, bf16[256,128]{1,0:T(8,128)(2,1)}, u32[]{:S(2)}) copy-start(bf16[256,128]{1,0:T(8,128)(2,1)} %layer_out.1) | copy-start | bytes 196612
  1.3 10.4 %collective-permute-start = (f32[336,128]{1,0:T(8,128)S(1)}, f32[336,128]{1,0:T(8,128)S(1)}, u32[]{:S(2)}, u32[]{:S(2)}) collective-permute-start(f32[336,128]{1,0:T(8,128)S(1)} %get-tuple-element.44), channel_id=1, source_target_pairs={{0,8},{8,0},{16,24},{24,16},{32,40},{40,32},{48,56},{56,48},{64,72... | collective-permute-start | bytes 516104 | tf_op jit(solution)/shard_map/ppermute | solution.py:552
  10.1 1.5 %copy-start.10 = (f32[64]{0:T(128)S(1)}, f32[64]{0:T(128)}, u32[]{:S(2)}) copy-start(f32[64]{0:T(128)} %param.20) | copy-start | bytes 772
  10.1 1.5 %copy-start.8 = (f32[256]{0:T(256)S(1)}, f32[256]{0:T(256)}, u32[]{:S(2)}) copy-start(f32[256]{0:T(256)} %param.16) | copy-start | bytes 3076
  10.1 1.5 %copy-start.9 = (f32[64]{0:T(128)S(1)}, f32[64]{0:T(128)}, u32[]{:S(2)}) copy-start(f32[64]{0:T(128)} %param.14) | copy-start | bytes 772
  10.2 19.8 %collective-permute-start.4 = (f32[16,128]{1,0:T(8,128)S(1)}, f32[16,128]{1,0:T(8,128)S(1)}, u32[]{:S(2)}, u32[]{:S(2)}) collective-permute-start(f32[16,128]{1,0:T(8,128)S(1)} %get-tuple-element.51), channel_id=1, source_target_pairs={{1,2},{2,1},{5,6},{6,5},{9,10},{10,9},{13,14},{14,13},{17,18},{18,... | collective-permute-start | bytes 24584 | tf_op jit(solution)/shard_map/ppermute | solution.py:573
  11.0 19.0 %collective-permute-start.1 = (f32[320,128]{1,0:T(8,128)S(1)}, f32[320,128]{1,0:T(8,128)S(1)}, u32[]{:S(2)}, u32[]{:S(2)}) collective-permute-start(f32[320,128]{1,0:T(8,128)S(1)} %get-tuple-element.49), channel_id=1, source_target_pairs={{120,128},{128,120},{248,256},{256,248},{376,384},{384,376},{504,0... | collective-permute-start | bytes 491528 | tf_op jit(solution)/shard_map/ppermute | solution.py:562
  11.8 15.4 %copy-start.7 = (f32[8,256]{1,0:T(8,128)S(1)}, f32[8,256]{1,0:T(8,128)}, u32[]{:S(2)}) copy-start(f32[8,256]{1,0:T(8,128)} %constant.35.clone.square_row) | copy-start | bytes 24580
  11.8 20.6 %collective-permute-start.5 = (f32[32,128]{1,0:T(8,128)S(1)}, f32[32,128]{1,0:T(8,128)S(1)}, u32[]{:S(2)}, u32[]{:S(2)}) collective-permute-start(f32[32,128]{1,0:T(8,128)S(1)} %slice_dynamic-update-slice_fusion), channel_id=1, source_target_pairs={{11,12},{12,11},{15,8},{8,15},{115,116},{116,115},{119,112},{112,1... | collective-permute-start | bytes 49160 | tf_op jit(solution)/shard_map/ppermute | solution.py:573
  24.3 8.1 %collective-permute-start.2 = (f32[320,128]{1,0:T(8,128)S(1)}, f32[320,128]{1,0:T(8,128)S(1)}, u32[]{:S(2)}, u32[]{:S(2)}) collective-permute-start(f32[320,128]{1,0:T(8,128)S(1)} %get-tuple-element.49), channel_id=1, source_target_pairs={{8,16},{16,8},{24,32},{32,24},{40,48},{48,40},{56,64},{64,56},{72,... | collective-permute-start | bytes 491528 | tf_op jit(solution)/shard_map/ppermute | solution.py:562
  27.2 5.2 %copy-start.3 = (f32[64,64]{1,0:T(8,128)S(1)}, f32[64,64]{1,0:T(8,128)}, u32[]{:S(2)}) copy-start(f32[64,64]{1,0:T(8,128)} %forward.3) | copy-start | bytes 49156
  28.0 4.4 %collective-permute-start.3 = (f32[16,128]{1,0:T(8,128)S(1)}, f32[16,128]{1,0:T(8,128)S(1)}, u32[]{:S(2)}, u32[]{:S(2)}) collective-permute-start(f32[16,128]{1,0:T(8,128)S(1)} %get-tuple-element.50), channel_id=1, source_target_pairs={{0,1},{1,0},{2,3},{3,2},{4,5},{5,4},{6,7},{7,6},{8,9},{9,8},{10,11... | collective-permute-start | bytes 24584 | tf_op jit(solution)/shard_map/ppermute | solution.py:552
  33.1 30.1 %copy-start.1 = (bf16[128,128]{1,0:T(8,128)(2,1)S(1)}, bf16[128,128]{1,0:T(8,128)(2,1)}, u32[]{:S(2)}) copy-start(bf16[128,128]{1,0:T(8,128)(2,1)} %constant.37.clone.basis_low) | copy-start | bytes 98308
  33.1 30.1 %copy-start.2 = (bf16[128,128]{1,0:T(8,128)(2,1)S(1)}, bf16[128,128]{1,0:T(8,128)(2,1)}, u32[]{:S(2)}) copy-start(bf16[128,128]{1,0:T(8,128)(2,1)} %constant.36.clone.basis_high) | copy-start | bytes 98308
  71.5 27.4 %all-to-all-start.2 = ((f32[128,1,384]{2,1,0:T(1,128)}), f32[128,1,384]{2,1,0:T(1,128)S(1)}, u32[]{:S(2)}, u32[]{:S(2)}) async-start(f32[128,1,384]{2,1,0:T(1,128)} %bitcast.3), calls=%async_computation.2 | async-start | bytes 393216 | tf_op jit(solution)/shard_map/all_to_all | solution.py:592
  78.8 3.6 %collective-permute-start.6 = (f32[32,128]{1,0:T(8,128)S(1)}, f32[32,128]{1,0:T(8,128)S(1)}, u32[]{:S(2)}, u32[]{:S(2)}) collective-permute-start(f32[32,128]{1,0:T(8,128)S(1)} %collective-permute-done.5.y_both), channel_id=1, source_target_pairs={{8,0},{11,3},{12,4},{15,7},{112,120},{115,123},{116,124},{119,127}... | collective-permute-start | bytes 49160 | tf_op jit(solution)/shard_map/ppermute | solution.py:584
  82.4 16.5 %copy-start.4 = (f32[64,64]{1,0:T(8,128)S(1)}, f32[64,64]{1,0:T(8,128)}, u32[]{:S(2)}) copy-start(f32[64,64]{1,0:T(8,128)} %back.3) | copy-start | bytes 49156

commit v15 on v13

--- a/solution.py
+++ b/solution.py
@@ -60,8 +60,9 @@
 
 
 def dot3(left, right):
-    dot = lambda a, b: jnp.dot(a, b, preferred_element_type=F32)
-    return dot(left[0], right[0]) + (dot(left[0], right[1]) + dot(left[1], right[0]))
+    long_left = jnp.concatenate([left[1], left[0], left[0]], axis=1)
+    long_right = jnp.concatenate([right[0], right[1], right[0]], axis=0)
+    return jnp.dot(long_left, long_right, preferred_element_type=F32)
 
 
 def level_difference(values):

time: 101 us -> 101 us (level)
  no operation moved by 1% of the time
where the time goes in v15:
time: 101 us; the launch traced here: 100 us
  starting transfers between devices  37.6 us (37%)
  blocking collectives  36.8 us (36%)
  waiting for transfers between devices  19.7 us (20%)
  Pallas kernels  4.64 us (5%)
  local copies, waits for them, and re-layouts  1.12 us (1%)
    all_to_all x1, blocking collectives, exchange(): lax.all_to_all(shaped, ('gx', 'gy'), 0, 0, tiled=True, axis_index_groups=...  30.2 us
    all_to_all x1, waiting for transfers between devices, exchange(): lax.all_to_all(shaped, ('gx', 'gy'), 0, 0, tiled=True, axis_index_groups=...  16.4 us
    ppermute x2, starting transfers between devices, swap_odd_y(): return lax.ppermute(values, ('gx', 'gy'), pairs)  13.2 us
    ppermute x2, starting transfers between devices, swap(): return lax.ppermute(values, axis, pairs)  10.8 us
    all_to_all x1, starting transfers between devices, exchange(): lax.all_to_all(shaped, ('gx', 'gy'), 0, 0, tiled=True, axis_index_groups=...  7.31 us
    all_to_all x1, blocking collectives, on_device(): lax.all_to_all(moments.reshape(4, 4, total_east), 'gy', 0, 0, tiled=True,...  6.57 us
    pallas_call x7, Pallas kernels, call(): pl.pallas_call(kernel, out_shape=[jax.ShapeDtypeStruct(s, F32) for s in s...  4.64 us
    ppermute x2, starting transfers between devices, swap_odd_x(): return lax.ppermute(values, 'gx', pairs)  3.5 us
  transfers between devices with their start and end apart: 8, of which 3 were waited for; matrix products, arithmetic and copies ran while one was open for 0% of the time, Pallas kernels for 1%

profile of v15, /device:TPU:1, one launch (start us, length us, event | category | flops | bytes accessed | tf_op | source)
XLA Modules:
  0.0 100.2 jit_solution(17108935750920358763)
XLA Ops:
  0.0 0.0 copy-start
  0.0 1.0 %copy-done = f32[4,64,4,128]{3,2,1,0:T(4,128)S(1)} copy-done((f32[4,64,4,128]{3,2,1,0:T(4,128)S(1)}, f32[4,64,4,128]{3,2,1,0:T(4,128)}, u32[]{:S(2)}) %copy-start) | copy-done | bytes 524312
  1.0 0.0 copy-start.8
  1.0 0.0 copy-start.9
  1.0 0.0 copy-start.10
  1.0 0.0 copy-start.5
  1.1 0.0 copy-start.7
  1.1 0.3 edges.1
  1.3 0.0 copy-start.6
  1.4 8.9 %collective-permute-start = (f32[336,128]{1,0:T(8,128)S(1)}, f32[336,128]{1,0:T(8,128)S(1)}, u32[]{:S(2)}, u32[]{:S(2)}) collective-permute-start(f32[336,128]{1,0:T(8,128)S(1)} %get-tuple-element.31), channel_id=1, source_target_pairs={{0,8},{8,0},{16,24},{24,16},{32,40},{40,32},{48,56},{56,48},{64,72... | collective-permute-start | bytes 516104 | tf_op jit(solution)/shard_map/ppermute | solution.py:551
  10.3 0.7 collective-permute-start.4
  11.0 0.7 collective-permute-start.1
  11.6 0.0 copy-done.8
  11.6 0.0 copy-done.9
  11.7 0.0 copy-done.10
  11.7 0.1 pad_maximum_fusion.1
  11.7 0.0 collective-permute-done.x_even
  11.8 12.5 %collective-permute-start.5 = (f32[32,128]{1,0:T(8,128)S(1)}, f32[32,128]{1,0:T(8,128)S(1)}, u32[]{:S(2)}, u32[]{:S(2)}) collective-permute-start(f32[32,128]{1,0:T(8,128)S(1)} %pad_maximum_fusion), channel_id=1, source_target_pairs={{11,12},{12,11},{15,8},{8,15},{115,116},{116,115},{119,112},{112,1... | collective-permute-start | bytes 49160 | tf_op jit(solution)/shard_map/ppermute | solution.py:572
  24.3 2.8 %collective-permute-start.2 = (f32[320,128]{1,0:T(8,128)S(1)}, f32[320,128]{1,0:T(8,128)S(1)}, u32[]{:S(2)}, u32[]{:S(2)}) collective-permute-start(f32[320,128]{1,0:T(8,128)S(1)} %get-tuple-element.36), channel_id=1, source_target_pairs={{8,16},{16,8},{24,32},{32,24},{40,48},{48,40},{56,64},{64,56},{72,... | collective-permute-start | bytes 491528 | tf_op jit(solution)/shard_map/ppermute | solution.py:561
  27.1 0.0 copy-done.5
  27.1 0.0 copy-done.7
  27.1 0.0 copy-done.6
  27.2 0.0 copy-start.3
  27.2 0.8 inner.1
  28.0 1.9 %collective-permute-start.3 = (f32[16,128]{1,0:T(8,128)S(1)}, f32[16,128]{1,0:T(8,128)S(1)}, u32[]{:S(2)}, u32[]{:S(2)}) collective-permute-start(f32[16,128]{1,0:T(8,128)S(1)} %get-tuple-element.37), channel_id=1, source_target_pairs={{0,1},{1,0},{2,3},{3,2},{4,5},{5,4},{6,7},{7,6},{8,9},{9,8},{10,11... | collective-permute-start | bytes 24584 | tf_op jit(solution)/shard_map/ppermute | solution.py:551
  29.9 0.0 collective-permute-done.4.y_odd
  29.9 0.0 collective-permute-done.1.x_far
  29.9 2.4 %collective-permute-done.3.y_even = f32[16,128]{1,0:T(8,128)S(1)} collective-permute-done((f32[16,128]{1,0:T(8,128)S(1)}, f32[16,128]{1,0:T(8,128)S(1)}, u32[]{:S(2)}, u32[]{:S(2)}) %collective-permute-start.3) | collective-permute-done | bytes 8224 | tf_op jit(solution)/shard_map/ppermute | solution.py:551
  32.4 0.0 collective-permute-done.5.y_both
  32.4 0.0 collective-permute-done.2.x_near
  32.4 0.0 copy-done.3
  32.4 0.6 outer.1
  33.0 0.0 copy-start.1
  33.0 0.0 copy-start.2
  33.1 30.2 %all_to_all.15 = f32[128,1,384]{2,1,0:T(1,128)S(1)} all-to-all(f32[128,1,384]{2,1,0:T(1,128)S(1)} %bitcast.6), channel_id=1, replica_groups={{0,4,8,12,16,20,24,28,32,36,40,44,48,52,56,60,64,68,72,76,80,84,88,92,9..., dimensions={0} | all-to-all | bytes 393216 | tf_op jit(solution)/shard_map/all_to_all | solution.py:591
  63.3 0.0 copy-done.1
  63.3 0.0 copy-done.2
  63.3 0.6 solve.1
  63.9 6.6 %all_to_all.16 = f32[4,4,256]{2,1,0:T(4,128)S(1)} all-to-all(f32[4,4,256]{2,1,0:T(4,128)S(1)} %reshape.27), channel_id=1, replica_groups={{0,1,2,3},{4,5,6,7},{8,9,10,11},{12,13,14,15},{16,17,18,19},{20,21,22,2..., dimensions={0} | all-to-all | bytes 32768 | tf_op jit(solution)/shard_map/all_to_all | solution.py:661
  70.5 1.1 %back.2 = f32[384,128]{1,0:T(8,128)} custom-call(f32[128,256]{1,0:T(8,128)S(1)} %get-tuple-element.43.local, f32[16,256]{1,0:T(8,128)S(1)} %reshape.28.moments, bf16[128,128]{1,0:T(8,128)(2,1)S(1)} %copy-done.2, bf16[128,128]{1,0:T(8,128)(2,1)S(1)} %copy-done.1, f32[72,256]{1,0:T(8,128)S(1)} %get-tuple-element.41.by_row, ...), custom_call_target="tpu_custom_call" | custom-call | tf_op jit(solution)/shard_map/back/pallas_call | solution.py:533
  71.6 7.3 %all-to-all-start.2 = ((f32[128,1,384]{2,1,0:T(1,128)}), f32[128,1,384]{2,1,0:T(1,128)S(1)}, u32[]{:S(2)}, u32[]{:S(2)}) async-start(f32[128,1,384]{2,1,0:T(1,128)} %bitcast.3), calls=%async_computation.2 | async-start | bytes 393216 | tf_op jit(solution)/shard_map/all_to_all | solution.py:591
  78.9 2.8 %collective-permute-start.6 = (f32[32,128]{1,0:T(8,128)S(1)}, f32[32,128]{1,0:T(8,128)S(1)}, u32[]{:S(2)}, u32[]{:S(2)}) collective-permute-start(f32[32,128]{1,0:T(8,128)S(1)} %collective-permute-done.5.y_both), channel_id=1, source_target_pairs={{8,0},{11,3},{12,4},{15,7},{112,120},{115,123},{116,124},{119,127}... | collective-permute-start | bytes 49160 | tf_op jit(solution)/shard_map/ppermute | solution.py:583
  81.7 0.8 collective-permute-done.6.relayed
  82.5 0.0 copy-start.4
  82.6 16.4 %all-to-all-done.2 = f32[128,1,384]{2,1,0:T(1,128)S(1)} async-done(((f32[128,1,384]{2,1,0:T(1,128)}), f32[128,1,384]{2,1,0:T(1,128)S(1)}, u32[]{:S(2)}, u32[]{:S(2)}) %all-to-all-start.2) | async-done | bytes 196640 | tf_op jit(solution)/shard_map/all_to_all | solution.py:591
  99.0 0.0 copy-done.4
  99.0 1.2 %final.1 = f32[1024,128]{1,0:T(8,128)} custom-call(f32[384,128]{1,0:T(8,128)S(1)} %bitcast.8, f32[128,128]{1,0:T(8,128)S(1)} %get-tuple-element.49.middle, f32[1024,128]{1,0:T(8,128)S(1)} %get-tuple-element.50.star, f32[64,64]{1,0:T(8,128)S(1)} %copy-done.4, f32[192,128]{1,0:T(8,128)S(1)} %get-tuple-element.39.by_level), custom_call_target="tpu_custom_call" | custom-call | tf_op jit(solution)/shard_map/final/pallas_call | solution.py:533
  (6 shorter events, 0.1 us)
Async XLA Ops:
  0.0 1.0 %copy-start = (f32[4,64,4,128]{3,2,1,0:T(4,128)S(1)}, f32[4,64,4,128]{3,2,1,0:T(4,128)}, u32[]{:S(2)}) copy-start(f32[4,64,4,128]{3,2,1,0:T(4,128)} %param.11) | copy-start | bytes 1572868
  1.0 10.6 %copy-start.8 = (f32[256]{0:T(256)S(1)}, f32[256]{0:T(256)}, u32[]{:S(2)}) copy-start(f32[256]{0:T(256)} %param.14) | copy-start | bytes 3076
  1.0 10.6 %copy-start.9 = (f32[64]{0:T(128)S(1)}, f32[64]{0:T(128)}, u32[]{:S(2)}) copy-start(f32[64]{0:T(128)} %param.12) | copy-start | bytes 772
  1.0 10.6 %copy-start.10 = (f32[64]{0:T(128)S(1)}, f32[64]{0:T(128)}, u32[]{:S(2)}) copy-start(f32[64]{0:T(128)} %param.18) | copy-start | bytes 772
  1.0 26.1 %copy-start.5 = (bf16[256,256]{1,0:T(8,128)(2,1)S(1)}, bf16[256,256]{1,0:T(8,128)(2,1)}, u32[]{:S(2)}) copy-start(bf16[256,256]{1,0:T(8,128)(2,1)} %layer_in.1) | copy-start | bytes 393220
  1.1 26.1 %copy-start.7 = (f32[8,256]{1,0:T(8,128)S(1)}, f32[8,256]{1,0:T(8,128)}, u32[]{:S(2)}) copy-start(f32[8,256]{1,0:T(8,128)} %constant.6.clone.square_row) | copy-start | bytes 24580
  1.3 25.8 %copy-start.6 = (bf16[256,128]{1,0:T(8,128)(2,1)S(1)}, bf16[256,128]{1,0:T(8,128)(2,1)}, u32[]{:S(2)}) copy-start(bf16[256,128]{1,0:T(8,128)(2,1)} %layer_out.1) | copy-start | bytes 196612
  1.4 10.4 %collective-permute-start = (f32[336,128]{1,0:T(8,128)S(1)}, f32[336,128]{1,0:T(8,128)S(1)}, u32[]{:S(2)}, u32[]{:S(2)}) collective-permute-start(f32[336,128]{1,0:T(8,128)S(1)} %get-tuple-element.31), channel_id=1, source_target_pairs={{0,8},{8,0},{16,24},{24,16},{32,40},{40,32},{48,56},{56,48},{64,72... | collective-permute-start | bytes 516104 | tf_op jit(solution)/shard_map/ppermute | solution.py:551
  10.3 19.6 %collective-permute-start.4 = (f32[16,128]{1,0:T(8,128)S(1)}, f32[16,128]{1,0:T(8,128)S(1)}, u32[]{:S(2)}, u32[]{:S(2)}) collective-permute-start(f32[16,128]{1,0:T(8,128)S(1)} %get-tuple-element.30), channel_id=1, source_target_pairs={{1,2},{2,1},{5,6},{6,5},{9,10},{10,9},{13,14},{14,13},{17,18},{18,... | collective-permute-start | bytes 24584 | tf_op jit(solution)/shard_map/ppermute | solution.py:572
  11.0 19.0 %collective-permute-start.1 = (f32[320,128]{1,0:T(8,128)S(1)}, f32[320,128]{1,0:T(8,128)S(1)}, u32[]{:S(2)}, u32[]{:S(2)}) collective-permute-start(f32[320,128]{1,0:T(8,128)S(1)} %get-tuple-element.36), channel_id=1, source_target_pairs={{120,128},{128,120},{248,256},{256,248},{376,384},{384,376},{504,0... | collective-permute-start | bytes 491528 | tf_op jit(solution)/shard_map/ppermute | solution.py:561
  11.8 20.6 %collective-permute-start.5 = (f32[32,128]{1,0:T(8,128)S(1)}, f32[32,128]{1,0:T(8,128)S(1)}, u32[]{:S(2)}, u32[]{:S(2)}) collective-permute-start(f32[32,128]{1,0:T(8,128)S(1)} %pad_maximum_fusion), channel_id=1, source_target_pairs={{11,12},{12,11},{15,8},{8,15},{115,116},{116,115},{119,112},{112,1... | collective-permute-start | bytes 49160 | tf_op jit(solution)/shard_map/ppermute | solution.py:572
  24.3 8.1 %collective-permute-start.2 = (f32[320,128]{1,0:T(8,128)S(1)}, f32[320,128]{1,0:T(8,128)S(1)}, u32[]{:S(2)}, u32[]{:S(2)}) collective-permute-start(f32[320,128]{1,0:T(8,128)S(1)} %get-tuple-element.36), channel_id=1, source_target_pairs={{8,16},{16,8},{24,32},{32,24},{40,48},{48,40},{56,64},{64,56},{72,... | collective-permute-start | bytes 491528 | tf_op jit(solution)/shard_map/ppermute | solution.py:561
  27.2 5.2 %copy-start.3 = (f32[64,64]{1,0:T(8,128)S(1)}, f32[64,64]{1,0:T(8,128)}, u32[]{:S(2)}) copy-start(f32[64,64]{1,0:T(8,128)} %forward.3) | copy-start | bytes 49156
  28.0 4.4 %collective-permute-start.3 = (f32[16,128]{1,0:T(8,128)S(1)}, f32[16,128]{1,0:T(8,128)S(1)}, u32[]{:S(2)}, u32[]{:S(2)}) collective-permute-start(f32[16,128]{1,0:T(8,128)S(1)} %get-tuple-element.37), channel_id=1, source_target_pairs={{0,1},{1,0},{2,3},{3,2},{4,5},{5,4},{6,7},{7,6},{8,9},{9,8},{10,11... | collective-permute-start | bytes 24584 | tf_op jit(solution)/shard_map/ppermute | solution.py:551
  33.0 30.3 %copy-start.1 = (bf16[128,128]{1,0:T(8,128)(2,1)S(1)}, bf16[128,128]{1,0:T(8,128)(2,1)}, u32[]{:S(2)}) copy-start(bf16[128,128]{1,0:T(8,128)(2,1)} %constant.8.clone.basis_low) | copy-start | bytes 98308
  33.0 30.3 %copy-start.2 = (bf16[128,128]{1,0:T(8,128)(2,1)S(1)}, bf16[128,128]{1,0:T(8,128)(2,1)}, u32[]{:S(2)}) copy-start(bf16[128,128]{1,0:T(8,128)(2,1)} %constant.7.clone.basis_high) | copy-start | bytes 98308
  71.6 27.4 %all-to-all-start.2 = ((f32[128,1,384]{2,1,0:T(1,128)}), f32[128,1,384]{2,1,0:T(1,128)S(1)}, u32[]{:S(2)}, u32[]{:S(2)}) async-start(f32[128,1,384]{2,1,0:T(1,128)} %bitcast.3), calls=%async_computation.2 | async-start | bytes 393216 | tf_op jit(solution)/shard_map/all_to_all | solution.py:591
  78.9 3.6 %collective-permute-start.6 = (f32[32,128]{1,0:T(8,128)S(1)}, f32[32,128]{1,0:T(8,128)S(1)}, u32[]{:S(2)}, u32[]{:S(2)}) collective-permute-start(f32[32,128]{1,0:T(8,128)S(1)} %collective-permute-done.5.y_both), channel_id=1, source_target_pairs={{8,0},{11,3},{12,4},{15,7},{112,120},{115,123},{116,124},{119,127}... | collective-permute-start | bytes 49160 | tf_op jit(solution)/shard_map/ppermute | solution.py:583
  82.5 16.5 %copy-start.4 = (f32[64,64]{1,0:T(8,128)S(1)}, f32[64,64]{1,0:T(8,128)}, u32[]{:S(2)}) copy-start(f32[64,64]{1,0:T(8,128)} %back.3) | copy-start | bytes 49156
